TPU v7x, 32 devices: a whole 2x2x4 slice. The times are simulated.
32 devices in a mesh: mem: 16 (over z, x, core), grp: 2 (over y).
Axes of the slice: x: 2, y: 2, z: 4, core: 2. Of those that a mesh axis runs over, the one named last changes fastest.
Arguments:
- queries: bfloat16 [2, 2048, 2048], P('grp', 'mem'), may hold values from -96 to 96
- d_out: bfloat16 [2, 2048, 2048], P('grp', 'mem'), may hold values from -16 to 16
- o_mem: bfloat16 [2, 2048, 2048], P('grp', 'mem'), may hold values from -3 to 3
- local_out: bfloat16 [2, 2048, 2048], P('grp', 'mem'), may hold values from -3 to 3
- mem_keys: bfloat16 [4096, 2048], P('mem'), may hold values from -4 to 4
- mem_values: bfloat16 [4096, 2048], P('mem'), may hold values from -5 to 5
- gate_logit: float32 [16], replicated, may hold values from -2 to 2
- block_ids: int32 [2, 128, 32], P('grp', 'mem'), may hold values from 0 to 255, as said below
Outputs:
- d_query: bfloat16 [2, 2048, 2048], P('grp', 'mem')
- d_gate: float32 [16], replicated
Inputs may be any that keep to these rules, and one draw needn't show every extreme that they name: `block_ids`: each row lists 8 distinct shards in turn, 4 distinct blocks of each in increasing order. The query blocks of one device name each shard at most 4 times, and in every group some shard is named 4 times by the blocks of every device.
All inputs are finite; a program needn't handle non-finite values.
Results may differ from a plain program's by a relative error of at most 0.008.
Values may be sent and summed in bfloat16 or wider, within the bound.
No kernel may reach another device: no remote copies, remote signals or barrier semaphores. Data moves between devices by JAX's collectives and lax.ppermute only.
A program may use at most 64 MiB of HBM per device.

v0:
```python
import math

import jax
import jax.numpy as jnp
from jax import lax
from jax.sharding import PartitionSpec as P

BLK = 16
NSH = 8
PICK = 4


def local(queries, d_out, o_mem, local_out, mem_keys, mem_values, gate_logit, block_ids):
    shards = lax.axis_size("mem")
    groups = lax.axis_size("grp")
    tokens = queries.shape[1]
    width = queries.shape[2]
    heads = gate_logit.shape[0]
    head_dim = width // heads
    blocks_here = mem_keys.shape[0] // BLK
    qblocks = tokens // BLK
    capacity = (qblocks * NSH + shards - 1) // shards
    scale = 1.0 / head_dim**0.5
    sig = jax.nn.sigmoid(gate_logit)
    dout_three = d_out.reshape(tokens, heads, head_dim)
    omem_three = o_mem.reshape(tokens, heads, head_dim)
    local_three = local_out.reshape(tokens, heads, head_dim)
    d_mem = (dout_three.astype(jnp.float32) * sig[:, None]).astype(jnp.bfloat16)
    delta = jnp.einsum("thd,thd->th", d_mem, omem_three, preferred_element_type=jnp.float32).astype(
        jnp.bfloat16
    )
    named = block_ids[0]
    shard_of = named[:, ::PICK] // blocks_here
    targets = jnp.arange(shards, dtype=jnp.int32)
    naming = jnp.sum((shard_of[:, :, None] == targets[None, None, :]).astype(jnp.int32), 1)
    before = jnp.cumsum(naming, 0) - naming
    slot_ids = jnp.arange(capacity, dtype=jnp.int32)
    select = (
        naming[:, :, None] * (before[:, :, None] == slot_ids[None, None, :]).astype(jnp.int32)
    ).astype(jnp.bfloat16)
    wanted = jnp.arange(shards * blocks_here, dtype=jnp.int32).reshape(shards, blocks_here)
    hits = jnp.sum((named[:, :, None, None] == wanted[None, None]).astype(jnp.int32), 1).astype(
        jnp.bfloat16
    )
    query_slots = jnp.einsum(
        "jsc,jrw->scrw",
        select,
        queries[0].reshape(qblocks, BLK, width),
        preferred_element_type=jnp.float32,
    ).astype(jnp.bfloat16)
    dmem_slots = jnp.einsum(
        "jsc,jrw->scrw",
        select,
        d_mem.reshape(qblocks, BLK, width),
        preferred_element_type=jnp.float32,
    ).astype(jnp.bfloat16)
    delta_slots = jnp.einsum(
        "jsc,jrh->scrh",
        select,
        delta.reshape(qblocks, BLK, heads),
        preferred_element_type=jnp.float32,
    ).astype(jnp.bfloat16)
    mask_slots = jnp.einsum(
        "jsc,jsb->scb", select, hits, preferred_element_type=jnp.float32
    ).astype(jnp.bfloat16)
    query_in, dmem_in, delta_in, mask_in = (
        lax.all_to_all(query_slots, "mem", split_axis=0, concat_axis=0, tiled=True),
        lax.all_to_all(dmem_slots, "mem", split_axis=0, concat_axis=0, tiled=True),
        lax.all_to_all(delta_slots, "mem", split_axis=0, concat_axis=0, tiled=True),
        lax.all_to_all(mask_slots, "mem", split_axis=0, concat_axis=0, tiled=True),
    )
    keys_blocked = mem_keys.reshape(blocks_here, BLK, heads, head_dim)
    values_blocked = mem_values.reshape(blocks_here, BLK, heads, head_dim)
    slots_all = shards * capacity

    def block_step(pieces):
        query_part, dmem_part, delta_part, mask_part = pieces
        count = query_part.shape[0]
        chosen = jnp.argsort(-(mask_part > 0.5).astype(jnp.int32), axis=1, stable=True)[:, :PICK]
        keys_sel = keys_blocked[chosen].reshape(count, PICK * BLK, heads, head_dim)
        values_sel = values_blocked[chosen].reshape(count, PICK * BLK, heads, head_dim)
        query_four = query_part.reshape(count, BLK, heads, head_dim)
        dmem_four = dmem_part.reshape(count, BLK, heads, head_dim)
        scores = (
            jnp.einsum("cqhd,ckhd->cqhk", query_four, keys_sel, preferred_element_type=jnp.float32)
            * scale
        )
        high = jnp.max(scores, -1)
        expo = jnp.exp(scores - high[..., None])
        total = jnp.sum(expo, -1)
        dprod = jnp.einsum(
            "cqhd,ckhd->cqhk", dmem_four, values_sel, preferred_element_type=jnp.float32
        )
        dscore = (expo * (dprod - delta_part.astype(jnp.float32)[..., None])).astype(jnp.bfloat16)
        part = (
            jnp.einsum("cqhk,ckhd->cqhd", dscore, keys_sel, preferred_element_type=jnp.float32)
            * scale
        )
        return (part.astype(jnp.bfloat16).reshape(count, BLK, width), high, total)

    per_step = math.gcd(slots_all, 8)
    steps_count = slots_all // per_step
    grouped = (
        query_in.reshape(steps_count, per_step, BLK, width),
        dmem_in.reshape(steps_count, per_step, BLK, width),
        delta_in.reshape(steps_count, per_step, BLK, heads),
        mask_in.reshape(steps_count, per_step, blocks_here),
    )
    part_all, high_all, total_all = lax.map(block_step, grouped)
    part_all = part_all.reshape(shards, capacity, BLK, width)
    high_all = high_all.reshape(shards, capacity, BLK, heads)
    total_all = total_all.reshape(shards, capacity, BLK, heads)
    parts_home = lax.all_to_all(part_all, "mem", split_axis=0, concat_axis=0, tiled=True)
    high_home, total_home = (
        lax.all_to_all(high_all, "mem", split_axis=0, concat_axis=0, tiled=True),
        lax.all_to_all(total_all, "mem", split_axis=0, concat_axis=0, tiled=True),
    )
    slot_rank = jnp.take_along_axis(before, shard_of, axis=1)
    slot_index = shard_of * capacity + slot_rank
    part_sel = parts_home.reshape(slots_all, BLK, width)[slot_index].reshape(
        qblocks, NSH, BLK, heads, head_dim
    )
    high_sel = high_home.reshape(slots_all, BLK, heads)[slot_index]
    total_sel = total_home.reshape(slots_all, BLK, heads)[slot_index]
    top = jnp.max(high_sel, 1, keepdims=True)
    lifted = jnp.exp(high_sel - top)
    weight = lifted / jnp.sum(total_sel * lifted, 1, keepdims=True)
    grad = jnp.sum(weight[..., None] * part_sel.astype(jnp.float32), 1)
    d_query = grad.reshape(1, tokens, width).astype(jnp.bfloat16)
    gate_terms = jnp.einsum(
        "thd,thd->h", dout_three, omem_three, preferred_element_type=jnp.float32
    ) - jnp.einsum("thd,thd->h", dout_three, local_three, preferred_element_type=jnp.float32)
    gate_total = lax.psum(gate_terms, ("mem", "grp"))
    d_gate = sig * (1.0 - sig) * gate_total / (shards * groups * tokens * head_dim) ** 0.5
    return (d_query, d_gate)


def solution(mesh):
    placed = (
        P("grp", "mem", None),
        P("grp", "mem", None),
        P("grp", "mem", None),
        P("grp", "mem", None),
        P("mem", None),
        P("mem", None),
        P(),
        P("grp", "mem", None),
    )
    return jax.shard_map(
        local, mesh=mesh, in_specs=placed, out_specs=(P("grp", "mem", None), P()), check_vma=False
    )
```

profile of v0, /device:TPU:11, one launch (start us, length us, event | category | flops | bytes accessed | tf_op | source)
XLA Modules:
  0.0 572.0 jit_solution(13189161768094132180)
XLA Ops:
  1.7 3.0 convert_reduce_fusion
  5.9 1.1 copy.110
  9.4 6.6 %all-to-all-start = ((bf16[16,4,16]{2,1,0:T(4,128)(2,1)}), bf16[16,4,16]{2,1,0:T(4,128)(2,1)}, u32[]{:S(2)}, u32[]{:S(2)}) async-start(bf16[16,4,16]{2,1,0:T(4,128)(2,1)} %convolution_convert_fusion.3), calls=%async_computation | async-start | bytes 32768 | tf_op jit(solution)/shard_map/all_to_all | solution.py:70
  16.0 39.0 %psum.7 = f32[16]{0:T(128)S(1)} all-reduce(f32[16]{0:T(128)S(1)} %sub.52), channel_id=1, replica_groups=mesh['mem'=16,'grp'=2] {'mem','grp'}, use_global_device_ids=true, to_apply=%region_11.12 | all-reduce | flops 16 | bytes 128 | tf_op jit(solution)/shard_map/psum | solution.py:133
  57.8 7.2 %all-to-all-start.3 = ((bf16[16,2,512]{2,1,0:T(2,128)(2,1)}), bf16[16,2,512]{2,1,0:T(2,128)(2,1)S(1)}, u32[]{:S(2)}, u32[]{:S(2)}) async-start(bf16[16,2,512]{2,1,0:T(2,128)(2,1)} %reshape.247), calls=%async_computation.3 | async-start | bytes 65536 | tf_op jit(solution)/shard_map/all_to_all | solution.py:69
  65.0 1.5 convolution_convert_fusion
  66.5 4.3 copy.79
  70.8 6.2 %all-to-all-start.2 = ((bf16[16,4,16,2048]{3,2,1,0:T(8,128)(2,1)}), bf16[16,4,16,2048]{3,2,1,0:T(8,128)(2,1)}, u32[]{:S(2)}, u32[]{:S(2)}) async-start(bf16[16,4,16,2048]{3,2,1,0:T(8,128)(2,1)} %copy.79), calls=%async_computation.2 | async-start | bytes 8388608 | tf_op jit(solution)/shard_map/all_to_all | solution.py:68
  76.9 1.5 convolution_convert_fusion.1
  78.5 4.3 copy.77
  82.7 86.6 %all-to-all-done.2 = bf16[16,4,16,2048]{3,2,1,0:T(8,128)(2,1)} async-done(((bf16[16,4,16,2048]{3,2,1,0:T(8,128)(2,1)}), bf16[16,4,16,2048]{3,2,1,0:T(8,128)(2,1)}, u32[]{:S(2)}, u32[]{:S(2)}) %all-to-all-start.2) | async-done | bytes 4194336 | tf_op jit(solution)/shard_map/all_to_all | solution.py:68
  169.4 4.9 all-to-all-start.1
  175.0 91.7 %all-to-all-done.1 = bf16[16,4,16,2048]{3,2,1,0:T(8,128)(2,1)} async-done(((bf16[16,4,16,2048]{3,2,1,0:T(8,128)(2,1)}), bf16[16,4,16,2048]{3,2,1,0:T(8,128)(2,1)}, u32[]{:S(2)}, u32[]{:S(2)}) %all-to-all-start.1) | async-done | bytes 4194336 | tf_op jit(solution)/shard_map/all_to_all | solution.py:67
  266.8 173.0 %while.14 = (s32[]{:T(128)}, bf16[8,8,16,2048]{3,2,1,0:T(8,128)(2,1)}, f32[8,8,16,16]{2,3,1,0:T(8,128)}, f32[8,8,16,16]{2,3,1,0:T(8,128)}, bf16[8,8,16]{2,1,0:T(...) while((s32[]{:T(128)}, ...), condition=%wide.region_7.8_spmd, body=%wide.region_3.7_spmd.sunk | while | flops 102236512 | bytes 25392652 | solution.py:109
  272.5 2.1 gather_fusion.1
  274.7 2.2 gather_fusion
  276.8 3.0 fusion.72
  279.8 5.0 fusion.73
  285.5 1.2 copy.182
  294.2 2.1 gather_fusion.1
  296.3 2.2 gather_fusion
  298.5 3.0 fusion.72
  301.5 5.0 fusion.73
  307.1 1.2 copy.182
  315.9 2.1 gather_fusion.1
  318.0 2.2 gather_fusion
  320.2 3.0 fusion.72
  323.1 5.0 fusion.73
  328.8 1.2 copy.182
  337.5 2.1 gather_fusion.1
  339.6 2.2 gather_fusion
  341.8 3.0 fusion.72
  344.7 5.0 fusion.73
  350.4 1.2 copy.182
  359.1 2.1 gather_fusion.1
  361.2 2.2 gather_fusion
  363.4 3.0 fusion.72
  366.4 5.0 fusion.73
  372.0 1.2 copy.182
  380.7 2.1 gather_fusion.1
  382.9 2.2 gather_fusion
  385.0 3.0 fusion.72
  388.0 5.0 fusion.73
  393.6 1.2 copy.182
  402.3 2.1 gather_fusion.1
  404.5 2.2 gather_fusion
  406.7 3.0 fusion.72
  409.6 5.0 fusion.73
  415.3 1.2 copy.182
  423.9 2.1 gather_fusion.1
  426.1 2.2 gather_fusion
  428.2 3.0 fusion.72
  431.2 5.0 fusion.73
  436.9 1.2 copy.182
  439.8 1.9 reshape.251
  441.7 4.9 all-to-all-start.5
  446.6 1.3 reshape.249
  447.8 3.0 all-to-all-done.5
  450.8 9.5 %all_to_all.35 = f32[16,1,1024]{2,1,0:T(1,128)S(1)} all-to-all(f32[16,1,1024]{2,1,0:T(1,128)S(1)} %reshape.249), channel_id=1, replica_groups=mesh['mem'=16,'grp'=2] {'mem'}, dimensions={0} | all-to-all | bytes 131072 | tf_op jit(solution)/shard_map/all_to_all | solution.py:115
  460.3 7.1 %all-to-all-start.6 = ((bf16[16,4,16,2048]{3,2,1,0:T(8,128)(2,1)}), bf16[16,4,16,2048]{3,2,1,0:T(8,128)(2,1)}, u32[]{:S(2)}, u32[]{:S(2)}) async-start(bf16[16,4,16,2048]{3,2,1,0:T(8,128)(2,1)} %bitcast.162), calls=%async_computation.6 | async-start | bytes 8388608 | tf_op jit(solution)/shard_map/all_to_all | solution.py:113
  472.6 87.2 %all-to-all-done.6 = bf16[16,4,16,2048]{3,2,1,0:T(8,128)(2,1)} async-done(((bf16[16,4,16,2048]{3,2,1,0:T(8,128)(2,1)}), bf16[16,4,16,2048]{3,2,1,0:T(8,128)(2,1)}, u32[]{:S(2)}, u32[]{:S(2)}) %all-to-all-start.6) | async-done | bytes 4194336 | tf_op jit(solution)/shard_map/all_to_all | solution.py:113
  559.8 5.0 gather_fusion.4
  564.8 3.5 copy.112
  568.3 2.7 multiply_reduce_fusion
  (213 shorter events, 79.4 us)
Async XLA Ops:
  0.6 57.1 %copy-start = (bf16[1,128,2048]{2,1,0:T(8,128)(2,1)S(1)}, bf16[1,128,2048]{2,1,0:T(8,128)(2,1)}, u32[]{:S(2)}) copy-start(bf16[1,128,2048]{2,1,0:T(8,128)(2,1)} %param.11) | copy-start | bytes 1572868
  0.6 54.3 %copy-start.4 = (f32[16]{0:T(128)S(1)}, f32[16]{0:T(128)}, u32[]{:S(2)}) copy-start(f32[16]{0:T(128)} %param.16) | copy-start | bytes 196
  9.4 48.4 %all-to-all-start = ((bf16[16,4,16]{2,1,0:T(4,128)(2,1)}), bf16[16,4,16]{2,1,0:T(4,128)(2,1)}, u32[]{:S(2)}, u32[]{:S(2)}) async-start(bf16[16,4,16]{2,1,0:T(4,128)(2,1)} %convolution_convert_fusion.3), calls=%async_computation | async-start | bytes 32768 | tf_op jit(solution)/shard_map/all_to_all | solution.py:70
  57.8 13.0 %all-to-all-start.3 = ((bf16[16,2,512]{2,1,0:T(2,128)(2,1)}), bf16[16,2,512]{2,1,0:T(2,128)(2,1)S(1)}, u32[]{:S(2)}, u32[]{:S(2)}) async-start(bf16[16,2,512]{2,1,0:T(2,128)(2,1)} %reshape.247), calls=%async_computation.3 | async-start | bytes 65536 | tf_op jit(solution)/shard_map/all_to_all | solution.py:69
  70.8 6.2 %copy-start.3 = (bf16[1,128,2048]{2,1,0:T(8,128)(2,1)S(1)}, bf16[1,128,2048]{2,1,0:T(8,128)(2,1)}, u32[]{:S(2)}) copy-start(bf16[1,128,2048]{2,1,0:T(8,128)(2,1)} %param.10) | copy-start | bytes 1572868
  70.8 98.6 %all-to-all-start.2 = ((bf16[16,4,16,2048]{3,2,1,0:T(8,128)(2,1)}), bf16[16,4,16,2048]{3,2,1,0:T(8,128)(2,1)}, u32[]{:S(2)}, u32[]{:S(2)}) async-start(bf16[16,4,16,2048]{3,2,1,0:T(8,128)(2,1)} %copy.79), calls=%async_computation.2 | async-start | bytes 8388608 | tf_op jit(solution)/shard_map/all_to_all | solution.py:68
  82.7 91.6 %copy-start.1 = (bf16[256,2048]{1,0:T(8,128)(2,1)S(1)}, bf16[256,2048]{1,0:T(8,128)(2,1)}, u32[]{:S(2)}) copy-start(bf16[256,2048]{1,0:T(8,128)(2,1)} %param.14) | copy-start | bytes 3145732
  82.7 91.8 %copy-start.2 = (bf16[256,2048]{1,0:T(8,128)(2,1)S(1)}, bf16[256,2048]{1,0:T(8,128)(2,1)}, u32[]{:S(2)}) copy-start(bf16[256,2048]{1,0:T(8,128)(2,1)} %param.15) | copy-start | bytes 3145732
  169.4 97.4 %all-to-all-start.1 = ((bf16[16,4,16,2048]{3,2,1,0:T(8,128)(2,1)}), bf16[16,4,16,2048]{3,2,1,0:T(8,128)(2,1)}, u32[]{:S(2)}, u32[]{:S(2)}) async-start(bf16[16,4,16,2048]{3,2,1,0:T(8,128)(2,1)} %copy.77), calls=%async_computation.1 | async-start | bytes 8388608 | tf_op jit(solution)/shard_map/all_to_all | solution.py:67
  441.7 9.2 %all-to-all-start.5 = ((f32[16,1,1024]{2,1,0:T(1,128)}), f32[16,1,1024]{2,1,0:T(1,128)S(1)}, u32[]{:S(2)}, u32[]{:S(2)}) async-start(f32[16,1,1024]{2,1,0:T(1,128)} %reshape.251), calls=%async_computation.5 | async-start | bytes 131072 | tf_op jit(solution)/shard_map/all_to_all | solution.py:116
  460.3 99.5 %all-to-all-start.6 = ((bf16[16,4,16,2048]{3,2,1,0:T(8,128)(2,1)}), bf16[16,4,16,2048]{3,2,1,0:T(8,128)(2,1)}, u32[]{:S(2)}, u32[]{:S(2)}) async-start(bf16[16,4,16,2048]{3,2,1,0:T(8,128)(2,1)} %bitcast.162), calls=%async_computation.6 | async-start | bytes 8388608 | tf_op jit(solution)/shard_map/all_to_all | solution.py:113
where the time goes:
time: 575 us; the launch traced here: 572 us
  waiting for transfers between devices  269 us (47%)
  local copies, waits for them, and re-layouts  124 us (22%)
  matrix products  67.7 us (12%)
  blocking collectives  48.4 us (8%)
  starting transfers between devices  36.7 us (6%)
  other arithmetic  25.8 us (4%)
    all_to_all x1, waiting for transfers between devices, local(): lax.all_to_all(query_slots, 'mem', split_axis=0, concat_axis=0, tiled=True)  91.7 us
    all_to_all x1, waiting for transfers between devices, local(): lax.all_to_all(part_all, 'mem', split_axis=0, concat_axis=0, tiled=True)  87.2 us
    all_to_all x1, waiting for transfers between devices, local(): lax.all_to_all(dmem_slots, 'mem', split_axis=0, concat_axis=0, tiled=True)  86.6 us
    dot_general x8, matrix products, block_step(): jnp.einsum('cqhk,ckhd->cqhd', dscore, keys_sel, preferred_element_type=jn...  40 us
    psum x1, blocking collectives, local(): gate_total = lax.psum(gate_terms, ('mem', 'grp'))  39 us
    dot_general x8, matrix products, block_step(): jnp.einsum('cqhd,ckhd->cqhk', query_four, keys_sel, preferred_element_typ...  23.6 us
    dynamic_slice x32, local copies, waits for them, and re-layouts, local(): part_all, high_all, total_all = lax.map(block_step, grouped)  18.1 us
    gather x8, local copies, waits for them, and re-layouts, block_step(): keys_sel = keys_blocked[chosen].reshape(count, PICK * BLK, heads, head_dim)  17.4 us
  transfers between devices with their start and end apart: 6, of which 4 were waited for; matrix products, arithmetic and copies ran while one was open for 4% of the time, Pallas kernels for 0%

commit v1 on v0

v1 whole, which is shorter than its diff:
```python
import functools
import math

import jax
import jax.numpy as jnp
from jax import lax
from jax.experimental import pallas as pl
from jax.experimental.pallas import tpu as pltpu
from jax.sharding import PartitionSpec as P

BLK = 16
LANES = 128
AXES = ("mem", "grp")
FAR = -1e30


def place(position):
    mem_index, parity = divmod(position, 2)
    return (mem_index >> 1) * 2 + parity, mem_index & 1


def pack_rows(quarter, heads, k_ref, v_ref, out_ref):
    parity = lax.axis_index("grp") % 2
    for position in range(2 * heads):
        head, half = place(position)
        rows = pl.ds(pl.multiple_of(parity * (2 * quarter) + half * quarter, quarter), quarter)
        cols = slice(head * LANES, (head + 1) * LANES)
        out_ref[position, :quarter, :] = k_ref[rows, cols]
        out_ref[position, quarter:, :] = v_ref[rows, cols]


def pack_tokens(
    heads, chunks, q_ref, dout_ref, omem_ref, local_ref, gate_ref, ids_ref, out_ref, ext_ref, delta_ref, gate_rows
):
    tokens = q_ref.shape[0]
    half_rows = tokens // 2
    qblocks, names = ids_ref.shape
    high = lax.Precision.HIGHEST
    parity = lax.axis_index("grp") % 2
    ones = jnp.ones((8, LANES), jnp.float32)
    gate_rows[...] = jnp.zeros_like(gate_rows)
    for head in range(heads):
        cols = slice(head * LANES, (head + 1) * LANES)
        sig = jax.nn.sigmoid(jnp.full((8, LANES), gate_ref[head], jnp.float32))[:1]
        d_out = dout_ref[:, cols].astype(jnp.float32)
        o_mem = omem_ref[:, cols].astype(jnp.float32)
        d_mem = (d_out * sig).astype(jnp.bfloat16)
        differ = o_mem - local_ref[:, cols].astype(jnp.float32)
        gate_rows[head : head + 1, :] = jnp.sum(d_out * differ, 0, keepdims=True)
        product = d_mem.astype(jnp.float32) * o_mem
        row = lax.dot_general(
            ones, product, (((1,), (1,)), ((), ())), precision=high, preferred_element_type=jnp.float32
        )
        delta_ref[head : head + 1, :] = row[:1]
        q = q_ref[:, cols]
        for half in range(2):
            position = ((head // 2) * 2 + half) * 2 + head % 2
            rows = slice(half * half_rows, (half + 1) * half_rows)
            out_ref[position, :half_rows, :] = q[rows]
            out_ref[position, half_rows : 2 * half_rows, :] = d_mem[rows]
    total = lax.dot_general(
        ones, gate_rows[...], (((1,), (1,)), ((), ())), precision=high, preferred_element_type=jnp.float32
    )[:1]
    first = total.astype(jnp.bfloat16).astype(jnp.float32)
    second = (total - first).astype(jnp.bfloat16).astype(jnp.float32)
    third = total - first - second
    lane = lax.broadcasted_iota(jnp.int32, (1, LANES), 1)
    shards_each = heads
    ids = ids_ref[...]
    tables = []
    for chunk in range(chunks):
        block = 16 * (chunk * shards_each + lane // 8) + 8 * ((lane // 4) % 2) + lane % 4
        pair = []
        for half in range(2):
            wanted = jnp.broadcast_to(block + 4 * half, (qblocks, LANES))
            hit = jnp.zeros((qblocks, LANES), jnp.float32)
            for name in range(names):
                hit = jnp.where(ids[:, name : name + 1] == wanted, 1.0, hit)
            pair.append(jnp.where(hit > 0.5, 0.0, FAR))
        tables.append(pair)
    bias_rows = 2 * chunks * (qblocks // 2)
    per = qblocks // 2
    for half in range(2):
        ext_ref[...] = jnp.zeros_like(ext_ref)
        for relative in range(2):
            for chunk in range(chunks):
                at = (relative * chunks + chunk) * per
                ext_ref[at : at + per, :] = tables[chunk][half ^ relative][half * per : (half + 1) * per]
        ext_ref[bias_rows + 1 : bias_rows + 2, :] = first
        ext_ref[bias_rows + 2 : bias_rows + 3, :] = second
        ext_ref[bias_rows + 3 : bias_rows + 4, :] = third
        in_half = (lane // half_rows) == parity
        for head in range(heads):
            row = delta_ref[head : head + 1, :]
            rolled = jnp.concatenate([row[:, half_rows:], row[:, :half_rows]], axis=1)
            row = jnp.where(parity == half, row, rolled)
            ext_ref[bias_rows : bias_rows + 1, :] = jnp.where(in_half, row, 0.0)
            position = ((head // 2) * 2 + half) * 2 + head % 2
            out_ref[position, 2 * half_rows :, :] = ext_ref[...].astype(jnp.bfloat16)


def attend(
    halves, per, width, own_ref, mate_ref, qd_ref, out_ref, gate_ref, kx, vx, qx, delta, scores, high, total, acc
):
    step = pl.program_id(0)
    sources, packet, _ = qd_ref.shape
    quarter = own_ref.shape[1] // 2
    tile = qx.shape[0]
    units = qx.shape[1] // LANES - 1
    rows_unit = kx.shape[0] // units
    steps_unit = rows_unit // width
    scale = 1.0 / math.sqrt(LANES)
    exponent = scale * math.log2(math.e)
    bias_rows = units * per

    @pl.when(step == 0)
    def _():
        for index, ref in enumerate((own_ref, mate_ref)):

            def fill(source, carry, index=index, ref=ref):
                at = pl.ds(pl.multiple_of((index * ref.shape[0] + source) * quarter, quarter), quarter)
                kx[at, :LANES] = ref[source, :quarter, :]
                vx[at, :] = ref[source, quarter:, :]
                return carry

            lax.fori_loop(0, ref.shape[0], fill, 0)

        lane = lax.broadcasted_iota(jnp.int32, (BLK, LANES), 1)

        def mark(block, carry):
            at = pl.ds(pl.multiple_of(block * BLK, BLK), BLK)
            kx[at, LANES:] = (lane == block % LANES).astype(jnp.float32).astype(jnp.bfloat16)
            return carry

        lax.fori_loop(0, kx.shape[0] // BLK, mark, 0)
        gate_ref[...] = jnp.zeros_like(gate_ref)

    rows_source = 2 * halves
    delta_rows = []
    gate_sum = jnp.zeros((1, LANES), jnp.float32)
    for source in range(sources):
        base = source * halves
        qx[base : base + halves, :LANES] = qd_ref[source, :halves, :]
        extra = qd_ref[source, rows_source:, :].astype(jnp.float32)
        for unit in range(units):
            for block in range(per):
                at = unit * per + block
                row = jnp.broadcast_to(extra[at : at + 1], (BLK, LANES)).astype(jnp.bfloat16)
                qx[base + block * BLK : base + (block + 1) * BLK, (1 + unit) * LANES : (2 + unit) * LANES] = row
        delta_rows.append(extra[bias_rows : bias_rows + 1])
        for part in range(1, 4):
            gate_sum = gate_sum + extra[bias_rows + part : bias_rows + part + 1]
    gate_ref[...] += jnp.broadcast_to(gate_sum, gate_ref.shape)
    for pair in range(sources // 2):
        row = delta_rows[2 * pair] + delta_rows[2 * pair + 1]
        delta[pair * LANES : (pair + 1) * LANES, :] = jnp.broadcast_to(row, (LANES, LANES)).T

    high[...] = jnp.full_like(high, -3e38)
    for unit in range(units):

        def score(index, carry, unit=unit):
            at = unit * steps_unit + index
            rows = pl.ds(pl.multiple_of(at * width, width), width)
            left = jnp.concatenate([qx[:, :LANES], qx[:, (1 + unit) * LANES : (2 + unit) * LANES]], axis=1)
            got = lax.dot_general(
                left, kx[rows, :], (((1,), (1,)), ((), ())), preferred_element_type=jnp.float32
            )
            scores[at] = got
            best = high[...]
            for column in range(width // LANES):
                best = jnp.maximum(best, got[:, column * LANES : (column + 1) * LANES])
            high[...] = best
            return carry

        lax.fori_loop(0, steps_unit, score, 0)
    high[...] = jnp.broadcast_to(jnp.max(high[...], 1, keepdims=True) * exponent, high.shape)
    total[...] = jnp.zeros_like(total)
    acc[...] = jnp.zeros_like(acc)

    def back(at, carry):
        rows = pl.ds(pl.multiple_of(at * width, width), width)
        d_mem = jnp.concatenate(
            [qd_ref[source, halves : 2 * halves, :] for source in range(sources)], axis=0
        )
        prod = lax.dot_general(
            d_mem, vx[rows, :], (((1,), (1,)), ((), ())), preferred_element_type=jnp.float32
        )
        got = scores[at]
        level = high[...]
        less = delta[...]
        added = total[...]
        pieces = []
        for column in range(width // LANES):
            cols = slice(column * LANES, (column + 1) * LANES)
            expo = jnp.exp2(got[:, cols] * exponent - level)
            added = added + expo
            pieces.append((expo * (prod[:, cols] - less)).astype(jnp.bfloat16))
        total[...] = added
        acc[...] += jnp.dot(
            jnp.concatenate(pieces, axis=1), kx[rows, :LANES], preferred_element_type=jnp.float32
        )
        return carry

    lax.fori_loop(0, units * steps_unit, back, 0)
    weight = scale / jnp.sum(total[...], 1, keepdims=True)
    result = (acc[...] * weight).astype(jnp.bfloat16)
    for source in range(sources):
        out_ref[source] = result[source * halves : (source + 1) * halves]


def unpack(heads, in_ref, out_ref):
    half_rows = in_ref.shape[1]
    for position in range(2 * heads):
        head, half = place(position)
        out_ref[half * half_rows : (half + 1) * half_rows, head * LANES : (head + 1) * LANES] = in_ref[position]


def local(queries, d_out, o_mem, local_out, mem_keys, mem_values, gate_logit, block_ids):
    shards = lax.axis_size("mem")
    groups = lax.axis_size("grp")
    tokens = queries.shape[1]
    width = queries.shape[2]
    heads = gate_logit.shape[0]
    rows_dev = mem_keys.shape[0]
    qblocks = tokens // BLK
    members = 2 * heads
    chunks = shards // heads
    assert width == heads * LANES and shards % heads == 0 and groups % 2 == 0
    assert rows_dev == 16 * BLK and heads * 8 == LANES and tokens == LANES
    quarter = rows_dev // 4
    halves = tokens // 2
    per = qblocks // 2
    bias_rows = 2 * chunks * per
    extra = -(-(bias_rows + 4) // 16) * 16
    packet = 2 * halves + extra
    vmem = pl.BlockSpec(memory_space=pltpu.VMEM)
    smem = pl.BlockSpec(memory_space=pltpu.SMEM)
    params = pltpu.CompilerParams(vmem_limit_bytes=56 << 20)

    if shards * groups == members:
        head_groups = None
    else:
        head_groups = [
            [(mo * heads + mi) * groups + 2 * go + gp for mi in range(heads) for gp in range(2)]
            for mo in range(chunks)
            for go in range(groups // 2)
        ]
    exchange = functools.partial(
        lax.all_to_all, axis_name=AXES, split_axis=0, concat_axis=0, tiled=True, axis_index_groups=head_groups
    )

    rows_out = pl.pallas_call(
        functools.partial(pack_rows, quarter, heads),
        out_shape=jax.ShapeDtypeStruct((members, 2 * quarter, LANES), jnp.bfloat16),
        in_specs=[vmem, vmem],
        out_specs=vmem,
        compiler_params=params,
        name="pack_rows",
    )(mem_keys, mem_values)
    own = exchange(rows_out)
    tokens_out = pl.pallas_call(
        functools.partial(pack_tokens, heads, chunks),
        out_shape=jax.ShapeDtypeStruct((members, packet, LANES), jnp.bfloat16),
        in_specs=[vmem, vmem, vmem, vmem, smem, vmem],
        out_specs=vmem,
        scratch_shapes=[
            pltpu.VMEM((extra, LANES), jnp.float32),
            pltpu.VMEM((max(heads, 8), LANES), jnp.float32),
            pltpu.VMEM((LANES, LANES), jnp.float32),
        ],
        compiler_params=params,
        name="pack_tokens",
    )(queries[0], d_out[0], o_mem[0], local_out[0], gate_logit, block_ids[0])
    qd = exchange(tokens_out)
    if chunks > 1:
        same = [[mo * heads + mi for mo in range(chunks)] for mi in range(heads)]
        own = lax.all_gather(own, "mem", axis_index_groups=same, axis=0, tiled=True)
    mate = lax.ppermute(own, "mem", [(i, i ^ 1) for i in range(shards)])

    units = 2 * chunks
    rows_all = 4 * quarter * shards
    tile = 512 if chunks == 1 else 256
    sources = tile // halves
    step_width = 512
    grad, gate_sum = pl.pallas_call(
        functools.partial(attend, halves, per, step_width),
        out_shape=(
            jax.ShapeDtypeStruct((members, halves, LANES), jnp.bfloat16),
            jax.ShapeDtypeStruct((8, LANES), jnp.float32),
        ),
        grid=(members // sources,),
        in_specs=[vmem, vmem, pl.BlockSpec((sources, packet, LANES), lambda i: (i, 0, 0))],
        out_specs=(
            pl.BlockSpec((sources, halves, LANES), lambda i: (i, 0, 0)),
            pl.BlockSpec((8, LANES), lambda i: (0, 0)),
        ),
        scratch_shapes=[
            pltpu.VMEM((rows_all, 2 * LANES), jnp.bfloat16),
            pltpu.VMEM((rows_all, LANES), jnp.bfloat16),
            pltpu.VMEM((tile, (1 + units) * LANES), jnp.bfloat16),
            pltpu.VMEM((tile, LANES), jnp.float32),
            pltpu.VMEM((rows_all // step_width, tile, step_width), jnp.float32),
            pltpu.VMEM((tile, LANES), jnp.float32),
            pltpu.VMEM((tile, LANES), jnp.float32),
            pltpu.VMEM((tile, LANES), jnp.float32),
        ],
        compiler_params=params,
        name="attend",
    )(own, mate, qd)
    home = exchange(grad)
    d_query = pl.pallas_call(
        functools.partial(unpack, heads),
        out_shape=jax.ShapeDtypeStruct((tokens, width), jnp.bfloat16),
        in_specs=[vmem],
        out_specs=vmem,
        compiler_params=params,
        name="unpack",
    )(home)
    gate_total = gate_sum[0, :heads]
    if head_groups is not None:
        gate_total = lax.psum(gate_total, AXES) / members
    sig = jax.nn.sigmoid(gate_logit)
    d_gate = sig * (1.0 - sig) * gate_total / (shards * groups * tokens * LANES) ** 0.5
    return (d_query[None], d_gate)


def solution(mesh):
    placed = (
        P("grp", "mem", None),
        P("grp", "mem", None),
        P("grp", "mem", None),
        P("grp", "mem", None),
        P("mem", None),
        P("mem", None),
        P(),
        P("grp", "mem", None),
    )
    return jax.shard_map(
        local, mesh=mesh, in_specs=placed, out_specs=(P("grp", "mem", None), P()), check_vma=False
    )
```

time: 575 us -> 126 us (0.22)
  the two profiles are of different devices: /device:TPU:11 before, /device:TPU:0 now
where the time goes in v1:
time: 126 us; the launch traced here: 125 us
  waiting for transfers between devices  64 us (51%)
  Pallas kernels  41.2 us (33%)
  starting transfers between devices  14.9 us (12%)
  local copies, waits for them, and re-layouts  2.82 us (2%)
    pallas_call x1, Pallas kernels, local(): pl.pallas_call(functools.partial(attend, halves, per, step_width), out_sh...  31.9 us
    all_to_all x1, waiting for transfers between devices, local(): qd = exchange(tokens_out)  28.7 us
    all_to_all x1, waiting for transfers between devices, local(): own = exchange(rows_out)  21.5 us
    all_to_all x1, waiting for transfers between devices, local(): home = exchange(grad)  13.8 us
    all_to_all x1, starting transfers between devices, local(): own = exchange(rows_out)  7.3 us
    pallas_call x1, Pallas kernels, local(): pl.pallas_call(functools.partial(pack_tokens, heads, chunks), out_shape=j...  4.69 us
    all_to_all x1, starting transfers between devices, local(): home = exchange(grad)  3.63 us
    all_to_all x1, starting transfers between devices, local(): qd = exchange(tokens_out)  3.62 us
  transfers between devices with their start and end apart: 4, of which 3 were waited for; matrix products, arithmetic and copies ran while one was open for 1% of the time, Pallas kernels for 4%

profile of v1, /device:TPU:0, one launch (start us, length us, event | category | flops | bytes accessed | tf_op | source)
XLA Modules:
  0.0 124.8 jit_solution(17642993249467732146)
XLA Ops:
  0.6 2.7 %pack_rows.1 = bf16[32,128,128]{2,1,0:T(8,128)(2,1)} custom-call(bf16[256,2048]{1,0:T(8,128)(2,1)} %k_ref.1, bf16[256,2048]{1,0:T(8,128)(2,1)} %v_ref.1), custom_call_target="tpu_custom_call" | custom-call | tf_op jit(solution)/shard_map/pack_rows/pallas_call | solution.py:252
  3.3 7.3 %all-to-all-start = ((bf16[32,128,128]{2,1,0:T(8,128)(2,1)}), bf16[32,128,128]{2,1,0:T(8,128)(2,1)S(1)}, u32[]{:S(2)}, u32[]{:S(2)}) async-start(bf16[32,128,128]{2,1,0:T(8,128)(2,1)} %pack_rows.1), calls=%async_computation | async-start | bytes 2097152 | tf_op jit(solution)/shard_map/all_to_all | solution.py:260
  10.6 4.7 %pack_tokens.1 = bf16[32,144,128]{2,1,0:T(8,128)(2,1)} custom-call(bf16[128,2048]{1,0:T(8,128)(2,1)} %bitcast.11, bf16[128,2048]{1,0:T(8,128)(2,1)} %bitcast.12, bf16[128,2048]{1,0:T(8,128)(2,1)} %bitcast.13, bf16[128,2048]{1,0:T(8,128)(2,1)} %bitcast.14, f32[16]{0:T(128)} %gate_ref.1, s32[8,32]{1,0:T(8,128)} %bitcast.15), custom_call_target="tpu_custom_call" | custom-call | tf_op jit(solution)/shard_map/pack_tokens/pallas_call | solution.py:261
  15.3 21.5 %all-to-all-done.own_ref = bf16[32,128,128]{2,1,0:T(8,128)(2,1)S(1)} async-done(((bf16[32,128,128]{2,1,0:T(8,128)(2,1)}), bf16[32,128,128]{2,1,0:T(8,128)(2,1)S(1)}, u32[]{:S(2)}, u32[]{:S(2)}) %all-to-all-start) | async-done | bytes 1048608 | tf_op jit(solution)/shard_map/all_to_all | solution.py:260
  36.9 0.0 copy-start.1
  36.9 3.6 %all-to-all-start.1 = ((bf16[32,144,128]{2,1,0:T(8,128)(2,1)}), bf16[32,144,128]{2,1,0:T(8,128)(2,1)S(1)}, u32[]{:S(2)}, u32[]{:S(2)}) async-start(bf16[32,144,128]{2,1,0:T(8,128)(2,1)} %pack_tokens.1), calls=%async_computation.1 | async-start | bytes 2359296 | tf_op jit(solution)/shard_map/all_to_all | solution.py:274
  40.5 0.0 copy-start.4
  40.5 0.3 collective-permute-start
  40.8 28.7 %all-to-all-done.1.qd_ref = bf16[32,144,128]{2,1,0:T(8,128)(2,1)S(1)} async-done(((bf16[32,144,128]{2,1,0:T(8,128)(2,1)}), bf16[32,144,128]{2,1,0:T(8,128)(2,1)S(1)}, u32[]{:S(2)}, u32[]{:S(2)}) %all-to-all-start.1) | async-done | bytes 1179680 | tf_op jit(solution)/shard_map/all_to_all | solution.py:274
  69.6 0.0 copy-start
  69.6 0.0 collective-permute-done.mate_ref
  69.6 0.0 copy-done.1
  69.6 1.0 copy-done
  70.6 0.0 copy-start.3
  70.6 1.0 copy-done.3
  71.6 31.9 %attend.1 = (bf16[32,64,128]{2,1,0:T(8,128)(2,1)}, f32[8,128]{1,0:T(8,128)}) custom-call(bf16[32,128,128]{2,1,0:T(8,128)(2,1)} %copy-done.1, bf16[32,128,128]{2,1,0:T(8,128)(2,1)} %copy-done.3, bf16[32,144,128]{2,1,0:T(8,128)(2,1)} %copy-done), custom_call_target="tpu_custom_call" | custom-call | tf_op jit(solution)/shard_map/attend/pallas_call | solution.py:285
  103.4 3.6 %all-to-all-start.2 = ((bf16[32,64,128]{2,1,0:T(8,128)(2,1)}), bf16[32,64,128]{2,1,0:T(8,128)(2,1)S(1)}, u32[]{:S(2)}, u32[]{:S(2)}) async-start(bf16[32,64,128]{2,1,0:T(8,128)(2,1)} %get-tuple-element.4), calls=%async_computation.2 | async-start | bytes 1048576 | tf_op jit(solution)/shard_map/all_to_all | solution.py:310
  107.1 0.0 copy-done.4
  107.1 1.2 fusion.1
  108.3 13.8 %all-to-all-done.2.in_ref = bf16[32,64,128]{2,1,0:T(8,128)(2,1)S(1)} async-done(((bf16[32,64,128]{2,1,0:T(8,128)(2,1)}), bf16[32,64,128]{2,1,0:T(8,128)(2,1)S(1)}, u32[]{:S(2)}, u32[]{:S(2)}) %all-to-all-start.2) | async-done | bytes 524320 | tf_op jit(solution)/shard_map/all_to_all | solution.py:310
  122.1 0.0 copy-start.2
  122.1 0.8 copy-done.2
  122.9 1.9 %unpack.1 = bf16[128,2048]{1,0:T(8,128)(2,1)} custom-call(bf16[32,64,128]{2,1,0:T(8,128)(2,1)} %copy-done.2), custom_call_target="tpu_custom_call" | custom-call | tf_op jit(solution)/shard_map/unpack/pallas_call | solution.py:311
Async XLA Ops:
  3.3 33.5 %all-to-all-start = ((bf16[32,128,128]{2,1,0:T(8,128)(2,1)}), bf16[32,128,128]{2,1,0:T(8,128)(2,1)S(1)}, u32[]{:S(2)}, u32[]{:S(2)}) async-start(bf16[32,128,128]{2,1,0:T(8,128)(2,1)} %pack_rows.1), calls=%async_computation | async-start | bytes 2097152 | tf_op jit(solution)/shard_map/all_to_all | solution.py:260
  36.9 32.7 %copy-start.1 = (bf16[32,128,128]{2,1,0:T(8,128)(2,1)}, bf16[32,128,128]{2,1,0:T(8,128)(2,1)S(1)}, u32[]{:S(2)}) copy-start(bf16[32,128,128]{2,1,0:T(8,128)(2,1)S(1)} %all-to-all-done.own_ref) | copy-start | bytes 3145732
  36.9 32.7 %all-to-all-start.1 = ((bf16[32,144,128]{2,1,0:T(8,128)(2,1)}), bf16[32,144,128]{2,1,0:T(8,128)(2,1)S(1)}, u32[]{:S(2)}, u32[]{:S(2)}) async-start(bf16[32,144,128]{2,1,0:T(8,128)(2,1)} %pack_tokens.1), calls=%async_computation.1 | async-start | bytes 2359296 | tf_op jit(solution)/shard_map/all_to_all | solution.py:274
  40.5 66.6 %copy-start.4 = (f32[16]{0:T(128)S(1)}, f32[16]{0:T(128)}, u32[]{:S(2)}) copy-start(f32[16]{0:T(128)} %gate_ref.1) | copy-start | bytes 196
  40.5 29.0 %collective-permute-start = (bf16[32,128,128]{2,1,0:T(8,128)(2,1)S(1)}, bf16[32,128,128]{2,1,0:T(8,128)(2,1)S(1)}, u32[]{:S(2)}, u32[]{:S(2)}) collective-permute-start(bf16[32,128,128]{2,1,0:T(8,128)(2,1)S(1)} %all-to-all-done.own_ref), channel_id=1, source_target_pairs={{0,2},{2,0},{4,6},{6,4},{8,10},{10,8},{12,14},{14,12},{16,18},{18,... | collective-permute-start | bytes 3145736 | tf_op jit(solution)/shard_map/ppermute | solution.py:278
  69.6 1.0 copy-start
  70.6 1.0 copy-start.3
  103.4 18.6 %all-to-all-start.2 = ((bf16[32,64,128]{2,1,0:T(8,128)(2,1)}), bf16[32,64,128]{2,1,0:T(8,128)(2,1)S(1)}, u32[]{:S(2)}, u32[]{:S(2)}) async-start(bf16[32,64,128]{2,1,0:T(8,128)(2,1)} %get-tuple-element.4), calls=%async_computation.2 | async-start | bytes 1048576 | tf_op jit(solution)/shard_map/all_to_all | solution.py:310
  122.1 0.8 copy-start.2

commit v2 on v1

v2 whole, which is shorter than its diff:
```python
import functools
import math

import jax
import jax.numpy as jnp
from jax import lax
from jax.experimental import pallas as pl
from jax.experimental.pallas import tpu as pltpu
from jax.sharding import PartitionSpec as P

BLK = 16
LANES = 128
AXES = ("mem", "grp")
FAR = -1e30


def position_here(heads):
    return (lax.axis_index("mem") % heads) * 2 + lax.axis_index("grp") % 2


def head_and_half(position):
    return (position >> 2) * 2 + (position & 1), (position >> 1) & 1


def pack_rows(quarter, heads, k_ref, v_ref, *outs):
    here = position_here(heads)
    parity = here & 1
    for step, out in enumerate(outs):
        head, half = head_and_half(here ^ step)
        rows = pl.ds(pl.multiple_of((parity * 2 + half) * quarter, quarter), quarter)
        cols = pl.ds(pl.multiple_of(head * LANES, LANES), LANES)
        out[:quarter, :] = k_ref[rows, cols]
        out[quarter:, :] = v_ref[rows, cols]


def pack_tokens(heads, chunks, q_ref, dout_ref, omem_ref, local_ref, gate_ref, ids_ref, *rest):
    members = 2 * heads
    outs = rest[:members]
    dmem_ref, halves_ref, ext_ref, delta_ref, gate_rows = rest[members:]
    tokens = q_ref.shape[0]
    half_rows = tokens // 2
    qblocks, names = ids_ref.shape
    high = lax.Precision.HIGHEST
    here = position_here(heads)
    parity = here & 1
    ones = jnp.ones((8, LANES), jnp.float32)
    gate_rows[...] = jnp.zeros_like(gate_rows)
    for head in range(heads):
        cols = slice(head * LANES, (head + 1) * LANES)
        sig = jax.nn.sigmoid(jnp.full((8, LANES), gate_ref[head], jnp.float32))[:1]
        d_out = dout_ref[:, cols].astype(jnp.float32)
        o_mem = omem_ref[:, cols].astype(jnp.float32)
        d_mem = (d_out * sig).astype(jnp.bfloat16)
        dmem_ref[:, cols] = d_mem
        differ = o_mem - local_ref[:, cols].astype(jnp.float32)
        gate_rows[head : head + 1, :] = jnp.sum(d_out * differ, 0, keepdims=True)
        product = d_mem.astype(jnp.float32) * o_mem
        row = lax.dot_general(
            ones, product, (((1,), (1,)), ((), ())), precision=high, preferred_element_type=jnp.float32
        )
        delta_ref[head : head + 1, :] = row[:1]
    total = lax.dot_general(
        ones, gate_rows[...], (((1,), (1,)), ((), ())), precision=high, preferred_element_type=jnp.float32
    )[:1]
    first = total.astype(jnp.bfloat16).astype(jnp.float32)
    second = (total - first).astype(jnp.bfloat16).astype(jnp.float32)
    third = total - first - second
    lane = lax.broadcasted_iota(jnp.int32, (1, LANES), 1)
    ids = ids_ref[...]
    per = qblocks // 2
    bias_rows = 2 * chunks * per
    halves_ref[...] = jnp.zeros_like(halves_ref)
    for chunk in range(chunks):
        block = 16 * (chunk * heads + lane // 8) + 8 * ((lane // 4) % 2) + lane % 4
        for side in range(2):
            wanted = jnp.broadcast_to(block + 4 * side, (qblocks, LANES))
            hit = jnp.zeros((qblocks, LANES), jnp.float32)
            for name in range(names):
                hit = jnp.where(ids[:, name : name + 1] == wanted, 1.0, hit)
            table = jnp.where(hit > 0.5, 0.0, FAR)
            for half in range(2):
                at = ((half ^ side) * chunks + chunk) * per
                halves_ref[half, at : at + per, :] = table[half * per : (half + 1) * per]
    for half in range(2):
        halves_ref[half, bias_rows + 1 : bias_rows + 2, :] = first
        halves_ref[half, bias_rows + 2 : bias_rows + 3, :] = second
        halves_ref[half, bias_rows + 3 : bias_rows + 4, :] = third
    in_half = (lane // half_rows) == parity
    for step, out in enumerate(outs):
        head, half = head_and_half(here ^ step)
        rows = pl.ds(pl.multiple_of(half * half_rows, half_rows), half_rows)
        cols = pl.ds(pl.multiple_of(head * LANES, LANES), LANES)
        out[:half_rows, :] = q_ref[rows, cols]
        out[half_rows : 2 * half_rows, :] = dmem_ref[rows, cols]
        row = delta_ref[pl.ds(head, 1), :]
        rolled = jnp.concatenate([row[:, half_rows:], row[:, :half_rows]], axis=1)
        ext_ref[...] = halves_ref[half]
        ext_ref[bias_rows : bias_rows + 1, :] = jnp.where(in_half, jnp.where(parity == half, row, rolled), 0.0)
        out[2 * half_rows :, :] = ext_ref[...].astype(jnp.bfloat16)


def assemble(heads, quarter, *refs):
    out = refs[-1]
    here = position_here(heads)
    for step, ref in enumerate(refs[:-1]):
        at = pl.ds(pl.multiple_of((here ^ step) * quarter, quarter), quarter)
        out[0, at, :] = ref[:quarter, :]
        out[1, at, :] = ref[quarter:, :]


def attend(count, halves, per, width, tile, own_ref, mate_ref, *refs):
    packets = refs[:count]
    outs = refs[count : 2 * count]
    gate_ref, mark, qx, dm, delta, scores, high, total, acc = refs[2 * count :]
    units = qx.shape[1] // LANES - 1
    sides = (own_ref, mate_ref)
    steps_side = own_ref.shape[1] // width
    rows_unit = mark.shape[0]
    scale = 1.0 / math.sqrt(LANES)
    exponent = scale * math.log2(math.e)
    bias_rows = units * per

    lane = lax.broadcasted_iota(jnp.int32, (BLK, LANES), 1)
    for block in range(LANES):
        mark[block * BLK : (block + 1) * BLK, :] = jnp.where(lane == block, 1.0, 0.0).astype(jnp.bfloat16)

    delta_rows = []
    gate_sum = jnp.zeros((1, LANES), jnp.float32)
    for source, packet in enumerate(packets):
        base = source * halves
        qx[base : base + halves, :LANES] = packet[:halves, :]
        dm[base : base + halves, :] = packet[halves : 2 * halves, :]
        extra = packet[2 * halves :, :].astype(jnp.float32)
        for unit in range(units):
            for block in range(per):
                at = unit * per + block
                row = jnp.broadcast_to(extra[at : at + 1], (BLK, LANES)).astype(jnp.bfloat16)
                qx[base + block * BLK : base + (block + 1) * BLK, (1 + unit) * LANES : (2 + unit) * LANES] = row
        delta_rows.append(extra[bias_rows : bias_rows + 1])
        for part in range(1, 4):
            gate_sum = gate_sum + extra[bias_rows + part : bias_rows + part + 1]
    gate_ref[...] = jnp.broadcast_to(gate_sum, gate_ref.shape)
    parity = lax.axis_index("grp") % 2
    for pair in range(count // 2):
        row = delta_rows[2 * pair] + delta_rows[2 * pair + 1]
        wide = jnp.broadcast_to(row, (LANES, LANES)).T
        lower, upper = wide[:halves], wide[halves:]
        delta[pair * LANES : pair * LANES + halves, :] = jnp.where(parity == 0, lower, upper)
        delta[pair * LANES + halves : (pair + 1) * LANES, :] = jnp.where(parity == 0, upper, lower)

    def one_tile(index, carry):
        here = pl.ds(pl.multiple_of(index * tile, tile), tile)
        high[...] = jnp.full_like(high, -3e38)
        for side, ref in enumerate(sides):
            for unit in range(units // 2):

                def score(at, carry, side=side, ref=ref, unit=unit):
                    rows = pl.ds(pl.multiple_of(unit * rows_unit + at * width, width), width)
                    marks = pl.ds(pl.multiple_of(at * width, width), width)
                    lanes = (1 + side * (units // 2) + unit) * LANES
                    left = jnp.concatenate([qx[here, :LANES], qx[here, lanes : lanes + LANES]], axis=1)
                    right = jnp.concatenate([ref[0, rows, :], mark[marks, :]], axis=1)
                    got = lax.dot_general(
                        left, right, (((1,), (1,)), ((), ())), preferred_element_type=jnp.float32
                    )
                    scores[side * steps_side + unit * (rows_unit // width) + at] = got
                    best = high[...]
                    for column in range(width // LANES):
                        best = jnp.maximum(best, got[:, column * LANES : (column + 1) * LANES])
                    high[...] = best
                    return carry

                lax.fori_loop(0, rows_unit // width, score, 0, unroll=2)
        high[...] = jnp.broadcast_to(jnp.max(high[...], 1, keepdims=True) * exponent, high.shape)
        total[...] = jnp.zeros_like(total)
        acc[...] = jnp.zeros_like(acc)
        for side, ref in enumerate(sides):

            def back(at, carry, side=side, ref=ref):
                rows = pl.ds(pl.multiple_of(at * width, width), width)
                prod = lax.dot_general(
                    dm[here, :], ref[1, rows, :], (((1,), (1,)), ((), ())), preferred_element_type=jnp.float32
                )
                got = scores[side * steps_side + at]
                level = high[...]
                less = delta[here, :]
                added = total[...]
                pieces = []
                for column in range(width // LANES):
                    cols = slice(column * LANES, (column + 1) * LANES)
                    expo = jnp.exp2(got[:, cols] * exponent - level)
                    added = added + expo
                    pieces.append((expo * (prod[:, cols] - less)).astype(jnp.bfloat16))
                total[...] = added
                acc[...] += jnp.dot(
                    jnp.concatenate(pieces, axis=1), ref[0, rows, :], preferred_element_type=jnp.float32
                )
                return carry

            lax.fori_loop(0, steps_side, back, 0, unroll=2)
        weight = scale / jnp.sum(total[...], 1, keepdims=True)
        dm[here, :] = (acc[...] * weight).astype(jnp.bfloat16)
        return carry

    lax.fori_loop(0, dm.shape[0] // tile, one_tile, 0)
    for source, out in enumerate(outs):
        out[...] = dm[source * halves : (source + 1) * halves, :]


def unpack(heads, *refs):
    out_ref = refs[-1]
    here = position_here(heads)
    for step, ref in enumerate(refs[:-1]):
        head, half = head_and_half(here ^ step)
        half_rows = ref.shape[0]
        rows = pl.ds(pl.multiple_of(half * half_rows, half_rows), half_rows)
        cols = pl.ds(pl.multiple_of(head * LANES, LANES), LANES)
        out_ref[rows, cols] = ref[...]


def local(queries, d_out, o_mem, local_out, mem_keys, mem_values, gate_logit, block_ids):
    shards = lax.axis_size("mem")
    groups = lax.axis_size("grp")
    tokens = queries.shape[1]
    width = queries.shape[2]
    heads = gate_logit.shape[0]
    rows_dev = mem_keys.shape[0]
    qblocks = tokens // BLK
    members = 2 * heads
    chunks = shards // heads
    assert width == heads * LANES and shards % heads == 0 and groups % 2 == 0
    assert rows_dev == 16 * BLK and heads * 8 == LANES and tokens == LANES
    quarter = rows_dev // 4
    halves = tokens // 2
    per = qblocks // 2
    units = 2 * chunks
    bias_rows = units * per
    extra = -(-(bias_rows + 4) // 16) * 16
    packet = 2 * halves + extra
    vmem = pl.BlockSpec(memory_space=pltpu.VMEM)
    smem = pl.BlockSpec(memory_space=pltpu.SMEM)
    bf16 = jnp.bfloat16

    def swap(pieces, only=None):
        got = list(pieces)
        for step in range(members) if only is None else only:
            if step == 0:
                continue
            pairs = []
            for mem in range(shards):
                for grp in range(groups):
                    other = ((mem % heads) * 2 + grp % 2) ^ step
                    to_mem = mem - mem % heads + (other >> 1)
                    to_grp = grp - grp % 2 + (other & 1)
                    pairs.append((mem * groups + grp, to_mem * groups + to_grp))
            got[step] = lax.ppermute(pieces[step], AXES, pairs)
        return got

    small = pltpu.CompilerParams(vmem_limit_bytes=24 << 20)
    rows_out = pl.pallas_call(
        functools.partial(pack_rows, quarter, heads),
        out_shape=[jax.ShapeDtypeStruct((2 * quarter, LANES), bf16)] * members,
        in_specs=[vmem, vmem],
        out_specs=[vmem] * members,
        compiler_params=small,
        name="pack_rows",
    )(mem_keys, mem_values)
    rows_in = swap(rows_out)
    tokens_out = pl.pallas_call(
        functools.partial(pack_tokens, heads, chunks),
        out_shape=[jax.ShapeDtypeStruct((packet, LANES), bf16)] * members,
        in_specs=[vmem, vmem, vmem, vmem, smem, vmem],
        out_specs=[vmem] * members,
        scratch_shapes=[
            pltpu.VMEM((tokens, width), bf16),
            pltpu.VMEM((2, extra, LANES), jnp.float32),
            pltpu.VMEM((extra, LANES), jnp.float32),
            pltpu.VMEM((heads, LANES), jnp.float32),
            pltpu.VMEM((LANES, LANES), jnp.float32),
        ],
        compiler_params=small,
        name="pack_tokens",
    )(queries[0], d_out[0], o_mem[0], local_out[0], gate_logit, block_ids[0])
    tokens_in = swap(tokens_out)
    own = pl.pallas_call(
        functools.partial(assemble, heads, quarter),
        out_shape=jax.ShapeDtypeStruct((2, members * quarter, LANES), bf16),
        in_specs=[vmem] * members,
        out_specs=vmem,
        compiler_params=small,
        name="assemble",
    )(*rows_in)
    if chunks > 1:
        same = [[mo * heads + mi for mo in range(chunks)] for mi in range(heads)]
        own = lax.all_gather(own, "mem", axis_index_groups=same, axis=1, tiled=True)
    mate = lax.ppermute(own, "mem", [(i, i ^ 1) for i in range(shards)])

    rows_all = 2 * own.shape[1]
    step_width = 512
    tile = 512 if chunks == 1 else 256
    calls = 2
    count = members // calls
    flops = 2 * count * halves * rows_all * LANES * 4

    def attend_some(packets):
        return pl.pallas_call(
            functools.partial(attend, count, halves, per, step_width, tile),
            out_shape=[jax.ShapeDtypeStruct((halves, LANES), bf16)] * count
            + [jax.ShapeDtypeStruct((8, LANES), jnp.float32)],
            in_specs=[vmem] * (2 + count),
            out_specs=[vmem] * (count + 1),
            scratch_shapes=[
                pltpu.VMEM((LANES * BLK, LANES), bf16),
                pltpu.VMEM((count * halves, (1 + units) * LANES), bf16),
                pltpu.VMEM((count * halves, LANES), bf16),
                pltpu.VMEM((count * halves, LANES), jnp.float32),
                pltpu.VMEM((rows_all // step_width, tile, step_width), jnp.float32),
                pltpu.VMEM((tile, LANES), jnp.float32),
                pltpu.VMEM((tile, LANES), jnp.float32),
                pltpu.VMEM((tile, LANES), jnp.float32),
            ],
            compiler_params=pltpu.CompilerParams(vmem_limit_bytes=(24 if chunks == 1 else 48) << 20),
            cost_estimate=pl.CostEstimate(
                flops=flops, bytes_accessed=4 * rows_all * LANES, transcendentals=count * halves * rows_all
            ),
            name="attend",
        )(own, mate, *packets)

    home = [None] * members
    gate_total = jnp.zeros((heads,), jnp.float32)
    for call in range(calls):
        steps = [s for s in range(members) if (s >> 1) % calls == call]
        *grads, gate_sum = attend_some([tokens_in[s] for s in steps])
        gate_total = gate_total + gate_sum[0, :heads]
        sparse = [None] * members
        for s, grad in zip(steps, grads):
            sparse[s] = grad
        back = swap(sparse, only=steps)
        for s in steps:
            home[s] = back[s]
    d_query = pl.pallas_call(
        functools.partial(unpack, heads),
        out_shape=jax.ShapeDtypeStruct((tokens, width), bf16),
        in_specs=[vmem] * members,
        out_specs=vmem,
        compiler_params=small,
        name="unpack",
    )(*home)
    if shards * groups != members:
        gate_total = lax.psum(gate_total, AXES) / members
    sig = jax.nn.sigmoid(gate_logit)
    d_gate = sig * (1.0 - sig) * gate_total / (shards * groups * tokens * LANES) ** 0.5
    return (d_query[None], d_gate)


def solution(mesh):
    placed = (
        P("grp", "mem", None),
        P("grp", "mem", None),
        P("grp", "mem", None),
        P("grp", "mem", None),
        P("mem", None),
        P("mem", None),
        P(),
        P("grp", "mem", None),
    )
    return jax.shard_map(
        local, mesh=mesh, in_specs=placed, out_specs=(P("grp", "mem", None), P()), check_vma=False
    )
```

time: 126 us -> 200 us (1.59)
  starting transfers between devices: 14.9 us -> 157 us
  waiting for transfers between devices: 64 us -> 10.5 us
  Pallas kernels: 41.2 us -> 27.2 us
    ppermute x0 -> x93, starting transfers between devices: none -> 152 us  [swap(): got[step] = lax.ppermute(pieces[step], AXES, pairs)]
    all_to_all x3 -> x0, waiting for transfers between devices: 64 us -> none  [the longest x1 28.7 us: local(): qd = exchange(tokens_out)]
    all_to_all x3 -> x0, starting transfers between devices: 14.5 us -> none  [the longest x1 7.3 us: local(): own = exchange(rows_out)]
    pallas_call x3 -> x5, Pallas kernels: 39.3 us -> 26.2 us  [the longest x2 22.9 us: attend_some(): pl.pallas_call(functools.partial(attend, count, halves, per, step_width,...]
    ppermute x0 -> x93, waiting for transfers between devices: none -> 10.5 us  [swap(): got[step] = lax.ppermute(pieces[step], AXES, pairs)]
    ppermute x1, starting transfers between devices: 0.32 us -> 4.27 us  [local(): mate = lax.ppermute(own, 'mem', [(i, i ^ 1) for i in range(shards)])]
  transfers between devices with their start and end apart: 4 -> 94, of which waited for: 3 -> 9; matrix products, arithmetic and copies ran while one was open for 1% -> 0% of each run, Pallas kernels for 4% -> 13%
where the time goes in v2:
time: 200 us; the launch traced here: 199 us
  starting transfers between devices  157 us (78%)
  Pallas kernels  27.2 us (14%)
  waiting for transfers between devices  10.5 us (5%)
  local copies, waits for them, and re-layouts  3.12 us (2%)
    ppermute x93, starting transfers between devices, swap(): got[step] = lax.ppermute(pieces[step], AXES, pairs)  152 us
    pallas_call x2, Pallas kernels, attend_some(): pl.pallas_call(functools.partial(attend, count, halves, per, step_width,...  22.9 us
    ppermute x93, waiting for transfers between devices, swap(): got[step] = lax.ppermute(pieces[step], AXES, pairs)  10.5 us
    ppermute x1, starting transfers between devices, local(): mate = lax.ppermute(own, 'mem', [(i, i ^ 1) for i in range(shards)])  4.27 us
  transfers between devices with their start and end apart: 94, of which 9 were waited for; matrix products, arithmetic and copies ran while one was open for 0% of the time, Pallas kernels for 13%

profile of v2, /device:TPU:0, one launch (start us, length us, event | category | flops | bytes accessed | tf_op | source)
XLA Modules:
  0.0 198.7 jit_solution(8526230967829250482)
XLA Ops:
  0.6 1.2 copy-done
  1.9 1.2 copy-done.1
  3.4 3.0 %collective-permute-start = (bf16[128,128]{1,0:T(8,128)(2,1)S(1)}, bf16[128,128]{1,0:T(8,128)(2,1)S(1)}, u32[]{:S(2)}, u32[]{:S(2)}) collective-permute-start(bf16[128,128]{1,0:T(8,128)(2,1)S(1)} %get-tuple-element.101), channel_id=1, source_target_pairs={{0,1},{1,0},{2,3},{3,2},{4,5},{5,4},{6,7},{7,6},{8,9},{9,8},{10,11... | collective-permute-start | bytes 98312 | tf_op jit(solution)/shard_map/ppermute | solution.py:256
  6.6 1.9 collective-permute-start.3
  8.5 1.5 collective-permute-start.4
  11.7 1.7 collective-permute-start.7
  13.4 1.3 collective-permute-start.8
  15.3 1.2 collective-permute-start.10
  16.4 2.6 %collective-permute-start.11 = (bf16[128,128]{1,0:T(8,128)(2,1)S(1)}, bf16[128,128]{1,0:T(8,128)(2,1)S(1)}, u32[]{:S(2)}, u32[]{:S(2)}) collective-permute-start(bf16[128,128]{1,0:T(8,128)(2,1)S(1)} %get-tuple-element.112), channel_id=1, source_target_pairs={{0,12},{1,13},{2,14},{3,15},{4,8},{5,9},{6,10},{7,11},{8,4},{9,5},... | collective-permute-start | bytes 98312 | tf_op jit(solution)/shard_map/ppermute | solution.py:256
  19.0 1.3 collective-permute-start.12
  20.8 2.2 %collective-permute-start.14 = (bf16[128,128]{1,0:T(8,128)(2,1)S(1)}, bf16[128,128]{1,0:T(8,128)(2,1)S(1)}, u32[]{:S(2)}, u32[]{:S(2)}) collective-permute-start(bf16[128,128]{1,0:T(8,128)(2,1)S(1)} %get-tuple-element.115), channel_id=1, source_target_pairs={{0,15},{1,14},{2,13},{3,12},{4,11},{5,10},{6,9},{7,8},{8,7},{9,6},... | collective-permute-start | bytes 98312 | tf_op jit(solution)/shard_map/ppermute | solution.py:256
  23.0 2.6 %collective-permute-start.15 = (bf16[128,128]{1,0:T(8,128)(2,1)S(1)}, bf16[128,128]{1,0:T(8,128)(2,1)S(1)}, u32[]{:S(2)}, u32[]{:S(2)}) collective-permute-start(bf16[128,128]{1,0:T(8,128)(2,1)S(1)} %get-tuple-element.116), channel_id=1, source_target_pairs={{0,16},{1,17},{2,18},{3,19},{4,20},{5,21},{6,22},{7,23},{8,24},{9,... | collective-permute-start | bytes 98312 | tf_op jit(solution)/shard_map/ppermute | solution.py:256
  25.6 1.2 collective-permute-start.16
  26.8 1.7 collective-permute-start.17
  29.4 3.6 %collective-permute-start.19 = (bf16[128,128]{1,0:T(8,128)(2,1)S(1)}, bf16[128,128]{1,0:T(8,128)(2,1)S(1)}, u32[]{:S(2)}, u32[]{:S(2)}) collective-permute-start(bf16[128,128]{1,0:T(8,128)(2,1)S(1)} %get-tuple-element.120), channel_id=1, source_target_pairs={{0,20},{1,21},{2,22},{3,23},{4,16},{5,17},{6,18},{7,19},{8,28},{9,... | collective-permute-start | bytes 98312 | tf_op jit(solution)/shard_map/ppermute | solution.py:256
  33.0 1.2 collective-permute-start.20
  34.2 1.5 collective-permute-start.21
  35.6 2.1 %collective-permute-start.22 = (bf16[128,128]{1,0:T(8,128)(2,1)S(1)}, bf16[128,128]{1,0:T(8,128)(2,1)S(1)}, u32[]{:S(2)}, u32[]{:S(2)}) collective-permute-start(bf16[128,128]{1,0:T(8,128)(2,1)S(1)} %get-tuple-element.123), channel_id=1, source_target_pairs={{0,23},{1,22},{2,21},{3,20},{4,19},{5,18},{6,17},{7,16},{8,31},{9,... | collective-permute-start | bytes 98312 | tf_op jit(solution)/shard_map/ppermute | solution.py:256
  37.7 3.6 %collective-permute-start.23 = (bf16[128,128]{1,0:T(8,128)(2,1)S(1)}, bf16[128,128]{1,0:T(8,128)(2,1)S(1)}, u32[]{:S(2)}, u32[]{:S(2)}) collective-permute-start(bf16[128,128]{1,0:T(8,128)(2,1)S(1)} %get-tuple-element.124), channel_id=1, source_target_pairs={{0,24},{1,25},{2,26},{3,27},{4,28},{5,29},{6,30},{7,31},{8,16},{9,... | collective-permute-start | bytes 98312 | tf_op jit(solution)/shard_map/ppermute | solution.py:256
  43.0 3.0 %collective-permute-start.26 = (bf16[128,128]{1,0:T(8,128)(2,1)S(1)}, bf16[128,128]{1,0:T(8,128)(2,1)S(1)}, u32[]{:S(2)}, u32[]{:S(2)}) collective-permute-start(bf16[128,128]{1,0:T(8,128)(2,1)S(1)} %get-tuple-element.127), channel_id=1, source_target_pairs={{0,27},{1,26},{2,25},{3,24},{4,31},{5,30},{6,29},{7,28},{8,19},{9,... | collective-permute-start | bytes 98312 | tf_op jit(solution)/shard_map/ppermute | solution.py:256
  46.0 4.6 %collective-permute-start.27 = (bf16[128,128]{1,0:T(8,128)(2,1)S(1)}, bf16[128,128]{1,0:T(8,128)(2,1)S(1)}, u32[]{:S(2)}, u32[]{:S(2)}) collective-permute-start(bf16[128,128]{1,0:T(8,128)(2,1)S(1)} %get-tuple-element.128), channel_id=1, source_target_pairs={{0,28},{1,29},{2,30},{3,31},{4,24},{5,25},{6,26},{7,27},{8,20},{9,... | collective-permute-start | bytes 98312 | tf_op jit(solution)/shard_map/ppermute | solution.py:256
  52.1 4.0 %collective-permute-start.30 = (bf16[128,128]{1,0:T(8,128)(2,1)S(1)}, bf16[128,128]{1,0:T(8,128)(2,1)S(1)}, u32[]{:S(2)}, u32[]{:S(2)}) collective-permute-start(bf16[128,128]{1,0:T(8,128)(2,1)S(1)} %get-tuple-element.131), channel_id=1, source_target_pairs={{0,31},{1,30},{2,29},{3,28},{4,27},{5,26},{6,25},{7,24},{8,23},{9,... | collective-permute-start | bytes 98312 | tf_op jit(solution)/shard_map/ppermute | solution.py:256
  56.1 2.0 %collective-permute-done.28.refs_29_ = bf16[128,128]{1,0:T(8,128)(2,1)S(1)} collective-permute-done((bf16[128,128]{1,0:T(8,128)(2,1)S(1)}, bf16[128,128]{1,0:T(8,128)(2,1)S(1)}, u32[]{:S(2)}, u32[]{:S(2)}) %collective-permute-start.28) | collective-permute-done | bytes 32800 | tf_op jit(solution)/shard_map/ppermute | solution.py:256
  59.3 4.3 %collective-permute-start.31 = (bf16[2,2048,128]{2,1,0:T(8,128)(2,1)S(1)}, bf16[2,2048,128]{2,1,0:T(8,128)(2,1)S(1)}, u32[]{:S(2)}, u32[]{:S(2)}) collective-permute-start(bf16[2,2048,128]{2,1,0:T(8,128)(2,1)S(1)} %assemble.1.own_ref), channel_id=1, source_target_pairs={{0,2},{2,0},{4,6},{6,4},{8,10},{10,8},{12,14},{14,12},{16,18},{18,... | collective-permute-start | bytes 3145736 | tf_op jit(solution)/shard_map/ppermute | solution.py:296
  64.2 2.8 %pack_tokens.1 = (bf16[144,128]{1,0:T(8,128)(2,1)S(1)}, bf16[144,128]{1,0:T(8,128)(2,1)S(1)}, bf16[144,128]{1,0:T(8,128)(2,1)S(1)}, bf16[144,128]{1,0:T(8,128)(2...) custom-call(bf16[128,2048]{1,0:T(8,128)(2,1)S(1)} %bitcast.10, ...), custom_call_target="tpu_custom_call" | custom-call | tf_op jit(solution)/shard_map/pack_tokens/pallas_call | solution.py:269
  68.3 2.4 %collective-permute-start.34 = (bf16[144,128]{1,0:T(8,128)(2,1)S(1)}, bf16[144,128]{1,0:T(8,128)(2,1)S(1)}, u32[]{:S(2)}, u32[]{:S(2)}) collective-permute-start(bf16[144,128]{1,0:T(8,128)(2,1)S(1)} %get-tuple-element.135), channel_id=1, source_target_pairs={{0,5},{1,4},{2,7},{3,6},{4,1},{5,0},{6,3},{7,2},{8,13},{9,12},{10,... | collective-permute-start | bytes 110600 | tf_op jit(solution)/shard_map/ppermute | solution.py:256
  71.1 1.6 collective-permute-start.36
  73.1 3.4 %collective-permute-start.38 = (bf16[144,128]{1,0:T(8,128)(2,1)S(1)}, bf16[144,128]{1,0:T(8,128)(2,1)S(1)}, u32[]{:S(2)}, u32[]{:S(2)}) collective-permute-start(bf16[144,128]{1,0:T(8,128)(2,1)S(1)} %get-tuple-element.139), channel_id=1, source_target_pairs={{0,13},{1,12},{2,15},{3,14},{4,9},{5,8},{6,11},{7,10},{8,5},{9,4},... | collective-permute-start | bytes 110600 | tf_op jit(solution)/shard_map/ppermute | solution.py:256
  76.5 3.0 %collective-permute-start.40 = (bf16[144,128]{1,0:T(8,128)(2,1)S(1)}, bf16[144,128]{1,0:T(8,128)(2,1)S(1)}, u32[]{:S(2)}, u32[]{:S(2)}) collective-permute-start(bf16[144,128]{1,0:T(8,128)(2,1)S(1)} %get-tuple-element.141), channel_id=1, source_target_pairs={{0,17},{1,16},{2,19},{3,18},{4,21},{5,20},{6,23},{7,22},{8,25},{9,... | collective-permute-start | bytes 110600 | tf_op jit(solution)/shard_map/ppermute | solution.py:256
  79.5 4.7 %collective-permute-start.42 = (bf16[144,128]{1,0:T(8,128)(2,1)S(1)}, bf16[144,128]{1,0:T(8,128)(2,1)S(1)}, u32[]{:S(2)}, u32[]{:S(2)}) collective-permute-start(bf16[144,128]{1,0:T(8,128)(2,1)S(1)} %get-tuple-element.143), channel_id=1, source_target_pairs={{0,21},{1,20},{2,23},{3,22},{4,17},{5,16},{6,19},{7,18},{8,29},{9,... | collective-permute-start | bytes 110600 | tf_op jit(solution)/shard_map/ppermute | solution.py:256
  84.7 3.3 %collective-permute-start.44 = (bf16[144,128]{1,0:T(8,128)(2,1)S(1)}, bf16[144,128]{1,0:T(8,128)(2,1)S(1)}, u32[]{:S(2)}, u32[]{:S(2)}) collective-permute-start(bf16[144,128]{1,0:T(8,128)(2,1)S(1)} %get-tuple-element.145), channel_id=1, source_target_pairs={{0,25},{1,24},{2,27},{3,26},{4,29},{5,28},{6,31},{7,30},{8,17},{9,... | collective-permute-start | bytes 110600 | tf_op jit(solution)/shard_map/ppermute | solution.py:256
  89.0 4.6 %collective-permute-start.46 = (bf16[144,128]{1,0:T(8,128)(2,1)S(1)}, bf16[144,128]{1,0:T(8,128)(2,1)S(1)}, u32[]{:S(2)}, u32[]{:S(2)}) collective-permute-start(bf16[144,128]{1,0:T(8,128)(2,1)S(1)} %get-tuple-element.147), channel_id=1, source_target_pairs={{0,29},{1,28},{2,31},{3,30},{4,25},{5,24},{6,27},{7,26},{8,21},{9,... | collective-permute-start | bytes 110600 | tf_op jit(solution)/shard_map/ppermute | solution.py:256
  94.7 1.9 collective-permute-done.46.refs_15_
  97.3 1.8 collective-permute-start.53
  100.9 1.7 collective-permute-start.55
  102.6 3.4 %collective-permute-start.56 = (bf16[144,128]{1,0:T(8,128)(2,1)S(1)}, bf16[144,128]{1,0:T(8,128)(2,1)S(1)}, u32[]{:S(2)}, u32[]{:S(2)}) collective-permute-start(bf16[144,128]{1,0:T(8,128)(2,1)S(1)} %get-tuple-element.158), channel_id=1, source_target_pairs={{0,18},{1,19},{2,16},{3,17},{4,22},{5,23},{6,20},{7,21},{8,26},{9,... | collective-permute-start | bytes 110600 | tf_op jit(solution)/shard_map/ppermute | solution.py:256
  106.1 3.0 %collective-permute-start.58 = (bf16[144,128]{1,0:T(8,128)(2,1)S(1)}, bf16[144,128]{1,0:T(8,128)(2,1)S(1)}, u32[]{:S(2)}, u32[]{:S(2)}) collective-permute-start(bf16[144,128]{1,0:T(8,128)(2,1)S(1)} %get-tuple-element.160), channel_id=1, source_target_pairs={{0,22},{1,23},{2,20},{3,21},{4,18},{5,19},{6,16},{7,17},{8,30},{9,... | collective-permute-start | bytes 110600 | tf_op jit(solution)/shard_map/ppermute | solution.py:256
  109.1 1.4 collective-permute-start.59
  110.6 3.3 %collective-permute-start.60 = (bf16[144,128]{1,0:T(8,128)(2,1)S(1)}, bf16[144,128]{1,0:T(8,128)(2,1)S(1)}, u32[]{:S(2)}, u32[]{:S(2)}) collective-permute-start(bf16[144,128]{1,0:T(8,128)(2,1)S(1)} %get-tuple-element.162), channel_id=1, source_target_pairs={{0,26},{1,27},{2,24},{3,25},{4,30},{5,31},{6,28},{7,29},{8,18},{9,... | collective-permute-start | bytes 110600 | tf_op jit(solution)/shard_map/ppermute | solution.py:256
  114.6 2.8 %collective-permute-start.62 = (bf16[144,128]{1,0:T(8,128)(2,1)S(1)}, bf16[144,128]{1,0:T(8,128)(2,1)S(1)}, u32[]{:S(2)}, u32[]{:S(2)}) collective-permute-start(bf16[144,128]{1,0:T(8,128)(2,1)S(1)} %get-tuple-element.164), channel_id=1, source_target_pairs={{0,30},{1,31},{2,28},{3,29},{4,26},{5,27},{6,24},{7,25},{8,22},{9,... | collective-permute-start | bytes 110600 | tf_op jit(solution)/shard_map/ppermute | solution.py:256
  117.4 2.0 %collective-permute-start.63 = (bf16[144,128]{1,0:T(8,128)(2,1)S(1)}, bf16[144,128]{1,0:T(8,128)(2,1)S(1)}, u32[]{:S(2)}, u32[]{:S(2)}) collective-permute-start(bf16[144,128]{1,0:T(8,128)(2,1)S(1)} %get-tuple-element.165), channel_id=1, source_target_pairs={{0,31},{1,30},{2,29},{3,28},{4,27},{5,26},{6,25},{7,24},{8,23},{9,... | collective-permute-start | bytes 110600 | tf_op jit(solution)/shard_map/ppermute | solution.py:256
  119.5 11.5 %attend.2 = (bf16[64,128]{1,0:T(8,128)(2,1)S(1)}, bf16[64,128]{1,0:T(8,128)(2,1)S(1)}, bf16[64,128]{1,0:T(8,128)(2,1)S(1)}, bf16[64,128]{1,0:T(8,128)(2,1)S(1)},...) custom-call(bf16[2,2048,128]{2,1,0:T(8,128)(2,1)S(1)} %assemble.1.ow, ...), custom_call_target="tpu_custom_call" | custom-call | flops 4294967296 | bytes 2097152 | tf_op jit(solution)/shard_map/attend/pallas_call | solution.py:306
  131.0 1.1 collective-permute-start.47
  132.6 1.9 collective-permute-start.67
  134.6 2.5 %collective-permute-start.71 = (bf16[64,128]{1,0:T(8,128)(2,1)S(1)}, bf16[64,128]{1,0:T(8,128)(2,1)S(1)}, u32[]{:S(2)}, u32[]{:S(2)}) collective-permute-start(bf16[64,128]{1,0:T(8,128)(2,1)S(1)} %get-tuple-element.173), channel_id=1, source_target_pairs={{0,9},{1,8},{2,11},{3,10},{4,13},{5,12},{6,15},{7,14},{8,1},{9,0},... | collective-permute-start | bytes 49160 | tf_op jit(solution)/shard_map/ppermute | solution.py:256
  137.1 3.3 %collective-permute-start.75 = (bf16[64,128]{1,0:T(8,128)(2,1)S(1)}, bf16[64,128]{1,0:T(8,128)(2,1)S(1)}, u32[]{:S(2)}, u32[]{:S(2)}) collective-permute-start(bf16[64,128]{1,0:T(8,128)(2,1)S(1)} %get-tuple-element.177), channel_id=1, source_target_pairs={{0,13},{1,12},{2,15},{3,14},{4,9},{5,8},{6,11},{7,10},{8,5},{9,4},... | collective-permute-start | bytes 49160 | tf_op jit(solution)/shard_map/ppermute | solution.py:256
  140.7 3.2 %collective-permute-start.79 = (bf16[64,128]{1,0:T(8,128)(2,1)S(1)}, bf16[64,128]{1,0:T(8,128)(2,1)S(1)}, u32[]{:S(2)}, u32[]{:S(2)}) collective-permute-start(bf16[64,128]{1,0:T(8,128)(2,1)S(1)} %get-tuple-element.181), channel_id=1, source_target_pairs={{0,17},{1,16},{2,19},{3,18},{4,21},{5,20},{6,23},{7,22},{8,25},{9,... | collective-permute-start | bytes 49160 | tf_op jit(solution)/shard_map/ppermute | solution.py:256
  145.0 3.1 %collective-permute-start.83 = (bf16[64,128]{1,0:T(8,128)(2,1)S(1)}, bf16[64,128]{1,0:T(8,128)(2,1)S(1)}, u32[]{:S(2)}, u32[]{:S(2)}) collective-permute-start(bf16[64,128]{1,0:T(8,128)(2,1)S(1)} %get-tuple-element.185), channel_id=1, source_target_pairs={{0,21},{1,20},{2,23},{3,22},{4,17},{5,16},{6,19},{7,18},{8,29},{9,... | collective-permute-start | bytes 49160 | tf_op jit(solution)/shard_map/ppermute | solution.py:256
  148.1 11.4 %attend.3 = (bf16[64,128]{1,0:T(8,128)(2,1)S(1)}, bf16[64,128]{1,0:T(8,128)(2,1)S(1)}, bf16[64,128]{1,0:T(8,128)(2,1)S(1)}, bf16[64,128]{1,0:T(8,128)(2,1)S(1)},...) custom-call(bf16[2,2048,128]{2,1,0:T(8,128)(2,1)S(1)} %assemble.1.ow, ...), custom_call_target="tpu_custom_call" | custom-call | flops 4294967296 | bytes 2097152 | tf_op jit(solution)/shard_map/attend/pallas_call | solution.py:306
  159.5 1.3 collective-permute-start.86
  160.8 3.1 %collective-permute-start.87 = (bf16[64,128]{1,0:T(8,128)(2,1)S(1)}, bf16[64,128]{1,0:T(8,128)(2,1)S(1)}, u32[]{:S(2)}, u32[]{:S(2)}) collective-permute-start(bf16[64,128]{1,0:T(8,128)(2,1)S(1)} %get-tuple-element.189), channel_id=1, source_target_pairs={{0,25},{1,24},{2,27},{3,26},{4,29},{5,28},{6,31},{7,30},{8,17},{9,... | collective-permute-start | bytes 49160 | tf_op jit(solution)/shard_map/ppermute | solution.py:256
  163.9 2.5 %collective-permute-start.90 = (bf16[64,128]{1,0:T(8,128)(2,1)S(1)}, bf16[64,128]{1,0:T(8,128)(2,1)S(1)}, u32[]{:S(2)}, u32[]{:S(2)}) collective-permute-start(bf16[64,128]{1,0:T(8,128)(2,1)S(1)} %get-tuple-element.192), channel_id=1, source_target_pairs={{0,28},{1,29},{2,30},{3,31},{4,24},{5,25},{6,26},{7,27},{8,20},{9,... | collective-permute-start | bytes 49160 | tf_op jit(solution)/shard_map/ppermute | solution.py:256
  166.4 2.6 %collective-permute-start.91 = (bf16[64,128]{1,0:T(8,128)(2,1)S(1)}, bf16[64,128]{1,0:T(8,128)(2,1)S(1)}, u32[]{:S(2)}, u32[]{:S(2)}) collective-permute-start(bf16[64,128]{1,0:T(8,128)(2,1)S(1)} %get-tuple-element.193), channel_id=1, source_target_pairs={{0,29},{1,28},{2,31},{3,30},{4,25},{5,24},{6,27},{7,26},{8,21},{9,... | collective-permute-start | bytes 49160 | tf_op jit(solution)/shard_map/ppermute | solution.py:256
  169.0 1.2 collective-permute-start.65
  170.4 2.0 collective-permute-start.69
  172.3 1.4 collective-permute-done.91.refs_29_
  173.7 1.9 collective-permute-start.73
  176.1 3.0 %collective-permute-start.77 = (bf16[64,128]{1,0:T(8,128)(2,1)S(1)}, bf16[64,128]{1,0:T(8,128)(2,1)S(1)}, u32[]{:S(2)}, u32[]{:S(2)}) collective-permute-start(bf16[64,128]{1,0:T(8,128)(2,1)S(1)} %get-tuple-element.179), channel_id=1, source_target_pairs={{0,15},{1,14},{2,13},{3,12},{4,11},{5,10},{6,9},{7,8},{8,7},{9,6},... | collective-permute-start | bytes 49160 | tf_op jit(solution)/shard_map/ppermute | solution.py:256
  179.0 2.8 %collective-permute-start.81 = (bf16[64,128]{1,0:T(8,128)(2,1)S(1)}, bf16[64,128]{1,0:T(8,128)(2,1)S(1)}, u32[]{:S(2)}, u32[]{:S(2)}) collective-permute-start(bf16[64,128]{1,0:T(8,128)(2,1)S(1)} %get-tuple-element.183), channel_id=1, source_target_pairs={{0,19},{1,18},{2,17},{3,16},{4,23},{5,22},{6,21},{7,20},{8,27},{9,... | collective-permute-start | bytes 49160 | tf_op jit(solution)/shard_map/ppermute | solution.py:256
  182.8 3.3 %collective-permute-start.85 = (bf16[64,128]{1,0:T(8,128)(2,1)S(1)}, bf16[64,128]{1,0:T(8,128)(2,1)S(1)}, u32[]{:S(2)}, u32[]{:S(2)}) collective-permute-start(bf16[64,128]{1,0:T(8,128)(2,1)S(1)} %get-tuple-element.187), channel_id=1, source_target_pairs={{0,23},{1,22},{2,21},{3,20},{4,19},{5,18},{6,17},{7,16},{8,31},{9,... | collective-permute-start | bytes 49160 | tf_op jit(solution)/shard_map/ppermute | solution.py:256
  186.2 3.7 %collective-permute-start.89 = (bf16[64,128]{1,0:T(8,128)(2,1)S(1)}, bf16[64,128]{1,0:T(8,128)(2,1)S(1)}, u32[]{:S(2)}, u32[]{:S(2)}) collective-permute-start(bf16[64,128]{1,0:T(8,128)(2,1)S(1)} %get-tuple-element.191), channel_id=1, source_target_pairs={{0,27},{1,26},{2,25},{3,24},{4,31},{5,30},{6,29},{7,28},{8,19},{9,... | collective-permute-start | bytes 49160 | tf_op jit(solution)/shard_map/ppermute | solution.py:256
  189.9 1.1 collective-permute-start.92
  191.0 4.0 %collective-permute-start.93 = (bf16[64,128]{1,0:T(8,128)(2,1)S(1)}, bf16[64,128]{1,0:T(8,128)(2,1)S(1)}, u32[]{:S(2)}, u32[]{:S(2)}) collective-permute-start(bf16[64,128]{1,0:T(8,128)(2,1)S(1)} %get-tuple-element.195), channel_id=1, source_target_pairs={{0,31},{1,30},{2,29},{3,28},{4,27},{5,26},{6,25},{7,24},{8,23},{9,... | collective-permute-start | bytes 49160 | tf_op jit(solution)/shard_map/ppermute | solution.py:256
  195.7 2.0 %collective-permute-done.93.refs_31_ = bf16[64,128]{1,0:T(8,128)(2,1)S(1)} collective-permute-done((bf16[64,128]{1,0:T(8,128)(2,1)S(1)}, bf16[64,128]{1,0:T(8,128)(2,1)S(1)}, u32[]{:S(2)}, u32[]{:S(2)}) %collective-permute-start.93) | collective-permute-done | bytes 16416 | tf_op jit(solution)/shard_map/ppermute | solution.py:256
  (147 shorter events, 22.5 us)
Async XLA Ops:
  6.6 6.8 %collective-permute-start.3 = (bf16[128,128]{1,0:T(8,128)(2,1)S(1)}, bf16[128,128]{1,0:T(8,128)(2,1)S(1)}, u32[]{:S(2)}, u32[]{:S(2)}) collective-permute-start(bf16[128,128]{1,0:T(8,128)(2,1)S(1)} %get-tuple-element.104), channel_id=1, source_target_pairs={{0,4},{1,5},{2,6},{3,7},{4,0},{5,1},{6,2},{7,3},{8,12},{9,13},{10,... | collective-permute-start | bytes 98312 | tf_op jit(solution)/shard_map/ppermute | solution.py:256
  11.7 7.3 %collective-permute-start.7 = (bf16[128,128]{1,0:T(8,128)(2,1)S(1)}, bf16[128,128]{1,0:T(8,128)(2,1)S(1)}, u32[]{:S(2)}, u32[]{:S(2)}) collective-permute-start(bf16[128,128]{1,0:T(8,128)(2,1)S(1)} %get-tuple-element.108), channel_id=1, source_target_pairs={{0,8},{1,9},{2,10},{3,11},{4,12},{5,13},{6,14},{7,15},{8,0},{9,1},... | collective-permute-start | bytes 98312 | tf_op jit(solution)/shard_map/ppermute | solution.py:256
  13.4 6.9 %collective-permute-start.8 = (bf16[128,128]{1,0:T(8,128)(2,1)S(1)}, bf16[128,128]{1,0:T(8,128)(2,1)S(1)}, u32[]{:S(2)}, u32[]{:S(2)}) collective-permute-start(bf16[128,128]{1,0:T(8,128)(2,1)S(1)} %get-tuple-element.109), channel_id=1, source_target_pairs={{0,9},{1,8},{2,11},{3,10},{4,13},{5,12},{6,15},{7,14},{8,1},{9,0},... | collective-permute-start | bytes 98312 | tf_op jit(solution)/shard_map/ppermute | solution.py:256
  15.3 7.7 %collective-permute-start.10 = (bf16[128,128]{1,0:T(8,128)(2,1)S(1)}, bf16[128,128]{1,0:T(8,128)(2,1)S(1)}, u32[]{:S(2)}, u32[]{:S(2)}) collective-permute-start(bf16[128,128]{1,0:T(8,128)(2,1)S(1)} %get-tuple-element.111), channel_id=1, source_target_pairs={{0,11},{1,10},{2,9},{3,8},{4,15},{5,14},{6,13},{7,12},{8,3},{9,2},... | collective-permute-start | bytes 98312 | tf_op jit(solution)/shard_map/ppermute | solution.py:256
  16.4 9.1 %collective-permute-start.11 = (bf16[128,128]{1,0:T(8,128)(2,1)S(1)}, bf16[128,128]{1,0:T(8,128)(2,1)S(1)}, u32[]{:S(2)}, u32[]{:S(2)}) collective-permute-start(bf16[128,128]{1,0:T(8,128)(2,1)S(1)} %get-tuple-element.112), channel_id=1, source_target_pairs={{0,12},{1,13},{2,14},{3,15},{4,8},{5,9},{6,10},{7,11},{8,4},{9,5},... | collective-permute-start | bytes 98312 | tf_op jit(solution)/shard_map/ppermute | solution.py:256
  19.0 7.8 %collective-permute-start.12 = (bf16[128,128]{1,0:T(8,128)(2,1)S(1)}, bf16[128,128]{1,0:T(8,128)(2,1)S(1)}, u32[]{:S(2)}, u32[]{:S(2)}) collective-permute-start(bf16[128,128]{1,0:T(8,128)(2,1)S(1)} %get-tuple-element.113), channel_id=1, source_target_pairs={{0,13},{1,12},{2,15},{3,14},{4,9},{5,8},{6,11},{7,10},{8,5},{9,4},... | collective-permute-start | bytes 98312 | tf_op jit(solution)/shard_map/ppermute | solution.py:256
  20.3 8.2 %collective-permute-start.13 = (bf16[128,128]{1,0:T(8,128)(2,1)S(1)}, bf16[128,128]{1,0:T(8,128)(2,1)S(1)}, u32[]{:S(2)}, u32[]{:S(2)}) collective-permute-start(bf16[128,128]{1,0:T(8,128)(2,1)S(1)} %get-tuple-element.114), channel_id=1, source_target_pairs={{0,14},{1,15},{2,12},{3,13},{4,10},{5,11},{6,8},{7,9},{8,6},{9,7},... | collective-permute-start | bytes 98312 | tf_op jit(solution)/shard_map/ppermute | solution.py:256
  20.8 8.7 %collective-permute-start.14 = (bf16[128,128]{1,0:T(8,128)(2,1)S(1)}, bf16[128,128]{1,0:T(8,128)(2,1)S(1)}, u32[]{:S(2)}, u32[]{:S(2)}) collective-permute-start(bf16[128,128]{1,0:T(8,128)(2,1)S(1)} %get-tuple-element.115), channel_id=1, source_target_pairs={{0,15},{1,14},{2,13},{3,12},{4,11},{5,10},{6,9},{7,8},{8,7},{9,6},... | collective-permute-start | bytes 98312 | tf_op jit(solution)/shard_map/ppermute | solution.py:256
  23.0 10.0 %collective-permute-start.15 = (bf16[128,128]{1,0:T(8,128)(2,1)S(1)}, bf16[128,128]{1,0:T(8,128)(2,1)S(1)}, u32[]{:S(2)}, u32[]{:S(2)}) collective-permute-start(bf16[128,128]{1,0:T(8,128)(2,1)S(1)} %get-tuple-element.116), channel_id=1, source_target_pairs={{0,16},{1,17},{2,18},{3,19},{4,20},{5,21},{6,22},{7,23},{8,24},{9,... | collective-permute-start | bytes 98312 | tf_op jit(solution)/shard_map/ppermute | solution.py:256
  25.6 8.6 %collective-permute-start.16 = (bf16[128,128]{1,0:T(8,128)(2,1)S(1)}, bf16[128,128]{1,0:T(8,128)(2,1)S(1)}, u32[]{:S(2)}, u32[]{:S(2)}) collective-permute-start(bf16[128,128]{1,0:T(8,128)(2,1)S(1)} %get-tuple-element.117), channel_id=1, source_target_pairs={{0,17},{1,16},{2,19},{3,18},{4,21},{5,20},{6,23},{7,22},{8,25},{9,... | collective-permute-start | bytes 98312 | tf_op jit(solution)/shard_map/ppermute | solution.py:256
  26.8 8.8 %collective-permute-start.17 = (bf16[128,128]{1,0:T(8,128)(2,1)S(1)}, bf16[128,128]{1,0:T(8,128)(2,1)S(1)}, u32[]{:S(2)}, u32[]{:S(2)}) collective-permute-start(bf16[128,128]{1,0:T(8,128)(2,1)S(1)} %get-tuple-element.118), channel_id=1, source_target_pairs={{0,18},{1,19},{2,16},{3,17},{4,22},{5,23},{6,20},{7,21},{8,26},{9,... | collective-permute-start | bytes 98312 | tf_op jit(solution)/shard_map/ppermute | solution.py:256
  28.5 9.2 %collective-permute-start.18 = (bf16[128,128]{1,0:T(8,128)(2,1)S(1)}, bf16[128,128]{1,0:T(8,128)(2,1)S(1)}, u32[]{:S(2)}, u32[]{:S(2)}) collective-permute-start(bf16[128,128]{1,0:T(8,128)(2,1)S(1)} %get-tuple-element.119), channel_id=1, source_target_pairs={{0,19},{1,18},{2,17},{3,16},{4,23},{5,22},{6,21},{7,20},{8,27},{9,... | collective-permute-start | bytes 98312 | tf_op jit(solution)/shard_map/ppermute | solution.py:256
  29.4 11.9 %collective-permute-start.19 = (bf16[128,128]{1,0:T(8,128)(2,1)S(1)}, bf16[128,128]{1,0:T(8,128)(2,1)S(1)}, u32[]{:S(2)}, u32[]{:S(2)}) collective-permute-start(bf16[128,128]{1,0:T(8,128)(2,1)S(1)} %get-tuple-element.120), channel_id=1, source_target_pairs={{0,20},{1,21},{2,22},{3,23},{4,16},{5,17},{6,18},{7,19},{8,28},{9,... | collective-permute-start | bytes 98312 | tf_op jit(solution)/shard_map/ppermute | solution.py:256
  33.0 9.5 %collective-permute-start.20 = (bf16[128,128]{1,0:T(8,128)(2,1)S(1)}, bf16[128,128]{1,0:T(8,128)(2,1)S(1)}, u32[]{:S(2)}, u32[]{:S(2)}) collective-permute-start(bf16[128,128]{1,0:T(8,128)(2,1)S(1)} %get-tuple-element.121), channel_id=1, source_target_pairs={{0,21},{1,20},{2,23},{3,22},{4,17},{5,16},{6,19},{7,18},{8,29},{9,... | collective-permute-start | bytes 98312 | tf_op jit(solution)/shard_map/ppermute | solution.py:256
  34.2 8.8 %collective-permute-start.21 = (bf16[128,128]{1,0:T(8,128)(2,1)S(1)}, bf16[128,128]{1,0:T(8,128)(2,1)S(1)}, u32[]{:S(2)}, u32[]{:S(2)}) collective-permute-start(bf16[128,128]{1,0:T(8,128)(2,1)S(1)} %get-tuple-element.122), channel_id=1, source_target_pairs={{0,22},{1,23},{2,20},{3,21},{4,18},{5,19},{6,16},{7,17},{8,30},{9,... | collective-permute-start | bytes 98312 | tf_op jit(solution)/shard_map/ppermute | solution.py:256
  35.6 10.4 %collective-permute-start.22 = (bf16[128,128]{1,0:T(8,128)(2,1)S(1)}, bf16[128,128]{1,0:T(8,128)(2,1)S(1)}, u32[]{:S(2)}, u32[]{:S(2)}) collective-permute-start(bf16[128,128]{1,0:T(8,128)(2,1)S(1)} %get-tuple-element.123), channel_id=1, source_target_pairs={{0,23},{1,22},{2,21},{3,20},{4,19},{5,18},{6,17},{7,16},{8,31},{9,... | collective-permute-start | bytes 98312 | tf_op jit(solution)/shard_map/ppermute | solution.py:256
  37.7 12.9 %collective-permute-start.23 = (bf16[128,128]{1,0:T(8,128)(2,1)S(1)}, bf16[128,128]{1,0:T(8,128)(2,1)S(1)}, u32[]{:S(2)}, u32[]{:S(2)}) collective-permute-start(bf16[128,128]{1,0:T(8,128)(2,1)S(1)} %get-tuple-element.124), channel_id=1, source_target_pairs={{0,24},{1,25},{2,26},{3,27},{4,28},{5,29},{6,30},{7,31},{8,16},{9,... | collective-permute-start | bytes 98312 | tf_op jit(solution)/shard_map/ppermute | solution.py:256
  41.4 10.3 %collective-permute-start.24 = (bf16[128,128]{1,0:T(8,128)(2,1)S(1)}, bf16[128,128]{1,0:T(8,128)(2,1)S(1)}, u32[]{:S(2)}, u32[]{:S(2)}) collective-permute-start(bf16[128,128]{1,0:T(8,128)(2,1)S(1)} %get-tuple-element.125), channel_id=1, source_target_pairs={{0,25},{1,24},{2,27},{3,26},{4,29},{5,28},{6,31},{7,30},{8,17},{9,... | collective-permute-start | bytes 98312 | tf_op jit(solution)/shard_map/ppermute | solution.py:256
  42.5 9.6 %collective-permute-start.25 = (bf16[128,128]{1,0:T(8,128)(2,1)S(1)}, bf16[128,128]{1,0:T(8,128)(2,1)S(1)}, u32[]{:S(2)}, u32[]{:S(2)}) collective-permute-start(bf16[128,128]{1,0:T(8,128)(2,1)S(1)} %get-tuple-element.126), channel_id=1, source_target_pairs={{0,26},{1,27},{2,24},{3,25},{4,30},{5,31},{6,28},{7,29},{8,18},{9,... | collective-permute-start | bytes 98312 | tf_op jit(solution)/shard_map/ppermute | solution.py:256
  43.0 13.1 %collective-permute-start.26 = (bf16[128,128]{1,0:T(8,128)(2,1)S(1)}, bf16[128,128]{1,0:T(8,128)(2,1)S(1)}, u32[]{:S(2)}, u32[]{:S(2)}) collective-permute-start(bf16[128,128]{1,0:T(8,128)(2,1)S(1)} %get-tuple-element.127), channel_id=1, source_target_pairs={{0,27},{1,26},{2,25},{3,24},{4,31},{5,30},{6,29},{7,28},{8,19},{9,... | collective-permute-start | bytes 98312 | tf_op jit(solution)/shard_map/ppermute | solution.py:256
  46.0 10.1 %collective-permute-start.27 = (bf16[128,128]{1,0:T(8,128)(2,1)S(1)}, bf16[128,128]{1,0:T(8,128)(2,1)S(1)}, u32[]{:S(2)}, u32[]{:S(2)}) collective-permute-start(bf16[128,128]{1,0:T(8,128)(2,1)S(1)} %get-tuple-element.128), channel_id=1, source_target_pairs={{0,28},{1,29},{2,30},{3,31},{4,24},{5,25},{6,26},{7,27},{8,20},{9,... | collective-permute-start | bytes 98312 | tf_op jit(solution)/shard_map/ppermute | solution.py:256
  50.6 7.5 %collective-permute-start.28 = (bf16[128,128]{1,0:T(8,128)(2,1)S(1)}, bf16[128,128]{1,0:T(8,128)(2,1)S(1)}, u32[]{:S(2)}, u32[]{:S(2)}) collective-permute-start(bf16[128,128]{1,0:T(8,128)(2,1)S(1)} %get-tuple-element.129), channel_id=1, source_target_pairs={{0,29},{1,28},{2,31},{3,30},{4,25},{5,24},{6,27},{7,26},{8,21},{9,... | collective-permute-start | bytes 98312 | tf_op jit(solution)/shard_map/ppermute | solution.py:256
  52.1 6.9 %collective-permute-start.30 = (bf16[128,128]{1,0:T(8,128)(2,1)S(1)}, bf16[128,128]{1,0:T(8,128)(2,1)S(1)}, u32[]{:S(2)}, u32[]{:S(2)}) collective-permute-start(bf16[128,128]{1,0:T(8,128)(2,1)S(1)} %get-tuple-element.131), channel_id=1, source_target_pairs={{0,31},{1,30},{2,29},{3,28},{4,27},{5,26},{6,25},{7,24},{8,23},{9,... | collective-permute-start | bytes 98312 | tf_op jit(solution)/shard_map/ppermute | solution.py:256
  59.3 58.2 %collective-permute-start.31 = (bf16[2,2048,128]{2,1,0:T(8,128)(2,1)S(1)}, bf16[2,2048,128]{2,1,0:T(8,128)(2,1)S(1)}, u32[]{:S(2)}, u32[]{:S(2)}) collective-permute-start(bf16[2,2048,128]{2,1,0:T(8,128)(2,1)S(1)} %assemble.1.own_ref), channel_id=1, source_target_pairs={{0,2},{2,0},{4,6},{6,4},{8,10},{10,8},{12,14},{14,12},{16,18},{18,... | collective-permute-start | bytes 3145736 | tf_op jit(solution)/shard_map/ppermute | solution.py:296
  72.7 6.8 %collective-permute-start.37 = (bf16[144,128]{1,0:T(8,128)(2,1)S(1)}, bf16[144,128]{1,0:T(8,128)(2,1)S(1)}, u32[]{:S(2)}, u32[]{:S(2)}) collective-permute-start(bf16[144,128]{1,0:T(8,128)(2,1)S(1)} %get-tuple-element.138), channel_id=1, source_target_pairs={{0,12},{1,13},{2,14},{3,15},{4,8},{5,9},{6,10},{7,11},{8,4},{9,5},... | collective-permute-start | bytes 110600 | tf_op jit(solution)/shard_map/ppermute | solution.py:256
  76.5 7.7 %collective-permute-start.39 = (bf16[144,128]{1,0:T(8,128)(2,1)S(1)}, bf16[144,128]{1,0:T(8,128)(2,1)S(1)}, u32[]{:S(2)}, u32[]{:S(2)}) collective-permute-start(bf16[144,128]{1,0:T(8,128)(2,1)S(1)} %get-tuple-element.140), channel_id=1, source_target_pairs={{0,16},{1,17},{2,18},{3,19},{4,20},{5,21},{6,22},{7,23},{8,24},{9,... | collective-permute-start | bytes 110600 | tf_op jit(solution)/shard_map/ppermute | solution.py:256
  76.5 8.2 %collective-permute-start.40 = (bf16[144,128]{1,0:T(8,128)(2,1)S(1)}, bf16[144,128]{1,0:T(8,128)(2,1)S(1)}, u32[]{:S(2)}, u32[]{:S(2)}) collective-permute-start(bf16[144,128]{1,0:T(8,128)(2,1)S(1)} %get-tuple-element.141), channel_id=1, source_target_pairs={{0,17},{1,16},{2,19},{3,18},{4,21},{5,20},{6,23},{7,22},{8,25},{9,... | collective-permute-start | bytes 110600 | tf_op jit(solution)/shard_map/ppermute | solution.py:256
  79.4 8.6 %collective-permute-start.41 = (bf16[144,128]{1,0:T(8,128)(2,1)S(1)}, bf16[144,128]{1,0:T(8,128)(2,1)S(1)}, u32[]{:S(2)}, u32[]{:S(2)}) collective-permute-start(bf16[144,128]{1,0:T(8,128)(2,1)S(1)} %get-tuple-element.142), channel_id=1, source_target_pairs={{0,20},{1,21},{2,22},{3,23},{4,16},{5,17},{6,18},{7,19},{8,28},{9,... | collective-permute-start | bytes 110600 | tf_op jit(solution)/shard_map/ppermute | solution.py:256
  79.5 9.5 %collective-permute-start.42 = (bf16[144,128]{1,0:T(8,128)(2,1)S(1)}, bf16[144,128]{1,0:T(8,128)(2,1)S(1)}, u32[]{:S(2)}, u32[]{:S(2)}) collective-permute-start(bf16[144,128]{1,0:T(8,128)(2,1)S(1)} %get-tuple-element.143), channel_id=1, source_target_pairs={{0,21},{1,20},{2,23},{3,22},{4,17},{5,16},{6,19},{7,18},{8,29},{9,... | collective-permute-start | bytes 110600 | tf_op jit(solution)/shard_map/ppermute | solution.py:256
  84.1 9.5 %collective-permute-start.43 = (bf16[144,128]{1,0:T(8,128)(2,1)S(1)}, bf16[144,128]{1,0:T(8,128)(2,1)S(1)}, u32[]{:S(2)}, u32[]{:S(2)}) collective-permute-start(bf16[144,128]{1,0:T(8,128)(2,1)S(1)} %get-tuple-element.144), channel_id=1, source_target_pairs={{0,24},{1,25},{2,26},{3,27},{4,28},{5,29},{6,30},{7,31},{8,16},{9,... | collective-permute-start | bytes 110600 | tf_op jit(solution)/shard_map/ppermute | solution.py:256
  84.7 8.9 %collective-permute-start.44 = (bf16[144,128]{1,0:T(8,128)(2,1)S(1)}, bf16[144,128]{1,0:T(8,128)(2,1)S(1)}, u32[]{:S(2)}, u32[]{:S(2)}) collective-permute-start(bf16[144,128]{1,0:T(8,128)(2,1)S(1)} %get-tuple-element.145), channel_id=1, source_target_pairs={{0,25},{1,24},{2,27},{3,26},{4,29},{5,28},{6,31},{7,30},{8,17},{9,... | collective-permute-start | bytes 110600 | tf_op jit(solution)/shard_map/ppermute | solution.py:256
  89.0 7.6 %collective-permute-start.46 = (bf16[144,128]{1,0:T(8,128)(2,1)S(1)}, bf16[144,128]{1,0:T(8,128)(2,1)S(1)}, u32[]{:S(2)}, u32[]{:S(2)}) collective-permute-start(bf16[144,128]{1,0:T(8,128)(2,1)S(1)} %get-tuple-element.147), channel_id=1, source_target_pairs={{0,29},{1,28},{2,31},{3,30},{4,25},{5,24},{6,27},{7,26},{8,21},{9,... | collective-permute-start | bytes 110600 | tf_op jit(solution)/shard_map/ppermute | solution.py:256
  97.3 8.7 %collective-permute-start.53 = (bf16[144,128]{1,0:T(8,128)(2,1)S(1)}, bf16[144,128]{1,0:T(8,128)(2,1)S(1)}, u32[]{:S(2)}, u32[]{:S(2)}) collective-permute-start(bf16[144,128]{1,0:T(8,128)(2,1)S(1)} %get-tuple-element.155), channel_id=1, source_target_pairs={{0,11},{1,10},{2,9},{3,8},{4,15},{5,14},{6,13},{7,12},{8,3},{9,2},... | collective-permute-start | bytes 110600 | tf_op jit(solution)/shard_map/ppermute | solution.py:256
  99.1 7.0 %collective-permute-start.54 = (bf16[144,128]{1,0:T(8,128)(2,1)S(1)}, bf16[144,128]{1,0:T(8,128)(2,1)S(1)}, u32[]{:S(2)}, u32[]{:S(2)}) collective-permute-start(bf16[144,128]{1,0:T(8,128)(2,1)S(1)} %get-tuple-element.156), channel_id=1, source_target_pairs={{0,14},{1,15},{2,12},{3,13},{4,10},{5,11},{6,8},{7,9},{8,6},{9,7},... | collective-permute-start | bytes 110600 | tf_op jit(solution)/shard_map/ppermute | solution.py:256
  100.9 8.2 %collective-permute-start.55 = (bf16[144,128]{1,0:T(8,128)(2,1)S(1)}, bf16[144,128]{1,0:T(8,128)(2,1)S(1)}, u32[]{:S(2)}, u32[]{:S(2)}) collective-permute-start(bf16[144,128]{1,0:T(8,128)(2,1)S(1)} %get-tuple-element.157), channel_id=1, source_target_pairs={{0,15},{1,14},{2,13},{3,12},{4,11},{5,10},{6,9},{7,8},{8,7},{9,6},... | collective-permute-start | bytes 110600 | tf_op jit(solution)/shard_map/ppermute | solution.py:256
  102.6 8.0 %collective-permute-start.56 = (bf16[144,128]{1,0:T(8,128)(2,1)S(1)}, bf16[144,128]{1,0:T(8,128)(2,1)S(1)}, u32[]{:S(2)}, u32[]{:S(2)}) collective-permute-start(bf16[144,128]{1,0:T(8,128)(2,1)S(1)} %get-tuple-element.158), channel_id=1, source_target_pairs={{0,18},{1,19},{2,16},{3,17},{4,22},{5,23},{6,20},{7,21},{8,26},{9,... | collective-permute-start | bytes 110600 | tf_op jit(solution)/shard_map/ppermute | solution.py:256
  106.0 7.8 %collective-permute-start.57 = (bf16[144,128]{1,0:T(8,128)(2,1)S(1)}, bf16[144,128]{1,0:T(8,128)(2,1)S(1)}, u32[]{:S(2)}, u32[]{:S(2)}) collective-permute-start(bf16[144,128]{1,0:T(8,128)(2,1)S(1)} %get-tuple-element.159), channel_id=1, source_target_pairs={{0,19},{1,18},{2,17},{3,16},{4,23},{5,22},{6,21},{7,20},{8,27},{9,... | collective-permute-start | bytes 110600 | tf_op jit(solution)/shard_map/ppermute | solution.py:256
  106.1 8.6 %collective-permute-start.58 = (bf16[144,128]{1,0:T(8,128)(2,1)S(1)}, bf16[144,128]{1,0:T(8,128)(2,1)S(1)}, u32[]{:S(2)}, u32[]{:S(2)}) collective-permute-start(bf16[144,128]{1,0:T(8,128)(2,1)S(1)} %get-tuple-element.160), channel_id=1, source_target_pairs={{0,22},{1,23},{2,20},{3,21},{4,18},{5,19},{6,16},{7,17},{8,30},{9,... | collective-permute-start | bytes 110600 | tf_op jit(solution)/shard_map/ppermute | solution.py:256
  109.1 21.9 %collective-permute-start.59 = (bf16[144,128]{1,0:T(8,128)(2,1)S(1)}, bf16[144,128]{1,0:T(8,128)(2,1)S(1)}, u32[]{:S(2)}, u32[]{:S(2)}) collective-permute-start(bf16[144,128]{1,0:T(8,128)(2,1)S(1)} %get-tuple-element.161), channel_id=1, source_target_pairs={{0,23},{1,22},{2,21},{3,20},{4,19},{5,18},{6,17},{7,16},{8,31},{9,... | collective-permute-start | bytes 110600 | tf_op jit(solution)/shard_map/ppermute | solution.py:256
  110.6 21.6 %collective-permute-start.60 = (bf16[144,128]{1,0:T(8,128)(2,1)S(1)}, bf16[144,128]{1,0:T(8,128)(2,1)S(1)}, u32[]{:S(2)}, u32[]{:S(2)}) collective-permute-start(bf16[144,128]{1,0:T(8,128)(2,1)S(1)} %get-tuple-element.162), channel_id=1, source_target_pairs={{0,26},{1,27},{2,24},{3,25},{4,30},{5,31},{6,28},{7,29},{8,18},{9,... | collective-permute-start | bytes 110600 | tf_op jit(solution)/shard_map/ppermute | solution.py:256
  113.9 18.8 %collective-permute-start.61 = (bf16[144,128]{1,0:T(8,128)(2,1)S(1)}, bf16[144,128]{1,0:T(8,128)(2,1)S(1)}, u32[]{:S(2)}, u32[]{:S(2)}) collective-permute-start(bf16[144,128]{1,0:T(8,128)(2,1)S(1)} %get-tuple-element.163), channel_id=1, source_target_pairs={{0,27},{1,26},{2,25},{3,24},{4,31},{5,30},{6,29},{7,28},{8,19},{9,... | collective-permute-start | bytes 110600 | tf_op jit(solution)/shard_map/ppermute | solution.py:256
  114.6 19.9 %collective-permute-start.62 = (bf16[144,128]{1,0:T(8,128)(2,1)S(1)}, bf16[144,128]{1,0:T(8,128)(2,1)S(1)}, u32[]{:S(2)}, u32[]{:S(2)}) collective-permute-start(bf16[144,128]{1,0:T(8,128)(2,1)S(1)} %get-tuple-element.164), channel_id=1, source_target_pairs={{0,30},{1,31},{2,28},{3,29},{4,26},{5,27},{6,24},{7,25},{8,22},{9,... | collective-permute-start | bytes 110600 | tf_op jit(solution)/shard_map/ppermute | solution.py:256
  117.4 17.1 %collective-permute-start.63 = (bf16[144,128]{1,0:T(8,128)(2,1)S(1)}, bf16[144,128]{1,0:T(8,128)(2,1)S(1)}, u32[]{:S(2)}, u32[]{:S(2)}) collective-permute-start(bf16[144,128]{1,0:T(8,128)(2,1)S(1)} %get-tuple-element.165), channel_id=1, source_target_pairs={{0,31},{1,30},{2,29},{3,28},{4,27},{5,26},{6,25},{7,24},{8,23},{9,... | collective-permute-start | bytes 110600 | tf_op jit(solution)/shard_map/ppermute | solution.py:256
  132.6 7.8 %collective-permute-start.67 = (bf16[64,128]{1,0:T(8,128)(2,1)S(1)}, bf16[64,128]{1,0:T(8,128)(2,1)S(1)}, u32[]{:S(2)}, u32[]{:S(2)}) collective-permute-start(bf16[64,128]{1,0:T(8,128)(2,1)S(1)} %get-tuple-element.169), channel_id=1, source_target_pairs={{0,5},{1,4},{2,7},{3,6},{4,1},{5,0},{6,3},{7,2},{8,13},{9,12},{10,... | collective-permute-start | bytes 49160 | tf_op jit(solution)/shard_map/ppermute | solution.py:256
  134.6 9.3 %collective-permute-start.71 = (bf16[64,128]{1,0:T(8,128)(2,1)S(1)}, bf16[64,128]{1,0:T(8,128)(2,1)S(1)}, u32[]{:S(2)}, u32[]{:S(2)}) collective-permute-start(bf16[64,128]{1,0:T(8,128)(2,1)S(1)} %get-tuple-element.173), channel_id=1, source_target_pairs={{0,9},{1,8},{2,11},{3,10},{4,13},{5,12},{6,15},{7,14},{8,1},{9,0},... | collective-permute-start | bytes 49160 | tf_op jit(solution)/shard_map/ppermute | solution.py:256
  137.1 7.9 %collective-permute-start.74 = (bf16[64,128]{1,0:T(8,128)(2,1)S(1)}, bf16[64,128]{1,0:T(8,128)(2,1)S(1)}, u32[]{:S(2)}, u32[]{:S(2)}) collective-permute-start(bf16[64,128]{1,0:T(8,128)(2,1)S(1)} %get-tuple-element.176), channel_id=1, source_target_pairs={{0,12},{1,13},{2,14},{3,15},{4,8},{5,9},{6,10},{7,11},{8,4},{9,5},... | collective-permute-start | bytes 49160 | tf_op jit(solution)/shard_map/ppermute | solution.py:256
  137.1 22.3 %collective-permute-start.75 = (bf16[64,128]{1,0:T(8,128)(2,1)S(1)}, bf16[64,128]{1,0:T(8,128)(2,1)S(1)}, u32[]{:S(2)}, u32[]{:S(2)}) collective-permute-start(bf16[64,128]{1,0:T(8,128)(2,1)S(1)} %get-tuple-element.177), channel_id=1, source_target_pairs={{0,13},{1,12},{2,15},{3,14},{4,9},{5,8},{6,11},{7,10},{8,5},{9,4},... | collective-permute-start | bytes 49160 | tf_op jit(solution)/shard_map/ppermute | solution.py:256
  140.4 20.3 %collective-permute-start.78 = (bf16[64,128]{1,0:T(8,128)(2,1)S(1)}, bf16[64,128]{1,0:T(8,128)(2,1)S(1)}, u32[]{:S(2)}, u32[]{:S(2)}) collective-permute-start(bf16[64,128]{1,0:T(8,128)(2,1)S(1)} %get-tuple-element.180), channel_id=1, source_target_pairs={{0,16},{1,17},{2,18},{3,19},{4,20},{5,21},{6,22},{7,23},{8,24},{9,... | collective-permute-start | bytes 49160 | tf_op jit(solution)/shard_map/ppermute | solution.py:256
  140.7 23.2 %collective-permute-start.79 = (bf16[64,128]{1,0:T(8,128)(2,1)S(1)}, bf16[64,128]{1,0:T(8,128)(2,1)S(1)}, u32[]{:S(2)}, u32[]{:S(2)}) collective-permute-start(bf16[64,128]{1,0:T(8,128)(2,1)S(1)} %get-tuple-element.181), channel_id=1, source_target_pairs={{0,17},{1,16},{2,19},{3,18},{4,21},{5,20},{6,23},{7,22},{8,25},{9,... | collective-permute-start | bytes 49160 | tf_op jit(solution)/shard_map/ppermute | solution.py:256
  143.9 22.5 %collective-permute-start.82 = (bf16[64,128]{1,0:T(8,128)(2,1)S(1)}, bf16[64,128]{1,0:T(8,128)(2,1)S(1)}, u32[]{:S(2)}, u32[]{:S(2)}) collective-permute-start(bf16[64,128]{1,0:T(8,128)(2,1)S(1)} %get-tuple-element.184), channel_id=1, source_target_pairs={{0,20},{1,21},{2,22},{3,23},{4,16},{5,17},{6,18},{7,19},{8,28},{9,... | collective-permute-start | bytes 49160 | tf_op jit(solution)/shard_map/ppermute | solution.py:256
  145.0 24.0 %collective-permute-start.83 = (bf16[64,128]{1,0:T(8,128)(2,1)S(1)}, bf16[64,128]{1,0:T(8,128)(2,1)S(1)}, u32[]{:S(2)}, u32[]{:S(2)}) collective-permute-start(bf16[64,128]{1,0:T(8,128)(2,1)S(1)} %get-tuple-element.185), channel_id=1, source_target_pairs={{0,21},{1,20},{2,23},{3,22},{4,17},{5,16},{6,19},{7,18},{8,29},{9,... | collective-permute-start | bytes 49160 | tf_op jit(solution)/shard_map/ppermute | solution.py:256
  159.5 9.5 %collective-permute-start.86 = (bf16[64,128]{1,0:T(8,128)(2,1)S(1)}, bf16[64,128]{1,0:T(8,128)(2,1)S(1)}, u32[]{:S(2)}, u32[]{:S(2)}) collective-permute-start(bf16[64,128]{1,0:T(8,128)(2,1)S(1)} %get-tuple-element.188), channel_id=1, source_target_pairs={{0,24},{1,25},{2,26},{3,27},{4,28},{5,29},{6,30},{7,31},{8,16},{9,... | collective-permute-start | bytes 49160 | tf_op jit(solution)/shard_map/ppermute | solution.py:256
  160.8 9.4 %collective-permute-start.87 = (bf16[64,128]{1,0:T(8,128)(2,1)S(1)}, bf16[64,128]{1,0:T(8,128)(2,1)S(1)}, u32[]{:S(2)}, u32[]{:S(2)}) collective-permute-start(bf16[64,128]{1,0:T(8,128)(2,1)S(1)} %get-tuple-element.189), channel_id=1, source_target_pairs={{0,25},{1,24},{2,27},{3,26},{4,29},{5,28},{6,31},{7,30},{8,17},{9,... | collective-permute-start | bytes 49160 | tf_op jit(solution)/shard_map/ppermute | solution.py:256
  166.4 7.3 %collective-permute-start.91 = (bf16[64,128]{1,0:T(8,128)(2,1)S(1)}, bf16[64,128]{1,0:T(8,128)(2,1)S(1)}, u32[]{:S(2)}, u32[]{:S(2)}) collective-permute-start(bf16[64,128]{1,0:T(8,128)(2,1)S(1)} %get-tuple-element.193), channel_id=1, source_target_pairs={{0,29},{1,28},{2,31},{3,30},{4,25},{5,24},{6,27},{7,26},{8,21},{9,... | collective-permute-start | bytes 49160 | tf_op jit(solution)/shard_map/ppermute | solution.py:256
  170.4 8.7 %collective-permute-start.69 = (bf16[64,128]{1,0:T(8,128)(2,1)S(1)}, bf16[64,128]{1,0:T(8,128)(2,1)S(1)}, u32[]{:S(2)}, u32[]{:S(2)}) collective-permute-start(bf16[64,128]{1,0:T(8,128)(2,1)S(1)} %get-tuple-element.171), channel_id=1, source_target_pairs={{0,7},{1,6},{2,5},{3,4},{4,3},{5,2},{6,1},{7,0},{8,15},{9,14},{10,... | collective-permute-start | bytes 49160 | tf_op jit(solution)/shard_map/ppermute | solution.py:256
  173.7 8.1 %collective-permute-start.73 = (bf16[64,128]{1,0:T(8,128)(2,1)S(1)}, bf16[64,128]{1,0:T(8,128)(2,1)S(1)}, u32[]{:S(2)}, u32[]{:S(2)}) collective-permute-start(bf16[64,128]{1,0:T(8,128)(2,1)S(1)} %get-tuple-element.175), channel_id=1, source_target_pairs={{0,11},{1,10},{2,9},{3,8},{4,15},{5,14},{6,13},{7,12},{8,3},{9,2},... | collective-permute-start | bytes 49160 | tf_op jit(solution)/shard_map/ppermute | solution.py:256
  175.6 7.2 %collective-permute-start.76 = (bf16[64,128]{1,0:T(8,128)(2,1)S(1)}, bf16[64,128]{1,0:T(8,128)(2,1)S(1)}, u32[]{:S(2)}, u32[]{:S(2)}) collective-permute-start(bf16[64,128]{1,0:T(8,128)(2,1)S(1)} %get-tuple-element.178), channel_id=1, source_target_pairs={{0,14},{1,15},{2,12},{3,13},{4,10},{5,11},{6,8},{7,9},{8,6},{9,7},... | collective-permute-start | bytes 49160 | tf_op jit(solution)/shard_map/ppermute | solution.py:256
  176.1 10.1 %collective-permute-start.77 = (bf16[64,128]{1,0:T(8,128)(2,1)S(1)}, bf16[64,128]{1,0:T(8,128)(2,1)S(1)}, u32[]{:S(2)}, u32[]{:S(2)}) collective-permute-start(bf16[64,128]{1,0:T(8,128)(2,1)S(1)} %get-tuple-element.179), channel_id=1, source_target_pairs={{0,15},{1,14},{2,13},{3,12},{4,11},{5,10},{6,9},{7,8},{8,7},{9,6},... | collective-permute-start | bytes 49160 | tf_op jit(solution)/shard_map/ppermute | solution.py:256
  179.0 7.1 %collective-permute-start.80 = (bf16[64,128]{1,0:T(8,128)(2,1)S(1)}, bf16[64,128]{1,0:T(8,128)(2,1)S(1)}, u32[]{:S(2)}, u32[]{:S(2)}) collective-permute-start(bf16[64,128]{1,0:T(8,128)(2,1)S(1)} %get-tuple-element.182), channel_id=1, source_target_pairs={{0,18},{1,19},{2,16},{3,17},{4,22},{5,23},{6,20},{7,21},{8,26},{9,... | collective-permute-start | bytes 49160 | tf_op jit(solution)/shard_map/ppermute | solution.py:256
  179.0 10.8 %collective-permute-start.81 = (bf16[64,128]{1,0:T(8,128)(2,1)S(1)}, bf16[64,128]{1,0:T(8,128)(2,1)S(1)}, u32[]{:S(2)}, u32[]{:S(2)}) collective-permute-start(bf16[64,128]{1,0:T(8,128)(2,1)S(1)} %get-tuple-element.183), channel_id=1, source_target_pairs={{0,19},{1,18},{2,17},{3,16},{4,23},{5,22},{6,21},{7,20},{8,27},{9,... | collective-permute-start | bytes 49160 | tf_op jit(solution)/shard_map/ppermute | solution.py:256
  181.9 9.1 %collective-permute-start.84 = (bf16[64,128]{1,0:T(8,128)(2,1)S(1)}, bf16[64,128]{1,0:T(8,128)(2,1)S(1)}, u32[]{:S(2)}, u32[]{:S(2)}) collective-permute-start(bf16[64,128]{1,0:T(8,128)(2,1)S(1)} %get-tuple-element.186), channel_id=1, source_target_pairs={{0,22},{1,23},{2,20},{3,21},{4,18},{5,19},{6,16},{7,17},{8,30},{9,... | collective-permute-start | bytes 49160 | tf_op jit(solution)/shard_map/ppermute | solution.py:256
  182.8 12.7 %collective-permute-start.85 = (bf16[64,128]{1,0:T(8,128)(2,1)S(1)}, bf16[64,128]{1,0:T(8,128)(2,1)S(1)}, u32[]{:S(2)}, u32[]{:S(2)}) collective-permute-start(bf16[64,128]{1,0:T(8,128)(2,1)S(1)} %get-tuple-element.187), channel_id=1, source_target_pairs={{0,23},{1,22},{2,21},{3,20},{4,19},{5,18},{6,17},{7,16},{8,31},{9,... | collective-permute-start | bytes 49160 | tf_op jit(solution)/shard_map/ppermute | solution.py:256
  186.1 9.4 %collective-permute-start.88 = (bf16[64,128]{1,0:T(8,128)(2,1)S(1)}, bf16[64,128]{1,0:T(8,128)(2,1)S(1)}, u32[]{:S(2)}, u32[]{:S(2)}) collective-permute-start(bf16[64,128]{1,0:T(8,128)(2,1)S(1)} %get-tuple-element.190), channel_id=1, source_target_pairs={{0,26},{1,27},{2,24},{3,25},{4,30},{5,31},{6,28},{7,29},{8,18},{9,... | collective-permute-start | bytes 49160 | tf_op jit(solution)/shard_map/ppermute | solution.py:256
  186.2 9.4 %collective-permute-start.89 = (bf16[64,128]{1,0:T(8,128)(2,1)S(1)}, bf16[64,128]{1,0:T(8,128)(2,1)S(1)}, u32[]{:S(2)}, u32[]{:S(2)}) collective-permute-start(bf16[64,128]{1,0:T(8,128)(2,1)S(1)} %get-tuple-element.191), channel_id=1, source_target_pairs={{0,27},{1,26},{2,25},{3,24},{4,31},{5,30},{6,29},{7,28},{8,19},{9,... | collective-permute-start | bytes 49160 | tf_op jit(solution)/shard_map/ppermute | solution.py:256
  (38 other events, 186.1 us)

commit v3 on v2

v3 whole, which is shorter than its diff:
```python
import functools
import math

import jax
import jax.numpy as jnp
from jax import lax
from jax.experimental import pallas as pl
from jax.experimental.pallas import tpu as pltpu
from jax.sharding import PartitionSpec as P

BLK = 16
LANES = 128
AXES = ("mem", "grp")
FAR = -1e30


def head_and_half(position):
    return (position >> 2) * 2 + (position & 1), (position >> 1) & 1


def pack(
    heads,
    chunks,
    early,
    k_hbm,
    v_hbm,
    q_hbm,
    dout_hbm,
    omem_hbm,
    local_hbm,
    gate_ref,
    ids_ref,
    first_out,
    second_out,
    k_ref,
    v_ref,
    q_ref,
    dout_ref,
    omem_ref,
    local_ref,
    dmem_ref,
    halves_ref,
    delta_ref,
    gate_rows,
    sems,
):
    tokens = q_ref.shape[0]
    half_rows = tokens // 2
    half_shard = k_ref.shape[0]
    quarter = half_shard // 2
    qblocks, names = ids_ref.shape
    high = lax.Precision.HIGHEST
    parity = lax.axis_index("grp") % 2
    mine = pl.ds(pl.multiple_of(parity * half_shard, half_shard), half_shard)
    copies = []
    for at, (source, target) in enumerate(
        (
            (dout_hbm, dout_ref),
            (omem_hbm, omem_ref),
            (local_hbm, local_ref),
            (q_hbm, q_ref),
            (k_hbm.at[mine, :], k_ref),
            (v_hbm.at[mine, :], v_ref),
        )
    ):
        copy = pltpu.make_async_copy(source, target, sems.at[at])
        copy.start()
        copies.append(copy)

    lane = lax.broadcasted_iota(jnp.int32, (1, LANES), 1)
    ids = ids_ref[...]
    per = qblocks // 2
    bias_rows = 2 * chunks * per
    halves_ref[...] = jnp.zeros_like(halves_ref)
    for chunk in range(chunks):
        block = 16 * (chunk * heads + lane // 8) + 8 * ((lane // 4) % 2) + lane % 4
        for side in range(2):
            wanted = jnp.broadcast_to(block + 4 * side, (qblocks, LANES))
            hit = jnp.zeros((qblocks, LANES), jnp.float32)
            for name in range(names):
                hit = jnp.where(ids[:, name : name + 1] == wanted, 1.0, hit)
            table = jnp.where(hit > 0.5, 0.0, FAR)
            for half in range(2):
                at = ((half ^ side) * chunks + chunk) * per
                halves_ref[half, at : at + per, :] = table[half * per : (half + 1) * per]

    ones = jnp.ones((8, LANES), jnp.float32)
    gate_rows[...] = jnp.zeros_like(gate_rows)
    for copy in copies[:3]:
        copy.wait()
    for head in range(heads):
        cols = slice(head * LANES, (head + 1) * LANES)
        sig = jax.nn.sigmoid(jnp.full((8, LANES), gate_ref[head], jnp.float32))[:1]
        d_out = dout_ref[:, cols].astype(jnp.float32)
        o_mem = omem_ref[:, cols].astype(jnp.float32)
        d_mem = (d_out * sig).astype(jnp.bfloat16)
        dmem_ref[:, cols] = d_mem
        differ = o_mem - local_ref[:, cols].astype(jnp.float32)
        gate_rows[head : head + 1, :] = jnp.sum(d_out * differ, 0, keepdims=True)
        product = d_mem.astype(jnp.float32) * o_mem
        row = lax.dot_general(
            ones, product, (((1,), (1,)), ((), ())), precision=high, preferred_element_type=jnp.float32
        )
        delta_ref[head : head + 1, :] = row[:1]
    total = lax.dot_general(
        ones, gate_rows[...], (((1,), (1,)), ((), ())), precision=high, preferred_element_type=jnp.float32
    )[:1]
    first = total.astype(jnp.bfloat16).astype(jnp.float32)
    second = (total - first).astype(jnp.bfloat16).astype(jnp.float32)
    third = total - first - second
    for half in range(2):
        halves_ref[half, bias_rows + 1 : bias_rows + 2, :] = first
        halves_ref[half, bias_rows + 2 : bias_rows + 3, :] = second
        halves_ref[half, bias_rows + 3 : bias_rows + 4, :] = third
    in_half = (lane // half_rows) == parity
    for copy in copies[3:]:
        copy.wait()
    for position in range(2 * heads):
        head, half = head_and_half(position)
        cols = slice(head * LANES, (head + 1) * LANES)
        base = half * half_rows
        at = 2 * quarter
        first_out[position, :quarter, :] = k_ref[half * quarter : (half + 1) * quarter, cols]
        first_out[position, quarter:at, :] = v_ref[half * quarter : (half + 1) * quarter, cols]
        first_out[position, at : at + early, :] = q_ref[base : base + early, cols]
        first_out[position, at + early : at + 2 * early, :] = dmem_ref[base : base + early, cols]
        late = half_rows - early
        second_out[position, :late, :] = q_ref[base + early : base + half_rows, cols]
        second_out[position, late:, :] = dmem_ref[base + early : base + half_rows, cols]
        row = delta_ref[head : head + 1, :]
        rolled = jnp.concatenate([row[:, half_rows:], row[:, :half_rows]], axis=1)
        halves_ref[half, bias_rows : bias_rows + 1, :] = jnp.where(
            in_half, jnp.where(parity == half, row, rolled), 0.0
        )
        first_out[position, at + 2 * early :, :] = halves_ref[half].astype(jnp.bfloat16)


def assemble(in_ref, out_ref):
    quarter = out_ref.shape[1] // in_ref.shape[0]
    for source in range(in_ref.shape[0]):
        rows = slice(source * quarter, (source + 1) * quarter)
        out_ref[0, rows, :] = in_ref[source, :quarter, :]
        out_ref[1, rows, :] = in_ref[source, quarter : 2 * quarter, :]


def attend(
    begin, count, q_at, ext_at, per, width, tile, final, own_ref, mate_ref, q_ref, ext_ref, *refs
):
    if final:
        before_ref, out_ref, mark, minus, qx, dx, scores, high, total, acc = refs
    else:
        out_ref, gate_ref, mark, minus, qx, dx, scores, high, total, acc = refs
    sources = q_ref.shape[0]
    units = qx.shape[1] // LANES - 1
    sides = (own_ref, mate_ref)
    steps_side = own_ref.shape[1] // width
    rows_unit = mark.shape[0]
    scale = 1.0 / math.sqrt(LANES)
    exponent = scale * math.log2(math.e)
    bias_rows = units * per

    lane = lax.broadcasted_iota(jnp.int32, (BLK, LANES), 1)
    for block in range(LANES):
        mark[block * BLK : (block + 1) * BLK, :] = jnp.where(lane == block, 1.0, 0.0).astype(jnp.bfloat16)
    wide_lane = lax.broadcasted_iota(jnp.int32, (LANES, LANES), 1)
    for block in range(width // LANES):
        minus[block * LANES : (block + 1) * LANES, :] = jnp.where(wide_lane == 0, -1.0, 0.0).astype(jnp.bfloat16)

    gate_sum = jnp.zeros((1, LANES), jnp.float32)
    delta_row = None
    for source in range(sources):
        base = source * count
        qx[base : base + count, :LANES] = q_ref[source, q_at : q_at + count, :]
        dx[base : base + count, :LANES] = q_ref[source, q_at + count : q_at + 2 * count, :]
        extra = ext_ref[source, ext_at:, :].astype(jnp.float32)
        for unit in range(units):
            for block in range(count // BLK):
                at = unit * per + begin // BLK + block
                row = jnp.broadcast_to(extra[at : at + 1], (BLK, LANES)).astype(jnp.bfloat16)
                qx[base + block * BLK : base + (block + 1) * BLK, (1 + unit) * LANES : (2 + unit) * LANES] = row
        if not final:
            for part in range(1, 4):
                gate_sum = gate_sum + extra[bias_rows + part : bias_rows + part + 1]
        row = extra[bias_rows : bias_rows + 1]
        if source % 2 == 0:
            delta_row = row
            continue
        wide = jnp.broadcast_to(delta_row + row, (LANES, LANES)).T
        wide = jnp.where(wide_lane == 0, wide, 0.0).astype(jnp.bfloat16)
        dx[base - count : base, LANES:] = wide[begin : begin + count]
        dx[base : base + count, LANES:] = wide[LANES // 2 + begin : LANES // 2 + begin + count]
    if not final:
        gate_ref[...] = jnp.broadcast_to(gate_sum, gate_ref.shape)

    def one_tile(index, carry):
        here = pl.ds(pl.multiple_of(index * tile, tile), tile)
        high[...] = jnp.full_like(high, -3e38)
        for side, ref in enumerate(sides):
            for unit in range(units // 2):

                def score(at, carry, side=side, ref=ref, unit=unit):
                    rows = pl.ds(pl.multiple_of(unit * rows_unit + at * width, width), width)
                    marks = pl.ds(pl.multiple_of(at * width, width), width)
                    lanes = (1 + side * (units // 2) + unit) * LANES
                    left = jnp.concatenate([qx[here, :LANES], qx[here, lanes : lanes + LANES]], axis=1)
                    right = jnp.concatenate([ref[0, rows, :], mark[marks, :]], axis=1)
                    got = lax.dot_general(
                        left, right, (((1,), (1,)), ((), ())), preferred_element_type=jnp.float32
                    )
                    scores[side * steps_side + unit * (rows_unit // width) + at] = got
                    best = high[...]
                    for column in range(width // LANES):
                        best = jnp.maximum(best, got[:, column * LANES : (column + 1) * LANES])
                    high[...] = best
                    return carry

                lax.fori_loop(0, rows_unit // width, score, 0, unroll=True)
        high[...] = jnp.broadcast_to(jnp.max(high[...], 1, keepdims=True) * exponent, high.shape)
        total[...] = jnp.zeros_like(total)
        acc[...] = jnp.zeros_like(acc)
        for side, ref in enumerate(sides):

            def back(at, carry, side=side, ref=ref):
                rows = pl.ds(pl.multiple_of(at * width, width), width)
                prod = lax.dot_general(
                    dx[here, :],
                    jnp.concatenate([ref[1, rows, :], minus[...]], axis=1),
                    (((1,), (1,)), ((), ())),
                    preferred_element_type=jnp.float32,
                )
                got = scores[side * steps_side + at]
                level = high[...]
                added = total[...]
                pieces = []
                for column in range(width // LANES):
                    cols = slice(column * LANES, (column + 1) * LANES)
                    expo = jnp.exp2(got[:, cols] * exponent - level)
                    added = added + expo
                    pieces.append((expo * prod[:, cols]).astype(jnp.bfloat16))
                total[...] = added
                acc[...] += jnp.dot(
                    jnp.concatenate(pieces, axis=1), ref[0, rows, :], preferred_element_type=jnp.float32
                )
                return carry

            lax.fori_loop(0, steps_side, back, 0, unroll=4)
        weight = scale / jnp.sum(total[...], 1, keepdims=True)
        qx[here, :LANES] = (acc[...] * weight).astype(jnp.bfloat16)
        return carry

    lax.fori_loop(0, qx.shape[0] // tile, one_tile, 0)
    for source in range(sources):
        got = qx[source * count : (source + 1) * count, :LANES]
        if final:
            out_ref[source, :begin, :] = before_ref[source]
            out_ref[source, begin:, :] = got
        else:
            out_ref[source] = got


def unpack(heads, in_ref, out_ref):
    half_rows = in_ref.shape[1]
    for position in range(2 * heads):
        head, half = head_and_half(position)
        out_ref[half * half_rows : (half + 1) * half_rows, head * LANES : (head + 1) * LANES] = in_ref[position]


def local(queries, d_out, o_mem, local_out, mem_keys, mem_values, gate_logit, block_ids):
    shards = lax.axis_size("mem")
    groups = lax.axis_size("grp")
    tokens = queries.shape[1]
    width = queries.shape[2]
    heads = gate_logit.shape[0]
    rows_dev = mem_keys.shape[0]
    qblocks = tokens // BLK
    members = 2 * heads
    chunks = shards // heads
    assert width == heads * LANES and shards % heads == 0 and groups % 2 == 0
    assert rows_dev == 16 * BLK and heads * 8 == LANES and tokens == LANES
    quarter = rows_dev // 4
    halves = tokens // 2
    per = qblocks // 2
    units = 2 * chunks
    early = halves // 2
    late = halves - early
    extra = -(-(units * per + 4) // 16) * 16
    ext_at = 2 * quarter + 2 * early
    packet = ext_at + extra
    vmem = pl.BlockSpec(memory_space=pltpu.VMEM)
    smem = pl.BlockSpec(memory_space=pltpu.SMEM)
    hbm = pl.BlockSpec(memory_space=pltpu.HBM)
    bf16 = jnp.bfloat16
    small = pltpu.CompilerParams(vmem_limit_bytes=24 << 20)

    if shards * groups == members:
        head_groups = None
    else:
        head_groups = [
            [(mo * heads + mi) * groups + 2 * go + gp for mi in range(heads) for gp in range(2)]
            for mo in range(chunks)
            for go in range(groups // 2)
        ]
    exchange = functools.partial(
        lax.all_to_all, axis_name=AXES, split_axis=0, concat_axis=0, tiled=True, axis_index_groups=head_groups
    )

    first_out, second_out = pl.pallas_call(
        functools.partial(pack, heads, chunks, early),
        out_shape=(
            jax.ShapeDtypeStruct((members, packet, LANES), bf16),
            jax.ShapeDtypeStruct((members, 2 * late, LANES), bf16),
        ),
        in_specs=[hbm] * 6 + [smem, vmem],
        out_specs=(vmem, vmem),
        scratch_shapes=[pltpu.VMEM((rows_dev // 2, width), bf16)] * 2
        + [pltpu.VMEM((tokens, width), bf16)] * 5
        + [
            pltpu.VMEM((2, extra, LANES), jnp.float32),
            pltpu.VMEM((heads, LANES), jnp.float32),
            pltpu.VMEM((LANES, LANES), jnp.float32),
            pltpu.SemaphoreType.DMA((6,)),
        ],
        compiler_params=pltpu.CompilerParams(vmem_limit_bytes=56 << 20),
        name="pack",
    )(mem_keys, mem_values, queries[0], d_out[0], o_mem[0], local_out[0], gate_logit, block_ids[0])
    first_in = exchange(first_out)
    second_in = exchange(second_out)
    own = pl.pallas_call(
        assemble,
        out_shape=jax.ShapeDtypeStruct((2, members * quarter, LANES), bf16),
        in_specs=[vmem],
        out_specs=vmem,
        compiler_params=small,
        name="assemble",
    )(first_in)
    if chunks > 1:
        same = [[mo * heads + mi for mo in range(chunks)] for mi in range(heads)]
        own = lax.all_gather(own, "mem", axis_index_groups=same, axis=1, tiled=True)
    mate = lax.ppermute(own, "mem", [(i, i ^ 1) for i in range(shards)])

    rows_all = 2 * own.shape[1]
    step_width = 512
    tile = 512 if chunks == 1 else 256

    def attend_some(begin, count, q_at, final, out_shape, *args):
        return pl.pallas_call(
            functools.partial(attend, begin, count, q_at, ext_at, per, step_width, tile, final),
            out_shape=out_shape,
            in_specs=[vmem] * len(args),
            out_specs=[vmem] * len(out_shape),
            scratch_shapes=[
                pltpu.VMEM((LANES * BLK, LANES), bf16),
                pltpu.VMEM((step_width, LANES), bf16),
                pltpu.VMEM((members * count, (1 + units) * LANES), bf16),
                pltpu.VMEM((members * count, 2 * LANES), bf16),
                pltpu.VMEM((rows_all // step_width, tile, step_width), jnp.float32),
                pltpu.VMEM((tile, LANES), jnp.float32),
                pltpu.VMEM((tile, LANES), jnp.float32),
                pltpu.VMEM((tile, LANES), jnp.float32),
            ],
            compiler_params=pltpu.CompilerParams(vmem_limit_bytes=(24 if chunks == 1 else 44) << 20),
            cost_estimate=pl.CostEstimate(
                flops=2 * members * count * rows_all * LANES * 5,
                bytes_accessed=4 * rows_all * LANES,
                transcendentals=members * count * rows_all,
            ),
            name="attend",
        )(*args)

    part, gate_sum = attend_some(
        0,
        early,
        2 * quarter,
        False,
        [jax.ShapeDtypeStruct((members, early, LANES), bf16), jax.ShapeDtypeStruct((8, LANES), jnp.float32)],
        own,
        mate,
        first_in,
        first_in,
    )
    (grad,) = attend_some(
        early,
        late,
        0,
        True,
        [jax.ShapeDtypeStruct((members, halves, LANES), bf16)],
        own,
        mate,
        second_in,
        first_in,
        part,
    )
    home = exchange(grad)
    d_query = pl.pallas_call(
        functools.partial(unpack, heads),
        out_shape=jax.ShapeDtypeStruct((tokens, width), bf16),
        in_specs=[vmem],
        out_specs=vmem,
        compiler_params=small,
        name="unpack",
    )(home)
    gate_total = gate_sum[0, :heads]
    if head_groups is not None:
        gate_total = lax.psum(gate_total, AXES) / members
    sig = jax.nn.sigmoid(gate_logit)
    d_gate = sig * (1.0 - sig) * gate_total / (shards * groups * tokens * LANES) ** 0.5
    return (d_query[None], d_gate)


def solution(mesh):
    placed = (
        P("grp", "mem", None),
        P("grp", "mem", None),
        P("grp", "mem", None),
        P("grp", "mem", None),
        P("mem", None),
        P("mem", None),
        P(),
        P("grp", "mem", None),
    )
    return jax.shard_map(
        local, mesh=mesh, in_specs=placed, out_specs=(P("grp", "mem", None), P()), check_vma=False
    )
```

time: 200 us -> 106 us (0.53)
  starting transfers between devices: 157 us -> 7.46 us
  blocking collectives: 0 us -> 47.6 us
  waiting for transfers between devices: 10.5 us -> 17.6 us
  Pallas kernels: 27.2 us -> 30.4 us
  local copies, waits for them, and re-layouts: 3.12 us -> 0.79 us
    ppermute x93 -> x0, starting transfers between devices: 152 us -> none  [swap(): got[step] = lax.ppermute(pieces[step], AXES, pairs)]
    all_to_all x0 -> x1, blocking collectives: none -> 47.6 us  [local(): first_in = exchange(first_out)]
    all_to_all x0 -> x2, waiting for transfers between devices: none -> 17.6 us  [the longest x1 14.5 us: local(): home = exchange(grad)]
    ppermute x93 -> x0, waiting for transfers between devices: 10.5 us -> none  [swap(): got[step] = lax.ppermute(pieces[step], AXES, pairs)]
    all_to_all x0 -> x2, starting transfers between devices: none -> 6.6 us  [the longest x1 3.62 us: local(): home = exchange(grad)]
    ppermute x1, starting transfers between devices: 4.27 us -> 0.87 us  [local(): mate = lax.ppermute(own, 'mem', [(i, i ^ 1) for i in range(shards)])]
    pallas_call x5 -> x4, Pallas kernels: 26.2 us -> 29.5 us  [the longest x2 23.7 us: attend_some(): pl.pallas_call(functools.partial(attend, begin, count, q_at, ext_at, per,...]
    unnamed x16 -> x4, local copies, waits for them, and re-layouts: 3.12 us -> 0.79 us
  transfers between devices with their start and end apart: 94 -> 3, of which waited for: 9 -> 2; matrix products, arithmetic and copies ran while one was open for 0% -> 1% of each run, Pallas kernels for 13% -> 11%
where the time goes in v3:
time: 106 us; the launch traced here: 105 us
  blocking collectives  47.6 us (45%)
  Pallas kernels  30.4 us (29%)
  waiting for transfers between devices  17.6 us (17%)
  starting transfers between devices  7.46 us (7%)
    all_to_all x1, blocking collectives, local(): first_in = exchange(first_out)  47.6 us
    pallas_call x2, Pallas kernels, attend_some(): pl.pallas_call(functools.partial(attend, begin, count, q_at, ext_at, per,...  23.7 us
    all_to_all x1, waiting for transfers between devices, local(): home = exchange(grad)  14.5 us
    pallas_call x1, Pallas kernels, local(): pl.pallas_call(functools.partial(pack, heads, chunks, early), out_shape=(...  5.71 us
    all_to_all x1, starting transfers between devices, local(): home = exchange(grad)  3.62 us
    all_to_all x1, waiting for transfers between devices, local(): second_in = exchange(second_out)  3.15 us
    all_to_all x1, starting transfers between devices, local(): second_in = exchange(second_out)  2.98 us
  transfers between devices with their start and end apart: 3, of which 2 were waited for; matrix products, arithmetic and copies ran while one was open for 1% of the time, Pallas kernels for 11%

profile of v3, /device:TPU:0, one launch (start us, length us, event | category | flops | bytes accessed | tf_op | source)
XLA Modules:
  0.0 105.1 jit_solution(6297988059409641285)
XLA Ops:
  0.6 5.7 %pack.1 = (bf16[32,208,128]{2,1,0:T(8,128)(2,1)}, bf16[32,64,128]{2,1,0:T(8,128)(2,1)}) custom-call(bf16[256,2048]{1,0:T(8,128)(2,1)} %k_hbm.1, bf16[256,2048]{1,0:T(8,128)(2,1)} %v_hbm.1, bf16[128,2048]{1,0:T(8,128)(2,1)} %bitcast.10, bf16[128,2048]{1,0:T(8,128)(2,1)} %bitcast.11, bf16[128,2048]{1,0:T(8,128)(2,1)} %bitcast.12, bf16[128,2048]{1,0:T(8,128)(2,1)} %bitcast.13, ...), custom_call_target="tpu_custom_call" | custom-call | tf_op jit(solution)/shard_map/pack/pallas_call | solution.py:307
  6.3 47.6 %all_to_all.15.in_ref.q_ref.ext_ref = bf16[32,208,128]{2,1,0:T(8,128)(2,1)S(1)} all-to-all(bf16[32,208,128]{2,1,0:T(8,128)(2,1)} %get-tuple-element.6), channel_id=1, replica_groups=mesh['mem'=16,'grp'=2] {'mem','grp'}, dimensions={0} | all-to-all | bytes 3407872 | tf_op jit(solution)/shard_map/all_to_all | solution.py:326
  53.9 0.1 assemble.1.own_ref
  54.0 0.9 collective-permute-start
  54.9 3.0 %all-to-all-start.1 = ((bf16[32,64,128]{2,1,0:T(8,128)(2,1)}), bf16[32,64,128]{2,1,0:T(8,128)(2,1)S(1)}, u32[]{:S(2)}, u32[]{:S(2)}) async-start(bf16[32,64,128]{2,1,0:T(8,128)(2,1)} %get-tuple-element.7), calls=%async_computation.1 | async-start | bytes 1048576 | tf_op jit(solution)/shard_map/all_to_all | solution.py:327
  57.9 0.0 collective-permute-done.mate_ref
  57.9 11.8 %attend.2 = (bf16[32,32,128]{2,1,0:T(8,128)(2,1)S(1)}, f32[8,128]{1,0:T(8,128)S(1)}) custom-call(bf16[2,2048,128]{2,1,0:T(8,128)(2,1)S(1)} %assemble.1.own_ref, bf16[2,2048,128]{2,1,0:T(8,128)(2,1)} %collective-permute-done.mate_ref, bf16[32,208,128]{2,1,0:T(8,128)(2,1)S(1)} %all_to_all.15.in_ref.q_ref.ext_ref, ...), custom_call_target="tpu_custom_call" | custom-call | flops 5368709120 | bytes 2097152 | tf_op jit(solution)/shard_map/attend/pallas_call | solution.py:346
  69.7 3.1 %all-to-all-done.1.q_ref = bf16[32,64,128]{2,1,0:T(8,128)(2,1)S(1)} async-done(((bf16[32,64,128]{2,1,0:T(8,128)(2,1)}), bf16[32,64,128]{2,1,0:T(8,128)(2,1)S(1)}, u32[]{:S(2)}, u32[]{:S(2)}) %all-to-all-start.1) | async-done | bytes 524320 | tf_op jit(solution)/shard_map/all_to_all | solution.py:327
  72.9 0.0 copy-start.1
  72.9 11.9 %attend.3 = bf16[32,64,128]{2,1,0:T(8,128)(2,1)S(1)} custom-call(bf16[2,2048,128]{2,1,0:T(8,128)(2,1)S(1)} %assemble.1.own_ref, bf16[2,2048,128]{2,1,0:T(8,128)(2,1)} %collective-permute-done.mate_ref, bf16[32,64,128]{2,1,0:T(8,128)(2,1)S(1)} %all-to-all-done.1.q_ref, bf16[32,208,128]{2,1,0:T(8,128)(2,1)S(1)} %all_to_all.15.in_ref.q_ref.ext_ref, ...), custom_call_target="tpu_custom_call" | custom-call | flops 5368709120 | bytes 2097152 | tf_op jit(solution)/shard_map/attend/pallas_call | solution.py:346
  84.7 0.0 copy-start
  84.7 0.8 copy-done
  85.5 3.6 %all-to-all-start.2 = ((bf16[32,64,128]{2,1,0:T(8,128)(2,1)}), bf16[32,64,128]{2,1,0:T(8,128)(2,1)S(1)}, u32[]{:S(2)}, u32[]{:S(2)}) async-start(bf16[32,64,128]{2,1,0:T(8,128)(2,1)} %copy-done), calls=%async_computation.2 | async-start | bytes 1048576 | tf_op jit(solution)/shard_map/all_to_all | solution.py:393
  89.2 0.0 copy-done.1
  89.2 0.5 fusion.1
  89.7 14.5 %all-to-all-done.2.in_ref = bf16[32,64,128]{2,1,0:T(8,128)(2,1)S(1)} async-done(((bf16[32,64,128]{2,1,0:T(8,128)(2,1)}), bf16[32,64,128]{2,1,0:T(8,128)(2,1)S(1)}, u32[]{:S(2)}, u32[]{:S(2)}) %all-to-all-start.2) | async-done | bytes 524320 | tf_op jit(solution)/shard_map/all_to_all | solution.py:393
  104.2 0.9 unpack.1
Async XLA Ops:
  54.0 3.9 %collective-permute-start = (bf16[2,2048,128]{2,1,0:T(8,128)(2,1)S(1)}, bf16[2,2048,128]{2,1,0:T(8,128)(2,1)}, u32[]{:S(2)}, u32[]{:S(2)}) collective-permute-start(bf16[2,2048,128]{2,1,0:T(8,128)(2,1)S(1)} %assemble.1.own_ref), channel_id=1, source_target_pairs={{0,2},{2,0},{4,6},{6,4},{8,10},{10,8},{12,14},{14,12},{16,18},{18,... | collective-permute-start | bytes 3145736 | tf_op jit(solution)/shard_map/ppermute | solution.py:339
  54.9 18.0 %all-to-all-start.1 = ((bf16[32,64,128]{2,1,0:T(8,128)(2,1)}), bf16[32,64,128]{2,1,0:T(8,128)(2,1)S(1)}, u32[]{:S(2)}, u32[]{:S(2)}) async-start(bf16[32,64,128]{2,1,0:T(8,128)(2,1)} %get-tuple-element.7), calls=%async_computation.1 | async-start | bytes 1048576 | tf_op jit(solution)/shard_map/all_to_all | solution.py:327
  72.9 16.3 %copy-start.1 = (f32[16]{0:T(128)S(1)}, f32[16]{0:T(128)}, u32[]{:S(2)}) copy-start(f32[16]{0:T(128)} %gate_ref.1) | copy-start | bytes 196
  84.7 0.8 copy-start
  85.5 18.6 %all-to-all-start.2 = ((bf16[32,64,128]{2,1,0:T(8,128)(2,1)}), bf16[32,64,128]{2,1,0:T(8,128)(2,1)S(1)}, u32[]{:S(2)}, u32[]{:S(2)}) async-start(bf16[32,64,128]{2,1,0:T(8,128)(2,1)} %copy-done), calls=%async_computation.2 | async-start | bytes 1048576 | tf_op jit(solution)/shard_map/all_to_all | solution.py:393

commit v4 on v3

--- a/solution.py
+++ b/solution.py
@@ -85,6 +85,7 @@
                 halves_ref[half, at : at + per, :] = table[half * per : (half + 1) * per]
 
     ones = jnp.ones((8, LANES), jnp.float32)
+    wide_ones = jnp.ones((16, 2 * LANES), jnp.bfloat16)
     gate_rows[...] = jnp.zeros_like(gate_rows)
     for copy in copies[:3]:
         copy.wait()
@@ -98,8 +99,13 @@
         differ = o_mem - local_ref[:, cols].astype(jnp.float32)
         gate_rows[head : head + 1, :] = jnp.sum(d_out * differ, 0, keepdims=True)
         product = d_mem.astype(jnp.float32) * o_mem
+        upper = product.astype(jnp.bfloat16)
+        lower = (product - upper.astype(jnp.float32)).astype(jnp.bfloat16)
         row = lax.dot_general(
-            ones, product, (((1,), (1,)), ((), ())), precision=high, preferred_element_type=jnp.float32
+            wide_ones,
+            jnp.concatenate([upper, lower], axis=1),
+            (((1,), (1,)), ((), ())),
+            preferred_element_type=jnp.float32,
         )
         delta_ref[head : head + 1, :] = row[:1]
     total = lax.dot_general(
@@ -147,7 +153,7 @@
     begin, count, q_at, ext_at, per, width, tile, final, own_ref, mate_ref, q_ref, ext_ref, *refs
 ):
     if final:
-        before_ref, out_ref, mark, minus, qx, dx, scores, high, total, acc = refs
+        before_ref, out_ref, mark, minus, qx, dx, scores, high, total, acc, kept = refs
     else:
         out_ref, gate_ref, mark, minus, qx, dx, scores, high, total, acc = refs
     sources = q_ref.shape[0]
@@ -194,6 +200,7 @@
 
     def one_tile(index, carry):
         here = pl.ds(pl.multiple_of(index * tile, tile), tile)
+        groups = [slice(at, at + 64) for at in range(0, tile, 64)]
         high[...] = jnp.full_like(high, -3e38)
         for side, ref in enumerate(sides):
             for unit in range(units // 2):
@@ -207,14 +214,14 @@
                     got = lax.dot_general(
                         left, right, (((1,), (1,)), ((), ())), preferred_element_type=jnp.float32
                     )
-                    scores[side * steps_side + unit * (rows_unit // width) + at] = got
-                    best = high[...]
-                    for column in range(width // LANES):
-                        best = jnp.maximum(best, got[:, column * LANES : (column + 1) * LANES])
-                    high[...] = best
+                    index = side * steps_side + unit * (rows_unit // width) + at
+                    for group in groups:
+                        piece = got[group]
+                        scores[index, group, :] = piece
+                        high[group] = jnp.maximum(high[group], jnp.maximum(piece[:, :LANES], piece[:, LANES:]))
                     return carry
 
-                lax.fori_loop(0, rows_unit // width, score, 0, unroll=True)
+                lax.fori_loop(0, rows_unit // width, score, 0, unroll=4)
         high[...] = jnp.broadcast_to(jnp.max(high[...], 1, keepdims=True) * exponent, high.shape)
         total[...] = jnp.zeros_like(total)
         acc[...] = jnp.zeros_like(acc)
@@ -228,22 +235,30 @@
                     (((1,), (1,)), ((), ())),
                     preferred_element_type=jnp.float32,
                 )
-                got = scores[side * steps_side + at]
-                level = high[...]
-                added = total[...]
                 pieces = []
-                for column in range(width // LANES):
-                    cols = slice(column * LANES, (column + 1) * LANES)
-                    expo = jnp.exp2(got[:, cols] * exponent - level)
-                    added = added + expo
-                    pieces.append((expo * prod[:, cols]).astype(jnp.bfloat16))
-                total[...] = added
-                acc[...] += jnp.dot(
-                    jnp.concatenate(pieces, axis=1), ref[0, rows, :], preferred_element_type=jnp.float32
-                )
+                for group in groups:
+                    got = scores[side * steps_side + at, group, :]
+                    level = high[group]
+                    expo = [jnp.exp2(got[:, c : c + LANES] * exponent - level) for c in (0, LANES)]
+                    total[group] += expo[0] + expo[1]
+                    piece = jnp.concatenate(
+                        [e * prod[group, c : c + LANES] for e, c in zip(expo, (0, LANES))], axis=1
+                    ).astype(jnp.bfloat16)
+                    if final:
+                        kept[group, pl.ds(pl.multiple_of(side * steps_side * width + at * width, width), width)] = piece
+                    else:
+                        pieces.append(piece)
+                if not final:
+                    acc[...] += jnp.dot(
+                        jnp.concatenate(pieces, axis=0), ref[0, rows, :], preferred_element_type=jnp.float32
+                    )
                 return carry
 
             lax.fori_loop(0, steps_side, back, 0, unroll=4)
+        if final:
+            for side, ref in enumerate(sides):
+                cols = slice(side * steps_side * width, (side + 1) * steps_side * width)
+                acc[...] += jnp.dot(kept[:, cols], ref[0], preferred_element_type=jnp.float32)
         weight = scale / jnp.sum(total[...], 1, keepdims=True)
         qx[here, :LANES] = (acc[...] * weight).astype(jnp.bfloat16)
         return carry
@@ -339,7 +354,7 @@
     mate = lax.ppermute(own, "mem", [(i, i ^ 1) for i in range(shards)])
 
     rows_all = 2 * own.shape[1]
-    step_width = 512
+    step_width = 2 * LANES
     tile = 512 if chunks == 1 else 256
 
     def attend_some(begin, count, q_at, final, out_shape, *args):
@@ -357,7 +372,8 @@
                 pltpu.VMEM((tile, LANES), jnp.float32),
                 pltpu.VMEM((tile, LANES), jnp.float32),
                 pltpu.VMEM((tile, LANES), jnp.float32),
-            ],
+            ]
+            + [pltpu.VMEM((tile, rows_all), bf16)] * final,
             compiler_params=pltpu.CompilerParams(vmem_limit_bytes=(24 if chunks == 1 else 44) << 20),
             cost_estimate=pl.CostEstimate(
                 flops=2 * members * count * rows_all * LANES * 5,

time: 106 us -> 107 us (level)
  Pallas kernels: 30.4 us -> 32.6 us
  waiting for transfers between devices: 17.6 us -> 15.8 us
    pallas_call x2, Pallas kernels: 23.7 us -> 27.1 us  [attend_some(): pl.pallas_call(functools.partial(attend, begin, count, q_at, ext_at, per,...]
    all_to_all x1, waiting for transfers between devices: 3.15 us -> 1.36 us  [local(): second_in = exchange(second_out)]
    pallas_call x1, Pallas kernels: 5.71 us -> 4.58 us  [local(): pl.pallas_call(functools.partial(pack, heads, chunks, early), out_shape=(...]
  transfers between devices with their start and end apart: 3 -> 3, of which waited for: 2 -> 2; matrix products, arithmetic and copies ran while one was open for 1% -> 0% of each run, Pallas kernels for 11% -> 13%
where the time goes in v4:
time: 107 us; the launch traced here: 106 us
  blocking collectives  47.6 us (44%)
  Pallas kernels  32.6 us (30%)
  waiting for transfers between devices  15.8 us (15%)
  starting transfers between devices  8.32 us (8%)
    all_to_all x1, blocking collectives, local(): first_in = exchange(first_out)  47.6 us
    pallas_call x2, Pallas kernels, attend_some(): pl.pallas_call(functools.partial(attend, begin, count, q_at, ext_at, per,...  27.1 us
    all_to_all x1, waiting for transfers between devices, local(): home = exchange(grad)  14.5 us
    pallas_call x1, Pallas kernels, local(): pl.pallas_call(functools.partial(pack, heads, chunks, early), out_shape=(...  4.58 us
    all_to_all x1, starting transfers between devices, local(): home = exchange(grad)  4.48 us
    all_to_all x1, starting transfers between devices, local(): second_in = exchange(second_out)  2.98 us
  transfers between devices with their start and end apart: 3, of which 2 were waited for; matrix products, arithmetic and copies ran while one was open for 0% of the time, Pallas kernels for 13%

profile of v4, /device:TPU:0, one launch (start us, length us, event | category | flops | bytes accessed | tf_op | source)
XLA Modules:
  0.0 106.4 jit_solution(5244532450304347037)
XLA Ops:
  0.6 4.6 %pack.1 = (bf16[32,208,128]{2,1,0:T(8,128)(2,1)}, bf16[32,64,128]{2,1,0:T(8,128)(2,1)}) custom-call(bf16[256,2048]{1,0:T(8,128)(2,1)} %k_hbm.1, bf16[256,2048]{1,0:T(8,128)(2,1)} %v_hbm.1, bf16[128,2048]{1,0:T(8,128)(2,1)} %bitcast.10, bf16[128,2048]{1,0:T(8,128)(2,1)} %bitcast.11, bf16[128,2048]{1,0:T(8,128)(2,1)} %bitcast.12, bf16[128,2048]{1,0:T(8,128)(2,1)} %bitcast.13, ...), custom_call_target="tpu_custom_call" | custom-call | tf_op jit(solution)/shard_map/pack/pallas_call | solution.py:322
  5.2 47.6 %all_to_all.15.in_ref.q_ref.ext_ref = bf16[32,208,128]{2,1,0:T(8,128)(2,1)S(1)} all-to-all(bf16[32,208,128]{2,1,0:T(8,128)(2,1)} %get-tuple-element.6), channel_id=1, replica_groups=mesh['mem'=16,'grp'=2] {'mem','grp'}, dimensions={0} | all-to-all | bytes 3407872 | tf_op jit(solution)/shard_map/all_to_all | solution.py:341
  52.8 0.1 assemble.1.own_ref
  52.9 0.9 collective-permute-start
  53.8 3.0 %all-to-all-start.1 = ((bf16[32,64,128]{2,1,0:T(8,128)(2,1)}), bf16[32,64,128]{2,1,0:T(8,128)(2,1)S(1)}, u32[]{:S(2)}, u32[]{:S(2)}) async-start(bf16[32,64,128]{2,1,0:T(8,128)(2,1)} %get-tuple-element.7), calls=%async_computation.1 | async-start | bytes 1048576 | tf_op jit(solution)/shard_map/all_to_all | solution.py:342
  56.7 0.0 collective-permute-done.mate_ref
  56.8 13.6 %attend.2 = (bf16[32,32,128]{2,1,0:T(8,128)(2,1)S(1)}, f32[8,128]{1,0:T(8,128)S(1)}) custom-call(bf16[2,2048,128]{2,1,0:T(8,128)(2,1)S(1)} %assemble.1.own_ref, bf16[2,2048,128]{2,1,0:T(8,128)(2,1)} %collective-permute-done.mate_ref, bf16[32,208,128]{2,1,0:T(8,128)(2,1)S(1)} %all_to_all.15.in_ref.q_ref.ext_ref, ...), custom_call_target="tpu_custom_call" | custom-call | flops 5368709120 | bytes 2097152 | tf_op jit(solution)/shard_map/attend/pallas_call | solution.py:361
  70.4 1.4 %all-to-all-done.1.q_ref = bf16[32,64,128]{2,1,0:T(8,128)(2,1)S(1)} async-done(((bf16[32,64,128]{2,1,0:T(8,128)(2,1)}), bf16[32,64,128]{2,1,0:T(8,128)(2,1)S(1)}, u32[]{:S(2)}, u32[]{:S(2)}) %all-to-all-start.1) | async-done | bytes 524320 | tf_op jit(solution)/shard_map/all_to_all | solution.py:342
  71.7 0.0 copy-start.1
  71.7 13.4 %attend.3 = bf16[32,64,128]{2,1,0:T(8,128)(2,1)S(1)} custom-call(bf16[2,2048,128]{2,1,0:T(8,128)(2,1)S(1)} %assemble.1.own_ref, bf16[2,2048,128]{2,1,0:T(8,128)(2,1)} %collective-permute-done.mate_ref, bf16[32,64,128]{2,1,0:T(8,128)(2,1)S(1)} %all-to-all-done.1.q_ref, bf16[32,208,128]{2,1,0:T(8,128)(2,1)S(1)} %all_to_all.15.in_ref.q_ref.ext_ref, ...), custom_call_target="tpu_custom_call" | custom-call | flops 5368709120 | bytes 2097152 | tf_op jit(solution)/shard_map/attend/pallas_call | solution.py:361
  85.2 0.0 copy-start
  85.2 0.8 copy-done
  86.0 4.5 %all-to-all-start.2 = ((bf16[32,64,128]{2,1,0:T(8,128)(2,1)}), bf16[32,64,128]{2,1,0:T(8,128)(2,1)S(1)}, u32[]{:S(2)}, u32[]{:S(2)}) async-start(bf16[32,64,128]{2,1,0:T(8,128)(2,1)} %copy-done), calls=%async_computation.2 | async-start | bytes 1048576 | tf_op jit(solution)/shard_map/all_to_all | solution.py:409
  90.5 0.0 copy-done.1
  90.5 0.5 fusion.1
  91.0 14.5 %all-to-all-done.2.in_ref = bf16[32,64,128]{2,1,0:T(8,128)(2,1)S(1)} async-done(((bf16[32,64,128]{2,1,0:T(8,128)(2,1)}), bf16[32,64,128]{2,1,0:T(8,128)(2,1)S(1)}, u32[]{:S(2)}, u32[]{:S(2)}) %all-to-all-start.2) | async-done | bytes 524320 | tf_op jit(solution)/shard_map/all_to_all | solution.py:409
  105.5 0.9 unpack.1
Async XLA Ops:
  52.9 3.9 %collective-permute-start = (bf16[2,2048,128]{2,1,0:T(8,128)(2,1)S(1)}, bf16[2,2048,128]{2,1,0:T(8,128)(2,1)}, u32[]{:S(2)}, u32[]{:S(2)}) collective-permute-start(bf16[2,2048,128]{2,1,0:T(8,128)(2,1)S(1)} %assemble.1.own_ref), channel_id=1, source_target_pairs={{0,2},{2,0},{4,6},{6,4},{8,10},{10,8},{12,14},{14,12},{16,18},{18,... | collective-permute-start | bytes 3145736 | tf_op jit(solution)/shard_map/ppermute | solution.py:354
  53.8 18.0 %all-to-all-start.1 = ((bf16[32,64,128]{2,1,0:T(8,128)(2,1)}), bf16[32,64,128]{2,1,0:T(8,128)(2,1)S(1)}, u32[]{:S(2)}, u32[]{:S(2)}) async-start(bf16[32,64,128]{2,1,0:T(8,128)(2,1)} %get-tuple-element.7), calls=%async_computation.1 | async-start | bytes 1048576 | tf_op jit(solution)/shard_map/all_to_all | solution.py:342
  71.7 18.7 %copy-start.1 = (f32[16]{0:T(128)S(1)}, f32[16]{0:T(128)}, u32[]{:S(2)}) copy-start(f32[16]{0:T(128)} %gate_ref.1) | copy-start | bytes 196
  85.2 0.8 copy-start
  86.0 19.5 %all-to-all-start.2 = ((bf16[32,64,128]{2,1,0:T(8,128)(2,1)}), bf16[32,64,128]{2,1,0:T(8,128)(2,1)S(1)}, u32[]{:S(2)}, u32[]{:S(2)}) async-start(bf16[32,64,128]{2,1,0:T(8,128)(2,1)} %copy-done), calls=%async_computation.2 | async-start | bytes 1048576 | tf_op jit(solution)/shard_map/all_to_all | solution.py:409

commit v5 on v3

--- a/solution.py
+++ b/solution.py
@@ -85,6 +85,7 @@
                 halves_ref[half, at : at + per, :] = table[half * per : (half + 1) * per]
 
     ones = jnp.ones((8, LANES), jnp.float32)
+    wide_ones = jnp.ones((16, 2 * LANES), jnp.bfloat16)
     gate_rows[...] = jnp.zeros_like(gate_rows)
     for copy in copies[:3]:
         copy.wait()
@@ -98,8 +99,13 @@
         differ = o_mem - local_ref[:, cols].astype(jnp.float32)
         gate_rows[head : head + 1, :] = jnp.sum(d_out * differ, 0, keepdims=True)
         product = d_mem.astype(jnp.float32) * o_mem
+        upper = product.astype(jnp.bfloat16)
+        lower = (product - upper.astype(jnp.float32)).astype(jnp.bfloat16)
         row = lax.dot_general(
-            ones, product, (((1,), (1,)), ((), ())), precision=high, preferred_element_type=jnp.float32
+            wide_ones,
+            jnp.concatenate([upper, lower], axis=1),
+            (((1,), (1,)), ((), ())),
+            preferred_element_type=jnp.float32,
         )
         delta_ref[head : head + 1, :] = row[:1]
     total = lax.dot_general(
@@ -147,7 +153,7 @@
     begin, count, q_at, ext_at, per, width, tile, final, own_ref, mate_ref, q_ref, ext_ref, *refs
 ):
     if final:
-        before_ref, out_ref, mark, minus, qx, dx, scores, high, total, acc = refs
+        out_ref, mark, minus, qx, dx, scores, high, total, acc = refs
     else:
         out_ref, gate_ref, mark, minus, qx, dx, scores, high, total, acc = refs
     sources = q_ref.shape[0]
@@ -250,19 +256,17 @@
 
     lax.fori_loop(0, qx.shape[0] // tile, one_tile, 0)
     for source in range(sources):
-        got = qx[source * count : (source + 1) * count, :LANES]
-        if final:
-            out_ref[source, :begin, :] = before_ref[source]
-            out_ref[source, begin:, :] = got
-        else:
-            out_ref[source] = got
-
-
-def unpack(heads, in_ref, out_ref):
-    half_rows = in_ref.shape[1]
+        out_ref[source] = qx[source * count : (source + 1) * count, :LANES]
+
+
+def unpack(heads, early_ref, late_ref, out_ref):
+    early, late = early_ref.shape[1], late_ref.shape[1]
     for position in range(2 * heads):
         head, half = head_and_half(position)
-        out_ref[half * half_rows : (half + 1) * half_rows, head * LANES : (head + 1) * LANES] = in_ref[position]
+        cols = slice(head * LANES, (head + 1) * LANES)
+        middle = half * (early + late) + early
+        out_ref[middle - early : middle, cols] = early_ref[position]
+        out_ref[middle : middle + late, cols] = late_ref[position]
 
 
 def local(queries, d_out, o_mem, local_out, mem_keys, mem_values, gate_logit, block_ids):
@@ -339,10 +343,10 @@
     mate = lax.ppermute(own, "mem", [(i, i ^ 1) for i in range(shards)])
 
     rows_all = 2 * own.shape[1]
-    step_width = 512
-    tile = 512 if chunks == 1 else 256
-
-    def attend_some(begin, count, q_at, final, out_shape, *args):
+
+    def attend_some(begin, count, q_at, final, tile, step_width, out_shape, *args):
+        if chunks > 1:
+            tile, step_width = 256, 512
         return pl.pallas_call(
             functools.partial(attend, begin, count, q_at, ext_at, per, step_width, tile, final),
             out_shape=out_shape,
@@ -358,7 +362,7 @@
                 pltpu.VMEM((tile, LANES), jnp.float32),
                 pltpu.VMEM((tile, LANES), jnp.float32),
             ],
-            compiler_params=pltpu.CompilerParams(vmem_limit_bytes=(24 if chunks == 1 else 44) << 20),
+            compiler_params=pltpu.CompilerParams(vmem_limit_bytes=(34 if chunks == 1 else 44) << 20),
             cost_estimate=pl.CostEstimate(
                 flops=2 * members * count * rows_all * LANES * 5,
                 bytes_accessed=4 * rows_all * LANES,
@@ -372,6 +376,8 @@
         early,
         2 * quarter,
         False,
+        1024,
+        512,
         [jax.ShapeDtypeStruct((members, early, LANES), bf16), jax.ShapeDtypeStruct((8, LANES), jnp.float32)],
         own,
         mate,
@@ -383,22 +389,23 @@
         late,
         0,
         True,
-        [jax.ShapeDtypeStruct((members, halves, LANES), bf16)],
+        512,
+        2048,
+        [jax.ShapeDtypeStruct((members, late, LANES), bf16)],
         own,
         mate,
         second_in,
         first_in,
-        part,
     )
-    home = exchange(grad)
+    home = (exchange(part), exchange(grad))
     d_query = pl.pallas_call(
         functools.partial(unpack, heads),
         out_shape=jax.ShapeDtypeStruct((tokens, width), bf16),
-        in_specs=[vmem],
+        in_specs=[vmem, vmem],
         out_specs=vmem,
         compiler_params=small,
         name="unpack",
-    )(home)
+    )(*home)
     gate_total = gate_sum[0, :heads]
     if head_groups is not None:
         gate_total = lax.psum(gate_total, AXES) / members

time: 106 us -> 107 us (level)
  starting transfers between devices: 7.46 us -> 13.3 us
  waiting for transfers between devices: 17.6 us -> 12.8 us
    all_to_all x1 -> x2, starting transfers between devices: 3.62 us -> 9.46 us  [local(): home = (exchange(part), exchange(grad))]
    all_to_all x1 -> x2, waiting for transfers between devices: 14.5 us -> 10.2 us  [local(): home = (exchange(part), exchange(grad))]
    pallas_call x1, Pallas kernels: 5.71 us -> 4.58 us  [local(): pl.pallas_call(functools.partial(pack, heads, chunks, early), out_shape=(...]
  transfers between devices with their start and end apart: 3 -> 4, of which waited for: 2 -> 2; matrix products, arithmetic and copies ran while one was open for 1% -> 0% of each run, Pallas kernels for 11% -> 23%
where the time goes in v5:
time: 107 us; the launch traced here: 106 us
  blocking collectives  47.6 us (44%)
  Pallas kernels  29.8 us (28%)
  starting transfers between devices  13.3 us (12%)
  waiting for transfers between devices  12.8 us (12%)
  local copies, waits for them, and re-layouts  1.41 us (1%)
    all_to_all x1, blocking collectives, local(): first_in = exchange(first_out)  47.6 us
    pallas_call x2, Pallas kernels, attend_some(): pl.pallas_call(functools.partial(attend, begin, count, q_at, ext_at, per,...  24.3 us
    all_to_all x2, waiting for transfers between devices, local(): home = (exchange(part), exchange(grad))  10.2 us
    all_to_all x2, starting transfers between devices, local(): home = (exchange(part), exchange(grad))  9.46 us
    pallas_call x1, Pallas kernels, local(): pl.pallas_call(functools.partial(pack, heads, chunks, early), out_shape=(...  4.58 us
    all_to_all x1, starting transfers between devices, local(): second_in = exchange(second_out)  2.98 us
    all_to_all x1, waiting for transfers between devices, local(): second_in = exchange(second_out)  2.65 us
  transfers between devices with their start and end apart: 4, of which 2 were waited for; matrix products, arithmetic and copies ran while one was open for 0% of the time, Pallas kernels for 23%

profile of v5, /device:TPU:0, one launch (start us, length us, event | category | flops | bytes accessed | tf_op | source)
XLA Modules:
  0.0 106.2 jit_solution(8969102636402060087)
XLA Ops:
  0.6 4.6 %pack.1 = (bf16[32,208,128]{2,1,0:T(8,128)(2,1)}, bf16[32,64,128]{2,1,0:T(8,128)(2,1)}) custom-call(bf16[256,2048]{1,0:T(8,128)(2,1)} %k_hbm.1, bf16[256,2048]{1,0:T(8,128)(2,1)} %v_hbm.1, bf16[128,2048]{1,0:T(8,128)(2,1)} %bitcast.10, bf16[128,2048]{1,0:T(8,128)(2,1)} %bitcast.11, bf16[128,2048]{1,0:T(8,128)(2,1)} %bitcast.12, bf16[128,2048]{1,0:T(8,128)(2,1)} %bitcast.13, ...), custom_call_target="tpu_custom_call" | custom-call | tf_op jit(solution)/shard_map/pack/pallas_call | solution.py:311
  5.2 47.6 %all_to_all.20.in_ref.q_ref.ext_ref = bf16[32,208,128]{2,1,0:T(8,128)(2,1)S(1)} all-to-all(bf16[32,208,128]{2,1,0:T(8,128)(2,1)} %get-tuple-element.6), channel_id=1, replica_groups=mesh['mem'=16,'grp'=2] {'mem','grp'}, dimensions={0} | all-to-all | bytes 3407872 | tf_op jit(solution)/shard_map/all_to_all | solution.py:330
  52.8 0.1 assemble.1.own_ref
  52.9 0.9 collective-permute-start
  53.8 3.0 %all-to-all-start.2 = ((bf16[32,64,128]{2,1,0:T(8,128)(2,1)}), bf16[32,64,128]{2,1,0:T(8,128)(2,1)S(1)}, u32[]{:S(2)}, u32[]{:S(2)}) async-start(bf16[32,64,128]{2,1,0:T(8,128)(2,1)} %get-tuple-element.8), calls=%async_computation.2 | async-start | bytes 1048576 | tf_op jit(solution)/shard_map/all_to_all | solution.py:331
  56.7 0.0 collective-permute-done.mate_ref
  56.8 11.6 %attend.2 = (bf16[32,32,128]{2,1,0:T(8,128)(2,1)S(1)}, f32[8,128]{1,0:T(8,128)S(1)}) custom-call(bf16[2,2048,128]{2,1,0:T(8,128)(2,1)S(1)} %assemble.1.own_ref, bf16[2,2048,128]{2,1,0:T(8,128)(2,1)} %collective-permute-done.mate_ref, bf16[32,208,128]{2,1,0:T(8,128)(2,1)S(1)} %all_to_all.20.in_ref.q_ref.ext_ref, ...), custom_call_target="tpu_custom_call" | custom-call | flops 5368709120 | bytes 2097152 | tf_op jit(solution)/shard_map/attend/pallas_call | solution.py:350
  68.4 0.0 copy-start
  68.4 0.7 copy-done
  69.1 2.6 %all-to-all-done.2.q_ref = bf16[32,64,128]{2,1,0:T(8,128)(2,1)S(1)} async-done(((bf16[32,64,128]{2,1,0:T(8,128)(2,1)}), bf16[32,64,128]{2,1,0:T(8,128)(2,1)S(1)}, u32[]{:S(2)}, u32[]{:S(2)}) %all-to-all-start.2) | async-done | bytes 524320 | tf_op jit(solution)/shard_map/all_to_all | solution.py:331
  71.7 3.8 %all-to-all-start.1 = ((bf16[32,32,128]{2,1,0:T(8,128)(2,1)}), bf16[32,32,128]{2,1,0:T(8,128)(2,1)S(1)}, u32[]{:S(2)}, u32[]{:S(2)}) async-start(bf16[32,32,128]{2,1,0:T(8,128)(2,1)} %copy-done), calls=%async_computation.1 | async-start | bytes 524288 | tf_op jit(solution)/shard_map/all_to_all | solution.py:400
  75.6 0.0 copy-start.2
  75.6 12.7 %attend.3 = bf16[32,32,128]{2,1,0:T(8,128)(2,1)S(1)} custom-call(bf16[2,2048,128]{2,1,0:T(8,128)(2,1)S(1)} %assemble.1.own_ref, bf16[2,2048,128]{2,1,0:T(8,128)(2,1)} %collective-permute-done.mate_ref, bf16[32,64,128]{2,1,0:T(8,128)(2,1)S(1)} %all-to-all-done.2.q_ref, bf16[32,208,128]{2,1,0:T(8,128)(2,1)S(1)} %all_to_all.20.in_ref.q_ref.ext_ref), custom_call_target="tpu_custom_call" | custom-call | flops 5368709120 | bytes 2097152 | tf_op jit(solution)/shard_map/attend/pallas_call | solution.py:350
  88.2 0.0 copy-start.1
  88.3 0.7 copy-done.1
  89.0 0.0 all-to-all-done.1.early_ref
  89.0 5.7 %all-to-all-start.3 = ((bf16[32,32,128]{2,1,0:T(8,128)(2,1)}), bf16[32,32,128]{2,1,0:T(8,128)(2,1)S(1)}, u32[]{:S(2)}, u32[]{:S(2)}) async-start(bf16[32,32,128]{2,1,0:T(8,128)(2,1)} %copy-done.1), calls=%async_computation.3 | async-start | bytes 524288 | tf_op jit(solution)/shard_map/all_to_all | solution.py:400
  94.6 0.0 copy-done.2
  94.6 0.5 fusion.1
  95.2 10.2 %all-to-all-done.3.late_ref = bf16[32,32,128]{2,1,0:T(8,128)(2,1)S(1)} async-done(((bf16[32,32,128]{2,1,0:T(8,128)(2,1)}), bf16[32,32,128]{2,1,0:T(8,128)(2,1)S(1)}, u32[]{:S(2)}, u32[]{:S(2)}) %all-to-all-start.3) | async-done | bytes 262176 | tf_op jit(solution)/shard_map/all_to_all | solution.py:400
  105.3 0.9 unpack.1
Async XLA Ops:
  52.9 3.9 %collective-permute-start = (bf16[2,2048,128]{2,1,0:T(8,128)(2,1)S(1)}, bf16[2,2048,128]{2,1,0:T(8,128)(2,1)}, u32[]{:S(2)}, u32[]{:S(2)}) collective-permute-start(bf16[2,2048,128]{2,1,0:T(8,128)(2,1)S(1)} %assemble.1.own_ref), channel_id=1, source_target_pairs={{0,2},{2,0},{4,6},{6,4},{8,10},{10,8},{12,14},{14,12},{16,18},{18,... | collective-permute-start | bytes 3145736 | tf_op jit(solution)/shard_map/ppermute | solution.py:343
  53.8 18.0 %all-to-all-start.2 = ((bf16[32,64,128]{2,1,0:T(8,128)(2,1)}), bf16[32,64,128]{2,1,0:T(8,128)(2,1)S(1)}, u32[]{:S(2)}, u32[]{:S(2)}) async-start(bf16[32,64,128]{2,1,0:T(8,128)(2,1)} %get-tuple-element.8), calls=%async_computation.2 | async-start | bytes 1048576 | tf_op jit(solution)/shard_map/all_to_all | solution.py:331
  68.4 0.7 copy-start
  71.7 17.2 %all-to-all-start.1 = ((bf16[32,32,128]{2,1,0:T(8,128)(2,1)}), bf16[32,32,128]{2,1,0:T(8,128)(2,1)S(1)}, u32[]{:S(2)}, u32[]{:S(2)}) async-start(bf16[32,32,128]{2,1,0:T(8,128)(2,1)} %copy-done), calls=%async_computation.1 | async-start | bytes 524288 | tf_op jit(solution)/shard_map/all_to_all | solution.py:400
  75.6 19.1 %copy-start.2 = (f32[16]{0:T(128)S(1)}, f32[16]{0:T(128)}, u32[]{:S(2)}) copy-start(f32[16]{0:T(128)} %gate_ref.1) | copy-start | bytes 196
  88.2 0.7 copy-start.1
  89.0 16.4 %all-to-all-start.3 = ((bf16[32,32,128]{2,1,0:T(8,128)(2,1)}), bf16[32,32,128]{2,1,0:T(8,128)(2,1)S(1)}, u32[]{:S(2)}, u32[]{:S(2)}) async-start(bf16[32,32,128]{2,1,0:T(8,128)(2,1)} %copy-done.1), calls=%async_computation.3 | async-start | bytes 524288 | tf_op jit(solution)/shard_map/all_to_all | solution.py:400

commit v6 on v3

--- a/solution.py
+++ b/solution.py
@@ -85,6 +85,7 @@
                 halves_ref[half, at : at + per, :] = table[half * per : (half + 1) * per]
 
     ones = jnp.ones((8, LANES), jnp.float32)
+    wide_ones = jnp.ones((16, 2 * LANES), jnp.bfloat16)
     gate_rows[...] = jnp.zeros_like(gate_rows)
     for copy in copies[:3]:
         copy.wait()
@@ -98,8 +99,13 @@
         differ = o_mem - local_ref[:, cols].astype(jnp.float32)
         gate_rows[head : head + 1, :] = jnp.sum(d_out * differ, 0, keepdims=True)
         product = d_mem.astype(jnp.float32) * o_mem
+        upper = product.astype(jnp.bfloat16)
+        lower = (product - upper.astype(jnp.float32)).astype(jnp.bfloat16)
         row = lax.dot_general(
-            ones, product, (((1,), (1,)), ((), ())), precision=high, preferred_element_type=jnp.float32
+            wide_ones,
+            jnp.concatenate([upper, lower], axis=1),
+            (((1,), (1,)), ((), ())),
+            preferred_element_type=jnp.float32,
         )
         delta_ref[head : head + 1, :] = row[:1]
     total = lax.dot_general(
@@ -112,7 +118,14 @@
         halves_ref[half, bias_rows + 1 : bias_rows + 2, :] = first
         halves_ref[half, bias_rows + 2 : bias_rows + 3, :] = second
         halves_ref[half, bias_rows + 3 : bias_rows + 4, :] = third
-    in_half = (lane // half_rows) == parity
+    turn = (lax.axis_index("mem") % 2) * 2 + parity
+    quarter_lanes = LANES // 4
+    in_turn = lax.broadcasted_iota(jnp.int32, (heads, LANES), 1) // quarter_lanes == turn
+    deltas = {}
+    for half in range(2):
+        for part in range(2):
+            shift = lax.rem(quarter_lanes * (turn + 8 - 2 * half - part), LANES)
+            deltas[half, part] = jnp.where(in_turn, pltpu.roll(delta_ref[...], shift, 1), 0.0)
     for copy in copies[3:]:
         copy.wait()
     for position in range(2 * heads):
@@ -127,11 +140,8 @@
         late = half_rows - early
         second_out[position, :late, :] = q_ref[base + early : base + half_rows, cols]
         second_out[position, late:, :] = dmem_ref[base + early : base + half_rows, cols]
-        row = delta_ref[head : head + 1, :]
-        rolled = jnp.concatenate([row[:, half_rows:], row[:, :half_rows]], axis=1)
-        halves_ref[half, bias_rows : bias_rows + 1, :] = jnp.where(
-            in_half, jnp.where(parity == half, row, rolled), 0.0
-        )
+        halves_ref[half, bias_rows : bias_rows + 1, :] = deltas[half, 0][head : head + 1]
+        halves_ref[half, bias_rows + 4 : bias_rows + 5, :] = deltas[half, 1][head : head + 1]
         first_out[position, at + 2 * early :, :] = halves_ref[half].astype(jnp.bfloat16)
 
 
@@ -144,34 +154,36 @@
 
 
 def attend(
-    begin, count, q_at, ext_at, per, width, tile, final, own_ref, mate_ref, q_ref, ext_ref, *refs
+    begin, count, q_at, ext_at, per, tile, width, final, own_ref, mate_ref, q_ref, ext_ref, *refs
 ):
     if final:
-        before_ref, out_ref, mark, minus, qx, dx, scores, high, total, acc = refs
+        kt, before_ref, out_ref, mark, qx, dm, delta, scores, acc = refs
     else:
-        out_ref, gate_ref, mark, minus, qx, dx, scores, high, total, acc = refs
+        out_ref, gate_ref, kt, mark, qx, dm, delta, scores, acc = refs
     sources = q_ref.shape[0]
     units = qx.shape[1] // LANES - 1
     sides = (own_ref, mate_ref)
-    steps_side = own_ref.shape[1] // width
+    rows_side = own_ref.shape[1]
     rows_unit = mark.shape[0]
     scale = 1.0 / math.sqrt(LANES)
     exponent = scale * math.log2(math.e)
     bias_rows = units * per
+    together = LANES // count
 
     lane = lax.broadcasted_iota(jnp.int32, (BLK, LANES), 1)
     for block in range(LANES):
         mark[block * BLK : (block + 1) * BLK, :] = jnp.where(lane == block, 1.0, 0.0).astype(jnp.bfloat16)
-    wide_lane = lax.broadcasted_iota(jnp.int32, (LANES, LANES), 1)
-    for block in range(width // LANES):
-        minus[block * LANES : (block + 1) * LANES, :] = jnp.where(wide_lane == 0, -1.0, 0.0).astype(jnp.bfloat16)
+    if not final:
+        for side, ref in enumerate(sides):
+            for at in range(0, rows_side, LANES):
+                turned = ref[0, at : at + LANES, :].astype(jnp.float32).T
+                kt[side, :, at : at + LANES] = turned.astype(jnp.bfloat16)
 
     gate_sum = jnp.zeros((1, LANES), jnp.float32)
-    delta_row = None
     for source in range(sources):
         base = source * count
         qx[base : base + count, :LANES] = q_ref[source, q_at : q_at + count, :]
-        dx[base : base + count, :LANES] = q_ref[source, q_at + count : q_at + 2 * count, :]
+        dm[base : base + count, :] = q_ref[source, q_at + count : q_at + 2 * count, :]
         extra = ext_ref[source, ext_at:, :].astype(jnp.float32)
         for unit in range(units):
             for block in range(count // BLK):
@@ -181,81 +193,63 @@
         if not final:
             for part in range(1, 4):
                 gate_sum = gate_sum + extra[bias_rows + part : bias_rows + part + 1]
-        row = extra[bias_rows : bias_rows + 1]
-        if source % 2 == 0:
-            delta_row = row
-            continue
-        wide = jnp.broadcast_to(delta_row + row, (LANES, LANES)).T
-        wide = jnp.where(wide_lane == 0, wide, 0.0).astype(jnp.bfloat16)
-        dx[base - count : base, LANES:] = wide[begin : begin + count]
-        dx[base : base + count, LANES:] = wide[LANES // 2 + begin : LANES // 2 + begin + count]
+        at = bias_rows + (4 if final else 0)
+        row = extra[at : at + 1]
+        delta_row = row if source % together == 0 else delta_row + row
+        if source % together == together - 1:
+            end = base + count
+            delta[:, end - LANES : end] = jnp.broadcast_to(delta_row, (8, LANES))
     if not final:
         gate_ref[...] = jnp.broadcast_to(gate_sum, gate_ref.shape)
 
-    def one_tile(index, carry):
-        here = pl.ds(pl.multiple_of(index * tile, tile), tile)
-        high[...] = jnp.full_like(high, -3e38)
+    for start in range(0, sources * count, tile):
+        here = slice(start, start + tile)
+        best = jnp.full((8, tile), -3e38, jnp.float32)
         for side, ref in enumerate(sides):
             for unit in range(units // 2):
-
-                def score(at, carry, side=side, ref=ref, unit=unit):
-                    rows = pl.ds(pl.multiple_of(unit * rows_unit + at * width, width), width)
-                    marks = pl.ds(pl.multiple_of(at * width, width), width)
-                    lanes = (1 + side * (units // 2) + unit) * LANES
-                    left = jnp.concatenate([qx[here, :LANES], qx[here, lanes : lanes + LANES]], axis=1)
-                    right = jnp.concatenate([ref[0, rows, :], mark[marks, :]], axis=1)
+                lanes = (1 + side * (units // 2) + unit) * LANES
+
+                def score(at, best, side=side, ref=ref, unit=unit, lanes=lanes):
+                    at = pl.multiple_of(at * width, width)
+                    rows = pl.ds(unit * rows_unit + at, width)
+                    left = jnp.concatenate([ref[0, rows, :], mark[pl.ds(at, width), :]], axis=1)
+                    right = jnp.concatenate([qx[here, :LANES], qx[here, lanes : lanes + LANES]], axis=1)
                     got = lax.dot_general(
                         left, right, (((1,), (1,)), ((), ())), preferred_element_type=jnp.float32
                     )
-                    scores[side * steps_side + unit * (rows_unit // width) + at] = got
-                    best = high[...]
-                    for column in range(width // LANES):
-                        best = jnp.maximum(best, got[:, column * LANES : (column + 1) * LANES])
-                    high[...] = best
-                    return carry
-
-                lax.fori_loop(0, rows_unit // width, score, 0, unroll=True)
-        high[...] = jnp.broadcast_to(jnp.max(high[...], 1, keepdims=True) * exponent, high.shape)
-        total[...] = jnp.zeros_like(total)
+                    scores[pl.ds(side * rows_side + unit * rows_unit + at, width), :] = got
+                    return jnp.maximum(best, jnp.max(got.reshape(width // 8, 8, tile), axis=0))
+
+                best = lax.fori_loop(0, rows_unit // width, score, best, unroll=2)
+        level = jnp.max(best, 0, keepdims=True) * exponent
+        less = delta[:1, here]
+        total = jnp.zeros((8, tile), jnp.float32)
         acc[...] = jnp.zeros_like(acc)
         for side, ref in enumerate(sides):
 
-            def back(at, carry, side=side, ref=ref):
-                rows = pl.ds(pl.multiple_of(at * width, width), width)
+            def back(at, total, side=side, ref=ref):
+                at = pl.multiple_of(at * width, width)
+                rows = pl.ds(at, width)
                 prod = lax.dot_general(
-                    dx[here, :],
-                    jnp.concatenate([ref[1, rows, :], minus[...]], axis=1),
-                    (((1,), (1,)), ((), ())),
-                    preferred_element_type=jnp.float32,
+                    ref[1, rows, :], dm[here, :], (((1,), (1,)), ((), ())), preferred_element_type=jnp.float32
                 )
-                got = scores[side * steps_side + at]
-                level = high[...]
-                added = total[...]
-                pieces = []
-                for column in range(width // LANES):
-                    cols = slice(column * LANES, (column + 1) * LANES)
-                    expo = jnp.exp2(got[:, cols] * exponent - level)
-                    added = added + expo
-                    pieces.append((expo * prod[:, cols]).astype(jnp.bfloat16))
-                total[...] = added
-                acc[...] += jnp.dot(
-                    jnp.concatenate(pieces, axis=1), ref[0, rows, :], preferred_element_type=jnp.float32
-                )
-                return carry
-
-            lax.fori_loop(0, steps_side, back, 0, unroll=4)
-        weight = scale / jnp.sum(total[...], 1, keepdims=True)
-        qx[here, :LANES] = (acc[...] * weight).astype(jnp.bfloat16)
-        return carry
-
-    lax.fori_loop(0, qx.shape[0] // tile, one_tile, 0)
-    for source in range(sources):
-        got = qx[source * count : (source + 1) * count, :LANES]
-        if final:
-            out_ref[source, :begin, :] = before_ref[source]
-            out_ref[source, begin:, :] = got
-        else:
-            out_ref[source] = got
+                expo = jnp.exp2(scores[pl.ds(side * rows_side + at, width), :] * exponent - level)
+                ds = (expo * (prod - less)).astype(jnp.bfloat16)
+                acc[...] += jnp.dot(kt[side, :, rows], ds, preferred_element_type=jnp.float32)
+                return total + jnp.sum(expo.reshape(width // 8, 8, tile), axis=0)
+
+            total = lax.fori_loop(0, rows_side // width, back, total, unroll=2)
+        weight = scale / jnp.sum(total, 0, keepdims=True)
+        for at in range(0, tile, LANES):
+            turned = (acc[:, at : at + LANES] * weight[:, at : at + LANES]).T.astype(jnp.bfloat16)
+            for inner in range(together):
+                source = (start + at) // count + inner
+                got = turned[inner * count : (inner + 1) * count]
+                if final:
+                    out_ref[source, :begin, :] = before_ref[source]
+                    out_ref[source, begin:, :] = got
+                else:
+                    out_ref[source] = got
 
 
 def unpack(heads, in_ref, out_ref):
@@ -283,7 +277,7 @@
     units = 2 * chunks
     early = halves // 2
     late = halves - early
-    extra = -(-(units * per + 4) // 16) * 16
+    extra = -(-(units * per + 5) // 16) * 16
     ext_at = 2 * quarter + 2 * early
     packet = ext_at + extra
     vmem = pl.BlockSpec(memory_space=pltpu.VMEM)
@@ -344,35 +338,38 @@
 
     def attend_some(begin, count, q_at, final, out_shape, *args):
         return pl.pallas_call(
-            functools.partial(attend, begin, count, q_at, ext_at, per, step_width, tile, final),
+            functools.partial(attend, begin, count, q_at, ext_at, per, tile, step_width, final),
             out_shape=out_shape,
             in_specs=[vmem] * len(args),
             out_specs=[vmem] * len(out_shape),
             scratch_shapes=[
                 pltpu.VMEM((LANES * BLK, LANES), bf16),
-                pltpu.VMEM((step_width, LANES), bf16),
                 pltpu.VMEM((members * count, (1 + units) * LANES), bf16),
-                pltpu.VMEM((members * count, 2 * LANES), bf16),
-                pltpu.VMEM((rows_all // step_width, tile, step_width), jnp.float32),
-                pltpu.VMEM((tile, LANES), jnp.float32),
-                pltpu.VMEM((tile, LANES), jnp.float32),
-                pltpu.VMEM((tile, LANES), jnp.float32),
+                pltpu.VMEM((members * count, LANES), bf16),
+                pltpu.VMEM((8, members * count), jnp.float32),
+                pltpu.VMEM((rows_all, tile), jnp.float32),
+                pltpu.VMEM((LANES, tile), jnp.float32),
             ],
             compiler_params=pltpu.CompilerParams(vmem_limit_bytes=(24 if chunks == 1 else 44) << 20),
             cost_estimate=pl.CostEstimate(
-                flops=2 * members * count * rows_all * LANES * 5,
+                flops=2 * members * count * rows_all * LANES * 4,
                 bytes_accessed=4 * rows_all * LANES,
                 transcendentals=members * count * rows_all,
             ),
             name="attend",
         )(*args)
 
-    part, gate_sum = attend_some(
+    assert early == late and 4 * early == 2 * halves == LANES
+    part, gate_sum, keys_turned = attend_some(
         0,
         early,
         2 * quarter,
         False,
-        [jax.ShapeDtypeStruct((members, early, LANES), bf16), jax.ShapeDtypeStruct((8, LANES), jnp.float32)],
+        [
+            jax.ShapeDtypeStruct((members, early, LANES), bf16),
+            jax.ShapeDtypeStruct((8, LANES), jnp.float32),
+            jax.ShapeDtypeStruct((2, LANES, rows_all // 2), bf16),
+        ],
         own,
         mate,
         first_in,
@@ -388,6 +385,7 @@
         mate,
         second_in,
         first_in,
+        keys_turned,
         part,
     )
     home = exchange(grad)

time: 106 us -> 108 us (1.019)
  local copies, waits for them, and re-layouts: 0.79 us -> 3.03 us
  waiting for transfers between devices: 17.6 us -> 15.5 us
  starting transfers between devices: 7.46 us -> 8.61 us
    unnamed x4 -> x8, local copies, waits for them, and re-layouts: 0.79 us -> 3.03 us
    all_to_all x1, waiting for transfers between devices: 3.15 us -> 1.07 us  [local(): second_in = exchange(second_out)]
    pallas_call x2, Pallas kernels: 23.7 us -> 25.4 us  [attend_some(): pl.pallas_call(functools.partial(attend, begin, count, q_at, ext_at, per,...]
    all_to_all x1, starting transfers between devices: 3.62 us -> 4.76 us  [local(): home = exchange(grad)]
  transfers between devices with their start and end apart: 3 -> 3, of which waited for: 2 -> 2; matrix products, arithmetic and copies ran while one was open for 1% -> 0% of each run, Pallas kernels for 11% -> 12%
where the time goes in v6:
time: 108 us; the launch traced here: 107 us
  blocking collectives  47.6 us (44%)
  Pallas kernels  31 us (29%)
  waiting for transfers between devices  15.5 us (14%)
  starting transfers between devices  8.61 us (8%)
  local copies, waits for them, and re-layouts  3.03 us (3%)
    all_to_all x1, blocking collectives, local(): first_in = exchange(first_out)  47.6 us
    pallas_call x2, Pallas kernels, attend_some(): pl.pallas_call(functools.partial(attend, begin, count, q_at, ext_at, per,...  25.4 us
    all_to_all x1, waiting for transfers between devices, local(): home = exchange(grad)  14.5 us
    all_to_all x1, starting transfers between devices, local(): home = exchange(grad)  4.76 us
    pallas_call x1, Pallas kernels, local(): pl.pallas_call(functools.partial(pack, heads, chunks, early), out_shape=(...  4.69 us
    unnamed x8, local copies, waits for them, and re-layouts  3.03 us
    all_to_all x1, starting transfers between devices, local(): second_in = exchange(second_out)  2.98 us
  transfers between devices with their start and end apart: 3, of which 2 were waited for; matrix products, arithmetic and copies ran while one was open for 0% of the time, Pallas kernels for 12%

profile of v6, /device:TPU:0, one launch (start us, length us, event | category | flops | bytes accessed | tf_op | source)
XLA Modules:
  0.0 107.0 jit_solution(14463021378634499482)
XLA Ops:
  0.6 4.7 %pack.1 = (bf16[32,208,128]{2,1,0:T(8,128)(2,1)}, bf16[32,64,128]{2,1,0:T(8,128)(2,1)}) custom-call(bf16[256,2048]{1,0:T(8,128)(2,1)} %k_hbm.1, bf16[256,2048]{1,0:T(8,128)(2,1)} %v_hbm.1, bf16[128,2048]{1,0:T(8,128)(2,1)} %bitcast.10, bf16[128,2048]{1,0:T(8,128)(2,1)} %bitcast.11, bf16[128,2048]{1,0:T(8,128)(2,1)} %bitcast.12, bf16[128,2048]{1,0:T(8,128)(2,1)} %bitcast.13, ...), custom_call_target="tpu_custom_call" | custom-call | tf_op jit(solution)/shard_map/pack/pallas_call | solution.py:301
  5.3 47.6 %all_to_all.15.in_ref.q_ref.ext_ref = bf16[32,208,128]{2,1,0:T(8,128)(2,1)S(1)} all-to-all(bf16[32,208,128]{2,1,0:T(8,128)(2,1)} %get-tuple-element.7), channel_id=1, replica_groups=mesh['mem'=16,'grp'=2] {'mem','grp'}, dimensions={0} | all-to-all | bytes 3407872 | tf_op jit(solution)/shard_map/all_to_all | solution.py:320
  52.9 0.1 assemble.1.own_ref
  53.0 0.9 collective-permute-start
  53.9 3.0 %all-to-all-start.1 = ((bf16[32,64,128]{2,1,0:T(8,128)(2,1)}), bf16[32,64,128]{2,1,0:T(8,128)(2,1)S(1)}, u32[]{:S(2)}, u32[]{:S(2)}) async-start(bf16[32,64,128]{2,1,0:T(8,128)(2,1)} %get-tuple-element.8), calls=%async_computation.1 | async-start | bytes 1048576 | tf_op jit(solution)/shard_map/all_to_all | solution.py:321
  56.9 0.0 collective-permute-done.mate_ref
  56.9 12.9 %attend.2 = (bf16[32,32,128]{2,1,0:T(8,128)(2,1)S(1)}, f32[8,128]{1,0:T(8,128)S(1)}, bf16[2,128,2048]{2,1,0:T(8,128)(2,1)S(1)}) custom-call(bf16[2,2048,128]{2,1,0:T(8,128)(2,1)S(1)} %assemble.1.own_ref, bf16[2,2048,128]{2,1,0:T(8,128)(2,1)} %collective-permute-done.mate_ref, bf16[32,208,128]{2,1,0:T(8,128)(2,1)S(1)} %all_to_all.15.in_ref.q_ref.ext_ref, ...), custom_call_target="tpu_custom_call" | custom-call | flops 4294967296 | bytes 2097152 | tf_op jit(solution)/shard_map/attend/pallas_call | solution.py:340
  69.8 0.0 copy-start.1
  69.8 1.0 copy-done.1
  70.8 1.1 all-to-all-done.1.q_ref
  71.9 0.0 copy-start.2
  71.9 1.2 %copy-done.2 = bf16[2,128,2048]{2,1,0:T(8,128)(2,1)S(1)} copy-done((bf16[2,128,2048]{2,1,0:T(8,128)(2,1)S(1)}, bf16[2,128,2048]{2,1,0:T(8,128)(2,1)}, u32[]{:S(2)}) %copy-start.2) | copy-done | bytes 1048600
  73.1 0.0 copy-start.3
  73.1 12.5 %attend.3 = bf16[32,64,128]{2,1,0:T(8,128)(2,1)S(1)} custom-call(bf16[2,2048,128]{2,1,0:T(8,128)(2,1)S(1)} %assemble.1.own_ref, bf16[2,2048,128]{2,1,0:T(8,128)(2,1)} %collective-permute-done.mate_ref, bf16[32,64,128]{2,1,0:T(8,128)(2,1)S(1)} %all-to-all-done.1.q_ref, bf16[32,208,128]{2,1,0:T(8,128)(2,1)S(1)} %all_to_all.15.in_ref.q_ref.ext_ref, ...), custom_call_target="tpu_custom_call" | custom-call | flops 4294967296 | bytes 2097152 | tf_op jit(solution)/shard_map/attend/pallas_call | solution.py:340
  85.5 0.0 copy-start
  85.6 0.8 copy-done
  86.3 4.8 %all-to-all-start.2 = ((bf16[32,64,128]{2,1,0:T(8,128)(2,1)}), bf16[32,64,128]{2,1,0:T(8,128)(2,1)S(1)}, u32[]{:S(2)}, u32[]{:S(2)}) async-start(bf16[32,64,128]{2,1,0:T(8,128)(2,1)} %copy-done), calls=%async_computation.2 | async-start | bytes 1048576 | tf_op jit(solution)/shard_map/all_to_all | solution.py:391
  91.1 0.0 copy-done.3
  91.1 0.5 fusion.1
  91.7 14.5 %all-to-all-done.2.in_ref = bf16[32,64,128]{2,1,0:T(8,128)(2,1)S(1)} async-done(((bf16[32,64,128]{2,1,0:T(8,128)(2,1)}), bf16[32,64,128]{2,1,0:T(8,128)(2,1)S(1)}, u32[]{:S(2)}, u32[]{:S(2)}) %all-to-all-start.2) | async-done | bytes 524320 | tf_op jit(solution)/shard_map/all_to_all | solution.py:391
  106.1 0.9 unpack.1
Async XLA Ops:
  53.0 3.9 %collective-permute-start = (bf16[2,2048,128]{2,1,0:T(8,128)(2,1)S(1)}, bf16[2,2048,128]{2,1,0:T(8,128)(2,1)}, u32[]{:S(2)}, u32[]{:S(2)}) collective-permute-start(bf16[2,2048,128]{2,1,0:T(8,128)(2,1)S(1)} %assemble.1.own_ref), channel_id=1, source_target_pairs={{0,2},{2,0},{4,6},{6,4},{8,10},{10,8},{12,14},{14,12},{16,18},{18,... | collective-permute-start | bytes 3145736 | tf_op jit(solution)/shard_map/ppermute | solution.py:333
  53.9 18.0 %all-to-all-start.1 = ((bf16[32,64,128]{2,1,0:T(8,128)(2,1)}), bf16[32,64,128]{2,1,0:T(8,128)(2,1)S(1)}, u32[]{:S(2)}, u32[]{:S(2)}) async-start(bf16[32,64,128]{2,1,0:T(8,128)(2,1)} %get-tuple-element.8), calls=%async_computation.1 | async-start | bytes 1048576 | tf_op jit(solution)/shard_map/all_to_all | solution.py:321
  69.8 1.0 copy-start.1
  71.9 1.2 %copy-start.2 = (bf16[2,128,2048]{2,1,0:T(8,128)(2,1)S(1)}, bf16[2,128,2048]{2,1,0:T(8,128)(2,1)}, u32[]{:S(2)}) copy-start(bf16[2,128,2048]{2,1,0:T(8,128)(2,1)} %copy-done.1) | copy-start | bytes 3145732
  73.1 18.0 %copy-start.3 = (f32[16]{0:T(128)S(1)}, f32[16]{0:T(128)}, u32[]{:S(2)}) copy-start(f32[16]{0:T(128)} %gate_ref.1) | copy-start | bytes 196
  85.5 0.8 copy-start
  86.3 19.8 %all-to-all-start.2 = ((bf16[32,64,128]{2,1,0:T(8,128)(2,1)}), bf16[32,64,128]{2,1,0:T(8,128)(2,1)S(1)}, u32[]{:S(2)}, u32[]{:S(2)}) async-start(bf16[32,64,128]{2,1,0:T(8,128)(2,1)} %copy-done), calls=%async_computation.2 | async-start | bytes 1048576 | tf_op jit(solution)/shard_map/all_to_all | solution.py:391

commit v7 on v3

v7 whole, which is shorter than its diff:
```python
import functools
import math

import jax
import jax.numpy as jnp
from jax import lax
from jax.experimental import pallas as pl
from jax.experimental.pallas import tpu as pltpu
from jax.sharding import PartitionSpec as P

BLK = 16
LANES = 128
AXES = ("mem", "grp")
FAR = -1e30


def pack(
    heads,
    chunks,
    early,
    k_hbm,
    v_hbm,
    q_hbm,
    dout_hbm,
    omem_hbm,
    local_hbm,
    gate_ref,
    ids_ref,
    first_hbm,
    second_hbm,
    k_ref,
    v_ref,
    q_ref,
    dout_ref,
    omem_ref,
    local_ref,
    dmem_ref,
    ext_ref,
    late_ref,
    delta_ref,
    gate_rows,
    first_out,
    second_out,
    sems,
    out_sems,
):
    tokens = q_ref.shape[0]
    half_shard = k_ref.shape[0]
    qblocks, names = ids_ref.shape
    high = lax.Precision.HIGHEST
    core = lax.axis_index("mem") % 2
    parity = lax.axis_index("grp") % 2
    mine = pl.ds(pl.multiple_of(parity * half_shard, half_shard), half_shard)
    copies = []
    for at, (source, target) in enumerate(
        (
            (dout_hbm, dout_ref),
            (omem_hbm, omem_ref),
            (local_hbm, local_ref),
            (q_hbm, q_ref),
            (k_hbm.at[mine, :], k_ref),
            (v_hbm.at[mine, :], v_ref),
        )
    ):
        copy = pltpu.make_async_copy(source, target, sems.at[at])
        copy.start()
        copies.append(copy)

    lane = lax.broadcasted_iota(jnp.int32, (1, LANES), 1)
    ids = ids_ref[...]
    per = qblocks // 2
    bias_rows = 2 * chunks * per
    ext_ref[...] = jnp.zeros_like(ext_ref)
    late_ref[...] = jnp.zeros_like(late_ref)
    for side in range(2):
        for chunk in range(chunks):
            shard = chunk * heads + 2 * (lane // 16) + (core + side) % 2
            wanted = jnp.broadcast_to(16 * shard + lane % 16, (qblocks, LANES))
            hit = jnp.zeros((qblocks, LANES), jnp.float32)
            for name in range(names):
                hit = jnp.where(ids[:, name : name + 1] == wanted, 1.0, hit)
            table = jnp.where(hit > 0.5, 0.0, FAR)
            at = (side * chunks + chunk) * per
            ext_ref[at : at + per, :] = table[:per]
            late_ref[at : at + per, :] = table[per:]

    ones = jnp.ones((8, LANES), jnp.float32)
    wide_ones = jnp.ones((16, 2 * LANES), jnp.bfloat16)
    gate_rows[...] = jnp.zeros_like(gate_rows)
    for copy in copies[:3]:
        copy.wait()
    for head in range(heads):
        cols = slice(head * LANES, (head + 1) * LANES)
        sig = jax.nn.sigmoid(jnp.full((8, LANES), gate_ref[head], jnp.float32))[:1]
        d_out = dout_ref[:, cols].astype(jnp.float32)
        o_mem = omem_ref[:, cols].astype(jnp.float32)
        d_mem = (d_out * sig).astype(jnp.bfloat16)
        dmem_ref[:, cols] = d_mem
        differ = o_mem - local_ref[:, cols].astype(jnp.float32)
        gate_rows[head : head + 1, :] = jnp.sum(d_out * differ, 0, keepdims=True)
        product = d_mem.astype(jnp.float32) * o_mem
        upper = product.astype(jnp.bfloat16)
        lower = (product - upper.astype(jnp.float32)).astype(jnp.bfloat16)
        row = lax.dot_general(
            wide_ones,
            jnp.concatenate([upper, lower], axis=1),
            (((1,), (1,)), ((), ())),
            preferred_element_type=jnp.float32,
        )
        delta_ref[head : head + 1, :] = row[:1]
    total = lax.dot_general(
        ones, gate_rows[...], (((1,), (1,)), ((), ())), precision=high, preferred_element_type=jnp.float32
    )
    first = total.astype(jnp.bfloat16).astype(jnp.float32)
    second = (total - first).astype(jnp.bfloat16).astype(jnp.float32)
    third = total - first - second
    addends = first + pltpu.roll(second, heads, 1) + pltpu.roll(third, 2 * heads, 1)
    ext_ref[bias_rows + 1 : bias_rows + 2, :] = addends[:1]
    late_extra = late_ref[...].astype(jnp.bfloat16)
    for copy in copies[3:]:
        copy.wait()
    at = 2 * half_shard
    late = tokens - early
    sent = []
    bunch = heads // 4
    for head in range(heads):
        cols = slice(head * LANES, (head + 1) * LANES)
        first_out[head, :half_shard, :] = k_ref[:, cols]
        first_out[head, half_shard:at, :] = v_ref[:, cols]
        first_out[head, at : at + early, :] = q_ref[:early, cols]
        first_out[head, at + early : at + 2 * early, :] = dmem_ref[:early, cols]
        ext_ref[bias_rows : bias_rows + 1, :] = delta_ref[head : head + 1, :]
        first_out[head, at + 2 * early :, :] = ext_ref[...].astype(jnp.bfloat16)
        second_out[head, :late, :] = q_ref[early:, cols]
        second_out[head, late : 2 * late, :] = dmem_ref[early:, cols]
        second_out[head, 2 * late :, :] = late_extra
        if head % bunch == bunch - 1:
            some = slice(head + 1 - bunch, head + 1)
            for index, (source, target) in enumerate(((first_out, first_hbm), (second_out, second_hbm))):
                copy = pltpu.make_async_copy(
                    source.at[some], target.at[some], out_sems.at[index, head // bunch]
                )
                copy.start()
                sent.append(copy)
    for copy in sent:
        copy.wait()


def assemble(in_ref, out_ref):
    part = out_ref.shape[1] // in_ref.shape[0]
    for source in range(in_ref.shape[0]):
        rows = slice(source * part, (source + 1) * part)
        out_ref[0, rows, :] = in_ref[source, :part, :]
        out_ref[1, rows, :] = in_ref[source, part : 2 * part, :]


def attend(begin, count, q_at, ext_at, per, width, tile, final, own_ref, mate_ref, q_ref, ext_ref, *refs):
    if final:
        before_ref, out_ref, mark, minus, qx, dx, scores, high, total, acc, stage, sems = refs
        early_copy = pltpu.make_async_copy(before_ref, out_ref.at[:, :begin, :], sems.at[0])
        early_copy.start()
    else:
        out_ref, gate_ref, mark, minus, qx, dx, scores, high, total, acc = refs
    sources = q_ref.shape[0]
    units = qx.shape[1] // LANES - 1
    sides = (own_ref, mate_ref)
    steps_side = own_ref.shape[1] // width
    rows_unit = mark.shape[0]
    scale = 1.0 / math.sqrt(LANES)
    exponent = scale * math.log2(math.e)
    bias_rows = units * per

    lane = lax.broadcasted_iota(jnp.int32, (BLK, LANES), 1)
    for block in range(LANES):
        mark[block * BLK : (block + 1) * BLK, :] = jnp.where(lane == block, 1.0, 0.0).astype(jnp.bfloat16)
    wide_lane = lax.broadcasted_iota(jnp.int32, (LANES, LANES), 1)
    for block in range(width // LANES):
        minus[block * LANES : (block + 1) * LANES, :] = jnp.where(wide_lane == 0, -1.0, 0.0).astype(jnp.bfloat16)

    gate_sum = jnp.zeros((1, LANES), jnp.float32)
    for source in range(sources):
        base = source * count
        qx[base : base + count, :LANES] = q_ref[source, q_at : q_at + count, :]
        dx[base : base + count, :LANES] = q_ref[source, q_at + count : q_at + 2 * count, :]
        bias = q_ref[source, q_at + 2 * count :, :].astype(jnp.float32)
        for unit in range(units):
            for block in range(count // BLK):
                at = unit * per + block
                row = jnp.broadcast_to(bias[at : at + 1], (BLK, LANES)).astype(jnp.bfloat16)
                qx[base + block * BLK : base + (block + 1) * BLK, (1 + unit) * LANES : (2 + unit) * LANES] = row
        extra = ext_ref[source, ext_at:, :].astype(jnp.float32)
        if not final:
            gate_sum = gate_sum + extra[bias_rows + 1 : bias_rows + 2]
        wide = jnp.broadcast_to(extra[bias_rows : bias_rows + 1], (LANES, LANES)).T
        wide = jnp.where(wide_lane == 0, wide, 0.0).astype(jnp.bfloat16)
        dx[base : base + count, LANES:] = wide[begin : begin + count]
    if not final:
        gate_ref[...] = jnp.broadcast_to(gate_sum, gate_ref.shape)

    def one_tile(index, carry):
        here = pl.ds(pl.multiple_of(index * tile, tile), tile)
        high[...] = jnp.full_like(high, -3e38)
        for side, ref in enumerate(sides):
            for unit in range(units // 2):

                def score(at, carry, side=side, ref=ref, unit=unit):
                    rows = pl.ds(pl.multiple_of(unit * rows_unit + at * width, width), width)
                    marks = pl.ds(pl.multiple_of(at * width, width), width)
                    lanes = (1 + side * (units // 2) + unit) * LANES
                    left = jnp.concatenate([qx[here, :LANES], qx[here, lanes : lanes + LANES]], axis=1)
                    right = jnp.concatenate([ref[0, rows, :], mark[marks, :]], axis=1)
                    got = lax.dot_general(
                        left, right, (((1,), (1,)), ((), ())), preferred_element_type=jnp.float32
                    )
                    scores[side * steps_side + unit * (rows_unit // width) + at] = got
                    best = high[...]
                    for column in range(width // LANES):
                        best = jnp.maximum(best, got[:, column * LANES : (column + 1) * LANES])
                    high[...] = best
                    return carry

                lax.fori_loop(0, rows_unit // width, score, 0, unroll=True)
        high[...] = jnp.broadcast_to(jnp.max(high[...], 1, keepdims=True) * exponent, high.shape)
        total[...] = jnp.zeros_like(total)
        acc[...] = jnp.zeros_like(acc)
        for side, ref in enumerate(sides):

            def back(at, carry, side=side, ref=ref):
                rows = pl.ds(pl.multiple_of(at * width, width), width)
                prod = lax.dot_general(
                    dx[here, :],
                    jnp.concatenate([ref[1, rows, :], minus[...]], axis=1),
                    (((1,), (1,)), ((), ())),
                    preferred_element_type=jnp.float32,
                )
                got = scores[side * steps_side + at]
                level = high[...]
                added = total[...]
                pieces = []
                for column in range(width // LANES):
                    cols = slice(column * LANES, (column + 1) * LANES)
                    expo = jnp.exp2(got[:, cols] * exponent - level)
                    added = added + expo
                    pieces.append((expo * prod[:, cols]).astype(jnp.bfloat16))
                total[...] = added
                acc[...] += jnp.dot(
                    jnp.concatenate(pieces, axis=1), ref[0, rows, :], preferred_element_type=jnp.float32
                )
                return carry

            lax.fori_loop(0, steps_side, back, 0, unroll=4)
        weight = scale / jnp.sum(total[...], 1, keepdims=True)
        qx[here, :LANES] = (acc[...] * weight).astype(jnp.bfloat16)
        return carry

    lax.fori_loop(0, qx.shape[0] // tile, one_tile, 0)
    for source in range(sources):
        (stage if final else out_ref)[source] = qx[source * count : (source + 1) * count, :LANES]
    if final:
        late_copy = pltpu.make_async_copy(stage, out_ref.at[:, begin:, :], sems.at[1])
        late_copy.start()
        early_copy.wait()
        late_copy.wait()


def unpack(in_ref, out_ref):
    for head in range(in_ref.shape[0]):
        out_ref[:, head * LANES : (head + 1) * LANES] = in_ref[head]


def local(queries, d_out, o_mem, local_out, mem_keys, mem_values, gate_logit, block_ids):
    shards = lax.axis_size("mem")
    groups = lax.axis_size("grp")
    tokens = queries.shape[1]
    width = queries.shape[2]
    heads = gate_logit.shape[0]
    rows_dev = mem_keys.shape[0]
    qblocks = tokens // BLK
    members = heads
    chunks = shards // heads
    assert width == heads * LANES and shards % heads == 0 and groups % 2 == 0
    assert rows_dev == 16 * BLK and heads * 8 == LANES and tokens == LANES
    half_shard = rows_dev // 2
    per = qblocks // 2
    units = 2 * chunks
    early = tokens // 2
    late = tokens - early
    extra = -(-(units * per + 2) // 16) * 16
    late_extra = -(-units * per // 16) * 16
    ext_at = 2 * half_shard + 2 * early
    vmem = pl.BlockSpec(memory_space=pltpu.VMEM)
    smem = pl.BlockSpec(memory_space=pltpu.SMEM)
    hbm = pl.BlockSpec(memory_space=pltpu.HBM)
    bf16 = jnp.bfloat16
    small = pltpu.CompilerParams(vmem_limit_bytes=24 << 20)

    core_groups = [
        [(mo * heads + 2 * chip + core) * groups + 2 * go + gp for chip in range(heads // 2) for gp in range(2)]
        for mo in range(chunks)
        for go in range(groups // 2)
        for core in range(2)
    ]
    exchange = functools.partial(
        lax.all_to_all, axis_name=AXES, split_axis=0, concat_axis=0, tiled=True, axis_index_groups=core_groups
    )

    first_shape = (members, ext_at + extra, LANES)
    second_shape = (members, 2 * late + late_extra, LANES)
    first_out, second_out = pl.pallas_call(
        functools.partial(pack, heads, chunks, early),
        out_shape=(pltpu.HBM(first_shape, bf16), pltpu.HBM(second_shape, bf16)),
        in_specs=[hbm] * 6 + [smem, vmem],
        out_specs=(hbm, hbm),
        scratch_shapes=[pltpu.VMEM((half_shard, width), bf16)] * 2
        + [pltpu.VMEM((tokens, width), bf16)] * 5
        + [
            pltpu.VMEM((extra, LANES), jnp.float32),
            pltpu.VMEM((late_extra, LANES), jnp.float32),
            pltpu.VMEM((heads, LANES), jnp.float32),
            pltpu.VMEM((LANES, LANES), jnp.float32),
            pltpu.VMEM(first_shape, bf16),
            pltpu.VMEM(second_shape, bf16),
            pltpu.SemaphoreType.DMA((6,)),
            pltpu.SemaphoreType.DMA((2, 4)),
        ],
        compiler_params=pltpu.CompilerParams(vmem_limit_bytes=56 << 20),
        name="pack",
    )(mem_keys, mem_values, queries[0], d_out[0], o_mem[0], local_out[0], gate_logit, block_ids[0])
    first_in = exchange(first_out)
    second_in = exchange(second_out)
    own = pl.pallas_call(
        assemble,
        out_shape=jax.ShapeDtypeStruct((2, members * half_shard, LANES), bf16),
        in_specs=[vmem],
        out_specs=vmem,
        compiler_params=small,
        name="assemble",
    )(first_in)
    if chunks > 1:
        same = [[mo * heads + mi for mo in range(chunks)] for mi in range(heads)]
        own = lax.all_gather(own, "mem", axis_index_groups=same, axis=1, tiled=True)
    mate = lax.ppermute(own, "mem", [(i, i ^ 1) for i in range(shards)])

    rows_all = 2 * own.shape[1]
    step_width = 512
    tile = 1024 if chunks == 1 else 256

    def attend_some(begin, count, q_at, final, out_shape, out_specs, *args):
        return pl.pallas_call(
            functools.partial(attend, begin, count, q_at, ext_at, per, step_width, tile, final),
            out_shape=out_shape,
            in_specs=[vmem] * len(args),
            out_specs=out_specs,
            scratch_shapes=[
                pltpu.VMEM((LANES * BLK, LANES), bf16),
                pltpu.VMEM((step_width, LANES), bf16),
                pltpu.VMEM((members * count, (1 + units) * LANES), bf16),
                pltpu.VMEM((members * count, 2 * LANES), bf16),
                pltpu.VMEM((rows_all // step_width, tile, step_width), jnp.float32),
                pltpu.VMEM((tile, LANES), jnp.float32),
                pltpu.VMEM((tile, LANES), jnp.float32),
                pltpu.VMEM((tile, LANES), jnp.float32),
            ]
            + [pltpu.VMEM((members, count, LANES), bf16), pltpu.SemaphoreType.DMA((2,))] * final,
            compiler_params=pltpu.CompilerParams(vmem_limit_bytes=(34 if chunks == 1 else 44) << 20),
            cost_estimate=pl.CostEstimate(
                flops=2 * members * count * rows_all * LANES * 5,
                bytes_accessed=4 * rows_all * LANES,
                transcendentals=members * count * rows_all,
            ),
            name="attend",
        )(*args)

    part, gate_sum = attend_some(
        0,
        early,
        2 * half_shard,
        False,
        [jax.ShapeDtypeStruct((members, early, LANES), bf16), jax.ShapeDtypeStruct((8, LANES), jnp.float32)],
        [vmem, vmem],
        own,
        mate,
        first_in,
        first_in,
    )
    gate_mate = lax.ppermute(gate_sum, "mem", [(i, i ^ 1) for i in range(shards)])
    grad = attend_some(
        early,
        late,
        0,
        True,
        pltpu.HBM((members, tokens, LANES), bf16),
        hbm,
        own,
        mate,
        second_in,
        first_in,
        part,
    )
    home = exchange(grad)
    d_query = pl.pallas_call(
        unpack,
        out_shape=jax.ShapeDtypeStruct((tokens, width), bf16),
        in_specs=[vmem],
        out_specs=vmem,
        compiler_params=small,
        name="unpack",
    )(home)
    addends = (gate_sum + gate_mate)[0, : 3 * heads]
    gate_total = addends[:heads] + addends[heads : 2 * heads] + addends[2 * heads :]
    if chunks > 1 or groups > 2:
        gate_total = lax.psum(gate_total, AXES) / (2 * members)
    sig = jax.nn.sigmoid(gate_logit)
    d_gate = sig * (1.0 - sig) * gate_total / (shards * groups * tokens * LANES) ** 0.5
    return (d_query[None], d_gate)


def solution(mesh):
    placed = (
        P("grp", "mem", None),
        P("grp", "mem", None),
        P("grp", "mem", None),
        P("grp", "mem", None),
        P("mem", None),
        P("mem", None),
        P(),
        P("grp", "mem", None),
    )
    return jax.shard_map(
        local, mesh=mesh, in_specs=placed, out_specs=(P("grp", "mem", None), P()), check_vma=False
    )
```

time: 106 us -> 107 us (level)
  waiting for transfers between devices: 17.6 us -> 18.9 us
    all_to_all x1, waiting for transfers between devices: 3.15 us -> 4.9 us  [local(): second_in = exchange(second_out)]
    all_to_all x1, waiting for transfers between devices: 14.5 us -> 12.9 us  [local(): home = exchange(grad)]
    pallas_call x1, Pallas kernels: 5.71 us -> 4.52 us  [local(): pl.pallas_call(functools.partial(pack, heads, chunks, early), out_shape=(...]
    ppermute x0 -> x1, waiting for transfers between devices: none -> 1.15 us  [local(): lax.ppermute(gate_sum, 'mem', [(i, i ^ 1) for i in range(shards)])]
    all_to_all x1, starting transfers between devices: 3.62 us -> 4.77 us  [local(): home = exchange(grad)]
  transfers between devices with their start and end apart: 3 -> 4, of which waited for: 2 -> 3; matrix products, arithmetic and copies ran while one was open for 1% -> 1% of each run, Pallas kernels for 11% -> 11%
where the time goes in v7:
time: 107 us
  blocking collectives  48.3 us (45%)
  Pallas kernels  29.7 us (28%)
  waiting for transfers between devices  18.9 us (18%)
  starting transfers between devices  8.5 us (8%)
    all_to_all x1, blocking collectives, local(): first_in = exchange(first_out)  48.3 us
    pallas_call x2, Pallas kernels, attend_some(): pl.pallas_call(functools.partial(attend, begin, count, q_at, ext_at, per,...  24.2 us
    all_to_all x1, waiting for transfers between devices, local(): home = exchange(grad)  12.9 us
    all_to_all x1, waiting for transfers between devices, local(): second_in = exchange(second_out)  4.9 us
    all_to_all x1, starting transfers between devices, local(): home = exchange(grad)  4.77 us
    pallas_call x1, Pallas kernels, local(): pl.pallas_call(functools.partial(pack, heads, chunks, early), out_shape=(...  4.52 us
    all_to_all x1, starting transfers between devices, local(): second_in = exchange(second_out)  3.59 us
  transfers between devices with their start and end apart: 4, of which 3 were waited for; matrix products, arithmetic and copies ran while one was open for 1% of the time, Pallas kernels for 11%

profile of v7, /device:TPU:0, one launch (start us, length us, event | category | flops | bytes accessed | tf_op | source)
XLA Modules:
  0.0 106.7 jit_solution(14854109975600080050)
XLA Ops:
  0.6 4.5 %pack.1 = (bf16[16,400,128]{2,1,0:T(8,128)(2,1)}, bf16[16,144,128]{2,1,0:T(8,128)(2,1)}) custom-call(bf16[256,2048]{1,0:T(8,128)(2,1)} %k_hbm.1, bf16[256,2048]{1,0:T(8,128)(2,1)} %v_hbm.1, bf16[128,2048]{1,0:T(8,128)(2,1)} %bitcast.10, bf16[128,2048]{1,0:T(8,128)(2,1)} %bitcast.11, bf16[128,2048]{1,0:T(8,128)(2,1)} %bitcast.12, bf16[128,2048]{1,0:T(8,128)(2,1)} %bitcast.13, ...), custom_call_target="tpu_custom_call" | custom-call | tf_op jit(solution)/shard_map/pack/pallas_call | solution.py:309
  5.2 48.3 %all_to_all.15.in_ref.q_ref.ext_ref = bf16[16,400,128]{2,1,0:T(8,128)(2,1)S(1)} all-to-all(bf16[16,400,128]{2,1,0:T(8,128)(2,1)} %get-tuple-element.6), channel_id=1, replica_groups={{0,1,4,5,8,9,12,13,16,17,20,21,24,25,28,29},{2,3,6,7,10,11,14,15,18,19,..., dimensions={0} | all-to-all | bytes 3276800 | tf_op jit(solution)/shard_map/all_to_all | solution.py:329
  53.4 0.1 assemble.1.own_ref
  53.5 0.1 collective-permute-start
  53.6 3.6 %all-to-all-start.1 = ((bf16[16,144,128]{2,1,0:T(8,128)(2,1)}), bf16[16,144,128]{2,1,0:T(8,128)(2,1)S(1)}, u32[]{:S(2)}, u32[]{:S(2)}) async-start(bf16[16,144,128]{2,1,0:T(8,128)(2,1)} %get-tuple-element.7), calls=%async_computation.1 | async-start | bytes 1179648 | tf_op jit(solution)/shard_map/all_to_all | solution.py:330
  57.2 0.0 collective-permute-done.mate_ref
  57.2 11.6 %attend.2 = (bf16[16,64,128]{2,1,0:T(8,128)(2,1)S(1)}, f32[8,128]{1,0:T(8,128)S(1)}) custom-call(bf16[2,2048,128]{2,1,0:T(8,128)(2,1)S(1)} %assemble.1.own_ref, bf16[2,2048,128]{2,1,0:T(8,128)(2,1)} %collective-permute-done.mate_ref, bf16[16,400,128]{2,1,0:T(8,128)(2,1)S(1)} %all_to_all.15.in_ref.q_ref.ext_ref, ...), custom_call_target="tpu_custom_call" | custom-call | flops 5368709120 | bytes 2097152 | tf_op jit(solution)/shard_map/attend/pallas_call | solution.py:349
  68.8 4.9 %all-to-all-done.1.q_ref = bf16[16,144,128]{2,1,0:T(8,128)(2,1)S(1)} async-done(((bf16[16,144,128]{2,1,0:T(8,128)(2,1)}), bf16[16,144,128]{2,1,0:T(8,128)(2,1)S(1)}, u32[]{:S(2)}, u32[]{:S(2)}) %all-to-all-start.1) | async-done | bytes 589856 | tf_op jit(solution)/shard_map/all_to_all | solution.py:330
  73.7 0.0 copy-start
  73.7 12.6 %attend.3 = bf16[16,128,128]{2,1,0:T(8,128)(2,1)} custom-call(bf16[2,2048,128]{2,1,0:T(8,128)(2,1)S(1)} %assemble.1.own_ref, bf16[2,2048,128]{2,1,0:T(8,128)(2,1)} %collective-permute-done.mate_ref, bf16[16,144,128]{2,1,0:T(8,128)(2,1)S(1)} %all-to-all-done.1.q_ref, bf16[16,400,128]{2,1,0:T(8,128)(2,1)S(1)} %all_to_all.15.in_ref.q_ref.ext_ref, ...), custom_call_target="tpu_custom_call" | custom-call | flops 5368709120 | bytes 2097152 | tf_op jit(solution)/shard_map/attend/pallas_call | solution.py:349
  86.3 4.8 %all-to-all-start.2 = ((bf16[16,128,128]{2,1,0:T(8,128)(2,1)}), bf16[16,128,128]{2,1,0:T(8,128)(2,1)S(1)}, u32[]{:S(2)}, u32[]{:S(2)}) async-start(bf16[16,128,128]{2,1,0:T(8,128)(2,1)} %attend.3), calls=%async_computation.2 | async-start | bytes 1048576 | tf_op jit(solution)/shard_map/all_to_all | solution.py:400
  91.1 0.1 collective-permute-start.1
  91.2 1.2 %collective-permute-done.1 = f32[8,128]{1,0:T(8,128)S(1)} collective-permute-done((f32[8,128]{1,0:T(8,128)S(1)}, f32[8,128]{1,0:T(8,128)S(1)}, u32[]{:S(2)}, u32[]{:S(2)}) %collective-permute-start.1) | collective-permute-done | bytes 4128 | tf_op jit(solution)/shard_map/ppermute | solution.py:386
  92.3 0.0 copy-done
  92.3 0.6 fusion.1
  92.9 12.9 %all-to-all-done.2.in_ref = bf16[16,128,128]{2,1,0:T(8,128)(2,1)S(1)} async-done(((bf16[16,128,128]{2,1,0:T(8,128)(2,1)}), bf16[16,128,128]{2,1,0:T(8,128)(2,1)S(1)}, u32[]{:S(2)}, u32[]{:S(2)}) %all-to-all-start.2) | async-done | bytes 524320 | tf_op jit(solution)/shard_map/all_to_all | solution.py:400
  105.8 0.9 unpack.1
  (1 shorter events, 0.0 us)
Async XLA Ops:
  53.5 3.7 %collective-permute-start = (bf16[2,2048,128]{2,1,0:T(8,128)(2,1)S(1)}, bf16[2,2048,128]{2,1,0:T(8,128)(2,1)}, u32[]{:S(2)}, u32[]{:S(2)}) collective-permute-start(bf16[2,2048,128]{2,1,0:T(8,128)(2,1)S(1)} %assemble.1.own_ref), channel_id=1, source_target_pairs={{0,2},{2,0},{4,6},{6,4},{8,10},{10,8},{12,14},{14,12},{16,18},{18,... | collective-permute-start | bytes 3145736 | tf_op jit(solution)/shard_map/ppermute | solution.py:342
  53.6 20.1 %all-to-all-start.1 = ((bf16[16,144,128]{2,1,0:T(8,128)(2,1)}), bf16[16,144,128]{2,1,0:T(8,128)(2,1)S(1)}, u32[]{:S(2)}, u32[]{:S(2)}) async-start(bf16[16,144,128]{2,1,0:T(8,128)(2,1)} %get-tuple-element.7), calls=%async_computation.1 | async-start | bytes 1179648 | tf_op jit(solution)/shard_map/all_to_all | solution.py:330
  73.7 18.6 %copy-start = (f32[16]{0:T(128)S(1)}, f32[16]{0:T(128)}, u32[]{:S(2)}) copy-start(f32[16]{0:T(128)} %gate_ref.1) | copy-start | bytes 196
  86.3 19.5 %all-to-all-start.2 = ((bf16[16,128,128]{2,1,0:T(8,128)(2,1)}), bf16[16,128,128]{2,1,0:T(8,128)(2,1)S(1)}, u32[]{:S(2)}, u32[]{:S(2)}) async-start(bf16[16,128,128]{2,1,0:T(8,128)(2,1)} %attend.3), calls=%async_computation.2 | async-start | bytes 1048576 | tf_op jit(solution)/shard_map/all_to_all | solution.py:400
  91.1 1.2 %collective-permute-start.1 = (f32[8,128]{1,0:T(8,128)S(1)}, f32[8,128]{1,0:T(8,128)S(1)}, u32[]{:S(2)}, u32[]{:S(2)}) collective-permute-start(f32[8,128]{1,0:T(8,128)S(1)} %get-tuple-element.9), channel_id=1, source_target_pairs={{0,2},{2,0},{4,6},{6,4},{8,10},{10,8},{12,14},{14,12},{16,18},{18,... | collective-permute-start | bytes 12296 | tf_op jit(solution)/shard_map/ppermute | solution.py:386

commit v8 on v7

--- a/solution.py
+++ b/solution.py
@@ -34,9 +34,7 @@
     dout_ref,
     omem_ref,
     local_ref,
-    dmem_ref,
     ext_ref,
-    late_ref,
     delta_ref,
     gate_rows,
     first_out,
@@ -47,55 +45,59 @@
     tokens = q_ref.shape[0]
     half_shard = k_ref.shape[0]
     qblocks, names = ids_ref.shape
-    high = lax.Precision.HIGHEST
     core = lax.axis_index("mem") % 2
     parity = lax.axis_index("grp") % 2
     mine = pl.ds(pl.multiple_of(parity * half_shard, half_shard), half_shard)
+    bunches = sems.shape[0]
+    bunch = heads // bunches
     copies = []
-    for at, (source, target) in enumerate(
-        (
-            (dout_hbm, dout_ref),
-            (omem_hbm, omem_ref),
-            (local_hbm, local_ref),
-            (q_hbm, q_ref),
-            (k_hbm.at[mine, :], k_ref),
-            (v_hbm.at[mine, :], v_ref),
-        )
-    ):
-        copy = pltpu.make_async_copy(source, target, sems.at[at])
-        copy.start()
-        copies.append(copy)
+    for index in range(bunches):
+        cols = slice(index * bunch * LANES, (index + 1) * bunch * LANES)
+        copies.append([])
+        for at, (source, target) in enumerate(
+            (
+                (dout_hbm.at[:, cols], dout_ref),
+                (omem_hbm.at[:, cols], omem_ref),
+                (local_hbm.at[:, cols], local_ref),
+                (q_hbm.at[:, cols], q_ref),
+                (k_hbm.at[mine, cols], k_ref),
+                (v_hbm.at[mine, cols], v_ref),
+            )
+        ):
+            copy = pltpu.make_async_copy(source, target.at[:, cols], sems.at[index, at])
+            copy.start()
+            copies[index].append(copy)
 
     lane = lax.broadcasted_iota(jnp.int32, (1, LANES), 1)
     ids = ids_ref[...]
-    per = qblocks // 2
-    bias_rows = 2 * chunks * per
+    bias_rows = chunks * qblocks
     ext_ref[...] = jnp.zeros_like(ext_ref)
-    late_ref[...] = jnp.zeros_like(late_ref)
-    for side in range(2):
-        for chunk in range(chunks):
+    for chunk in range(chunks):
+        hits = []
+        for side in range(2):
             shard = chunk * heads + 2 * (lane // 16) + (core + side) % 2
             wanted = jnp.broadcast_to(16 * shard + lane % 16, (qblocks, LANES))
             hit = jnp.zeros((qblocks, LANES), jnp.float32)
             for name in range(names):
                 hit = jnp.where(ids[:, name : name + 1] == wanted, 1.0, hit)
-            table = jnp.where(hit > 0.5, 0.0, FAR)
-            at = (side * chunks + chunk) * per
-            ext_ref[at : at + per, :] = table[:per]
-            late_ref[at : at + per, :] = table[per:]
+            hits.append(hit)
+        ext_ref[chunk * qblocks : (chunk + 1) * qblocks, :] = hits[0] + 2.0 * hits[1]
 
     ones = jnp.ones((8, LANES), jnp.float32)
     wide_ones = jnp.ones((16, 2 * LANES), jnp.bfloat16)
     gate_rows[...] = jnp.zeros_like(gate_rows)
-    for copy in copies[:3]:
-        copy.wait()
+    at = 2 * half_shard
+    late = tokens - early
+    sent = []
     for head in range(heads):
+        if head % bunch == 0:
+            for copy in copies[head // bunch]:
+                copy.wait()
         cols = slice(head * LANES, (head + 1) * LANES)
         sig = jax.nn.sigmoid(jnp.full((8, LANES), gate_ref[head], jnp.float32))[:1]
         d_out = dout_ref[:, cols].astype(jnp.float32)
         o_mem = omem_ref[:, cols].astype(jnp.float32)
         d_mem = (d_out * sig).astype(jnp.bfloat16)
-        dmem_ref[:, cols] = d_mem
         differ = o_mem - local_ref[:, cols].astype(jnp.float32)
         gate_rows[head : head + 1, :] = jnp.sum(d_out * differ, 0, keepdims=True)
         product = d_mem.astype(jnp.float32) * o_mem
@@ -108,40 +110,40 @@
             preferred_element_type=jnp.float32,
         )
         delta_ref[head : head + 1, :] = row[:1]
+        first_out[head, :half_shard, :] = k_ref[:, cols]
+        first_out[head, half_shard:at, :] = v_ref[:, cols]
+        first_out[head, at : at + early, :] = q_ref[:early, cols]
+        first_out[head, at + early : at + 2 * early, :] = d_mem[:early]
+        second_out[head, :late, :] = q_ref[early:, cols]
+        second_out[head, late:, :] = d_mem[early:]
+        if head % bunch == bunch - 1:
+            some = slice(head + 1 - bunch, head + 1)
+            body = slice(0, at + 2 * early)
+            for index, (source, target) in enumerate(
+                ((first_out.at[some, body], first_hbm.at[some, body]), (second_out.at[some], second_hbm.at[some]))
+            ):
+                copy = pltpu.make_async_copy(source, target, out_sems.at[index, head // bunch])
+                copy.start()
+                sent.append(copy)
     total = lax.dot_general(
-        ones, gate_rows[...], (((1,), (1,)), ((), ())), precision=high, preferred_element_type=jnp.float32
+        ones,
+        gate_rows[...],
+        (((1,), (1,)), ((), ())),
+        precision=lax.Precision.HIGHEST,
+        preferred_element_type=jnp.float32,
     )
     first = total.astype(jnp.bfloat16).astype(jnp.float32)
     second = (total - first).astype(jnp.bfloat16).astype(jnp.float32)
     third = total - first - second
     addends = first + pltpu.roll(second, heads, 1) + pltpu.roll(third, 2 * heads, 1)
     ext_ref[bias_rows + 1 : bias_rows + 2, :] = addends[:1]
-    late_extra = late_ref[...].astype(jnp.bfloat16)
-    for copy in copies[3:]:
-        copy.wait()
-    at = 2 * half_shard
-    late = tokens - early
-    sent = []
-    bunch = heads // 4
     for head in range(heads):
-        cols = slice(head * LANES, (head + 1) * LANES)
-        first_out[head, :half_shard, :] = k_ref[:, cols]
-        first_out[head, half_shard:at, :] = v_ref[:, cols]
-        first_out[head, at : at + early, :] = q_ref[:early, cols]
-        first_out[head, at + early : at + 2 * early, :] = dmem_ref[:early, cols]
         ext_ref[bias_rows : bias_rows + 1, :] = delta_ref[head : head + 1, :]
         first_out[head, at + 2 * early :, :] = ext_ref[...].astype(jnp.bfloat16)
-        second_out[head, :late, :] = q_ref[early:, cols]
-        second_out[head, late : 2 * late, :] = dmem_ref[early:, cols]
-        second_out[head, 2 * late :, :] = late_extra
-        if head % bunch == bunch - 1:
-            some = slice(head + 1 - bunch, head + 1)
-            for index, (source, target) in enumerate(((first_out, first_hbm), (second_out, second_hbm))):
-                copy = pltpu.make_async_copy(
-                    source.at[some], target.at[some], out_sems.at[index, head // bunch]
-                )
-                copy.start()
-                sent.append(copy)
+    body = slice(at + 2 * early, first_out.shape[1])
+    copy = pltpu.make_async_copy(first_out.at[:, body], first_hbm.at[:, body], out_sems.at[0, bunches])
+    copy.start()
+    sent.append(copy)
     for copy in sent:
         copy.wait()
 
@@ -154,7 +156,7 @@
         out_ref[1, rows, :] = in_ref[source, part : 2 * part, :]
 
 
-def attend(begin, count, q_at, ext_at, per, width, tile, final, own_ref, mate_ref, q_ref, ext_ref, *refs):
+def attend(begin, count, q_at, ext_at, qblocks, width, tile, final, own_ref, mate_ref, q_ref, ext_ref, *refs):
     if final:
         before_ref, out_ref, mark, minus, qx, dx, scores, high, total, acc, stage, sems = refs
         early_copy = pltpu.make_async_copy(before_ref, out_ref.at[:, :begin, :], sems.at[0])
@@ -168,7 +170,8 @@
     rows_unit = mark.shape[0]
     scale = 1.0 / math.sqrt(LANES)
     exponent = scale * math.log2(math.e)
-    bias_rows = units * per
+    chunks = units // 2
+    bias_rows = chunks * qblocks
 
     lane = lax.broadcasted_iota(jnp.int32, (BLK, LANES), 1)
     for block in range(LANES):
@@ -182,13 +185,18 @@
         base = source * count
         qx[base : base + count, :LANES] = q_ref[source, q_at : q_at + count, :]
         dx[base : base + count, :LANES] = q_ref[source, q_at + count : q_at + 2 * count, :]
-        bias = q_ref[source, q_at + 2 * count :, :].astype(jnp.float32)
-        for unit in range(units):
-            for block in range(count // BLK):
-                at = unit * per + block
-                row = jnp.broadcast_to(bias[at : at + 1], (BLK, LANES)).astype(jnp.bfloat16)
-                qx[base + block * BLK : base + (block + 1) * BLK, (1 + unit) * LANES : (2 + unit) * LANES] = row
         extra = ext_ref[source, ext_at:, :].astype(jnp.float32)
+        code = extra[:bias_rows]
+        second = jnp.where(code > 1.5, 1.0, 0.0)
+        first = code - 2.0 * second
+        for side, hit in enumerate((first, second)):
+            bias = jnp.where(hit > 0.5, 0.0, FAR)
+            for chunk in range(chunks):
+                lanes = (1 + side * chunks + chunk) * LANES
+                for block in range(count // BLK):
+                    at = chunk * qblocks + begin // BLK + block
+                    row = jnp.broadcast_to(bias[at : at + 1], (BLK, LANES)).astype(jnp.bfloat16)
+                    qx[base + block * BLK : base + (block + 1) * BLK, lanes : lanes + LANES] = row
         if not final:
             gate_sum = gate_sum + extra[bias_rows + 1 : bias_rows + 2]
         wide = jnp.broadcast_to(extra[bias_rows : bias_rows + 1], (LANES, LANES)).T
@@ -219,7 +227,7 @@
                     high[...] = best
                     return carry
 
-                lax.fori_loop(0, rows_unit // width, score, 0, unroll=True)
+                lax.fori_loop(0, rows_unit // width, score, 0, unroll=2)
         high[...] = jnp.broadcast_to(jnp.max(high[...], 1, keepdims=True) * exponent, high.shape)
         total[...] = jnp.zeros_like(total)
         acc[...] = jnp.zeros_like(acc)
@@ -248,7 +256,7 @@
                 )
                 return carry
 
-            lax.fori_loop(0, steps_side, back, 0, unroll=4)
+            lax.fori_loop(0, steps_side, back, 0, unroll=2)
         weight = scale / jnp.sum(total[...], 1, keepdims=True)
         qx[here, :LANES] = (acc[...] * weight).astype(jnp.bfloat16)
         return carry
@@ -281,12 +289,10 @@
     assert width == heads * LANES and shards % heads == 0 and groups % 2 == 0
     assert rows_dev == 16 * BLK and heads * 8 == LANES and tokens == LANES
     half_shard = rows_dev // 2
-    per = qblocks // 2
     units = 2 * chunks
-    early = tokens // 2
+    early = 5 * tokens // 8
     late = tokens - early
-    extra = -(-(units * per + 2) // 16) * 16
-    late_extra = -(-units * per // 16) * 16
+    extra = -(-(chunks * qblocks + 2) // 16) * 16
     ext_at = 2 * half_shard + 2 * early
     vmem = pl.BlockSpec(memory_space=pltpu.VMEM)
     smem = pl.BlockSpec(memory_space=pltpu.SMEM)
@@ -305,23 +311,22 @@
     )
 
     first_shape = (members, ext_at + extra, LANES)
-    second_shape = (members, 2 * late + late_extra, LANES)
+    second_shape = (members, 2 * late, LANES)
     first_out, second_out = pl.pallas_call(
         functools.partial(pack, heads, chunks, early),
         out_shape=(pltpu.HBM(first_shape, bf16), pltpu.HBM(second_shape, bf16)),
         in_specs=[hbm] * 6 + [smem, vmem],
         out_specs=(hbm, hbm),
         scratch_shapes=[pltpu.VMEM((half_shard, width), bf16)] * 2
-        + [pltpu.VMEM((tokens, width), bf16)] * 5
+        + [pltpu.VMEM((tokens, width), bf16)] * 4
         + [
             pltpu.VMEM((extra, LANES), jnp.float32),
-            pltpu.VMEM((late_extra, LANES), jnp.float32),
             pltpu.VMEM((heads, LANES), jnp.float32),
             pltpu.VMEM((LANES, LANES), jnp.float32),
             pltpu.VMEM(first_shape, bf16),
             pltpu.VMEM(second_shape, bf16),
-            pltpu.SemaphoreType.DMA((6,)),
-            pltpu.SemaphoreType.DMA((2, 4)),
+            pltpu.SemaphoreType.DMA((4, 6)),
+            pltpu.SemaphoreType.DMA((2, 5)),
         ],
         compiler_params=pltpu.CompilerParams(vmem_limit_bytes=56 << 20),
         name="pack",
@@ -343,11 +348,11 @@
 
     rows_all = 2 * own.shape[1]
     step_width = 512
-    tile = 1024 if chunks == 1 else 256
 
     def attend_some(begin, count, q_at, final, out_shape, out_specs, *args):
+        tile = members * count if chunks == 1 else 256
         return pl.pallas_call(
-            functools.partial(attend, begin, count, q_at, ext_at, per, step_width, tile, final),
+            functools.partial(attend, begin, count, q_at, ext_at, qblocks, step_width, tile, final),
             out_shape=out_shape,
             in_specs=[vmem] * len(args),
             out_specs=out_specs,
@@ -362,7 +367,7 @@
                 pltpu.VMEM((tile, LANES), jnp.float32),
             ]
             + [pltpu.VMEM((members, count, LANES), bf16), pltpu.SemaphoreType.DMA((2,))] * final,
-            compiler_params=pltpu.CompilerParams(vmem_limit_bytes=(34 if chunks == 1 else 44) << 20),
+            compiler_params=pltpu.CompilerParams(vmem_limit_bytes=(40 if chunks == 1 else 44) << 20),
             cost_estimate=pl.CostEstimate(
                 flops=2 * members * count * rows_all * LANES * 5,
                 bytes_accessed=4 * rows_all * LANES,

time: 107 us -> 105 us (0.981)
  waiting for transfers between devices: 18.9 us -> 15.2 us
  Pallas kernels: 29.7 us -> 27.1 us
  blocking collectives: 48.3 us -> 50.8 us
  starting transfers between devices: 8.5 us -> 10.2 us
    all_to_all x1, waiting for transfers between devices: 4.9 us -> 0.42 us  [local(): second_in = exchange(second_out)]
    all_to_all x1, blocking collectives: 48.3 us -> 50.8 us  [local(): first_in = exchange(first_out)]
    pallas_call x2, Pallas kernels: 24.2 us -> 21.9 us  [attend_some(): pl.pallas_call(functools.partial(attend, begin, count, q_at, ext_at, qblo...]
    all_to_all x1, starting transfers between devices: 4.77 us -> 6.48 us  [local(): home = exchange(grad)]
  transfers between devices with their start and end apart: 4 -> 4, of which waited for: 3 -> 3; matrix products, arithmetic and copies ran while one was open for 1% -> 1% of each run, Pallas kernels for 11% -> 12%
where the time goes in v8:
time: 105 us
  blocking collectives  50.8 us (48%)
  Pallas kernels  27.1 us (26%)
  waiting for transfers between devices  15.2 us (14%)
  starting transfers between devices  10.2 us (10%)
    all_to_all x1, blocking collectives, local(): first_in = exchange(first_out)  50.8 us
    pallas_call x2, Pallas kernels, attend_some(): pl.pallas_call(functools.partial(attend, begin, count, q_at, ext_at, qblo...  21.9 us
    all_to_all x1, waiting for transfers between devices, local(): home = exchange(grad)  13.6 us
    all_to_all x1, starting transfers between devices, local(): home = exchange(grad)  6.48 us
    pallas_call x1, Pallas kernels, local(): pl.pallas_call(functools.partial(pack, heads, chunks, early), out_shape=(...  4.2 us
    all_to_all x1, starting transfers between devices, local(): second_in = exchange(second_out)  3.57 us
  transfers between devices with their start and end apart: 4, of which 3 were waited for; matrix products, arithmetic and copies ran while one was open for 1% of the time, Pallas kernels for 12%

profile of v8, /device:TPU:0, one launch (start us, length us, event | category | flops | bytes accessed | tf_op | source)
XLA Modules:
  0.0 104.6 jit_solution(11888849984136533153)
XLA Ops:
  0.6 4.2 %pack.1 = (bf16[16,432,128]{2,1,0:T(8,128)(2,1)}, bf16[16,96,128]{2,1,0:T(8,128)(2,1)}) custom-call(bf16[256,2048]{1,0:T(8,128)(2,1)} %k_hbm.1, bf16[256,2048]{1,0:T(8,128)(2,1)} %v_hbm.1, bf16[128,2048]{1,0:T(8,128)(2,1)} %bitcast.10, bf16[128,2048]{1,0:T(8,128)(2,1)} %bitcast.11, bf16[128,2048]{1,0:T(8,128)(2,1)} %bitcast.12, bf16[128,2048]{1,0:T(8,128)(2,1)} %bitcast.13, ...), custom_call_target="tpu_custom_call" | custom-call | tf_op jit(solution)/shard_map/pack/pallas_call | solution.py:315
  4.8 50.8 %all_to_all.15.in_ref.q_ref.ext_ref = bf16[16,432,128]{2,1,0:T(8,128)(2,1)S(1)} all-to-all(bf16[16,432,128]{2,1,0:T(8,128)(2,1)} %get-tuple-element.6), channel_id=1, replica_groups={{0,1,4,5,8,9,12,13,16,17,20,21,24,25,28,29},{2,3,6,7,10,11,14,15,18,19,..., dimensions={0} | all-to-all | bytes 3538944 | tf_op jit(solution)/shard_map/all_to_all | solution.py:334
  55.6 0.1 assemble.1.own_ref
  55.7 0.1 collective-permute-start
  55.8 3.6 %all-to-all-start.1 = ((bf16[16,96,128]{2,1,0:T(8,128)(2,1)}), bf16[16,96,128]{2,1,0:T(8,128)(2,1)S(1)}, u32[]{:S(2)}, u32[]{:S(2)}) async-start(bf16[16,96,128]{2,1,0:T(8,128)(2,1)} %get-tuple-element.7), calls=%async_computation.1 | async-start | bytes 786432 | tf_op jit(solution)/shard_map/all_to_all | solution.py:335
  59.4 0.0 collective-permute-done.mate_ref
  59.4 12.4 %attend.2 = (bf16[16,80,128]{2,1,0:T(8,128)(2,1)S(1)}, f32[8,128]{1,0:T(8,128)S(1)}) custom-call(bf16[2,2048,128]{2,1,0:T(8,128)(2,1)S(1)} %assemble.1.own_ref, bf16[2,2048,128]{2,1,0:T(8,128)(2,1)} %collective-permute-done.mate_ref, bf16[16,432,128]{2,1,0:T(8,128)(2,1)S(1)} %all_to_all.15.in_ref.q_ref.ext_ref, ...), custom_call_target="tpu_custom_call" | custom-call | flops 6710886400 | bytes 2097152 | tf_op jit(solution)/shard_map/attend/pallas_call | solution.py:354
  71.8 0.4 all-to-all-done.1.q_ref
  72.2 0.0 copy-start
  72.2 9.5 %attend.3 = bf16[16,128,128]{2,1,0:T(8,128)(2,1)} custom-call(bf16[2,2048,128]{2,1,0:T(8,128)(2,1)S(1)} %assemble.1.own_ref, bf16[2,2048,128]{2,1,0:T(8,128)(2,1)} %collective-permute-done.mate_ref, bf16[16,96,128]{2,1,0:T(8,128)(2,1)S(1)} %all-to-all-done.1.q_ref, bf16[16,432,128]{2,1,0:T(8,128)(2,1)S(1)} %all_to_all.15.in_ref.q_ref.ext_ref, ...), custom_call_target="tpu_custom_call" | custom-call | flops 4026531840 | bytes 2097152 | tf_op jit(solution)/shard_map/attend/pallas_call | solution.py:354
  81.7 6.5 %all-to-all-start.2 = ((bf16[16,128,128]{2,1,0:T(8,128)(2,1)}), bf16[16,128,128]{2,1,0:T(8,128)(2,1)S(1)}, u32[]{:S(2)}, u32[]{:S(2)}) async-start(bf16[16,128,128]{2,1,0:T(8,128)(2,1)} %attend.3), calls=%async_computation.2 | async-start | bytes 1048576 | tf_op jit(solution)/shard_map/all_to_all | solution.py:405
  88.2 0.1 collective-permute-start.1
  88.3 1.2 %collective-permute-done.1 = f32[8,128]{1,0:T(8,128)S(1)} collective-permute-done((f32[8,128]{1,0:T(8,128)S(1)}, f32[8,128]{1,0:T(8,128)S(1)}, u32[]{:S(2)}, u32[]{:S(2)}) %collective-permute-start.1) | collective-permute-done | bytes 4128 | tf_op jit(solution)/shard_map/ppermute | solution.py:391
  89.4 0.0 copy-done
  89.5 0.6 fusion.1
  90.0 13.6 %all-to-all-done.2.in_ref = bf16[16,128,128]{2,1,0:T(8,128)(2,1)S(1)} async-done(((bf16[16,128,128]{2,1,0:T(8,128)(2,1)}), bf16[16,128,128]{2,1,0:T(8,128)(2,1)S(1)}, u32[]{:S(2)}, u32[]{:S(2)}) %all-to-all-start.2) | async-done | bytes 524320 | tf_op jit(solution)/shard_map/all_to_all | solution.py:405
  103.7 0.9 unpack.1
  (1 shorter events, 0.0 us)
Async XLA Ops:
  55.7 3.7 %collective-permute-start = (bf16[2,2048,128]{2,1,0:T(8,128)(2,1)S(1)}, bf16[2,2048,128]{2,1,0:T(8,128)(2,1)}, u32[]{:S(2)}, u32[]{:S(2)}) collective-permute-start(bf16[2,2048,128]{2,1,0:T(8,128)(2,1)S(1)} %assemble.1.own_ref), channel_id=1, source_target_pairs={{0,2},{2,0},{4,6},{6,4},{8,10},{10,8},{12,14},{14,12},{16,18},{18,... | collective-permute-start | bytes 3145736 | tf_op jit(solution)/shard_map/ppermute | solution.py:347
  55.8 16.4 %all-to-all-start.1 = ((bf16[16,96,128]{2,1,0:T(8,128)(2,1)}), bf16[16,96,128]{2,1,0:T(8,128)(2,1)S(1)}, u32[]{:S(2)}, u32[]{:S(2)}) async-start(bf16[16,96,128]{2,1,0:T(8,128)(2,1)} %get-tuple-element.7), calls=%async_computation.1 | async-start | bytes 786432 | tf_op jit(solution)/shard_map/all_to_all | solution.py:335
  72.2 17.3 %copy-start = (f32[16]{0:T(128)S(1)}, f32[16]{0:T(128)}, u32[]{:S(2)}) copy-start(f32[16]{0:T(128)} %gate_ref.1) | copy-start | bytes 196
  81.7 21.9 %all-to-all-start.2 = ((bf16[16,128,128]{2,1,0:T(8,128)(2,1)}), bf16[16,128,128]{2,1,0:T(8,128)(2,1)S(1)}, u32[]{:S(2)}, u32[]{:S(2)}) async-start(bf16[16,128,128]{2,1,0:T(8,128)(2,1)} %attend.3), calls=%async_computation.2 | async-start | bytes 1048576 | tf_op jit(solution)/shard_map/all_to_all | solution.py:405
  88.2 1.2 %collective-permute-start.1 = (f32[8,128]{1,0:T(8,128)S(1)}, f32[8,128]{1,0:T(8,128)S(1)}, u32[]{:S(2)}, u32[]{:S(2)}) collective-permute-start(f32[8,128]{1,0:T(8,128)S(1)} %get-tuple-element.9), channel_id=1, source_target_pairs={{0,2},{2,0},{4,6},{6,4},{8,10},{10,8},{12,14},{14,12},{16,18},{18,... | collective-permute-start | bytes 12296 | tf_op jit(solution)/shard_map/ppermute | solution.py:391

commit v9 on v8

--- a/solution.py
+++ b/solution.py
@@ -28,23 +28,24 @@
     ids_ref,
     first_hbm,
     second_hbm,
-    k_ref,
-    v_ref,
-    q_ref,
     dout_ref,
     omem_ref,
     local_ref,
     ext_ref,
     delta_ref,
     gate_rows,
-    first_out,
-    second_out,
+    early_ref,
+    late_ref,
+    extras_ref,
     sems,
+    through_sems,
     out_sems,
 ):
-    tokens = q_ref.shape[0]
-    half_shard = k_ref.shape[0]
+    tokens = q_hbm.shape[0]
+    half_shard = k_hbm.shape[0] // 2
     qblocks, names = ids_ref.shape
+    late = tokens - early
+    at = 2 * half_shard
     core = lax.axis_index("mem") % 2
     parity = lax.axis_index("grp") % 2
     mine = pl.ds(pl.multiple_of(parity * half_shard, half_shard), half_shard)
@@ -54,19 +55,26 @@
     for index in range(bunches):
         cols = slice(index * bunch * LANES, (index + 1) * bunch * LANES)
         copies.append([])
-        for at, (source, target) in enumerate(
+        for which, (source, target) in enumerate(
+            ((dout_hbm, dout_ref), (omem_hbm, omem_ref), (local_hbm, local_ref))
+        ):
+            copy = pltpu.make_async_copy(source.at[:, cols], target.at[:, cols], sems.at[index, which])
+            copy.start()
+            copies[index].append(copy)
+    sent = []
+    for head in range(heads):
+        cols = slice(head * LANES, (head + 1) * LANES)
+        for which, (source, target) in enumerate(
             (
-                (dout_hbm.at[:, cols], dout_ref),
-                (omem_hbm.at[:, cols], omem_ref),
-                (local_hbm.at[:, cols], local_ref),
-                (q_hbm.at[:, cols], q_ref),
-                (k_hbm.at[mine, cols], k_ref),
-                (v_hbm.at[mine, cols], v_ref),
+                (k_hbm.at[mine, cols], first_hbm.at[head, :half_shard]),
+                (v_hbm.at[mine, cols], first_hbm.at[head, half_shard:at]),
+                (q_hbm.at[:early, cols], first_hbm.at[head, at : at + early]),
+                (q_hbm.at[early:, cols], second_hbm.at[head, :late]),
             )
         ):
-            copy = pltpu.make_async_copy(source, target.at[:, cols], sems.at[index, at])
+            copy = pltpu.make_async_copy(source, target, through_sems.at[which, head])
             copy.start()
-            copies[index].append(copy)
+            sent.append(copy)
 
     lane = lax.broadcasted_iota(jnp.int32, (1, LANES), 1)
     ids = ids_ref[...]
@@ -86,9 +94,6 @@
     ones = jnp.ones((8, LANES), jnp.float32)
     wide_ones = jnp.ones((16, 2 * LANES), jnp.bfloat16)
     gate_rows[...] = jnp.zeros_like(gate_rows)
-    at = 2 * half_shard
-    late = tokens - early
-    sent = []
     for head in range(heads):
         if head % bunch == 0:
             for copy in copies[head // bunch]:
@@ -110,17 +115,15 @@
             preferred_element_type=jnp.float32,
         )
         delta_ref[head : head + 1, :] = row[:1]
-        first_out[head, :half_shard, :] = k_ref[:, cols]
-        first_out[head, half_shard:at, :] = v_ref[:, cols]
-        first_out[head, at : at + early, :] = q_ref[:early, cols]
-        first_out[head, at + early : at + 2 * early, :] = d_mem[:early]
-        second_out[head, :late, :] = q_ref[early:, cols]
-        second_out[head, late:, :] = d_mem[early:]
+        early_ref[head] = d_mem[:early]
+        late_ref[head] = d_mem[early:]
         if head % bunch == bunch - 1:
             some = slice(head + 1 - bunch, head + 1)
-            body = slice(0, at + 2 * early)
             for index, (source, target) in enumerate(
-                ((first_out.at[some, body], first_hbm.at[some, body]), (second_out.at[some], second_hbm.at[some]))
+                (
+                    (early_ref.at[some], first_hbm.at[some, at + early : at + 2 * early]),
+                    (late_ref.at[some], second_hbm.at[some, late:]),
+                )
             ):
                 copy = pltpu.make_async_copy(source, target, out_sems.at[index, head // bunch])
                 copy.start()
@@ -139,21 +142,32 @@
     ext_ref[bias_rows + 1 : bias_rows + 2, :] = addends[:1]
     for head in range(heads):
         ext_ref[bias_rows : bias_rows + 1, :] = delta_ref[head : head + 1, :]
-        first_out[head, at + 2 * early :, :] = ext_ref[...].astype(jnp.bfloat16)
-    body = slice(at + 2 * early, first_out.shape[1])
-    copy = pltpu.make_async_copy(first_out.at[:, body], first_hbm.at[:, body], out_sems.at[0, bunches])
+        extras_ref[head] = ext_ref[...].astype(jnp.bfloat16)
+    copy = pltpu.make_async_copy(extras_ref, first_hbm.at[:, at + 2 * early :], out_sems.at[0, bunches])
     copy.start()
     sent.append(copy)
     for copy in sent:
         copy.wait()
 
 
-def assemble(in_ref, out_ref):
-    part = out_ref.shape[1] // in_ref.shape[0]
-    for source in range(in_ref.shape[0]):
+def assemble(gate_at, in_ref, out_ref):
+    sources = in_ref.shape[0]
+    part = (out_ref.shape[1] - BLK) // sources
+    gate = jnp.zeros((1, LANES), jnp.float32)
+    for source in range(sources):
         rows = slice(source * part, (source + 1) * part)
         out_ref[0, rows, :] = in_ref[source, :part, :]
         out_ref[1, rows, :] = in_ref[source, part : 2 * part, :]
+        block = gate_at // BLK * BLK
+        extra = in_ref[source, block : block + BLK, :].astype(jnp.float32)
+        gate = gate + extra[gate_at - block : gate_at - block + 1]
+    first = gate.astype(jnp.bfloat16).astype(jnp.float32)
+    second = (gate - first).astype(jnp.bfloat16).astype(jnp.float32)
+    third = gate - first - second
+    row = lax.broadcasted_iota(jnp.int32, (BLK, LANES), 0)
+    split = jnp.where(row == 0, first, jnp.where(row == 1, second, jnp.where(row == 2, third, 0.0)))
+    out_ref[0, sources * part :, :] = split.astype(jnp.bfloat16)
+    out_ref[1, sources * part :, :] = jnp.zeros((BLK, LANES), jnp.bfloat16)
 
 
 def attend(begin, count, q_at, ext_at, qblocks, width, tile, final, own_ref, mate_ref, q_ref, ext_ref, *refs):
@@ -166,8 +180,9 @@
     sources = q_ref.shape[0]
     units = qx.shape[1] // LANES - 1
     sides = (own_ref, mate_ref)
-    steps_side = own_ref.shape[1] // width
     rows_unit = mark.shape[0]
+    stride = rows_unit + BLK
+    steps_unit = rows_unit // width
     scale = 1.0 / math.sqrt(LANES)
     exponent = scale * math.log2(math.e)
     chunks = units // 2
@@ -177,10 +192,9 @@
     for block in range(LANES):
         mark[block * BLK : (block + 1) * BLK, :] = jnp.where(lane == block, 1.0, 0.0).astype(jnp.bfloat16)
     wide_lane = lax.broadcasted_iota(jnp.int32, (LANES, LANES), 1)
-    for block in range(width // LANES):
-        minus[block * LANES : (block + 1) * LANES, :] = jnp.where(wide_lane == 0, -1.0, 0.0).astype(jnp.bfloat16)
-
-    gate_sum = jnp.zeros((1, LANES), jnp.float32)
+    wide_row = lax.broadcasted_iota(jnp.int32, (LANES, LANES), 0)
+    minus[...] = jnp.full_like(minus, -1.0)
+
     for source in range(sources):
         base = source * count
         qx[base : base + count, :LANES] = q_ref[source, q_at : q_at + count, :]
@@ -197,12 +211,14 @@
                     at = chunk * qblocks + begin // BLK + block
                     row = jnp.broadcast_to(bias[at : at + 1], (BLK, LANES)).astype(jnp.bfloat16)
                     qx[base + block * BLK : base + (block + 1) * BLK, lanes : lanes + LANES] = row
-        if not final:
-            gate_sum = gate_sum + extra[bias_rows + 1 : bias_rows + 2]
-        wide = jnp.broadcast_to(extra[bias_rows : bias_rows + 1], (LANES, LANES)).T
-        wide = jnp.where(wide_lane == 0, wide, 0.0).astype(jnp.bfloat16)
+        wide = jnp.where(wide_lane == wide_row, extra[bias_rows : bias_rows + 1], 0.0).astype(jnp.bfloat16)
         dx[base : base + count, LANES:] = wide[begin : begin + count]
     if not final:
+        gate_sum = jnp.zeros((1, LANES), jnp.float32)
+        for ref in sides:
+            for unit in range(units // 2):
+                at = unit * stride + rows_unit
+                gate_sum = gate_sum + jnp.sum(ref[0, at : at + BLK, :].astype(jnp.float32), 0, keepdims=True)
         gate_ref[...] = jnp.broadcast_to(gate_sum, gate_ref.shape)
 
     def one_tile(index, carry):
@@ -212,7 +228,7 @@
             for unit in range(units // 2):
 
                 def score(at, carry, side=side, ref=ref, unit=unit):
-                    rows = pl.ds(pl.multiple_of(unit * rows_unit + at * width, width), width)
+                    rows = pl.ds(pl.multiple_of(unit * stride + at * width, BLK), width)
                     marks = pl.ds(pl.multiple_of(at * width, width), width)
                     lanes = (1 + side * (units // 2) + unit) * LANES
                     left = jnp.concatenate([qx[here, :LANES], qx[here, lanes : lanes + LANES]], axis=1)
@@ -220,43 +236,44 @@
                     got = lax.dot_general(
                         left, right, (((1,), (1,)), ((), ())), preferred_element_type=jnp.float32
                     )
-                    scores[side * steps_side + unit * (rows_unit // width) + at] = got
+                    scores[(side * (units // 2) + unit) * steps_unit + at] = got
                     best = high[...]
                     for column in range(width // LANES):
                         best = jnp.maximum(best, got[:, column * LANES : (column + 1) * LANES])
                     high[...] = best
                     return carry
 
-                lax.fori_loop(0, rows_unit // width, score, 0, unroll=2)
+                lax.fori_loop(0, steps_unit, score, 0, unroll=2)
         high[...] = jnp.broadcast_to(jnp.max(high[...], 1, keepdims=True) * exponent, high.shape)
         total[...] = jnp.zeros_like(total)
         acc[...] = jnp.zeros_like(acc)
         for side, ref in enumerate(sides):
-
-            def back(at, carry, side=side, ref=ref):
-                rows = pl.ds(pl.multiple_of(at * width, width), width)
-                prod = lax.dot_general(
-                    dx[here, :],
-                    jnp.concatenate([ref[1, rows, :], minus[...]], axis=1),
-                    (((1,), (1,)), ((), ())),
-                    preferred_element_type=jnp.float32,
-                )
-                got = scores[side * steps_side + at]
-                level = high[...]
-                added = total[...]
-                pieces = []
-                for column in range(width // LANES):
-                    cols = slice(column * LANES, (column + 1) * LANES)
-                    expo = jnp.exp2(got[:, cols] * exponent - level)
-                    added = added + expo
-                    pieces.append((expo * prod[:, cols]).astype(jnp.bfloat16))
-                total[...] = added
-                acc[...] += jnp.dot(
-                    jnp.concatenate(pieces, axis=1), ref[0, rows, :], preferred_element_type=jnp.float32
-                )
-                return carry
-
-            lax.fori_loop(0, steps_side, back, 0, unroll=2)
+            for unit in range(units // 2):
+
+                def back(at, carry, side=side, ref=ref, unit=unit):
+                    rows = pl.ds(pl.multiple_of(unit * stride + at * width, BLK), width)
+                    prod = lax.dot_general(
+                        dx[here, :],
+                        jnp.concatenate([ref[1, rows, :], minus[...]], axis=1),
+                        (((1,), (1,)), ((), ())),
+                        preferred_element_type=jnp.float32,
+                    )
+                    got = scores[(side * (units // 2) + unit) * steps_unit + at]
+                    level = high[...]
+                    added = total[...]
+                    pieces = []
+                    for column in range(width // LANES):
+                        cols = slice(column * LANES, (column + 1) * LANES)
+                        expo = jnp.exp2(got[:, cols] * exponent - level)
+                        added = added + expo
+                        pieces.append((expo * prod[:, cols]).astype(jnp.bfloat16))
+                    total[...] = added
+                    acc[...] += jnp.dot(
+                        jnp.concatenate(pieces, axis=1), ref[0, rows, :], preferred_element_type=jnp.float32
+                    )
+                    return carry
+
+                lax.fori_loop(0, steps_unit, back, 0, unroll=2)
         weight = scale / jnp.sum(total[...], 1, keepdims=True)
         qx[here, :LANES] = (acc[...] * weight).astype(jnp.bfloat16)
         return carry
@@ -271,9 +288,14 @@
         late_copy.wait()
 
 
-def unpack(in_ref, out_ref):
+def unpack(in_ref, out_hbm, sems):
+    copies = []
     for head in range(in_ref.shape[0]):
-        out_ref[:, head * LANES : (head + 1) * LANES] = in_ref[head]
+        cols = slice(head * LANES, (head + 1) * LANES)
+        copies.append(pltpu.make_async_copy(in_ref.at[head], out_hbm.at[:, cols], sems.at[head]))
+        copies[-1].start()
+    for copy in copies:
+        copy.wait()
 
 
 def local(queries, d_out, o_mem, local_out, mem_keys, mem_values, gate_logit, block_ids):
@@ -317,15 +339,16 @@
         out_shape=(pltpu.HBM(first_shape, bf16), pltpu.HBM(second_shape, bf16)),
         in_specs=[hbm] * 6 + [smem, vmem],
         out_specs=(hbm, hbm),
-        scratch_shapes=[pltpu.VMEM((half_shard, width), bf16)] * 2
-        + [pltpu.VMEM((tokens, width), bf16)] * 4
+        scratch_shapes=[pltpu.VMEM((tokens, width), bf16)] * 3
         + [
             pltpu.VMEM((extra, LANES), jnp.float32),
             pltpu.VMEM((heads, LANES), jnp.float32),
             pltpu.VMEM((LANES, LANES), jnp.float32),
-            pltpu.VMEM(first_shape, bf16),
-            pltpu.VMEM(second_shape, bf16),
-            pltpu.SemaphoreType.DMA((4, 6)),
+            pltpu.VMEM((members, early, LANES), bf16),
+            pltpu.VMEM((members, late, LANES), bf16),
+            pltpu.VMEM((members, extra, LANES), bf16),
+            pltpu.SemaphoreType.DMA((4, 3)),
+            pltpu.SemaphoreType.DMA((4, heads)),
             pltpu.SemaphoreType.DMA((2, 5)),
         ],
         compiler_params=pltpu.CompilerParams(vmem_limit_bytes=56 << 20),
@@ -334,8 +357,8 @@
     first_in = exchange(first_out)
     second_in = exchange(second_out)
     own = pl.pallas_call(
-        assemble,
-        out_shape=jax.ShapeDtypeStruct((2, members * half_shard, LANES), bf16),
+        functools.partial(assemble, ext_at + chunks * qblocks + 1),
+        out_shape=jax.ShapeDtypeStruct((2, members * half_shard + BLK, LANES), bf16),
         in_specs=[vmem],
         out_specs=vmem,
         compiler_params=small,
@@ -346,7 +369,7 @@
         own = lax.all_gather(own, "mem", axis_index_groups=same, axis=1, tiled=True)
     mate = lax.ppermute(own, "mem", [(i, i ^ 1) for i in range(shards)])
 
-    rows_all = 2 * own.shape[1]
+    rows_all = rows_dev * shards
     step_width = 512
 
     def attend_some(begin, count, q_at, final, out_shape, out_specs, *args):
@@ -388,7 +411,6 @@
         first_in,
         first_in,
     )
-    gate_mate = lax.ppermute(gate_sum, "mem", [(i, i ^ 1) for i in range(shards)])
     grad = attend_some(
         early,
         late,
@@ -405,16 +427,17 @@
     home = exchange(grad)
     d_query = pl.pallas_call(
         unpack,
-        out_shape=jax.ShapeDtypeStruct((tokens, width), bf16),
+        out_shape=pltpu.HBM((tokens, width), bf16),
         in_specs=[vmem],
-        out_specs=vmem,
+        out_specs=hbm,
+        scratch_shapes=[pltpu.SemaphoreType.DMA((heads,))],
         compiler_params=small,
         name="unpack",
     )(home)
-    addends = (gate_sum + gate_mate)[0, : 3 * heads]
+    addends = gate_sum[0, : 3 * heads]
     gate_total = addends[:heads] + addends[heads : 2 * heads] + addends[2 * heads :]
     if chunks > 1 or groups > 2:
-        gate_total = lax.psum(gate_total, AXES) / (2 * members)
+        gate_total = lax.psum(gate_total, AXES) / (2 * shards)
     sig = jax.nn.sigmoid(gate_logit)
     d_gate = sig * (1.0 - sig) * gate_total / (shards * groups * tokens * LANES) ** 0.5
     return (d_query[None], d_gate)

time: 105 us -> 152 us (1.45)
  Pallas kernels: 27.1 us -> 74.2 us
    pallas_call x1, Pallas kernels: 4.2 us -> 50.3 us  [local(): pl.pallas_call(functools.partial(pack, heads, chunks, early), out_shape=(...]
  transfers between devices with their start and end apart: 4 -> 3, of which waited for: 3 -> 1; matrix products, arithmetic and copies ran while one was open for 1% -> 0% of each run, Pallas kernels for 12% -> 9%
where the time goes in v9:
time: 152 us
  Pallas kernels  74.2 us (49%)
  blocking collectives  50.8 us (33%)
  waiting for transfers between devices  14.9 us (10%)
  starting transfers between devices  10.5 us (7%)
    all_to_all x1, blocking collectives, local(): first_in = exchange(first_out)  50.8 us
    pallas_call x1, Pallas kernels, local(): pl.pallas_call(functools.partial(pack, heads, chunks, early), out_shape=(...  50.3 us
    pallas_call x2, Pallas kernels, attend_some(): pl.pallas_call(functools.partial(attend, begin, count, q_at, ext_at, qblo...  22.9 us
    all_to_all x1, waiting for transfers between devices, local(): home = exchange(grad)  14.9 us
    all_to_all x1, starting transfers between devices, local(): home = exchange(grad)  6.89 us
    all_to_all x1, starting transfers between devices, local(): second_in = exchange(second_out)  3.57 us
  transfers between devices with their start and end apart: 3, of which 1 were waited for; matrix products, arithmetic and copies ran while one was open for 0% of the time, Pallas kernels for 9%

profile of v9, /device:TPU:0, one launch (start us, length us, event | category | flops | bytes accessed | tf_op | source)
XLA Modules:
  0.0 151.6 jit_solution(6826468459964405305)
XLA Ops:
  0.6 50.3 %pack.1 = (bf16[16,432,128]{2,1,0:T(8,128)(2,1)}, bf16[16,96,128]{2,1,0:T(8,128)(2,1)}) custom-call(bf16[256,2048]{1,0:T(8,128)(2,1)} %k_hbm.1, bf16[256,2048]{1,0:T(8,128)(2,1)} %v_hbm.1, bf16[128,2048]{1,0:T(8,128)(2,1)} %bitcast.10, bf16[128,2048]{1,0:T(8,128)(2,1)} %bitcast.11, bf16[128,2048]{1,0:T(8,128)(2,1)} %bitcast.12, bf16[128,2048]{1,0:T(8,128)(2,1)} %bitcast.13, ...), custom_call_target="tpu_custom_call" | custom-call | tf_op jit(solution)/shard_map/pack/pallas_call | solution.py:337
  50.9 50.8 %all_to_all.15.in_ref.q_ref.ext_ref = bf16[16,432,128]{2,1,0:T(8,128)(2,1)S(1)} all-to-all(bf16[16,432,128]{2,1,0:T(8,128)(2,1)} %get-tuple-element.6), channel_id=1, replica_groups={{0,1,4,5,8,9,12,13,16,17,20,21,24,25,28,29},{2,3,6,7,10,11,14,15,18,19,..., dimensions={0} | all-to-all | bytes 3538944 | tf_op jit(solution)/shard_map/all_to_all | solution.py:357
  101.7 0.1 assemble.1.own_ref
  101.8 0.1 collective-permute-start
  101.9 3.6 %all-to-all-start.1 = ((bf16[16,96,128]{2,1,0:T(8,128)(2,1)}), bf16[16,96,128]{2,1,0:T(8,128)(2,1)S(1)}, u32[]{:S(2)}, u32[]{:S(2)}) async-start(bf16[16,96,128]{2,1,0:T(8,128)(2,1)} %get-tuple-element.7), calls=%async_computation.1 | async-start | bytes 786432 | tf_op jit(solution)/shard_map/all_to_all | solution.py:358
  105.5 0.0 collective-permute-done.mate_ref
  105.5 13.0 %attend.2 = (bf16[16,80,128]{2,1,0:T(8,128)(2,1)S(1)}, f32[8,128]{1,0:T(8,128)S(1)}) custom-call(bf16[2,2064,128]{2,1,0:T(8,128)(2,1)S(1)} %assemble.1.own_ref, bf16[2,2064,128]{2,1,0:T(8,128)(2,1)} %collective-permute-done.mate_ref, bf16[16,432,128]{2,1,0:T(8,128)(2,1)S(1)} %all_to_all.15.in_ref.q_ref.ext_ref, ...), custom_call_target="tpu_custom_call" | custom-call | flops 6710886400 | bytes 2097152 | tf_op jit(solution)/shard_map/attend/pallas_call | solution.py:377
  118.5 0.0 all-to-all-done.1.q_ref
  118.5 0.0 copy-start
  118.5 9.8 %attend.3 = bf16[16,128,128]{2,1,0:T(8,128)(2,1)} custom-call(bf16[2,2064,128]{2,1,0:T(8,128)(2,1)S(1)} %assemble.1.own_ref, bf16[2,2064,128]{2,1,0:T(8,128)(2,1)} %collective-permute-done.mate_ref, bf16[16,96,128]{2,1,0:T(8,128)(2,1)S(1)} %all-to-all-done.1.q_ref, bf16[16,432,128]{2,1,0:T(8,128)(2,1)S(1)} %all_to_all.15.in_ref.q_ref.ext_ref, ...), custom_call_target="tpu_custom_call" | custom-call | flops 4026531840 | bytes 2097152 | tf_op jit(solution)/shard_map/attend/pallas_call | solution.py:377
  128.4 6.9 %all-to-all-start.2 = ((bf16[16,128,128]{2,1,0:T(8,128)(2,1)}), bf16[16,128,128]{2,1,0:T(8,128)(2,1)S(1)}, u32[]{:S(2)}, u32[]{:S(2)}) async-start(bf16[16,128,128]{2,1,0:T(8,128)(2,1)} %attend.3), calls=%async_computation.2 | async-start | bytes 1048576 | tf_op jit(solution)/shard_map/all_to_all | solution.py:427
  135.3 0.0 copy-done
  135.3 0.6 fusion.1
  135.9 14.9 %all-to-all-done.2.in_ref = bf16[16,128,128]{2,1,0:T(8,128)(2,1)S(1)} async-done(((bf16[16,128,128]{2,1,0:T(8,128)(2,1)}), bf16[16,128,128]{2,1,0:T(8,128)(2,1)S(1)}, u32[]{:S(2)}, u32[]{:S(2)}) %all-to-all-start.2) | async-done | bytes 524320 | tf_op jit(solution)/shard_map/all_to_all | solution.py:427
  150.7 0.9 unpack.1
Async XLA Ops:
  101.8 3.7 %collective-permute-start = (bf16[2,2064,128]{2,1,0:T(8,128)(2,1)S(1)}, bf16[2,2064,128]{2,1,0:T(8,128)(2,1)}, u32[]{:S(2)}, u32[]{:S(2)}) collective-permute-start(bf16[2,2064,128]{2,1,0:T(8,128)(2,1)S(1)} %assemble.1.own_ref), channel_id=1, source_target_pairs={{0,2},{2,0},{4,6},{6,4},{8,10},{10,8},{12,14},{14,12},{16,18},{18,... | collective-permute-start | bytes 3170312 | tf_op jit(solution)/shard_map/ppermute | solution.py:370
  101.9 16.6 %all-to-all-start.1 = ((bf16[16,96,128]{2,1,0:T(8,128)(2,1)}), bf16[16,96,128]{2,1,0:T(8,128)(2,1)S(1)}, u32[]{:S(2)}, u32[]{:S(2)}) async-start(bf16[16,96,128]{2,1,0:T(8,128)(2,1)} %get-tuple-element.7), calls=%async_computation.1 | async-start | bytes 786432 | tf_op jit(solution)/shard_map/all_to_all | solution.py:358
  118.5 16.8 %copy-start = (f32[16]{0:T(128)S(1)}, f32[16]{0:T(128)}, u32[]{:S(2)}) copy-start(f32[16]{0:T(128)} %gate_ref.1) | copy-start | bytes 196
  128.4 22.3 %all-to-all-start.2 = ((bf16[16,128,128]{2,1,0:T(8,128)(2,1)}), bf16[16,128,128]{2,1,0:T(8,128)(2,1)S(1)}, u32[]{:S(2)}, u32[]{:S(2)}) async-start(bf16[16,128,128]{2,1,0:T(8,128)(2,1)} %attend.3), calls=%async_computation.2 | async-start | bytes 1048576 | tf_op jit(solution)/shard_map/all_to_all | solution.py:427

commit v10 on v8

--- a/solution.py
+++ b/solution.py
@@ -12,6 +12,11 @@
 LANES = 128
 AXES = ("mem", "grp")
 FAR = -1e30
+FAN = 4
+
+
+def position_here(heads):
+    return (lax.axis_index("mem") % heads) // 2 * 2 + lax.axis_index("grp") % 2
 
 
 def pack(
@@ -148,26 +153,37 @@
         copy.wait()
 
 
-def assemble(in_ref, out_ref):
-    part = out_ref.shape[1] // in_ref.shape[0]
-    for source in range(in_ref.shape[0]):
+def assemble(gate_at, in_ref, out_ref):
+    sources = in_ref.shape[0]
+    part = (out_ref.shape[1] - BLK) // sources
+    gate = jnp.zeros((1, LANES), jnp.float32)
+    for source in range(sources):
         rows = slice(source * part, (source + 1) * part)
         out_ref[0, rows, :] = in_ref[source, :part, :]
         out_ref[1, rows, :] = in_ref[source, part : 2 * part, :]
+        block = gate_at // BLK * BLK
+        extra = in_ref[source, block : block + BLK, :].astype(jnp.float32)
+        gate = gate + extra[gate_at - block : gate_at - block + 1]
+    first = gate.astype(jnp.bfloat16).astype(jnp.float32)
+    second = (gate - first).astype(jnp.bfloat16).astype(jnp.float32)
+    third = gate - first - second
+    row = lax.broadcasted_iota(jnp.int32, (BLK, LANES), 0)
+    split = jnp.where(row == 0, first, jnp.where(row == 1, second, jnp.where(row == 2, third, 0.0)))
+    out_ref[0, sources * part :, :] = split.astype(jnp.bfloat16)
+    out_ref[1, sources * part :, :] = jnp.zeros((BLK, LANES), jnp.bfloat16)
 
 
 def attend(begin, count, q_at, ext_at, qblocks, width, tile, final, own_ref, mate_ref, q_ref, ext_ref, *refs):
     if final:
-        before_ref, out_ref, mark, minus, qx, dx, scores, high, total, acc, stage, sems = refs
-        early_copy = pltpu.make_async_copy(before_ref, out_ref.at[:, :begin, :], sems.at[0])
-        early_copy.start()
+        outs, (mark, minus, qx, dx, scores, high, total, acc) = refs[:FAN], refs[FAN:]
     else:
-        out_ref, gate_ref, mark, minus, qx, dx, scores, high, total, acc = refs
+        outs, (gate_ref, mark, minus, qx, dx, scores, high, total, acc) = refs[:FAN], refs[FAN:]
     sources = q_ref.shape[0]
     units = qx.shape[1] // LANES - 1
     sides = (own_ref, mate_ref)
-    steps_side = own_ref.shape[1] // width
     rows_unit = mark.shape[0]
+    stride = rows_unit + BLK
+    steps_unit = rows_unit // width
     scale = 1.0 / math.sqrt(LANES)
     exponent = scale * math.log2(math.e)
     chunks = units // 2
@@ -180,7 +196,6 @@
     for block in range(width // LANES):
         minus[block * LANES : (block + 1) * LANES, :] = jnp.where(wide_lane == 0, -1.0, 0.0).astype(jnp.bfloat16)
 
-    gate_sum = jnp.zeros((1, LANES), jnp.float32)
     for source in range(sources):
         base = source * count
         qx[base : base + count, :LANES] = q_ref[source, q_at : q_at + count, :]
@@ -197,12 +212,15 @@
                     at = chunk * qblocks + begin // BLK + block
                     row = jnp.broadcast_to(bias[at : at + 1], (BLK, LANES)).astype(jnp.bfloat16)
                     qx[base + block * BLK : base + (block + 1) * BLK, lanes : lanes + LANES] = row
-        if not final:
-            gate_sum = gate_sum + extra[bias_rows + 1 : bias_rows + 2]
         wide = jnp.broadcast_to(extra[bias_rows : bias_rows + 1], (LANES, LANES)).T
         wide = jnp.where(wide_lane == 0, wide, 0.0).astype(jnp.bfloat16)
         dx[base : base + count, LANES:] = wide[begin : begin + count]
     if not final:
+        gate_sum = jnp.zeros((1, LANES), jnp.float32)
+        for ref in sides:
+            for unit in range(units // 2):
+                at = unit * stride + rows_unit
+                gate_sum = gate_sum + jnp.sum(ref[0, at : at + BLK, :].astype(jnp.float32), 0, keepdims=True)
         gate_ref[...] = jnp.broadcast_to(gate_sum, gate_ref.shape)
 
     def one_tile(index, carry):
@@ -212,7 +230,7 @@
             for unit in range(units // 2):
 
                 def score(at, carry, side=side, ref=ref, unit=unit):
-                    rows = pl.ds(pl.multiple_of(unit * rows_unit + at * width, width), width)
+                    rows = pl.ds(unit * stride + pl.multiple_of(at * width, width), width)
                     marks = pl.ds(pl.multiple_of(at * width, width), width)
                     lanes = (1 + side * (units // 2) + unit) * LANES
                     left = jnp.concatenate([qx[here, :LANES], qx[here, lanes : lanes + LANES]], axis=1)
@@ -220,60 +238,73 @@
                     got = lax.dot_general(
                         left, right, (((1,), (1,)), ((), ())), preferred_element_type=jnp.float32
                     )
-                    scores[side * steps_side + unit * (rows_unit // width) + at] = got
+                    scores[(side * (units // 2) + unit) * steps_unit + at] = got
                     best = high[...]
                     for column in range(width // LANES):
                         best = jnp.maximum(best, got[:, column * LANES : (column + 1) * LANES])
                     high[...] = best
                     return carry
 
-                lax.fori_loop(0, rows_unit // width, score, 0, unroll=2)
+                lax.fori_loop(0, steps_unit, score, 0, unroll=2)
         high[...] = jnp.broadcast_to(jnp.max(high[...], 1, keepdims=True) * exponent, high.shape)
         total[...] = jnp.zeros_like(total)
         acc[...] = jnp.zeros_like(acc)
         for side, ref in enumerate(sides):
-
-            def back(at, carry, side=side, ref=ref):
-                rows = pl.ds(pl.multiple_of(at * width, width), width)
-                prod = lax.dot_general(
-                    dx[here, :],
-                    jnp.concatenate([ref[1, rows, :], minus[...]], axis=1),
-                    (((1,), (1,)), ((), ())),
-                    preferred_element_type=jnp.float32,
-                )
-                got = scores[side * steps_side + at]
-                level = high[...]
-                added = total[...]
-                pieces = []
-                for column in range(width // LANES):
-                    cols = slice(column * LANES, (column + 1) * LANES)
-                    expo = jnp.exp2(got[:, cols] * exponent - level)
-                    added = added + expo
-                    pieces.append((expo * prod[:, cols]).astype(jnp.bfloat16))
-                total[...] = added
-                acc[...] += jnp.dot(
-                    jnp.concatenate(pieces, axis=1), ref[0, rows, :], preferred_element_type=jnp.float32
-                )
-                return carry
-
-            lax.fori_loop(0, steps_side, back, 0, unroll=2)
+            for unit in range(units // 2):
+
+                def back(at, carry, side=side, ref=ref, unit=unit):
+                    rows = pl.ds(unit * stride + pl.multiple_of(at * width, width), width)
+                    prod = lax.dot_general(
+                        dx[here, :],
+                        jnp.concatenate([ref[1, rows, :], minus[...]], axis=1),
+                        (((1,), (1,)), ((), ())),
+                        preferred_element_type=jnp.float32,
+                    )
+                    got = scores[(side * (units // 2) + unit) * steps_unit + at]
+                    level = high[...]
+                    added = total[...]
+                    pieces = []
+                    for column in range(width // LANES):
+                        cols = slice(column * LANES, (column + 1) * LANES)
+                        expo = jnp.exp2(got[:, cols] * exponent - level)
+                        added = added + expo
+                        pieces.append((expo * prod[:, cols]).astype(jnp.bfloat16))
+                    total[...] = added
+                    acc[...] += jnp.dot(
+                        jnp.concatenate(pieces, axis=1), ref[0, rows, :], preferred_element_type=jnp.float32
+                    )
+                    return carry
+
+                lax.fori_loop(0, steps_unit, back, 0, unroll=2)
         weight = scale / jnp.sum(total[...], 1, keepdims=True)
         qx[here, :LANES] = (acc[...] * weight).astype(jnp.bfloat16)
         return carry
 
     lax.fori_loop(0, qx.shape[0] // tile, one_tile, 0)
-    for source in range(sources):
-        (stage if final else out_ref)[source] = qx[source * count : (source + 1) * count, :LANES]
-    if final:
-        late_copy = pltpu.make_async_copy(stage, out_ref.at[:, begin:, :], sems.at[1])
-        late_copy.start()
-        early_copy.wait()
-        late_copy.wait()
-
-
-def unpack(in_ref, out_ref):
-    for head in range(in_ref.shape[0]):
-        out_ref[:, head * LANES : (head + 1) * LANES] = in_ref[head]
+    upper = position_here(sources) // FAN
+    for step, out in enumerate(outs):
+        for lower in range(FAN):
+            at = ((upper ^ step) * FAN + lower) * count
+            out[lower] = qx[pl.ds(pl.multiple_of(at, BLK), count), :LANES]
+
+
+def turn(*refs):
+    early, late, outs = refs[:FAN], refs[FAN : 2 * FAN], refs[2 * FAN :]
+    begin = early[0].shape[1]
+    lower = position_here(FAN * FAN) % FAN
+    for step in range(FAN):
+        for other in range(FAN):
+            outs[other][step, :begin, :] = early[step][lower ^ other]
+            outs[other][step, begin:, :] = late[step][lower ^ other]
+
+
+def unpack(*refs):
+    out_ref = refs[-1]
+    here = position_here(FAN * FAN)
+    for other, ref in enumerate(refs[:-1]):
+        for step in range(FAN):
+            head = here ^ (step * FAN + other)
+            out_ref[:, pl.ds(pl.multiple_of(head * LANES, LANES), LANES)] = ref[step]
 
 
 def local(queries, d_out, o_mem, local_out, mem_keys, mem_values, gate_logit, block_ids):
@@ -287,7 +318,7 @@
     members = heads
     chunks = shards // heads
     assert width == heads * LANES and shards % heads == 0 and groups % 2 == 0
-    assert rows_dev == 16 * BLK and heads * 8 == LANES and tokens == LANES
+    assert heads == FAN * FAN and rows_dev == 16 * BLK and heads * 8 == LANES and tokens == LANES
     half_shard = rows_dev // 2
     units = 2 * chunks
     early = 5 * tokens // 8
@@ -334,8 +365,8 @@
     first_in = exchange(first_out)
     second_in = exchange(second_out)
     own = pl.pallas_call(
-        assemble,
-        out_shape=jax.ShapeDtypeStruct((2, members * half_shard, LANES), bf16),
+        functools.partial(assemble, ext_at + chunks * qblocks + 1),
+        out_shape=jax.ShapeDtypeStruct((2, members * half_shard + BLK, LANES), bf16),
         in_specs=[vmem],
         out_specs=vmem,
         compiler_params=small,
@@ -346,7 +377,7 @@
         own = lax.all_gather(own, "mem", axis_index_groups=same, axis=1, tiled=True)
     mate = lax.ppermute(own, "mem", [(i, i ^ 1) for i in range(shards)])
 
-    rows_all = 2 * own.shape[1]
+    rows_all = rows_dev * shards
     step_width = 512
 
     def attend_some(begin, count, q_at, final, out_shape, out_specs, *args):
@@ -365,8 +396,7 @@
                 pltpu.VMEM((tile, LANES), jnp.float32),
                 pltpu.VMEM((tile, LANES), jnp.float32),
                 pltpu.VMEM((tile, LANES), jnp.float32),
-            ]
-            + [pltpu.VMEM((members, count, LANES), bf16), pltpu.SemaphoreType.DMA((2,))] * final,
+            ],
             compiler_params=pltpu.CompilerParams(vmem_limit_bytes=(40 if chunks == 1 else 44) << 20),
             cost_estimate=pl.CostEstimate(
                 flops=2 * members * count * rows_all * LANES * 5,
@@ -376,45 +406,66 @@
             name="attend",
         )(*args)
 
-    part, gate_sum = attend_some(
+    def swap(pieces, unit):
+        got = [pieces[0]]
+        for step in range(1, FAN):
+            pairs = []
+            for mem in range(shards):
+                for grp in range(groups):
+                    other = ((mem % heads) // 2 * 2 + grp % 2) ^ (step * unit)
+                    to_mem = mem - mem % heads + other // 2 * 2 + mem % 2
+                    pairs.append((mem * groups + grp, to_mem * groups + grp - grp % 2 + other % 2))
+            got.append(lax.ppermute(pieces[step], AXES, pairs))
+        return got
+
+    *early_parts, gate_sum = attend_some(
         0,
         early,
         2 * half_shard,
         False,
-        [jax.ShapeDtypeStruct((members, early, LANES), bf16), jax.ShapeDtypeStruct((8, LANES), jnp.float32)],
-        [vmem, vmem],
+        [jax.ShapeDtypeStruct((FAN, early, LANES), bf16)] * FAN + [jax.ShapeDtypeStruct((8, LANES), jnp.float32)],
+        [vmem] * (FAN + 1),
         own,
         mate,
         first_in,
         first_in,
     )
-    gate_mate = lax.ppermute(gate_sum, "mem", [(i, i ^ 1) for i in range(shards)])
-    grad = attend_some(
+    early_home = swap(early_parts, FAN)
+    second_in, gate_sum = lax.optimization_barrier((second_in, gate_sum))
+    late_parts = attend_some(
         early,
         late,
         0,
         True,
-        pltpu.HBM((members, tokens, LANES), bf16),
-        hbm,
+        [jax.ShapeDtypeStruct((FAN, late, LANES), bf16)] * FAN,
+        [vmem] * FAN,
         own,
         mate,
         second_in,
         first_in,
-        part,
-    )
-    home = exchange(grad)
+    )
+    early_home, late_parts = lax.optimization_barrier((early_home, late_parts))
+    late_home = swap(late_parts, FAN)
+    turned = pl.pallas_call(
+        turn,
+        out_shape=[jax.ShapeDtypeStruct((FAN, tokens, LANES), bf16)] * FAN,
+        in_specs=[vmem] * (2 * FAN),
+        out_specs=[vmem] * FAN,
+        compiler_params=small,
+        name="turn",
+    )(*early_home, *late_home)
     d_query = pl.pallas_call(
         unpack,
         out_shape=jax.ShapeDtypeStruct((tokens, width), bf16),
-        in_specs=[vmem],
+        in_specs=[vmem] * FAN,
         out_specs=vmem,
         compiler_params=small,
         name="unpack",
-    )(home)
-    addends = (gate_sum + gate_mate)[0, : 3 * heads]
+    )(*swap(turned, 1))
+    addends = gate_sum[0, : 3 * heads]
     gate_total = addends[:heads] + addends[heads : 2 * heads] + addends[2 * heads :]
     if chunks > 1 or groups > 2:
-        gate_total = lax.psum(gate_total, AXES) / (2 * members)
+        gate_total = lax.psum(gate_total, AXES) / (2 * shards)
     sig = jax.nn.sigmoid(gate_logit)
     d_gate = sig * (1.0 - sig) * gate_total / (shards * groups * tokens * LANES) ** 0.5
     return (d_query[None], d_gate)

time: 105 us -> 107 us (1.019)
  starting transfers between devices: 10.2 us -> 16.1 us
  waiting for transfers between devices: 15.2 us -> 10.5 us
    all_to_all x1 -> x0, waiting for transfers between devices: 13.6 us -> none  [local(): home = exchange(grad)]
    ppermute x1 -> x9, starting transfers between devices: 0.07 us -> 12.5 us  [swap(): got.append(lax.ppermute(pieces[step], AXES, pairs))]
    ppermute x1 -> x9, waiting for transfers between devices: 1.15 us -> 10.5 us  [swap(): got.append(lax.ppermute(pieces[step], AXES, pairs))]
    all_to_all x1 -> x0, starting transfers between devices: 6.48 us -> none  [local(): home = exchange(grad)]
  transfers between devices with their start and end apart: 4 -> 11, of which waited for: 3 -> 5; matrix products, arithmetic and copies ran while one was open for 1% -> 1% of each run, Pallas kernels for 12% -> 21%
where the time goes in v10:
time: 107 us; the launch traced here: 106 us
  blocking collectives  50.8 us (47%)
  Pallas kernels  27.5 us (26%)
  starting transfers between devices  16.1 us (15%)
  waiting for transfers between devices  10.5 us (10%)
    all_to_all x1, blocking collectives, local(): first_in = exchange(first_out)  50.8 us
    pallas_call x2, Pallas kernels, attend_some(): pl.pallas_call(functools.partial(attend, begin, count, q_at, ext_at, qblo...  22.2 us
    ppermute x9, starting transfers between devices, swap(): got.append(lax.ppermute(pieces[step], AXES, pairs))  12.5 us
    ppermute x9, waiting for transfers between devices, swap(): got.append(lax.ppermute(pieces[step], AXES, pairs))  10.5 us
    pallas_call x1, Pallas kernels, local(): pl.pallas_call(functools.partial(pack, heads, chunks, early), out_shape=(...  4.2 us
    all_to_all x1, starting transfers between devices, local(): second_in = exchange(second_out)  3.57 us
  transfers between devices with their start and end apart: 11, of which 5 were waited for; matrix products, arithmetic and copies ran while one was open for 1% of the time, Pallas kernels for 21%

profile of v10, /device:TPU:0, one launch (start us, length us, event | category | flops | bytes accessed | tf_op | source)
XLA Modules:
  0.0 106.2 jit_solution(15995850167741948226)
XLA Ops:
  0.6 4.2 %pack.1 = (bf16[16,432,128]{2,1,0:T(8,128)(2,1)}, bf16[16,96,128]{2,1,0:T(8,128)(2,1)}) custom-call(bf16[256,2048]{1,0:T(8,128)(2,1)} %k_hbm.1, bf16[256,2048]{1,0:T(8,128)(2,1)} %v_hbm.1, bf16[128,2048]{1,0:T(8,128)(2,1)} %bitcast.10, bf16[128,2048]{1,0:T(8,128)(2,1)} %bitcast.11, bf16[128,2048]{1,0:T(8,128)(2,1)} %bitcast.12, bf16[128,2048]{1,0:T(8,128)(2,1)} %bitcast.13, ...), custom_call_target="tpu_custom_call" | custom-call | tf_op jit(solution)/shard_map/pack/pallas_call | solution.py:346
  4.8 50.8 %all_to_all.10.in_ref.q_ref.ext_ref = bf16[16,432,128]{2,1,0:T(8,128)(2,1)S(1)} all-to-all(bf16[16,432,128]{2,1,0:T(8,128)(2,1)} %get-tuple-element.27), channel_id=1, replica_groups={{0,1,4,5,8,9,12,13,16,17,20,21,24,25,28,29},{2,3,6,7,10,11,14,15,18,19,..., dimensions={0} | all-to-all | bytes 3538944 | tf_op jit(solution)/shard_map/all_to_all | solution.py:365
  55.6 0.1 assemble.1.own_ref
  55.7 0.1 collective-permute-start
  55.8 3.6 %all-to-all-start.1 = ((bf16[16,96,128]{2,1,0:T(8,128)(2,1)}), bf16[16,96,128]{2,1,0:T(8,128)(2,1)S(1)}, u32[]{:S(2)}, u32[]{:S(2)}) async-start(bf16[16,96,128]{2,1,0:T(8,128)(2,1)} %get-tuple-element.32), calls=%async_computation.1 | async-start | bytes 786432 | tf_op jit(solution)/shard_map/all_to_all | solution.py:366
  59.4 0.0 collective-permute-done.mate_ref
  59.4 13.0 %attend.2 = (bf16[4,80,128]{2,1,0:T(8,128)(2,1)S(1)}, bf16[4,80,128]{2,1,0:T(8,128)(2,1)S(1)}, bf16[4,80,128]{2,1,0:T(8,128)(2,1)S(1)}, bf16[4,80,128]{2,1,0:T(8,128)(2,1)S(1)}, f32[8,128]{1,0:T(8,128)S(1)}) custom-call(bf16[2,2064,128]{2,1,0:T(8,128)(2,1)S(1)} %assemble.1.own_ref, bf16[2,2064,128]{2,1,0:T(8,128)(2,1)} %collective-permute-done.mate_ref, ...), custom_call_target="tpu_custom_call" | custom-call | flops 6710886400 | bytes 2097152 | tf_op jit(solution)/shard_map/attend/pallas_call | solution.py:385
  72.4 0.0 all-to-all-done.1.q_ref
  72.4 1.9 %collective-permute-start.1 = (bf16[4,80,128]{2,1,0:T(8,128)(2,1)S(1)}, bf16[4,80,128]{2,1,0:T(8,128)(2,1)S(1)}, u32[]{:S(2)}, u32[]{:S(2)}) collective-permute-start(bf16[4,80,128]{2,1,0:T(8,128)(2,1)S(1)} %get-tuple-element.29), channel_id=1, source_target_pairs={{0,8},{1,9},{2,10},{3,11},{4,12},{5,13},{6,14},{7,15},{8,0},{9,1},... | collective-permute-start | bytes 245768 | tf_op jit(solution)/shard_map/ppermute | solution.py:418
  74.3 2.4 %collective-permute-start.2 = (bf16[4,80,128]{2,1,0:T(8,128)(2,1)S(1)}, bf16[4,80,128]{2,1,0:T(8,128)(2,1)S(1)}, u32[]{:S(2)}, u32[]{:S(2)}) collective-permute-start(bf16[4,80,128]{2,1,0:T(8,128)(2,1)S(1)} %get-tuple-element.30), channel_id=1, source_target_pairs={{0,16},{1,17},{2,18},{3,19},{4,20},{5,21},{6,22},{7,23},{8,24},{9,... | collective-permute-start | bytes 245768 | tf_op jit(solution)/shard_map/ppermute | solution.py:418
  76.7 0.0 copy-start
  76.7 0.1 collective-permute-start.3
  76.9 9.2 %attend.3 = (bf16[4,48,128]{2,1,0:T(8,128)(2,1)S(1)}, bf16[4,48,128]{2,1,0:T(8,128)(2,1)S(1)}, bf16[4,48,128]{2,1,0:T(8,128)(2,1)S(1)}, bf16[4,48,128]{2,1,0:T(8,128)(2,1)S(1)}) custom-call(bf16[2,2064,128]{2,1,0:T(8,128)(2,1)S(1)} %assemble.1.own_ref, bf16[2,2064,128]{2,1,0:T(8,128)(2,1)} %collective-permute-done.mate_ref, ...), custom_call_target="tpu_custom_call" | custom-call | flops 4026531840 | bytes 2097152 | tf_op jit(solution)/shard_map/attend/pallas_call | solution.py:385
  86.1 0.0 collective-permute-done.1.refs_1_
  86.1 0.0 collective-permute-done.2.refs_2_
  86.1 0.0 collective-permute-done.3.refs_3_
  86.1 1.0 collective-permute-start.4
  87.1 3.3 %collective-permute-start.5 = (bf16[4,48,128]{2,1,0:T(8,128)(2,1)S(1)}, bf16[4,48,128]{2,1,0:T(8,128)(2,1)S(1)}, u32[]{:S(2)}, u32[]{:S(2)}) collective-permute-start(bf16[4,48,128]{2,1,0:T(8,128)(2,1)S(1)} %get-tuple-element.45), channel_id=1, source_target_pairs={{0,16},{1,17},{2,18},{3,19},{4,20},{5,21},{6,22},{7,23},{8,24},{9,... | collective-permute-start | bytes 147464 | tf_op jit(solution)/shard_map/ppermute | solution.py:418
  90.4 0.1 collective-permute-start.6
  90.6 0.0 collective-permute-done.4.refs_5_
  90.6 2.6 %collective-permute-done.5.refs_6_ = bf16[4,48,128]{2,1,0:T(8,128)(2,1)S(1)} collective-permute-done((bf16[4,48,128]{2,1,0:T(8,128)(2,1)S(1)}, bf16[4,48,128]{2,1,0:T(8,128)(2,1)S(1)}, u32[]{:S(2)}, u32[]{:S(2)}) %collective-permute-start.5) | collective-permute-done | bytes 49184 | tf_op jit(solution)/shard_map/ppermute | solution.py:418
  93.2 3.1 %collective-permute-done.6.refs_7_ = bf16[4,48,128]{2,1,0:T(8,128)(2,1)S(1)} collective-permute-done((bf16[4,48,128]{2,1,0:T(8,128)(2,1)S(1)}, bf16[4,48,128]{2,1,0:T(8,128)(2,1)S(1)}, u32[]{:S(2)}, u32[]{:S(2)}) %collective-permute-start.6) | collective-permute-done | bytes 49184 | tf_op jit(solution)/shard_map/ppermute | solution.py:418
  96.4 1.5 %collective-permute-start.7 = (bf16[4,128,128]{2,1,0:T(8,128)(2,1)S(1)}, bf16[4,128,128]{2,1,0:T(8,128)(2,1)S(1)}, u32[]{:S(2)}, u32[]{:S(2)}) collective-permute-start(bf16[4,128,128]{2,1,0:T(8,128)(2,1)S(1)} %get-tuple-element.48), channel_id=1, source_target_pairs={{0,1},{1,0},{2,3},{3,2},{4,5},{5,4},{6,7},{7,6},{8,9},{9,8},{10,11... | collective-permute-start | bytes 393224 | tf_op jit(solution)/shard_map/ppermute | solution.py:418
  97.9 1.5 %collective-permute-start.8 = (bf16[4,128,128]{2,1,0:T(8,128)(2,1)S(1)}, bf16[4,128,128]{2,1,0:T(8,128)(2,1)S(1)}, u32[]{:S(2)}, u32[]{:S(2)}) collective-permute-start(bf16[4,128,128]{2,1,0:T(8,128)(2,1)S(1)} %get-tuple-element.49), channel_id=1, source_target_pairs={{0,4},{1,5},{2,6},{3,7},{4,0},{5,1},{6,2},{7,3},{8,12},{9,13},{10,... | collective-permute-start | bytes 393224 | tf_op jit(solution)/shard_map/ppermute | solution.py:418
  99.4 0.6 collective-permute-start.9
  99.9 0.0 copy-done
  99.9 0.6 fusion.1
  100.5 2.3 %collective-permute-done.7.refs_1_ = bf16[4,128,128]{2,1,0:T(8,128)(2,1)S(1)} collective-permute-done((bf16[4,128,128]{2,1,0:T(8,128)(2,1)S(1)}, bf16[4,128,128]{2,1,0:T(8,128)(2,1)S(1)}, u32[]{:S(2)}, u32[]{:S(2)}) %collective-permute-start.7) | collective-permute-done | bytes 131104 | tf_op jit(solution)/shard_map/ppermute | solution.py:418
  102.8 0.1 collective-permute-done.8.refs_2_
  102.9 2.4 %collective-permute-done.9.refs_3_ = bf16[4,128,128]{2,1,0:T(8,128)(2,1)S(1)} collective-permute-done((bf16[4,128,128]{2,1,0:T(8,128)(2,1)S(1)}, bf16[4,128,128]{2,1,0:T(8,128)(2,1)S(1)}, u32[]{:S(2)}, u32[]{:S(2)}) %collective-permute-start.9) | collective-permute-done | bytes 131104 | tf_op jit(solution)/shard_map/ppermute | solution.py:418
  105.2 0.9 unpack.1
  (1 shorter events, 0.0 us)
Async XLA Ops:
  55.7 3.7 %collective-permute-start = (bf16[2,2064,128]{2,1,0:T(8,128)(2,1)S(1)}, bf16[2,2064,128]{2,1,0:T(8,128)(2,1)}, u32[]{:S(2)}, u32[]{:S(2)}) collective-permute-start(bf16[2,2064,128]{2,1,0:T(8,128)(2,1)S(1)} %assemble.1.own_ref), channel_id=1, source_target_pairs={{0,2},{2,0},{4,6},{6,4},{8,10},{10,8},{12,14},{14,12},{16,18},{18,... | collective-permute-start | bytes 3170312 | tf_op jit(solution)/shard_map/ppermute | solution.py:378
  55.8 16.6 %all-to-all-start.1 = ((bf16[16,96,128]{2,1,0:T(8,128)(2,1)}), bf16[16,96,128]{2,1,0:T(8,128)(2,1)S(1)}, u32[]{:S(2)}, u32[]{:S(2)}) async-start(bf16[16,96,128]{2,1,0:T(8,128)(2,1)} %get-tuple-element.32), calls=%async_computation.1 | async-start | bytes 786432 | tf_op jit(solution)/shard_map/all_to_all | solution.py:366
  72.4 13.7 %collective-permute-start.1 = (bf16[4,80,128]{2,1,0:T(8,128)(2,1)S(1)}, bf16[4,80,128]{2,1,0:T(8,128)(2,1)S(1)}, u32[]{:S(2)}, u32[]{:S(2)}) collective-permute-start(bf16[4,80,128]{2,1,0:T(8,128)(2,1)S(1)} %get-tuple-element.29), channel_id=1, source_target_pairs={{0,8},{1,9},{2,10},{3,11},{4,12},{5,13},{6,14},{7,15},{8,0},{9,1},... | collective-permute-start | bytes 245768 | tf_op jit(solution)/shard_map/ppermute | solution.py:418
  74.3 11.8 %collective-permute-start.2 = (bf16[4,80,128]{2,1,0:T(8,128)(2,1)S(1)}, bf16[4,80,128]{2,1,0:T(8,128)(2,1)S(1)}, u32[]{:S(2)}, u32[]{:S(2)}) collective-permute-start(bf16[4,80,128]{2,1,0:T(8,128)(2,1)S(1)} %get-tuple-element.30), channel_id=1, source_target_pairs={{0,16},{1,17},{2,18},{3,19},{4,20},{5,21},{6,22},{7,23},{8,24},{9,... | collective-permute-start | bytes 245768 | tf_op jit(solution)/shard_map/ppermute | solution.py:418
  76.7 23.2 %copy-start = (f32[16]{0:T(128)S(1)}, f32[16]{0:T(128)}, u32[]{:S(2)}) copy-start(f32[16]{0:T(128)} %gate_ref.1) | copy-start | bytes 196
  76.7 9.4 %collective-permute-start.3 = (bf16[4,80,128]{2,1,0:T(8,128)(2,1)S(1)}, bf16[4,80,128]{2,1,0:T(8,128)(2,1)S(1)}, u32[]{:S(2)}, u32[]{:S(2)}) collective-permute-start(bf16[4,80,128]{2,1,0:T(8,128)(2,1)S(1)} %get-tuple-element.31), channel_id=1, source_target_pairs={{0,24},{1,25},{2,26},{3,27},{4,28},{5,29},{6,30},{7,31},{8,16},{9,... | collective-permute-start | bytes 245768 | tf_op jit(solution)/shard_map/ppermute | solution.py:418
  86.1 4.5 %collective-permute-start.4 = (bf16[4,48,128]{2,1,0:T(8,128)(2,1)S(1)}, bf16[4,48,128]{2,1,0:T(8,128)(2,1)S(1)}, u32[]{:S(2)}, u32[]{:S(2)}) collective-permute-start(bf16[4,48,128]{2,1,0:T(8,128)(2,1)S(1)} %get-tuple-element.44), channel_id=1, source_target_pairs={{0,8},{1,9},{2,10},{3,11},{4,12},{5,13},{6,14},{7,15},{8,0},{9,1},... | collective-permute-start | bytes 147464 | tf_op jit(solution)/shard_map/ppermute | solution.py:418
  87.1 6.1 %collective-permute-start.5 = (bf16[4,48,128]{2,1,0:T(8,128)(2,1)S(1)}, bf16[4,48,128]{2,1,0:T(8,128)(2,1)S(1)}, u32[]{:S(2)}, u32[]{:S(2)}) collective-permute-start(bf16[4,48,128]{2,1,0:T(8,128)(2,1)S(1)} %get-tuple-element.45), channel_id=1, source_target_pairs={{0,16},{1,17},{2,18},{3,19},{4,20},{5,21},{6,22},{7,23},{8,24},{9,... | collective-permute-start | bytes 147464 | tf_op jit(solution)/shard_map/ppermute | solution.py:418
  90.4 5.9 %collective-permute-start.6 = (bf16[4,48,128]{2,1,0:T(8,128)(2,1)S(1)}, bf16[4,48,128]{2,1,0:T(8,128)(2,1)S(1)}, u32[]{:S(2)}, u32[]{:S(2)}) collective-permute-start(bf16[4,48,128]{2,1,0:T(8,128)(2,1)S(1)} %get-tuple-element.46), channel_id=1, source_target_pairs={{0,24},{1,25},{2,26},{3,27},{4,28},{5,29},{6,30},{7,31},{8,16},{9,... | collective-permute-start | bytes 147464 | tf_op jit(solution)/shard_map/ppermute | solution.py:418
  96.4 6.4 %collective-permute-start.7 = (bf16[4,128,128]{2,1,0:T(8,128)(2,1)S(1)}, bf16[4,128,128]{2,1,0:T(8,128)(2,1)S(1)}, u32[]{:S(2)}, u32[]{:S(2)}) collective-permute-start(bf16[4,128,128]{2,1,0:T(8,128)(2,1)S(1)} %get-tuple-element.48), channel_id=1, source_target_pairs={{0,1},{1,0},{2,3},{3,2},{4,5},{5,4},{6,7},{7,6},{8,9},{9,8},{10,11... | collective-permute-start | bytes 393224 | tf_op jit(solution)/shard_map/ppermute | solution.py:418
  97.9 5.0 %collective-permute-start.8 = (bf16[4,128,128]{2,1,0:T(8,128)(2,1)S(1)}, bf16[4,128,128]{2,1,0:T(8,128)(2,1)S(1)}, u32[]{:S(2)}, u32[]{:S(2)}) collective-permute-start(bf16[4,128,128]{2,1,0:T(8,128)(2,1)S(1)} %get-tuple-element.49), channel_id=1, source_target_pairs={{0,4},{1,5},{2,6},{3,7},{4,0},{5,1},{6,2},{7,3},{8,12},{9,13},{10,... | collective-permute-start | bytes 393224 | tf_op jit(solution)/shard_map/ppermute | solution.py:418
  99.4 5.9 %collective-permute-start.9 = (bf16[4,128,128]{2,1,0:T(8,128)(2,1)S(1)}, bf16[4,128,128]{2,1,0:T(8,128)(2,1)S(1)}, u32[]{:S(2)}, u32[]{:S(2)}) collective-permute-start(bf16[4,128,128]{2,1,0:T(8,128)(2,1)S(1)} %get-tuple-element.50), channel_id=1, source_target_pairs={{0,5},{1,4},{2,7},{3,6},{4,1},{5,0},{6,3},{7,2},{8,13},{9,12},{10,... | collective-permute-start | bytes 393224 | tf_op jit(solution)/shard_map/ppermute | solution.py:418

commit v11 on v8

--- a/solution.py
+++ b/solution.py
@@ -89,17 +89,15 @@
     at = 2 * half_shard
     late = tokens - early
     sent = []
-    for head in range(heads):
-        if head % bunch == 0:
-            for copy in copies[head // bunch]:
-                copy.wait()
-        cols = slice(head * LANES, (head + 1) * LANES)
+
+    def one_head(head, carry):
+        cols = pl.ds(pl.multiple_of(head * LANES, LANES), LANES)
         sig = jax.nn.sigmoid(jnp.full((8, LANES), gate_ref[head], jnp.float32))[:1]
         d_out = dout_ref[:, cols].astype(jnp.float32)
         o_mem = omem_ref[:, cols].astype(jnp.float32)
         d_mem = (d_out * sig).astype(jnp.bfloat16)
         differ = o_mem - local_ref[:, cols].astype(jnp.float32)
-        gate_rows[head : head + 1, :] = jnp.sum(d_out * differ, 0, keepdims=True)
+        gate_rows[pl.ds(head, 1), :] = jnp.sum(d_out * differ, 0, keepdims=True)
         product = d_mem.astype(jnp.float32) * o_mem
         upper = product.astype(jnp.bfloat16)
         lower = (product - upper.astype(jnp.float32)).astype(jnp.bfloat16)
@@ -109,22 +107,27 @@
             (((1,), (1,)), ((), ())),
             preferred_element_type=jnp.float32,
         )
-        delta_ref[head : head + 1, :] = row[:1]
+        delta_ref[pl.ds(head, 1), :] = row[:1]
         first_out[head, :half_shard, :] = k_ref[:, cols]
         first_out[head, half_shard:at, :] = v_ref[:, cols]
         first_out[head, at : at + early, :] = q_ref[:early, cols]
         first_out[head, at + early : at + 2 * early, :] = d_mem[:early]
         second_out[head, :late, :] = q_ref[early:, cols]
         second_out[head, late:, :] = d_mem[early:]
-        if head % bunch == bunch - 1:
-            some = slice(head + 1 - bunch, head + 1)
-            body = slice(0, at + 2 * early)
-            for index, (source, target) in enumerate(
-                ((first_out.at[some, body], first_hbm.at[some, body]), (second_out.at[some], second_hbm.at[some]))
-            ):
-                copy = pltpu.make_async_copy(source, target, out_sems.at[index, head // bunch])
-                copy.start()
-                sent.append(copy)
+        return carry
+
+    for index in range(bunches):
+        for copy in copies[index]:
+            copy.wait()
+        lax.fori_loop(index * bunch, (index + 1) * bunch, one_head, 0)
+        some = slice(index * bunch, (index + 1) * bunch)
+        body = slice(0, at + 2 * early)
+        for which, (source, target) in enumerate(
+            ((first_out.at[some, body], first_hbm.at[some, body]), (second_out.at[some], second_hbm.at[some]))
+        ):
+            copy = pltpu.make_async_copy(source, target, out_sems.at[which, index])
+            copy.start()
+            sent.append(copy)
     total = lax.dot_general(
         ones,
         gate_rows[...],
@@ -174,17 +177,23 @@
     bias_rows = chunks * qblocks
 
     lane = lax.broadcasted_iota(jnp.int32, (BLK, LANES), 1)
-    for block in range(LANES):
-        mark[block * BLK : (block + 1) * BLK, :] = jnp.where(lane == block, 1.0, 0.0).astype(jnp.bfloat16)
+
+    def note(block, carry):
+        at = pl.ds(pl.multiple_of(block * BLK, BLK), BLK)
+        mark[at, :] = jnp.where(lane == block, 1.0, 0.0).astype(jnp.bfloat16)
+        return carry
+
+    lax.fori_loop(0, LANES, note, 0, unroll=8)
     wide_lane = lax.broadcasted_iota(jnp.int32, (LANES, LANES), 1)
     for block in range(width // LANES):
         minus[block * LANES : (block + 1) * LANES, :] = jnp.where(wide_lane == 0, -1.0, 0.0).astype(jnp.bfloat16)
 
-    gate_sum = jnp.zeros((1, LANES), jnp.float32)
-    for source in range(sources):
-        base = source * count
-        qx[base : base + count, :LANES] = q_ref[source, q_at : q_at + count, :]
-        dx[base : base + count, :LANES] = q_ref[source, q_at + count : q_at + 2 * count, :]
+
+    def take(source, gate_sum):
+        base = pl.multiple_of(source * count, BLK)
+        mine = pl.ds(base, count)
+        qx[mine, :LANES] = q_ref[source, q_at : q_at + count, :]
+        dx[mine, :LANES] = q_ref[source, q_at + count : q_at + 2 * count, :]
         extra = ext_ref[source, ext_at:, :].astype(jnp.float32)
         code = extra[:bias_rows]
         second = jnp.where(code > 1.5, 1.0, 0.0)
@@ -196,12 +205,13 @@
                 for block in range(count // BLK):
                     at = chunk * qblocks + begin // BLK + block
                     row = jnp.broadcast_to(bias[at : at + 1], (BLK, LANES)).astype(jnp.bfloat16)
-                    qx[base + block * BLK : base + (block + 1) * BLK, lanes : lanes + LANES] = row
-        if not final:
-            gate_sum = gate_sum + extra[bias_rows + 1 : bias_rows + 2]
+                    qx[pl.ds(base + block * BLK, BLK), lanes : lanes + LANES] = row
         wide = jnp.broadcast_to(extra[bias_rows : bias_rows + 1], (LANES, LANES)).T
         wide = jnp.where(wide_lane == 0, wide, 0.0).astype(jnp.bfloat16)
-        dx[base : base + count, LANES:] = wide[begin : begin + count]
+        dx[mine, LANES:] = wide[begin : begin + count]
+        return gate_sum + extra[bias_rows + 1 : bias_rows + 2]
+
+    gate_sum = lax.fori_loop(0, sources, take, jnp.zeros((1, LANES), jnp.float32))
     if not final:
         gate_ref[...] = jnp.broadcast_to(gate_sum, gate_ref.shape)
 
@@ -227,7 +237,7 @@
                     high[...] = best
                     return carry
 
-                lax.fori_loop(0, rows_unit // width, score, 0, unroll=2)
+                lax.fori_loop(0, rows_unit // width, score, 0)
         high[...] = jnp.broadcast_to(jnp.max(high[...], 1, keepdims=True) * exponent, high.shape)
         total[...] = jnp.zeros_like(total)
         acc[...] = jnp.zeros_like(acc)
@@ -256,14 +266,19 @@
                 )
                 return carry
 
-            lax.fori_loop(0, steps_side, back, 0, unroll=2)
+            lax.fori_loop(0, steps_side, back, 0)
         weight = scale / jnp.sum(total[...], 1, keepdims=True)
         qx[here, :LANES] = (acc[...] * weight).astype(jnp.bfloat16)
         return carry
 
     lax.fori_loop(0, qx.shape[0] // tile, one_tile, 0)
-    for source in range(sources):
-        (stage if final else out_ref)[source] = qx[source * count : (source + 1) * count, :LANES]
+
+    def give(source, carry):
+        at = pl.ds(pl.multiple_of(source * count, BLK), count)
+        (stage if final else out_ref)[source] = qx[at, :LANES]
+        return carry
+
+    lax.fori_loop(0, sources, give, 0)
     if final:
         late_copy = pltpu.make_async_copy(stage, out_ref.at[:, begin:, :], sems.at[1])
         late_copy.start()

time: 105 us -> 113 us (1.076)
  Pallas kernels: 27.1 us -> 35.2 us
    pallas_call x2, Pallas kernels: 21.9 us -> 28.1 us  [attend_some(): pl.pallas_call(functools.partial(attend, begin, count, q_at, ext_at, qblo...]
    pallas_call x1, Pallas kernels: 4.2 us -> 6.15 us  [local(): pl.pallas_call(functools.partial(pack, heads, chunks, early), out_shape=(...]
  transfers between devices with their start and end apart: 4 -> 4, of which waited for: 3 -> 2; matrix products, arithmetic and copies ran while one was open for 1% -> 1% of each run, Pallas kernels for 12% -> 14%
where the time goes in v11:
time: 113 us
  blocking collectives  50.8 us (45%)
  Pallas kernels  35.2 us (31%)
  waiting for transfers between devices  14.8 us (13%)
  starting transfers between devices  10.6 us (9%)
    all_to_all x1, blocking collectives, local(): first_in = exchange(first_out)  50.8 us
    pallas_call x2, Pallas kernels, attend_some(): pl.pallas_call(functools.partial(attend, begin, count, q_at, ext_at, qblo...  28.1 us
    all_to_all x1, waiting for transfers between devices, local(): home = exchange(grad)  13.6 us
    all_to_all x1, starting transfers between devices, local(): home = exchange(grad)  6.89 us
    pallas_call x1, Pallas kernels, local(): pl.pallas_call(functools.partial(pack, heads, chunks, early), out_shape=(...  6.15 us
    all_to_all x1, starting transfers between devices, local(): second_in = exchange(second_out)  3.57 us
  transfers between devices with their start and end apart: 4, of which 2 were waited for; matrix products, arithmetic and copies ran while one was open for 1% of the time, Pallas kernels for 14%

profile of v11, /device:TPU:0, one launch (start us, length us, event | category | flops | bytes accessed | tf_op | source)
XLA Modules:
  0.0 112.7 jit_solution(16520237734185654127)
XLA Ops:
  0.6 6.2 %pack.1 = (bf16[16,432,128]{2,1,0:T(8,128)(2,1)}, bf16[16,96,128]{2,1,0:T(8,128)(2,1)}) custom-call(bf16[256,2048]{1,0:T(8,128)(2,1)} %k_hbm.1, bf16[256,2048]{1,0:T(8,128)(2,1)} %v_hbm.1, bf16[128,2048]{1,0:T(8,128)(2,1)} %bitcast.10, bf16[128,2048]{1,0:T(8,128)(2,1)} %bitcast.11, bf16[128,2048]{1,0:T(8,128)(2,1)} %bitcast.12, bf16[128,2048]{1,0:T(8,128)(2,1)} %bitcast.13, ...), custom_call_target="tpu_custom_call" | custom-call | tf_op jit(solution)/shard_map/pack/pallas_call | solution.py:330
  6.8 50.8 %all_to_all.15.in_ref.q_ref.ext_ref = bf16[16,432,128]{2,1,0:T(8,128)(2,1)S(1)} all-to-all(bf16[16,432,128]{2,1,0:T(8,128)(2,1)} %get-tuple-element.6), channel_id=1, replica_groups={{0,1,4,5,8,9,12,13,16,17,20,21,24,25,28,29},{2,3,6,7,10,11,14,15,18,19,..., dimensions={0} | all-to-all | bytes 3538944 | tf_op jit(solution)/shard_map/all_to_all | solution.py:349
  57.6 0.1 assemble.1.own_ref
  57.7 0.1 collective-permute-start
  57.7 3.6 %all-to-all-start.1 = ((bf16[16,96,128]{2,1,0:T(8,128)(2,1)}), bf16[16,96,128]{2,1,0:T(8,128)(2,1)S(1)}, u32[]{:S(2)}, u32[]{:S(2)}) async-start(bf16[16,96,128]{2,1,0:T(8,128)(2,1)} %get-tuple-element.7), calls=%async_computation.1 | async-start | bytes 786432 | tf_op jit(solution)/shard_map/all_to_all | solution.py:350
  61.3 0.0 collective-permute-done.mate_ref
  61.3 15.5 %attend.2 = (bf16[16,80,128]{2,1,0:T(8,128)(2,1)S(1)}, f32[8,128]{1,0:T(8,128)S(1)}) custom-call(bf16[2,2048,128]{2,1,0:T(8,128)(2,1)S(1)} %assemble.1.own_ref, bf16[2,2048,128]{2,1,0:T(8,128)(2,1)} %collective-permute-done.mate_ref, bf16[16,432,128]{2,1,0:T(8,128)(2,1)S(1)} %all_to_all.15.in_ref.q_ref.ext_ref, ...), custom_call_target="tpu_custom_call" | custom-call | flops 6710886400 | bytes 2097152 | tf_op jit(solution)/shard_map/attend/pallas_call | solution.py:369
  76.8 0.0 all-to-all-done.1.q_ref
  76.8 0.0 copy-start
  76.8 12.6 %attend.3 = bf16[16,128,128]{2,1,0:T(8,128)(2,1)} custom-call(bf16[2,2048,128]{2,1,0:T(8,128)(2,1)S(1)} %assemble.1.own_ref, bf16[2,2048,128]{2,1,0:T(8,128)(2,1)} %collective-permute-done.mate_ref, bf16[16,96,128]{2,1,0:T(8,128)(2,1)S(1)} %all-to-all-done.1.q_ref, bf16[16,432,128]{2,1,0:T(8,128)(2,1)S(1)} %all_to_all.15.in_ref.q_ref.ext_ref, ...), custom_call_target="tpu_custom_call" | custom-call | flops 4026531840 | bytes 2097152 | tf_op jit(solution)/shard_map/attend/pallas_call | solution.py:369
  89.4 6.9 %all-to-all-start.2 = ((bf16[16,128,128]{2,1,0:T(8,128)(2,1)}), bf16[16,128,128]{2,1,0:T(8,128)(2,1)S(1)}, u32[]{:S(2)}, u32[]{:S(2)}) async-start(bf16[16,128,128]{2,1,0:T(8,128)(2,1)} %attend.3), calls=%async_computation.2 | async-start | bytes 1048576 | tf_op jit(solution)/shard_map/all_to_all | solution.py:420
  96.3 0.1 collective-permute-start.1
  96.4 1.2 %collective-permute-done.1 = f32[8,128]{1,0:T(8,128)S(1)} collective-permute-done((f32[8,128]{1,0:T(8,128)S(1)}, f32[8,128]{1,0:T(8,128)S(1)}, u32[]{:S(2)}, u32[]{:S(2)}) %collective-permute-start.1) | collective-permute-done | bytes 4128 | tf_op jit(solution)/shard_map/ppermute | solution.py:406
  97.6 0.0 copy-done
  97.6 0.6 fusion.1
  98.2 13.6 %all-to-all-done.2.in_ref = bf16[16,128,128]{2,1,0:T(8,128)(2,1)S(1)} async-done(((bf16[16,128,128]{2,1,0:T(8,128)(2,1)}), bf16[16,128,128]{2,1,0:T(8,128)(2,1)S(1)}, u32[]{:S(2)}, u32[]{:S(2)}) %all-to-all-start.2) | async-done | bytes 524320 | tf_op jit(solution)/shard_map/all_to_all | solution.py:420
  111.8 0.9 unpack.1
  (1 shorter events, 0.0 us)
Async XLA Ops:
  57.7 3.7 %collective-permute-start = (bf16[2,2048,128]{2,1,0:T(8,128)(2,1)S(1)}, bf16[2,2048,128]{2,1,0:T(8,128)(2,1)}, u32[]{:S(2)}, u32[]{:S(2)}) collective-permute-start(bf16[2,2048,128]{2,1,0:T(8,128)(2,1)S(1)} %assemble.1.own_ref), channel_id=1, source_target_pairs={{0,2},{2,0},{4,6},{6,4},{8,10},{10,8},{12,14},{14,12},{16,18},{18,... | collective-permute-start | bytes 3145736 | tf_op jit(solution)/shard_map/ppermute | solution.py:362
  57.7 19.1 %all-to-all-start.1 = ((bf16[16,96,128]{2,1,0:T(8,128)(2,1)}), bf16[16,96,128]{2,1,0:T(8,128)(2,1)S(1)}, u32[]{:S(2)}, u32[]{:S(2)}) async-start(bf16[16,96,128]{2,1,0:T(8,128)(2,1)} %get-tuple-element.7), calls=%async_computation.1 | async-start | bytes 786432 | tf_op jit(solution)/shard_map/all_to_all | solution.py:350
  76.8 20.7 %copy-start = (f32[16]{0:T(128)S(1)}, f32[16]{0:T(128)}, u32[]{:S(2)}) copy-start(f32[16]{0:T(128)} %gate_ref.1) | copy-start | bytes 196
  89.4 22.4 %all-to-all-start.2 = ((bf16[16,128,128]{2,1,0:T(8,128)(2,1)}), bf16[16,128,128]{2,1,0:T(8,128)(2,1)S(1)}, u32[]{:S(2)}, u32[]{:S(2)}) async-start(bf16[16,128,128]{2,1,0:T(8,128)(2,1)} %attend.3), calls=%async_computation.2 | async-start | bytes 1048576 | tf_op jit(solution)/shard_map/all_to_all | solution.py:420
  96.3 1.2 %collective-permute-start.1 = (f32[8,128]{1,0:T(8,128)S(1)}, f32[8,128]{1,0:T(8,128)S(1)}, u32[]{:S(2)}, u32[]{:S(2)}) collective-permute-start(f32[8,128]{1,0:T(8,128)S(1)} %get-tuple-element.9), channel_id=1, source_target_pairs={{0,2},{2,0},{4,6},{6,4},{8,10},{10,8},{12,14},{14,12},{16,18},{18,... | collective-permute-start | bytes 12296 | tf_op jit(solution)/shard_map/ppermute | solution.py:406

commit v12 on v8

--- a/solution.py
+++ b/solution.py
@@ -227,7 +227,7 @@
                     high[...] = best
                     return carry
 
-                lax.fori_loop(0, rows_unit // width, score, 0, unroll=2)
+                lax.fori_loop(0, rows_unit // width, score, 0, unroll=2 if final else 1)
         high[...] = jnp.broadcast_to(jnp.max(high[...], 1, keepdims=True) * exponent, high.shape)
         total[...] = jnp.zeros_like(total)
         acc[...] = jnp.zeros_like(acc)
@@ -256,7 +256,7 @@
                 )
                 return carry
 
-            lax.fori_loop(0, steps_side, back, 0, unroll=2)
+            lax.fori_loop(0, steps_side, back, 0, unroll=2 if final else 1)
         weight = scale / jnp.sum(total[...], 1, keepdims=True)
         qx[here, :LANES] = (acc[...] * weight).astype(jnp.bfloat16)
         return carry
@@ -290,7 +290,7 @@
     assert rows_dev == 16 * BLK and heads * 8 == LANES and tokens == LANES
     half_shard = rows_dev // 2
     units = 2 * chunks
-    early = 5 * tokens // 8
+    early = tokens // 2
     late = tokens - early
     extra = -(-(chunks * qblocks + 2) // 16) * 16
     ext_at = 2 * half_shard + 2 * early
@@ -325,8 +325,8 @@
             pltpu.VMEM((LANES, LANES), jnp.float32),
             pltpu.VMEM(first_shape, bf16),
             pltpu.VMEM(second_shape, bf16),
-            pltpu.SemaphoreType.DMA((4, 6)),
-            pltpu.SemaphoreType.DMA((2, 5)),
+            pltpu.SemaphoreType.DMA((2, 6)),
+            pltpu.SemaphoreType.DMA((2, 3)),
         ],
         compiler_params=pltpu.CompilerParams(vmem_limit_bytes=56 << 20),
         name="pack",

time: 105 us -> 104 us (level)
  blocking collectives: 50.8 us -> 48.3 us
  waiting for transfers between devices: 15.2 us -> 17 us
  starting transfers between devices: 10.2 us -> 8.58 us
  Pallas kernels: 27.1 us -> 28.6 us
    all_to_all x1, blocking collectives: 50.8 us -> 48.3 us  [local(): first_in = exchange(first_out)]
    all_to_all x1, waiting for transfers between devices: 0.42 us -> 2.96 us  [local(): second_in = exchange(second_out)]
    all_to_all x1, starting transfers between devices: 6.48 us -> 4.85 us  [local(): home = exchange(grad)]
    pallas_call x2, Pallas kernels: 21.9 us -> 23.4 us  [attend_some(): pl.pallas_call(functools.partial(attend, begin, count, q_at, ext_at, qblo...]
where the time goes in v12:
time: 104 us
  blocking collectives  48.3 us (46%)
  Pallas kernels  28.6 us (28%)
  waiting for transfers between devices  17 us (16%)
  starting transfers between devices  8.58 us (8%)
    all_to_all x1, blocking collectives, local(): first_in = exchange(first_out)  48.3 us
    pallas_call x2, Pallas kernels, attend_some(): pl.pallas_call(functools.partial(attend, begin, count, q_at, ext_at, qblo...  23.4 us
    all_to_all x1, waiting for transfers between devices, local(): home = exchange(grad)  12.9 us
    all_to_all x1, starting transfers between devices, local(): home = exchange(grad)  4.85 us
    pallas_call x1, Pallas kernels, local(): pl.pallas_call(functools.partial(pack, heads, chunks, early), out_shape=(...  4.19 us
    all_to_all x1, starting transfers between devices, local(): second_in = exchange(second_out)  3.59 us
    all_to_all x1, waiting for transfers between devices, local(): second_in = exchange(second_out)  2.96 us
  transfers between devices with their start and end apart: 4, of which 3 were waited for; matrix products, arithmetic and copies ran while one was open for 1% of the time, Pallas kernels for 12%

profile of v12, /device:TPU:0, one launch (start us, length us, event | category | flops | bytes accessed | tf_op | source)
XLA Modules:
  0.0 103.7 jit_solution(2285475273352922000)
XLA Ops:
  0.6 4.2 %pack.1 = (bf16[16,400,128]{2,1,0:T(8,128)(2,1)}, bf16[16,128,128]{2,1,0:T(8,128)(2,1)}) custom-call(bf16[256,2048]{1,0:T(8,128)(2,1)} %k_hbm.1, bf16[256,2048]{1,0:T(8,128)(2,1)} %v_hbm.1, bf16[128,2048]{1,0:T(8,128)(2,1)} %bitcast.10, bf16[128,2048]{1,0:T(8,128)(2,1)} %bitcast.11, bf16[128,2048]{1,0:T(8,128)(2,1)} %bitcast.12, bf16[128,2048]{1,0:T(8,128)(2,1)} %bitcast.13, ...), custom_call_target="tpu_custom_call" | custom-call | tf_op jit(solution)/shard_map/pack/pallas_call | solution.py:315
  4.8 48.3 %all_to_all.15.in_ref.q_ref.ext_ref = bf16[16,400,128]{2,1,0:T(8,128)(2,1)S(1)} all-to-all(bf16[16,400,128]{2,1,0:T(8,128)(2,1)} %get-tuple-element.6), channel_id=1, replica_groups={{0,1,4,5,8,9,12,13,16,17,20,21,24,25,28,29},{2,3,6,7,10,11,14,15,18,19,..., dimensions={0} | all-to-all | bytes 3276800 | tf_op jit(solution)/shard_map/all_to_all | solution.py:334
  53.1 0.1 assemble.1.own_ref
  53.2 0.1 collective-permute-start
  53.2 3.6 %all-to-all-start.1 = ((bf16[16,128,128]{2,1,0:T(8,128)(2,1)}), bf16[16,128,128]{2,1,0:T(8,128)(2,1)S(1)}, u32[]{:S(2)}, u32[]{:S(2)}) async-start(bf16[16,128,128]{2,1,0:T(8,128)(2,1)} %get-tuple-element.7), calls=%async_computation.1 | async-start | bytes 1048576 | tf_op jit(solution)/shard_map/all_to_all | solution.py:335
  56.8 0.0 collective-permute-done.mate_ref
  56.8 12.1 %attend.2 = (bf16[16,64,128]{2,1,0:T(8,128)(2,1)S(1)}, f32[8,128]{1,0:T(8,128)S(1)}) custom-call(bf16[2,2048,128]{2,1,0:T(8,128)(2,1)S(1)} %assemble.1.own_ref, bf16[2,2048,128]{2,1,0:T(8,128)(2,1)} %collective-permute-done.mate_ref, bf16[16,400,128]{2,1,0:T(8,128)(2,1)S(1)} %all_to_all.15.in_ref.q_ref.ext_ref, ...), custom_call_target="tpu_custom_call" | custom-call | flops 5368709120 | bytes 2097152 | tf_op jit(solution)/shard_map/attend/pallas_call | solution.py:354
  68.9 3.0 %all-to-all-done.1.q_ref = bf16[16,128,128]{2,1,0:T(8,128)(2,1)S(1)} async-done(((bf16[16,128,128]{2,1,0:T(8,128)(2,1)}), bf16[16,128,128]{2,1,0:T(8,128)(2,1)S(1)}, u32[]{:S(2)}, u32[]{:S(2)}) %all-to-all-start.1) | async-done | bytes 524320 | tf_op jit(solution)/shard_map/all_to_all | solution.py:335
  71.9 0.0 copy-start
  71.9 11.3 %attend.3 = bf16[16,128,128]{2,1,0:T(8,128)(2,1)} custom-call(bf16[2,2048,128]{2,1,0:T(8,128)(2,1)S(1)} %assemble.1.own_ref, bf16[2,2048,128]{2,1,0:T(8,128)(2,1)} %collective-permute-done.mate_ref, bf16[16,128,128]{2,1,0:T(8,128)(2,1)S(1)} %all-to-all-done.1.q_ref, bf16[16,400,128]{2,1,0:T(8,128)(2,1)S(1)} %all_to_all.15.in_ref.q_ref.ext_ref, ...), custom_call_target="tpu_custom_call" | custom-call | flops 5368709120 | bytes 2097152 | tf_op jit(solution)/shard_map/attend/pallas_call | solution.py:354
  83.2 4.8 %all-to-all-start.2 = ((bf16[16,128,128]{2,1,0:T(8,128)(2,1)}), bf16[16,128,128]{2,1,0:T(8,128)(2,1)S(1)}, u32[]{:S(2)}, u32[]{:S(2)}) async-start(bf16[16,128,128]{2,1,0:T(8,128)(2,1)} %attend.3), calls=%async_computation.2 | async-start | bytes 1048576 | tf_op jit(solution)/shard_map/all_to_all | solution.py:405
  88.1 0.1 collective-permute-start.1
  88.2 1.2 %collective-permute-done.1 = f32[8,128]{1,0:T(8,128)S(1)} collective-permute-done((f32[8,128]{1,0:T(8,128)S(1)}, f32[8,128]{1,0:T(8,128)S(1)}, u32[]{:S(2)}, u32[]{:S(2)}) %collective-permute-start.1) | collective-permute-done | bytes 4128 | tf_op jit(solution)/shard_map/ppermute | solution.py:391
  89.3 0.0 copy-done
  89.3 0.6 fusion.1
  89.9 12.9 %all-to-all-done.2.in_ref = bf16[16,128,128]{2,1,0:T(8,128)(2,1)S(1)} async-done(((bf16[16,128,128]{2,1,0:T(8,128)(2,1)}), bf16[16,128,128]{2,1,0:T(8,128)(2,1)S(1)}, u32[]{:S(2)}, u32[]{:S(2)}) %all-to-all-start.2) | async-done | bytes 524320 | tf_op jit(solution)/shard_map/all_to_all | solution.py:405
  102.8 0.9 unpack.1
  (1 shorter events, 0.0 us)
Async XLA Ops:
  53.2 3.7 %collective-permute-start = (bf16[2,2048,128]{2,1,0:T(8,128)(2,1)S(1)}, bf16[2,2048,128]{2,1,0:T(8,128)(2,1)}, u32[]{:S(2)}, u32[]{:S(2)}) collective-permute-start(bf16[2,2048,128]{2,1,0:T(8,128)(2,1)S(1)} %assemble.1.own_ref), channel_id=1, source_target_pairs={{0,2},{2,0},{4,6},{6,4},{8,10},{10,8},{12,14},{14,12},{16,18},{18,... | collective-permute-start | bytes 3145736 | tf_op jit(solution)/shard_map/ppermute | solution.py:347
  53.2 18.7 %all-to-all-start.1 = ((bf16[16,128,128]{2,1,0:T(8,128)(2,1)}), bf16[16,128,128]{2,1,0:T(8,128)(2,1)S(1)}, u32[]{:S(2)}, u32[]{:S(2)}) async-start(bf16[16,128,128]{2,1,0:T(8,128)(2,1)} %get-tuple-element.7), calls=%async_computation.1 | async-start | bytes 1048576 | tf_op jit(solution)/shard_map/all_to_all | solution.py:335
  71.9 17.4 %copy-start = (f32[16]{0:T(128)S(1)}, f32[16]{0:T(128)}, u32[]{:S(2)}) copy-start(f32[16]{0:T(128)} %gate_ref.1) | copy-start | bytes 196
  83.2 19.6 %all-to-all-start.2 = ((bf16[16,128,128]{2,1,0:T(8,128)(2,1)}), bf16[16,128,128]{2,1,0:T(8,128)(2,1)S(1)}, u32[]{:S(2)}, u32[]{:S(2)}) async-start(bf16[16,128,128]{2,1,0:T(8,128)(2,1)} %attend.3), calls=%async_computation.2 | async-start | bytes 1048576 | tf_op jit(solution)/shard_map/all_to_all | solution.py:405
  88.1 1.2 %collective-permute-start.1 = (f32[8,128]{1,0:T(8,128)S(1)}, f32[8,128]{1,0:T(8,128)S(1)}, u32[]{:S(2)}, u32[]{:S(2)}) collective-permute-start(f32[8,128]{1,0:T(8,128)S(1)} %get-tuple-element.9), channel_id=1, source_target_pairs={{0,2},{2,0},{4,6},{6,4},{8,10},{10,8},{12,14},{14,12},{16,18},{18,... | collective-permute-start | bytes 12296 | tf_op jit(solution)/shard_map/ppermute | solution.py:391

commit v13 on v12

--- a/solution.py
+++ b/solution.py
@@ -162,7 +162,7 @@
         early_copy = pltpu.make_async_copy(before_ref, out_ref.at[:, :begin, :], sems.at[0])
         early_copy.start()
     else:
-        out_ref, gate_ref, mark, minus, qx, dx, scores, high, total, acc = refs
+        out_ref, gate_ref, mark, minus, qx, dx, scores, high, total, acc, delta = refs
     sources = q_ref.shape[0]
     units = qx.shape[1] // LANES - 1
     sides = (own_ref, mate_ref)
@@ -200,8 +200,11 @@
         if not final:
             gate_sum = gate_sum + extra[bias_rows + 1 : bias_rows + 2]
         wide = jnp.broadcast_to(extra[bias_rows : bias_rows + 1], (LANES, LANES)).T
-        wide = jnp.where(wide_lane == 0, wide, 0.0).astype(jnp.bfloat16)
-        dx[base : base + count, LANES:] = wide[begin : begin + count]
+        if final:
+            wide = jnp.where(wide_lane == 0, wide, 0.0).astype(jnp.bfloat16)
+            dx[base : base + count, LANES:] = wide[begin : begin + count]
+        else:
+            delta[base : base + count, :] = wide[begin : begin + count]
     if not final:
         gate_ref[...] = jnp.broadcast_to(gate_sum, gate_ref.shape)
 
@@ -227,7 +230,7 @@
                     high[...] = best
                     return carry
 
-                lax.fori_loop(0, rows_unit // width, score, 0, unroll=2 if final else 1)
+                lax.fori_loop(0, rows_unit // width, score, 0, unroll=4 if final else 2)
         high[...] = jnp.broadcast_to(jnp.max(high[...], 1, keepdims=True) * exponent, high.shape)
         total[...] = jnp.zeros_like(total)
         acc[...] = jnp.zeros_like(acc)
@@ -235,12 +238,15 @@
 
             def back(at, carry, side=side, ref=ref):
                 rows = pl.ds(pl.multiple_of(at * width, width), width)
+                if final:
+                    left, right = dx[here, :], jnp.concatenate([ref[1, rows, :], minus[...]], axis=1)
+                else:
+                    left, right = dx[here, :LANES], ref[1, rows, :]
                 prod = lax.dot_general(
-                    dx[here, :],
-                    jnp.concatenate([ref[1, rows, :], minus[...]], axis=1),
-                    (((1,), (1,)), ((), ())),
-                    preferred_element_type=jnp.float32,
+                    left, right, (((1,), (1,)), ((), ())), preferred_element_type=jnp.float32
                 )
+                if not final:
+                    less = delta[here, :]
                 got = scores[side * steps_side + at]
                 level = high[...]
                 added = total[...]
@@ -249,14 +255,15 @@
                     cols = slice(column * LANES, (column + 1) * LANES)
                     expo = jnp.exp2(got[:, cols] * exponent - level)
                     added = added + expo
-                    pieces.append((expo * prod[:, cols]).astype(jnp.bfloat16))
+                    moved = prod[:, cols] if final else prod[:, cols] - less
+                    pieces.append((expo * moved).astype(jnp.bfloat16))
                 total[...] = added
                 acc[...] += jnp.dot(
                     jnp.concatenate(pieces, axis=1), ref[0, rows, :], preferred_element_type=jnp.float32
                 )
                 return carry
 
-            lax.fori_loop(0, steps_side, back, 0, unroll=2 if final else 1)
+            lax.fori_loop(0, steps_side, back, 0, unroll=2)
         weight = scale / jnp.sum(total[...], 1, keepdims=True)
         qx[here, :LANES] = (acc[...] * weight).astype(jnp.bfloat16)
         return carry
@@ -366,7 +373,8 @@
                 pltpu.VMEM((tile, LANES), jnp.float32),
                 pltpu.VMEM((tile, LANES), jnp.float32),
             ]
-            + [pltpu.VMEM((members, count, LANES), bf16), pltpu.SemaphoreType.DMA((2,))] * final,
+            + [pltpu.VMEM((members, count, LANES), bf16), pltpu.SemaphoreType.DMA((2,))] * final
+            + [pltpu.VMEM((members * count, LANES), jnp.float32)] * (not final),
             compiler_params=pltpu.CompilerParams(vmem_limit_bytes=(40 if chunks == 1 else 44) << 20),
             cost_estimate=pl.CostEstimate(
                 flops=2 * members * count * rows_all * LANES * 5,

time: 104 us -> 103 us (level)
  Pallas kernels: 28.6 us -> 26.2 us
  waiting for transfers between devices: 17 us -> 18.5 us
    pallas_call x2, Pallas kernels: 23.4 us -> 21 us  [attend_some(): pl.pallas_call(functools.partial(attend, begin, count, q_at, ext_at, qblo...]
    all_to_all x1, waiting for transfers between devices: 2.96 us -> 4.46 us  [local(): second_in = exchange(second_out)]
  transfers between devices with their start and end apart: 4 -> 4, of which waited for: 3 -> 3; matrix products, arithmetic and copies ran while one was open for 1% -> 1% of each run, Pallas kernels for 12% -> 10%
where the time goes in v13:
time: 103 us
  blocking collectives  48.3 us (47%)
  Pallas kernels  26.2 us (25%)
  waiting for transfers between devices  18.5 us (18%)
  starting transfers between devices  8.57 us (8%)
    all_to_all x1, blocking collectives, local(): first_in = exchange(first_out)  48.3 us
    pallas_call x2, Pallas kernels, attend_some(): pl.pallas_call(functools.partial(attend, begin, count, q_at, ext_at, qblo...  21 us
    all_to_all x1, waiting for transfers between devices, local(): home = exchange(grad)  12.9 us
    all_to_all x1, starting transfers between devices, local(): home = exchange(grad)  4.84 us
    all_to_all x1, waiting for transfers between devices, local(): second_in = exchange(second_out)  4.46 us
    pallas_call x1, Pallas kernels, local(): pl.pallas_call(functools.partial(pack, heads, chunks, early), out_shape=(...  4.19 us
    all_to_all x1, starting transfers between devices, local(): second_in = exchange(second_out)  3.59 us
  transfers between devices with their start and end apart: 4, of which 3 were waited for; matrix products, arithmetic and copies ran while one was open for 1% of the time, Pallas kernels for 10%

profile of v13, /device:TPU:0, one launch (start us, length us, event | category | flops | bytes accessed | tf_op | source)
XLA Modules:
  0.0 102.9 jit_solution(10652991811977838381)
XLA Ops:
  0.6 4.2 %pack.1 = (bf16[16,400,128]{2,1,0:T(8,128)(2,1)}, bf16[16,128,128]{2,1,0:T(8,128)(2,1)}) custom-call(bf16[256,2048]{1,0:T(8,128)(2,1)} %k_hbm.1, bf16[256,2048]{1,0:T(8,128)(2,1)} %v_hbm.1, bf16[128,2048]{1,0:T(8,128)(2,1)} %bitcast.10, bf16[128,2048]{1,0:T(8,128)(2,1)} %bitcast.11, bf16[128,2048]{1,0:T(8,128)(2,1)} %bitcast.12, bf16[128,2048]{1,0:T(8,128)(2,1)} %bitcast.13, ...), custom_call_target="tpu_custom_call" | custom-call | tf_op jit(solution)/shard_map/pack/pallas_call | solution.py:322
  4.8 48.3 %all_to_all.15.in_ref.q_ref.ext_ref = bf16[16,400,128]{2,1,0:T(8,128)(2,1)S(1)} all-to-all(bf16[16,400,128]{2,1,0:T(8,128)(2,1)} %get-tuple-element.6), channel_id=1, replica_groups={{0,1,4,5,8,9,12,13,16,17,20,21,24,25,28,29},{2,3,6,7,10,11,14,15,18,19,..., dimensions={0} | all-to-all | bytes 3276800 | tf_op jit(solution)/shard_map/all_to_all | solution.py:341
  53.1 0.1 assemble.1.own_ref
  53.2 0.1 collective-permute-start
  53.2 3.6 %all-to-all-start.1 = ((bf16[16,128,128]{2,1,0:T(8,128)(2,1)}), bf16[16,128,128]{2,1,0:T(8,128)(2,1)S(1)}, u32[]{:S(2)}, u32[]{:S(2)}) async-start(bf16[16,128,128]{2,1,0:T(8,128)(2,1)} %get-tuple-element.7), calls=%async_computation.1 | async-start | bytes 1048576 | tf_op jit(solution)/shard_map/all_to_all | solution.py:342
  56.8 0.0 collective-permute-done.mate_ref
  56.8 10.6 %attend.2 = (bf16[16,64,128]{2,1,0:T(8,128)(2,1)S(1)}, f32[8,128]{1,0:T(8,128)S(1)}) custom-call(bf16[2,2048,128]{2,1,0:T(8,128)(2,1)S(1)} %assemble.1.own_ref, bf16[2,2048,128]{2,1,0:T(8,128)(2,1)} %collective-permute-done.mate_ref, bf16[16,400,128]{2,1,0:T(8,128)(2,1)S(1)} %all_to_all.15.in_ref.q_ref.ext_ref, ...), custom_call_target="tpu_custom_call" | custom-call | flops 5368709120 | bytes 2097152 | tf_op jit(solution)/shard_map/attend/pallas_call | solution.py:361
  67.4 4.5 %all-to-all-done.1.q_ref = bf16[16,128,128]{2,1,0:T(8,128)(2,1)S(1)} async-done(((bf16[16,128,128]{2,1,0:T(8,128)(2,1)}), bf16[16,128,128]{2,1,0:T(8,128)(2,1)S(1)}, u32[]{:S(2)}, u32[]{:S(2)}) %all-to-all-start.1) | async-done | bytes 524320 | tf_op jit(solution)/shard_map/all_to_all | solution.py:342
  71.9 0.0 copy-start
  71.9 10.4 %attend.3 = bf16[16,128,128]{2,1,0:T(8,128)(2,1)} custom-call(bf16[2,2048,128]{2,1,0:T(8,128)(2,1)S(1)} %assemble.1.own_ref, bf16[2,2048,128]{2,1,0:T(8,128)(2,1)} %collective-permute-done.mate_ref, bf16[16,128,128]{2,1,0:T(8,128)(2,1)S(1)} %all-to-all-done.1.q_ref, bf16[16,400,128]{2,1,0:T(8,128)(2,1)S(1)} %all_to_all.15.in_ref.q_ref.ext_ref, ...), custom_call_target="tpu_custom_call" | custom-call | flops 5368709120 | bytes 2097152 | tf_op jit(solution)/shard_map/attend/pallas_call | solution.py:361
  82.4 4.8 %all-to-all-start.2 = ((bf16[16,128,128]{2,1,0:T(8,128)(2,1)}), bf16[16,128,128]{2,1,0:T(8,128)(2,1)S(1)}, u32[]{:S(2)}, u32[]{:S(2)}) async-start(bf16[16,128,128]{2,1,0:T(8,128)(2,1)} %attend.3), calls=%async_computation.2 | async-start | bytes 1048576 | tf_op jit(solution)/shard_map/all_to_all | solution.py:413
  87.2 0.1 collective-permute-start.1
  87.3 1.2 %collective-permute-done.1 = f32[8,128]{1,0:T(8,128)S(1)} collective-permute-done((f32[8,128]{1,0:T(8,128)S(1)}, f32[8,128]{1,0:T(8,128)S(1)}, u32[]{:S(2)}, u32[]{:S(2)}) %collective-permute-start.1) | collective-permute-done | bytes 4128 | tf_op jit(solution)/shard_map/ppermute | solution.py:399
  88.4 0.0 copy-done
  88.4 0.6 fusion.1
  89.0 12.9 %all-to-all-done.2.in_ref = bf16[16,128,128]{2,1,0:T(8,128)(2,1)S(1)} async-done(((bf16[16,128,128]{2,1,0:T(8,128)(2,1)}), bf16[16,128,128]{2,1,0:T(8,128)(2,1)S(1)}, u32[]{:S(2)}, u32[]{:S(2)}) %all-to-all-start.2) | async-done | bytes 524320 | tf_op jit(solution)/shard_map/all_to_all | solution.py:413
  101.9 0.9 unpack.1
  (1 shorter events, 0.0 us)
Async XLA Ops:
  53.2 3.7 %collective-permute-start = (bf16[2,2048,128]{2,1,0:T(8,128)(2,1)S(1)}, bf16[2,2048,128]{2,1,0:T(8,128)(2,1)}, u32[]{:S(2)}, u32[]{:S(2)}) collective-permute-start(bf16[2,2048,128]{2,1,0:T(8,128)(2,1)S(1)} %assemble.1.own_ref), channel_id=1, source_target_pairs={{0,2},{2,0},{4,6},{6,4},{8,10},{10,8},{12,14},{14,12},{16,18},{18,... | collective-permute-start | bytes 3145736 | tf_op jit(solution)/shard_map/ppermute | solution.py:354
  53.2 18.7 %all-to-all-start.1 = ((bf16[16,128,128]{2,1,0:T(8,128)(2,1)}), bf16[16,128,128]{2,1,0:T(8,128)(2,1)S(1)}, u32[]{:S(2)}, u32[]{:S(2)}) async-start(bf16[16,128,128]{2,1,0:T(8,128)(2,1)} %get-tuple-element.7), calls=%async_computation.1 | async-start | bytes 1048576 | tf_op jit(solution)/shard_map/all_to_all | solution.py:342
  71.9 16.5 %copy-start = (f32[16]{0:T(128)S(1)}, f32[16]{0:T(128)}, u32[]{:S(2)}) copy-start(f32[16]{0:T(128)} %gate_ref.1) | copy-start | bytes 196
  82.4 19.6 %all-to-all-start.2 = ((bf16[16,128,128]{2,1,0:T(8,128)(2,1)}), bf16[16,128,128]{2,1,0:T(8,128)(2,1)S(1)}, u32[]{:S(2)}, u32[]{:S(2)}) async-start(bf16[16,128,128]{2,1,0:T(8,128)(2,1)} %attend.3), calls=%async_computation.2 | async-start | bytes 1048576 | tf_op jit(solution)/shard_map/all_to_all | solution.py:413
  87.2 1.2 %collective-permute-start.1 = (f32[8,128]{1,0:T(8,128)S(1)}, f32[8,128]{1,0:T(8,128)S(1)}, u32[]{:S(2)}, u32[]{:S(2)}) collective-permute-start(f32[8,128]{1,0:T(8,128)S(1)} %get-tuple-element.9), channel_id=1, source_target_pairs={{0,2},{2,0},{4,6},{6,4},{8,10},{10,8},{12,14},{14,12},{16,18},{18,... | collective-permute-start | bytes 12296 | tf_op jit(solution)/shard_map/ppermute | solution.py:399

commit v14 on v12

--- a/solution.py
+++ b/solution.py
@@ -70,7 +70,8 @@
 
     lane = lax.broadcasted_iota(jnp.int32, (1, LANES), 1)
     ids = ids_ref[...]
-    bias_rows = chunks * qblocks
+    per = qblocks // 2
+    bias_rows = chunks * per
     ext_ref[...] = jnp.zeros_like(ext_ref)
     for chunk in range(chunks):
         hits = []
@@ -81,7 +82,8 @@
             for name in range(names):
                 hit = jnp.where(ids[:, name : name + 1] == wanted, 1.0, hit)
             hits.append(hit)
-        ext_ref[chunk * qblocks : (chunk + 1) * qblocks, :] = hits[0] + 2.0 * hits[1]
+        code = hits[0] + 2.0 * hits[1]
+        ext_ref[chunk * per : (chunk + 1) * per, :] = code[:per] + 4.0 * code[per:]
 
     ones = jnp.ones((8, LANES), jnp.float32)
     wide_ones = jnp.ones((16, 2 * LANES), jnp.bfloat16)
@@ -118,13 +120,9 @@
         second_out[head, late:, :] = d_mem[early:]
         if head % bunch == bunch - 1:
             some = slice(head + 1 - bunch, head + 1)
-            body = slice(0, at + 2 * early)
-            for index, (source, target) in enumerate(
-                ((first_out.at[some, body], first_hbm.at[some, body]), (second_out.at[some], second_hbm.at[some]))
-            ):
-                copy = pltpu.make_async_copy(source, target, out_sems.at[index, head // bunch])
-                copy.start()
-                sent.append(copy)
+            copy = pltpu.make_async_copy(second_out.at[some], second_hbm.at[some], out_sems.at[1, head // bunch])
+            copy.start()
+            sent.append(copy)
     total = lax.dot_general(
         ones,
         gate_rows[...],
@@ -140,10 +138,11 @@
     for head in range(heads):
         ext_ref[bias_rows : bias_rows + 1, :] = delta_ref[head : head + 1, :]
         first_out[head, at + 2 * early :, :] = ext_ref[...].astype(jnp.bfloat16)
-    body = slice(at + 2 * early, first_out.shape[1])
-    copy = pltpu.make_async_copy(first_out.at[:, body], first_hbm.at[:, body], out_sems.at[0, bunches])
-    copy.start()
-    sent.append(copy)
+        if head % 4 == 3:
+            some = slice(head - 3, head + 1)
+            copy = pltpu.make_async_copy(first_out.at[some], first_hbm.at[some], out_sems.at[0, head // 4])
+            copy.start()
+            sent.append(copy)
     for copy in sent:
         copy.wait()
 
@@ -171,7 +170,8 @@
     scale = 1.0 / math.sqrt(LANES)
     exponent = scale * math.log2(math.e)
     chunks = units // 2
-    bias_rows = chunks * qblocks
+    per = qblocks // 2
+    bias_rows = chunks * per
 
     lane = lax.broadcasted_iota(jnp.int32, (BLK, LANES), 1)
     for block in range(LANES):
@@ -187,6 +187,8 @@
         dx[base : base + count, :LANES] = q_ref[source, q_at + count : q_at + 2 * count, :]
         extra = ext_ref[source, ext_at:, :].astype(jnp.float32)
         code = extra[:bias_rows]
+        upper = jnp.floor(code * 0.25)
+        code = upper if final else code - 4.0 * upper
         second = jnp.where(code > 1.5, 1.0, 0.0)
         first = code - 2.0 * second
         for side, hit in enumerate((first, second)):
@@ -194,7 +196,7 @@
             for chunk in range(chunks):
                 lanes = (1 + side * chunks + chunk) * LANES
                 for block in range(count // BLK):
-                    at = chunk * qblocks + begin // BLK + block
+                    at = chunk * per + block
                     row = jnp.broadcast_to(bias[at : at + 1], (BLK, LANES)).astype(jnp.bfloat16)
                     qx[base + block * BLK : base + (block + 1) * BLK, lanes : lanes + LANES] = row
         if not final:
@@ -227,7 +229,7 @@
                     high[...] = best
                     return carry
 
-                lax.fori_loop(0, rows_unit // width, score, 0, unroll=2 if final else 1)
+                lax.fori_loop(0, rows_unit // width, score, 0, unroll=True)
         high[...] = jnp.broadcast_to(jnp.max(high[...], 1, keepdims=True) * exponent, high.shape)
         total[...] = jnp.zeros_like(total)
         acc[...] = jnp.zeros_like(acc)
@@ -265,10 +267,14 @@
     for source in range(sources):
         (stage if final else out_ref)[source] = qx[source * count : (source + 1) * count, :LANES]
     if final:
-        late_copy = pltpu.make_async_copy(stage, out_ref.at[:, begin:, :], sems.at[1])
-        late_copy.start()
-        early_copy.wait()
-        late_copy.wait()
+        copies = [early_copy]
+        for part in range(4):
+            some = slice(part * sources // 4, (part + 1) * sources // 4)
+            copy = pltpu.make_async_copy(stage.at[some], out_ref.at[some, begin:, :], sems.at[1 + part])
+            copy.start()
+            copies.append(copy)
+        for copy in copies:
+            copy.wait()
 
 
 def unpack(in_ref, out_ref):
@@ -292,7 +298,7 @@
     units = 2 * chunks
     early = tokens // 2
     late = tokens - early
-    extra = -(-(chunks * qblocks + 2) // 16) * 16
+    extra = -(-(chunks * (qblocks // 2) + 2) // 8) * 8
     ext_at = 2 * half_shard + 2 * early
     vmem = pl.BlockSpec(memory_space=pltpu.VMEM)
     smem = pl.BlockSpec(memory_space=pltpu.SMEM)
@@ -326,7 +332,7 @@
             pltpu.VMEM(first_shape, bf16),
             pltpu.VMEM(second_shape, bf16),
             pltpu.SemaphoreType.DMA((2, 6)),
-            pltpu.SemaphoreType.DMA((2, 3)),
+            pltpu.SemaphoreType.DMA((2, heads // 4)),
         ],
         compiler_params=pltpu.CompilerParams(vmem_limit_bytes=56 << 20),
         name="pack",
@@ -366,7 +372,7 @@
                 pltpu.VMEM((tile, LANES), jnp.float32),
                 pltpu.VMEM((tile, LANES), jnp.float32),
             ]
-            + [pltpu.VMEM((members, count, LANES), bf16), pltpu.SemaphoreType.DMA((2,))] * final,
+            + [pltpu.VMEM((members, count, LANES), bf16), pltpu.SemaphoreType.DMA((5,))] * final,
             compiler_params=pltpu.CompilerParams(vmem_limit_bytes=(40 if chunks == 1 else 44) << 20),
             cost_estimate=pl.CostEstimate(
                 flops=2 * members * count * rows_all * LANES * 5,

time: 104 us -> 103 us (level)
  Pallas kernels: 28.6 us -> 26.4 us
  waiting for transfers between devices: 17 us -> 18.6 us
    pallas_call x2, Pallas kernels: 23.4 us -> 20.9 us  [attend_some(): pl.pallas_call(functools.partial(attend, begin, count, q_at, ext_at, qblo...]
    all_to_all x1, waiting for transfers between devices: 2.96 us -> 4.6 us  [local(): second_in = exchange(second_out)]
  transfers between devices with their start and end apart: 4 -> 4, of which waited for: 3 -> 3; matrix products, arithmetic and copies ran while one was open for 1% -> 1% of each run, Pallas kernels for 12% -> 10%
where the time goes in v14:
time: 103 us
  blocking collectives  47.6 us (46%)
  Pallas kernels  26.4 us (26%)
  waiting for transfers between devices  18.6 us (18%)
  starting transfers between devices  8.58 us (8%)
    all_to_all x1, blocking collectives, local(): first_in = exchange(first_out)  47.6 us
    pallas_call x2, Pallas kernels, attend_some(): pl.pallas_call(functools.partial(attend, begin, count, q_at, ext_at, qblo...  20.9 us
    all_to_all x1, waiting for transfers between devices, local(): home = exchange(grad)  12.9 us
    all_to_all x1, starting transfers between devices, local(): home = exchange(grad)  4.85 us
    all_to_all x1, waiting for transfers between devices, local(): second_in = exchange(second_out)  4.6 us
    pallas_call x1, Pallas kernels, local(): pl.pallas_call(functools.partial(pack, heads, chunks, early), out_shape=(...  4.51 us
    all_to_all x1, starting transfers between devices, local(): second_in = exchange(second_out)  3.59 us
  transfers between devices with their start and end apart: 4, of which 3 were waited for; matrix products, arithmetic and copies ran while one was open for 1% of the time, Pallas kernels for 10%

profile of v14, /device:TPU:0, one launch (start us, length us, event | category | flops | bytes accessed | tf_op | source)
XLA Modules:
  0.0 102.5 jit_solution(8839945263921924338)
XLA Ops:
  0.6 4.5 %pack.1 = (bf16[16,392,128]{2,1,0:T(8,128)(2,1)}, bf16[16,128,128]{2,1,0:T(8,128)(2,1)}) custom-call(bf16[256,2048]{1,0:T(8,128)(2,1)} %k_hbm.1, bf16[256,2048]{1,0:T(8,128)(2,1)} %v_hbm.1, bf16[128,2048]{1,0:T(8,128)(2,1)} %bitcast.10, bf16[128,2048]{1,0:T(8,128)(2,1)} %bitcast.11, bf16[128,2048]{1,0:T(8,128)(2,1)} %bitcast.12, bf16[128,2048]{1,0:T(8,128)(2,1)} %bitcast.13, ...), custom_call_target="tpu_custom_call" | custom-call | tf_op jit(solution)/shard_map/pack/pallas_call | solution.py:321
  5.1 47.6 %all_to_all.15.in_ref.q_ref.ext_ref = bf16[16,392,128]{2,1,0:T(8,128)(2,1)S(1)} all-to-all(bf16[16,392,128]{2,1,0:T(8,128)(2,1)} %get-tuple-element.6), channel_id=1, replica_groups={{0,1,4,5,8,9,12,13,16,17,20,21,24,25,28,29},{2,3,6,7,10,11,14,15,18,19,..., dimensions={0} | all-to-all | bytes 3211264 | tf_op jit(solution)/shard_map/all_to_all | solution.py:340
  52.8 0.1 assemble.1.own_ref
  52.8 0.1 collective-permute-start
  52.9 3.6 %all-to-all-start.1 = ((bf16[16,128,128]{2,1,0:T(8,128)(2,1)}), bf16[16,128,128]{2,1,0:T(8,128)(2,1)S(1)}, u32[]{:S(2)}, u32[]{:S(2)}) async-start(bf16[16,128,128]{2,1,0:T(8,128)(2,1)} %get-tuple-element.7), calls=%async_computation.1 | async-start | bytes 1048576 | tf_op jit(solution)/shard_map/all_to_all | solution.py:341
  56.5 0.0 collective-permute-done.mate_ref
  56.5 10.4 %attend.2 = (bf16[16,64,128]{2,1,0:T(8,128)(2,1)S(1)}, f32[8,128]{1,0:T(8,128)S(1)}) custom-call(bf16[2,2048,128]{2,1,0:T(8,128)(2,1)S(1)} %assemble.1.own_ref, bf16[2,2048,128]{2,1,0:T(8,128)(2,1)} %collective-permute-done.mate_ref, bf16[16,392,128]{2,1,0:T(8,128)(2,1)S(1)} %all_to_all.15.in_ref.q_ref.ext_ref, ...), custom_call_target="tpu_custom_call" | custom-call | flops 5368709120 | bytes 2097152 | tf_op jit(solution)/shard_map/attend/pallas_call | solution.py:360
  67.0 4.6 %all-to-all-done.1.q_ref = bf16[16,128,128]{2,1,0:T(8,128)(2,1)S(1)} async-done(((bf16[16,128,128]{2,1,0:T(8,128)(2,1)}), bf16[16,128,128]{2,1,0:T(8,128)(2,1)S(1)}, u32[]{:S(2)}, u32[]{:S(2)}) %all-to-all-start.1) | async-done | bytes 524320 | tf_op jit(solution)/shard_map/all_to_all | solution.py:341
  71.6 0.0 copy-start
  71.6 10.5 %attend.3 = bf16[16,128,128]{2,1,0:T(8,128)(2,1)} custom-call(bf16[2,2048,128]{2,1,0:T(8,128)(2,1)S(1)} %assemble.1.own_ref, bf16[2,2048,128]{2,1,0:T(8,128)(2,1)} %collective-permute-done.mate_ref, bf16[16,128,128]{2,1,0:T(8,128)(2,1)S(1)} %all-to-all-done.1.q_ref, bf16[16,392,128]{2,1,0:T(8,128)(2,1)S(1)} %all_to_all.15.in_ref.q_ref.ext_ref, ...), custom_call_target="tpu_custom_call" | custom-call | flops 5368709120 | bytes 2097152 | tf_op jit(solution)/shard_map/attend/pallas_call | solution.py:360
  82.1 4.8 %all-to-all-start.2 = ((bf16[16,128,128]{2,1,0:T(8,128)(2,1)}), bf16[16,128,128]{2,1,0:T(8,128)(2,1)S(1)}, u32[]{:S(2)}, u32[]{:S(2)}) async-start(bf16[16,128,128]{2,1,0:T(8,128)(2,1)} %attend.3), calls=%async_computation.2 | async-start | bytes 1048576 | tf_op jit(solution)/shard_map/all_to_all | solution.py:411
  86.9 0.1 collective-permute-start.1
  87.0 1.2 %collective-permute-done.1 = f32[8,128]{1,0:T(8,128)S(1)} collective-permute-done((f32[8,128]{1,0:T(8,128)S(1)}, f32[8,128]{1,0:T(8,128)S(1)}, u32[]{:S(2)}, u32[]{:S(2)}) %collective-permute-start.1) | collective-permute-done | bytes 4128 | tf_op jit(solution)/shard_map/ppermute | solution.py:397
  88.1 0.0 copy-done
  88.1 0.6 fusion.1
  88.7 12.9 %all-to-all-done.2.in_ref = bf16[16,128,128]{2,1,0:T(8,128)(2,1)S(1)} async-done(((bf16[16,128,128]{2,1,0:T(8,128)(2,1)}), bf16[16,128,128]{2,1,0:T(8,128)(2,1)S(1)}, u32[]{:S(2)}, u32[]{:S(2)}) %all-to-all-start.2) | async-done | bytes 524320 | tf_op jit(solution)/shard_map/all_to_all | solution.py:411
  101.6 0.9 unpack.1
  (1 shorter events, 0.0 us)
Async XLA Ops:
  52.8 3.7 %collective-permute-start = (bf16[2,2048,128]{2,1,0:T(8,128)(2,1)S(1)}, bf16[2,2048,128]{2,1,0:T(8,128)(2,1)}, u32[]{:S(2)}, u32[]{:S(2)}) collective-permute-start(bf16[2,2048,128]{2,1,0:T(8,128)(2,1)S(1)} %assemble.1.own_ref), channel_id=1, source_target_pairs={{0,2},{2,0},{4,6},{6,4},{8,10},{10,8},{12,14},{14,12},{16,18},{18,... | collective-permute-start | bytes 3145736 | tf_op jit(solution)/shard_map/ppermute | solution.py:353
  52.9 18.7 %all-to-all-start.1 = ((bf16[16,128,128]{2,1,0:T(8,128)(2,1)}), bf16[16,128,128]{2,1,0:T(8,128)(2,1)S(1)}, u32[]{:S(2)}, u32[]{:S(2)}) async-start(bf16[16,128,128]{2,1,0:T(8,128)(2,1)} %get-tuple-element.7), calls=%async_computation.1 | async-start | bytes 1048576 | tf_op jit(solution)/shard_map/all_to_all | solution.py:341
  71.6 16.6 %copy-start = (f32[16]{0:T(128)S(1)}, f32[16]{0:T(128)}, u32[]{:S(2)}) copy-start(f32[16]{0:T(128)} %gate_ref.1) | copy-start | bytes 196
  82.1 19.6 %all-to-all-start.2 = ((bf16[16,128,128]{2,1,0:T(8,128)(2,1)}), bf16[16,128,128]{2,1,0:T(8,128)(2,1)S(1)}, u32[]{:S(2)}, u32[]{:S(2)}) async-start(bf16[16,128,128]{2,1,0:T(8,128)(2,1)} %attend.3), calls=%async_computation.2 | async-start | bytes 1048576 | tf_op jit(solution)/shard_map/all_to_all | solution.py:411
  86.9 1.2 %collective-permute-start.1 = (f32[8,128]{1,0:T(8,128)S(1)}, f32[8,128]{1,0:T(8,128)S(1)}, u32[]{:S(2)}, u32[]{:S(2)}) collective-permute-start(f32[8,128]{1,0:T(8,128)S(1)} %get-tuple-element.9), channel_id=1, source_target_pairs={{0,2},{2,0},{4,6},{6,4},{8,10},{10,8},{12,14},{14,12},{16,18},{18,... | collective-permute-start | bytes 12296 | tf_op jit(solution)/shard_map/ppermute | solution.py:397

commit v15 on v14

--- a/solution.py
+++ b/solution.py
@@ -26,7 +26,7 @@
     local_hbm,
     gate_ref,
     ids_ref,
-    first_hbm,
+    first_out,
     second_hbm,
     k_ref,
     v_ref,
@@ -37,7 +37,6 @@
     ext_ref,
     delta_ref,
     gate_rows,
-    first_out,
     second_out,
     sems,
     out_sems,
@@ -138,11 +137,6 @@
     for head in range(heads):
         ext_ref[bias_rows : bias_rows + 1, :] = delta_ref[head : head + 1, :]
         first_out[head, at + 2 * early :, :] = ext_ref[...].astype(jnp.bfloat16)
-        if head % 4 == 3:
-            some = slice(head - 3, head + 1)
-            copy = pltpu.make_async_copy(first_out.at[some], first_hbm.at[some], out_sems.at[0, head // 4])
-            copy.start()
-            sent.append(copy)
     for copy in sent:
         copy.wait()
 
@@ -157,13 +151,14 @@
 
 def attend(begin, count, q_at, ext_at, qblocks, width, tile, final, own_ref, mate_ref, q_ref, ext_ref, *refs):
     if final:
-        before_ref, out_ref, mark, minus, qx, dx, scores, high, total, acc, stage, sems = refs
+        before_ref, bias_ref, delta_ref, out_ref, mark, minus, qx, dx, scores, high, total, acc, stage, sems = refs
         early_copy = pltpu.make_async_copy(before_ref, out_ref.at[:, :begin, :], sems.at[0])
         early_copy.start()
     else:
-        out_ref, gate_ref, mark, minus, qx, dx, scores, high, total, acc = refs
+        out_ref, gate_ref, bias_next, delta_next, mark, minus, qx, dx, scores, high, total, acc = refs
+        bias_ref, delta_ref = qx.at[:, LANES:], dx.at[:, LANES:]
     sources = q_ref.shape[0]
-    units = qx.shape[1] // LANES - 1
+    units = bias_ref.shape[1] // LANES
     sides = (own_ref, mate_ref)
     steps_side = own_ref.shape[1] // width
     rows_unit = mark.shape[0]
@@ -185,25 +180,30 @@
         base = source * count
         qx[base : base + count, :LANES] = q_ref[source, q_at : q_at + count, :]
         dx[base : base + count, :LANES] = q_ref[source, q_at + count : q_at + 2 * count, :]
+        if final:
+            continue
         extra = ext_ref[source, ext_at:, :].astype(jnp.float32)
-        code = extra[:bias_rows]
-        upper = jnp.floor(code * 0.25)
-        code = upper if final else code - 4.0 * upper
-        second = jnp.where(code > 1.5, 1.0, 0.0)
-        first = code - 2.0 * second
-        for side, hit in enumerate((first, second)):
-            bias = jnp.where(hit > 0.5, 0.0, FAR)
-            for chunk in range(chunks):
-                lanes = (1 + side * chunks + chunk) * LANES
-                for block in range(count // BLK):
-                    at = chunk * per + block
-                    row = jnp.broadcast_to(bias[at : at + 1], (BLK, LANES)).astype(jnp.bfloat16)
-                    qx[base + block * BLK : base + (block + 1) * BLK, lanes : lanes + LANES] = row
-        if not final:
-            gate_sum = gate_sum + extra[bias_rows + 1 : bias_rows + 2]
+        gate_sum = gate_sum + extra[bias_rows + 1 : bias_rows + 2]
         wide = jnp.broadcast_to(extra[bias_rows : bias_rows + 1], (LANES, LANES)).T
         wide = jnp.where(wide_lane == 0, wide, 0.0).astype(jnp.bfloat16)
-        dx[base : base + count, LANES:] = wide[begin : begin + count]
+        dx[base : base + count, LANES:] = wide[:count]
+        delta_next[base : base + count, :] = wide[count:]
+        upper = jnp.floor(extra[:bias_rows] * 0.25)
+        for late, code in enumerate((extra[:bias_rows] - 4.0 * upper, upper)):
+            second = jnp.where(code > 1.5, 1.0, 0.0)
+            first = code - 2.0 * second
+            for side, hit in enumerate((first, second)):
+                bias = jnp.where(hit > 0.5, 0.0, FAR)
+                for chunk in range(chunks):
+                    at_lane = (side * chunks + chunk) * LANES
+                    for block in range(per):
+                        at = chunk * per + block
+                        row = jnp.broadcast_to(bias[at : at + 1], (BLK, LANES)).astype(jnp.bfloat16)
+                        rows = slice(base + block * BLK, base + (block + 1) * BLK)
+                        if late:
+                            bias_next[rows, at_lane : at_lane + LANES] = row
+                        else:
+                            qx[rows, LANES + at_lane : 2 * LANES + at_lane] = row
     if not final:
         gate_ref[...] = jnp.broadcast_to(gate_sum, gate_ref.shape)
 
@@ -216,8 +216,8 @@
                 def score(at, carry, side=side, ref=ref, unit=unit):
                     rows = pl.ds(pl.multiple_of(unit * rows_unit + at * width, width), width)
                     marks = pl.ds(pl.multiple_of(at * width, width), width)
-                    lanes = (1 + side * (units // 2) + unit) * LANES
-                    left = jnp.concatenate([qx[here, :LANES], qx[here, lanes : lanes + LANES]], axis=1)
+                    lanes = (side * (units // 2) + unit) * LANES
+                    left = jnp.concatenate([qx[here, :LANES], bias_ref[here, lanes : lanes + LANES]], axis=1)
                     right = jnp.concatenate([ref[0, rows, :], mark[marks, :]], axis=1)
                     got = lax.dot_general(
                         left, right, (((1,), (1,)), ((), ())), preferred_element_type=jnp.float32
@@ -238,7 +238,7 @@
             def back(at, carry, side=side, ref=ref):
                 rows = pl.ds(pl.multiple_of(at * width, width), width)
                 prod = lax.dot_general(
-                    dx[here, :],
+                    jnp.concatenate([dx[here, :LANES], delta_ref[here, :]], axis=1),
                     jnp.concatenate([ref[1, rows, :], minus[...]], axis=1),
                     (((1,), (1,)), ((), ())),
                     preferred_element_type=jnp.float32,
@@ -258,7 +258,7 @@
                 )
                 return carry
 
-            lax.fori_loop(0, steps_side, back, 0, unroll=2 if final else 1)
+            lax.fori_loop(0, steps_side, back, 0, unroll=2 if final else 2)
         weight = scale / jnp.sum(total[...], 1, keepdims=True)
         qx[here, :LANES] = (acc[...] * weight).astype(jnp.bfloat16)
         return carry
@@ -293,7 +293,7 @@
     members = heads
     chunks = shards // heads
     assert width == heads * LANES and shards % heads == 0 and groups % 2 == 0
-    assert rows_dev == 16 * BLK and heads * 8 == LANES and tokens == LANES
+    assert qblocks == 8 and rows_dev == 16 * BLK and heads * 8 == LANES and tokens == LANES
     half_shard = rows_dev // 2
     units = 2 * chunks
     early = tokens // 2
@@ -320,19 +320,18 @@
     second_shape = (members, 2 * late, LANES)
     first_out, second_out = pl.pallas_call(
         functools.partial(pack, heads, chunks, early),
-        out_shape=(pltpu.HBM(first_shape, bf16), pltpu.HBM(second_shape, bf16)),
+        out_shape=(pltpu.VMEM(first_shape, bf16), pltpu.HBM(second_shape, bf16)),
         in_specs=[hbm] * 6 + [smem, vmem],
-        out_specs=(hbm, hbm),
+        out_specs=(vmem, hbm),
         scratch_shapes=[pltpu.VMEM((half_shard, width), bf16)] * 2
         + [pltpu.VMEM((tokens, width), bf16)] * 4
         + [
             pltpu.VMEM((extra, LANES), jnp.float32),
             pltpu.VMEM((heads, LANES), jnp.float32),
             pltpu.VMEM((LANES, LANES), jnp.float32),
-            pltpu.VMEM(first_shape, bf16),
             pltpu.VMEM(second_shape, bf16),
             pltpu.SemaphoreType.DMA((2, 6)),
-            pltpu.SemaphoreType.DMA((2, heads // 4)),
+            pltpu.SemaphoreType.DMA((2, 2)),
         ],
         compiler_params=pltpu.CompilerParams(vmem_limit_bytes=56 << 20),
         name="pack",
@@ -365,8 +364,8 @@
             scratch_shapes=[
                 pltpu.VMEM((LANES * BLK, LANES), bf16),
                 pltpu.VMEM((step_width, LANES), bf16),
-                pltpu.VMEM((members * count, (1 + units) * LANES), bf16),
-                pltpu.VMEM((members * count, 2 * LANES), bf16),
+                pltpu.VMEM((members * count, (1 if final else 1 + units) * LANES), bf16),
+                pltpu.VMEM((members * count, (1 if final else 2) * LANES), bf16),
                 pltpu.VMEM((rows_all // step_width, tile, step_width), jnp.float32),
                 pltpu.VMEM((tile, LANES), jnp.float32),
                 pltpu.VMEM((tile, LANES), jnp.float32),
@@ -382,13 +381,18 @@
             name="attend",
         )(*args)
 
-    part, gate_sum = attend_some(
+    part, gate_sum, bias_late, delta_late = attend_some(
         0,
         early,
         2 * half_shard,
         False,
-        [jax.ShapeDtypeStruct((members, early, LANES), bf16), jax.ShapeDtypeStruct((8, LANES), jnp.float32)],
-        [vmem, vmem],
+        [
+            jax.ShapeDtypeStruct((members, early, LANES), bf16),
+            jax.ShapeDtypeStruct((8, LANES), jnp.float32),
+            jax.ShapeDtypeStruct((members * late, units * LANES), bf16),
+            jax.ShapeDtypeStruct((members * late, LANES), bf16),
+        ],
+        [vmem] * 4,
         own,
         mate,
         first_in,
@@ -407,6 +411,8 @@
         second_in,
         first_in,
         part,
+        bias_late,
+        delta_late,
     )
     home = exchange(grad)
     d_query = pl.pallas_call(

time: 103 us -> 104 us (level)
  local copies, waits for them, and re-layouts: 0.01 us -> 3.51 us
  Pallas kernels: 26.4 us -> 25.2 us
    unnamed x2 -> x10, local copies, waits for them, and re-layouts: 0.01 us -> 3.51 us
  transfers between devices with their start and end apart: 4 -> 4, of which waited for: 3 -> 3; matrix products, arithmetic and copies ran while one was open for 1% -> 1% of each run, Pallas kernels for 10% -> 9%
where the time goes in v15:
time: 104 us
  blocking collectives  47.4 us (46%)
  Pallas kernels  25.2 us (24%)
  waiting for transfers between devices  17.8 us (17%)
  starting transfers between devices  8.58 us (8%)
  local copies, waits for them, and re-layouts  3.51 us (3%)
    all_to_all x1, blocking collectives, local(): first_in = exchange(first_out)  47.4 us
    pallas_call x2, Pallas kernels, attend_some(): pl.pallas_call(functools.partial(attend, begin, count, q_at, ext_at, qblo...  20.1 us
    all_to_all x1, waiting for transfers between devices, local(): home = exchange(grad)  12.9 us
    all_to_all x1, starting transfers between devices, local(): home = exchange(grad)  4.85 us
    pallas_call x1, Pallas kernels, local(): pl.pallas_call(functools.partial(pack, heads, chunks, early), out_shape=(...  4.06 us
    all_to_all x1, waiting for transfers between devices, local(): second_in = exchange(second_out)  3.8 us
    all_to_all x1, starting transfers between devices, local(): second_in = exchange(second_out)  3.59 us
    unnamed x10, local copies, waits for them, and re-layouts  3.51 us
  transfers between devices with their start and end apart: 4, of which 3 were waited for; matrix products, arithmetic and copies ran while one was open for 1% of the time, Pallas kernels for 9%

profile of v15, /device:TPU:0, one launch (start us, length us, event | category | flops | bytes accessed | tf_op | source)
XLA Modules:
  0.0 103.9 jit_solution(3696310591456797723)
XLA Ops:
  0.6 4.1 %pack.1 = (bf16[16,392,128]{2,1,0:T(8,128)(2,1)S(1)}, bf16[16,128,128]{2,1,0:T(8,128)(2,1)}) custom-call(bf16[256,2048]{1,0:T(8,128)(2,1)} %k_hbm.1, bf16[256,2048]{1,0:T(8,128)(2,1)} %v_hbm.1, bf16[128,2048]{1,0:T(8,128)(2,1)} %bitcast.10, bf16[128,2048]{1,0:T(8,128)(2,1)} %bitcast.11, bf16[128,2048]{1,0:T(8,128)(2,1)} %bitcast.12, ...), custom_call_target="tpu_custom_call" | custom-call | tf_op jit(solution)/shard_map/pack/pallas_call | solution.py:321
  4.7 47.4 %all_to_all.15.in_ref.q_ref.ext_ref = bf16[16,392,128]{2,1,0:T(8,128)(2,1)S(1)} all-to-all(bf16[16,392,128]{2,1,0:T(8,128)(2,1)S(1)} %get-tuple-element.8), channel_id=1, replica_groups={{0,1,4,5,8,9,12,13,16,17,20,21,24,25,28,29},{2,3,6,7,10,11,14,15,18,19,..., dimensions={0} | all-to-all | bytes 3211264 | tf_op jit(solution)/shard_map/all_to_all | solution.py:339
  52.1 0.1 assemble.1.own_ref
  52.2 0.1 collective-permute-start
  52.3 3.6 %all-to-all-start.1 = ((bf16[16,128,128]{2,1,0:T(8,128)(2,1)}), bf16[16,128,128]{2,1,0:T(8,128)(2,1)S(1)}, u32[]{:S(2)}, u32[]{:S(2)}) async-start(bf16[16,128,128]{2,1,0:T(8,128)(2,1)} %get-tuple-element.9), calls=%async_computation.1 | async-start | bytes 1048576 | tf_op jit(solution)/shard_map/all_to_all | solution.py:340
  55.9 0.0 collective-permute-done.mate_ref
  55.9 9.7 %attend.2 = (bf16[16,64,128]{2,1,0:T(8,128)(2,1)S(1)}, f32[8,128]{1,0:T(8,128)S(1)}, bf16[1024,256]{1,0:T(8,128)(2,1)S(1)}, bf16[1024,128]{1,0:T(8,128)(2,1)S(1)}) custom-call(bf16[2,2048,128]{2,1,0:T(8,128)(2,1)S(1)} %assemble.1.own_ref, bf16[2,2048,128]{2,1,0:T(8,128)(2,1)} %collective-permute-done.mate_ref, ...), custom_call_target="tpu_custom_call" | custom-call | flops 5368709120 | bytes 2097152 | tf_op jit(solution)/shard_map/attend/pallas_call | solution.py:359
  65.6 0.0 copy-start
  65.6 0.8 copy-done
  66.4 0.0 copy-start.2
  66.4 0.7 copy-done.2
  67.1 3.8 %all-to-all-done.1.q_ref = bf16[16,128,128]{2,1,0:T(8,128)(2,1)S(1)} async-done(((bf16[16,128,128]{2,1,0:T(8,128)(2,1)}), bf16[16,128,128]{2,1,0:T(8,128)(2,1)S(1)}, u32[]{:S(2)}, u32[]{:S(2)}) %all-to-all-start.1) | async-done | bytes 524320 | tf_op jit(solution)/shard_map/all_to_all | solution.py:340
  70.9 0.0 copy-start.1
  70.9 1.0 %copy-done.1 = bf16[1024,256]{1,0:T(8,128)(2,1)S(1)} copy-done((bf16[1024,256]{1,0:T(8,128)(2,1)S(1)}, bf16[1024,256]{1,0:T(8,128)(2,1)}, u32[]{:S(2)}) %copy-start.1) | copy-done | bytes 524312
  72.0 0.0 copy-start.3
  72.0 0.9 copy-done.3
  72.9 0.0 copy-start.4
  72.9 10.4 %attend.3 = bf16[16,128,128]{2,1,0:T(8,128)(2,1)} custom-call(bf16[2,2048,128]{2,1,0:T(8,128)(2,1)S(1)} %assemble.1.own_ref, bf16[2,2048,128]{2,1,0:T(8,128)(2,1)} %collective-permute-done.mate_ref, bf16[16,128,128]{2,1,0:T(8,128)(2,1)S(1)} %all-to-all-done.1.q_ref, bf16[16,392,128]{2,1,0:T(8,128)(2,1)S(1)} %all_to_all.15.in_ref.q_ref.ext_ref, ...), custom_call_target="tpu_custom_call" | custom-call | flops 5368709120 | bytes 2097152 | tf_op jit(solution)/shard_map/attend/pallas_call | solution.py:359
  83.4 4.8 %all-to-all-start.2 = ((bf16[16,128,128]{2,1,0:T(8,128)(2,1)}), bf16[16,128,128]{2,1,0:T(8,128)(2,1)S(1)}, u32[]{:S(2)}, u32[]{:S(2)}) async-start(bf16[16,128,128]{2,1,0:T(8,128)(2,1)} %attend.3), calls=%async_computation.2 | async-start | bytes 1048576 | tf_op jit(solution)/shard_map/all_to_all | solution.py:417
  88.2 0.1 collective-permute-start.1
  88.3 1.2 %collective-permute-done.1 = f32[8,128]{1,0:T(8,128)S(1)} collective-permute-done((f32[8,128]{1,0:T(8,128)S(1)}, f32[8,128]{1,0:T(8,128)S(1)}, u32[]{:S(2)}, u32[]{:S(2)}) %collective-permute-start.1) | collective-permute-done | bytes 4128 | tf_op jit(solution)/shard_map/ppermute | solution.py:401
  89.4 0.0 copy-done.4
  89.4 0.6 fusion.1
  90.0 12.9 %all-to-all-done.2.in_ref = bf16[16,128,128]{2,1,0:T(8,128)(2,1)S(1)} async-done(((bf16[16,128,128]{2,1,0:T(8,128)(2,1)}), bf16[16,128,128]{2,1,0:T(8,128)(2,1)S(1)}, u32[]{:S(2)}, u32[]{:S(2)}) %all-to-all-start.2) | async-done | bytes 524320 | tf_op jit(solution)/shard_map/all_to_all | solution.py:417
  102.9 0.9 unpack.1
  (1 shorter events, 0.0 us)
Async XLA Ops:
  52.2 3.7 %collective-permute-start = (bf16[2,2048,128]{2,1,0:T(8,128)(2,1)S(1)}, bf16[2,2048,128]{2,1,0:T(8,128)(2,1)}, u32[]{:S(2)}, u32[]{:S(2)}) collective-permute-start(bf16[2,2048,128]{2,1,0:T(8,128)(2,1)S(1)} %assemble.1.own_ref), channel_id=1, source_target_pairs={{0,2},{2,0},{4,6},{6,4},{8,10},{10,8},{12,14},{14,12},{16,18},{18,... | collective-permute-start | bytes 3145736 | tf_op jit(solution)/shard_map/ppermute | solution.py:352
  52.3 18.7 %all-to-all-start.1 = ((bf16[16,128,128]{2,1,0:T(8,128)(2,1)}), bf16[16,128,128]{2,1,0:T(8,128)(2,1)S(1)}, u32[]{:S(2)}, u32[]{:S(2)}) async-start(bf16[16,128,128]{2,1,0:T(8,128)(2,1)} %get-tuple-element.9), calls=%async_computation.1 | async-start | bytes 1048576 | tf_op jit(solution)/shard_map/all_to_all | solution.py:340
  65.6 0.8 copy-start
  66.4 0.7 copy-start.2
  70.9 1.0 %copy-start.1 = (bf16[1024,256]{1,0:T(8,128)(2,1)S(1)}, bf16[1024,256]{1,0:T(8,128)(2,1)}, u32[]{:S(2)}) copy-start(bf16[1024,256]{1,0:T(8,128)(2,1)} %copy-done) | copy-start | bytes 1572868
  72.0 0.9 copy-start.3
  72.9 16.5 %copy-start.4 = (f32[16]{0:T(128)S(1)}, f32[16]{0:T(128)}, u32[]{:S(2)}) copy-start(f32[16]{0:T(128)} %gate_ref.1) | copy-start | bytes 196
  83.4 19.6 %all-to-all-start.2 = ((bf16[16,128,128]{2,1,0:T(8,128)(2,1)}), bf16[16,128,128]{2,1,0:T(8,128)(2,1)S(1)}, u32[]{:S(2)}, u32[]{:S(2)}) async-start(bf16[16,128,128]{2,1,0:T(8,128)(2,1)} %attend.3), calls=%async_computation.2 | async-start | bytes 1048576 | tf_op jit(solution)/shard_map/all_to_all | solution.py:417
  88.2 1.2 %collective-permute-start.1 = (f32[8,128]{1,0:T(8,128)S(1)}, f32[8,128]{1,0:T(8,128)S(1)}, u32[]{:S(2)}, u32[]{:S(2)}) collective-permute-start(f32[8,128]{1,0:T(8,128)S(1)} %get-tuple-element.13), channel_id=1, source_target_pairs={{0,2},{2,0},{4,6},{6,4},{8,10},{10,8},{12,14},{14,12},{16,18},{18,... | collective-permute-start | bytes 12296 | tf_op jit(solution)/shard_map/ppermute | solution.py:401

commit v16 on v14

--- a/solution.py
+++ b/solution.py
@@ -26,7 +26,7 @@
     local_hbm,
     gate_ref,
     ids_ref,
-    first_hbm,
+    first_out,
     second_hbm,
     k_ref,
     v_ref,
@@ -37,7 +37,6 @@
     ext_ref,
     delta_ref,
     gate_rows,
-    first_out,
     second_out,
     sems,
     out_sems,
@@ -138,11 +137,6 @@
     for head in range(heads):
         ext_ref[bias_rows : bias_rows + 1, :] = delta_ref[head : head + 1, :]
         first_out[head, at + 2 * early :, :] = ext_ref[...].astype(jnp.bfloat16)
-        if head % 4 == 3:
-            some = slice(head - 3, head + 1)
-            copy = pltpu.make_async_copy(first_out.at[some], first_hbm.at[some], out_sems.at[0, head // 4])
-            copy.start()
-            sent.append(copy)
     for copy in sent:
         copy.wait()
 
@@ -233,9 +227,8 @@
         high[...] = jnp.broadcast_to(jnp.max(high[...], 1, keepdims=True) * exponent, high.shape)
         total[...] = jnp.zeros_like(total)
         acc[...] = jnp.zeros_like(acc)
-        for side, ref in enumerate(sides):
-
-            def back(at, carry, side=side, ref=ref):
+        def back(at, carry):
+            for side, ref in enumerate(sides):
                 rows = pl.ds(pl.multiple_of(at * width, width), width)
                 prod = lax.dot_general(
                     dx[here, :],
@@ -256,9 +249,9 @@
                 acc[...] += jnp.dot(
                     jnp.concatenate(pieces, axis=1), ref[0, rows, :], preferred_element_type=jnp.float32
                 )
-                return carry
-
-            lax.fori_loop(0, steps_side, back, 0, unroll=2 if final else 1)
+            return carry
+
+        lax.fori_loop(0, steps_side, back, 0, unroll=1 if final else 2)
         weight = scale / jnp.sum(total[...], 1, keepdims=True)
         qx[here, :LANES] = (acc[...] * weight).astype(jnp.bfloat16)
         return carry
@@ -320,19 +313,18 @@
     second_shape = (members, 2 * late, LANES)
     first_out, second_out = pl.pallas_call(
         functools.partial(pack, heads, chunks, early),
-        out_shape=(pltpu.HBM(first_shape, bf16), pltpu.HBM(second_shape, bf16)),
+        out_shape=(pltpu.VMEM(first_shape, bf16), pltpu.HBM(second_shape, bf16)),
         in_specs=[hbm] * 6 + [smem, vmem],
-        out_specs=(hbm, hbm),
+        out_specs=(vmem, hbm),
         scratch_shapes=[pltpu.VMEM((half_shard, width), bf16)] * 2
         + [pltpu.VMEM((tokens, width), bf16)] * 4
         + [
             pltpu.VMEM((extra, LANES), jnp.float32),
             pltpu.VMEM((heads, LANES), jnp.float32),
             pltpu.VMEM((LANES, LANES), jnp.float32),
-            pltpu.VMEM(first_shape, bf16),
             pltpu.VMEM(second_shape, bf16),
             pltpu.SemaphoreType.DMA((2, 6)),
-            pltpu.SemaphoreType.DMA((2, heads // 4)),
+            pltpu.SemaphoreType.DMA((2, 2)),
         ],
         compiler_params=pltpu.CompilerParams(vmem_limit_bytes=56 << 20),
         name="pack",

time: 103 us -> 102 us (level)
  Pallas kernels: 26.4 us -> 24.6 us
  waiting for transfers between devices: 18.6 us -> 20 us
    all_to_all x1, waiting for transfers between devices: 4.6 us -> 5.96 us  [local(): second_in = exchange(second_out)]
    pallas_call x2, Pallas kernels: 20.9 us -> 19.6 us  [attend_some(): pl.pallas_call(functools.partial(attend, begin, count, q_at, ext_at, qblo...]
  transfers between devices with their start and end apart: 4 -> 4, of which waited for: 3 -> 3; matrix products, arithmetic and copies ran while one was open for 1% -> 1% of each run, Pallas kernels for 10% -> 9%
where the time goes in v16:
time: 102 us
  blocking collectives  47.4 us (46%)
  Pallas kernels  24.6 us (24%)
  waiting for transfers between devices  20 us (20%)
  starting transfers between devices  8.58 us (8%)
    all_to_all x1, blocking collectives, local(): first_in = exchange(first_out)  47.4 us
    pallas_call x2, Pallas kernels, attend_some(): pl.pallas_call(functools.partial(attend, begin, count, q_at, ext_at, qblo...  19.6 us
    all_to_all x1, waiting for transfers between devices, local(): home = exchange(grad)  12.9 us
    all_to_all x1, waiting for transfers between devices, local(): second_in = exchange(second_out)  5.96 us
    all_to_all x1, starting transfers between devices, local(): home = exchange(grad)  4.85 us
    pallas_call x1, Pallas kernels, local(): pl.pallas_call(functools.partial(pack, heads, chunks, early), out_shape=(...  4.06 us
    all_to_all x1, starting transfers between devices, local(): second_in = exchange(second_out)  3.59 us
  transfers between devices with their start and end apart: 4, of which 3 were waited for; matrix products, arithmetic and copies ran while one was open for 1% of the time, Pallas kernels for 9%

profile of v16, /device:TPU:0, one launch (start us, length us, event | category | flops | bytes accessed | tf_op | source)
XLA Modules:
  0.0 101.9 jit_solution(3926582007555793170)
XLA Ops:
  0.6 4.1 %pack.1 = (bf16[16,392,128]{2,1,0:T(8,128)(2,1)S(1)}, bf16[16,128,128]{2,1,0:T(8,128)(2,1)}) custom-call(bf16[256,2048]{1,0:T(8,128)(2,1)} %k_hbm.1, bf16[256,2048]{1,0:T(8,128)(2,1)} %v_hbm.1, bf16[128,2048]{1,0:T(8,128)(2,1)} %bitcast.10, bf16[128,2048]{1,0:T(8,128)(2,1)} %bitcast.11, bf16[128,2048]{1,0:T(8,128)(2,1)} %bitcast.12, ...), custom_call_target="tpu_custom_call" | custom-call | tf_op jit(solution)/shard_map/pack/pallas_call | solution.py:314
  4.7 47.4 %all_to_all.15.in_ref.q_ref.ext_ref = bf16[16,392,128]{2,1,0:T(8,128)(2,1)S(1)} all-to-all(bf16[16,392,128]{2,1,0:T(8,128)(2,1)S(1)} %get-tuple-element.6), channel_id=1, replica_groups={{0,1,4,5,8,9,12,13,16,17,20,21,24,25,28,29},{2,3,6,7,10,11,14,15,18,19,..., dimensions={0} | all-to-all | bytes 3211264 | tf_op jit(solution)/shard_map/all_to_all | solution.py:332
  52.1 0.1 assemble.1.own_ref
  52.2 0.1 collective-permute-start
  52.3 3.6 %all-to-all-start.1 = ((bf16[16,128,128]{2,1,0:T(8,128)(2,1)}), bf16[16,128,128]{2,1,0:T(8,128)(2,1)S(1)}, u32[]{:S(2)}, u32[]{:S(2)}) async-start(bf16[16,128,128]{2,1,0:T(8,128)(2,1)} %get-tuple-element.7), calls=%async_computation.1 | async-start | bytes 1048576 | tf_op jit(solution)/shard_map/all_to_all | solution.py:333
  55.9 0.0 collective-permute-done.mate_ref
  55.9 9.1 %attend.2 = (bf16[16,64,128]{2,1,0:T(8,128)(2,1)S(1)}, f32[8,128]{1,0:T(8,128)S(1)}) custom-call(bf16[2,2048,128]{2,1,0:T(8,128)(2,1)S(1)} %assemble.1.own_ref, bf16[2,2048,128]{2,1,0:T(8,128)(2,1)} %collective-permute-done.mate_ref, bf16[16,392,128]{2,1,0:T(8,128)(2,1)S(1)} %all_to_all.15.in_ref.q_ref.ext_ref, ...), custom_call_target="tpu_custom_call" | custom-call | flops 5368709120 | bytes 2097152 | tf_op jit(solution)/shard_map/attend/pallas_call | solution.py:352
  65.0 6.0 %all-to-all-done.1.q_ref = bf16[16,128,128]{2,1,0:T(8,128)(2,1)S(1)} async-done(((bf16[16,128,128]{2,1,0:T(8,128)(2,1)}), bf16[16,128,128]{2,1,0:T(8,128)(2,1)S(1)}, u32[]{:S(2)}, u32[]{:S(2)}) %all-to-all-start.1) | async-done | bytes 524320 | tf_op jit(solution)/shard_map/all_to_all | solution.py:333
  70.9 0.0 copy-start
  70.9 10.5 %attend.3 = bf16[16,128,128]{2,1,0:T(8,128)(2,1)} custom-call(bf16[2,2048,128]{2,1,0:T(8,128)(2,1)S(1)} %assemble.1.own_ref, bf16[2,2048,128]{2,1,0:T(8,128)(2,1)} %collective-permute-done.mate_ref, bf16[16,128,128]{2,1,0:T(8,128)(2,1)S(1)} %all-to-all-done.1.q_ref, bf16[16,392,128]{2,1,0:T(8,128)(2,1)S(1)} %all_to_all.15.in_ref.q_ref.ext_ref, ...), custom_call_target="tpu_custom_call" | custom-call | flops 5368709120 | bytes 2097152 | tf_op jit(solution)/shard_map/attend/pallas_call | solution.py:352
  81.4 4.8 %all-to-all-start.2 = ((bf16[16,128,128]{2,1,0:T(8,128)(2,1)}), bf16[16,128,128]{2,1,0:T(8,128)(2,1)S(1)}, u32[]{:S(2)}, u32[]{:S(2)}) async-start(bf16[16,128,128]{2,1,0:T(8,128)(2,1)} %attend.3), calls=%async_computation.2 | async-start | bytes 1048576 | tf_op jit(solution)/shard_map/all_to_all | solution.py:403
  86.3 0.1 collective-permute-start.1
  86.3 1.2 %collective-permute-done.1 = f32[8,128]{1,0:T(8,128)S(1)} collective-permute-done((f32[8,128]{1,0:T(8,128)S(1)}, f32[8,128]{1,0:T(8,128)S(1)}, u32[]{:S(2)}, u32[]{:S(2)}) %collective-permute-start.1) | collective-permute-done | bytes 4128 | tf_op jit(solution)/shard_map/ppermute | solution.py:389
  87.5 0.0 copy-done
  87.5 0.6 fusion.1
  88.1 12.9 %all-to-all-done.2.in_ref = bf16[16,128,128]{2,1,0:T(8,128)(2,1)S(1)} async-done(((bf16[16,128,128]{2,1,0:T(8,128)(2,1)}), bf16[16,128,128]{2,1,0:T(8,128)(2,1)S(1)}, u32[]{:S(2)}, u32[]{:S(2)}) %all-to-all-start.2) | async-done | bytes 524320 | tf_op jit(solution)/shard_map/all_to_all | solution.py:403
  101.0 0.9 unpack.1
  (1 shorter events, 0.0 us)
Async XLA Ops:
  52.2 3.7 %collective-permute-start = (bf16[2,2048,128]{2,1,0:T(8,128)(2,1)S(1)}, bf16[2,2048,128]{2,1,0:T(8,128)(2,1)}, u32[]{:S(2)}, u32[]{:S(2)}) collective-permute-start(bf16[2,2048,128]{2,1,0:T(8,128)(2,1)S(1)} %assemble.1.own_ref), channel_id=1, source_target_pairs={{0,2},{2,0},{4,6},{6,4},{8,10},{10,8},{12,14},{14,12},{16,18},{18,... | collective-permute-start | bytes 3145736 | tf_op jit(solution)/shard_map/ppermute | solution.py:345
  52.3 18.7 %all-to-all-start.1 = ((bf16[16,128,128]{2,1,0:T(8,128)(2,1)}), bf16[16,128,128]{2,1,0:T(8,128)(2,1)S(1)}, u32[]{:S(2)}, u32[]{:S(2)}) async-start(bf16[16,128,128]{2,1,0:T(8,128)(2,1)} %get-tuple-element.7), calls=%async_computation.1 | async-start | bytes 1048576 | tf_op jit(solution)/shard_map/all_to_all | solution.py:333
  70.9 16.6 %copy-start = (f32[16]{0:T(128)S(1)}, f32[16]{0:T(128)}, u32[]{:S(2)}) copy-start(f32[16]{0:T(128)} %gate_ref.1) | copy-start | bytes 196
  81.4 19.6 %all-to-all-start.2 = ((bf16[16,128,128]{2,1,0:T(8,128)(2,1)}), bf16[16,128,128]{2,1,0:T(8,128)(2,1)S(1)}, u32[]{:S(2)}, u32[]{:S(2)}) async-start(bf16[16,128,128]{2,1,0:T(8,128)(2,1)} %attend.3), calls=%async_computation.2 | async-start | bytes 1048576 | tf_op jit(solution)/shard_map/all_to_all | solution.py:403
  86.3 1.2 %collective-permute-start.1 = (f32[8,128]{1,0:T(8,128)S(1)}, f32[8,128]{1,0:T(8,128)S(1)}, u32[]{:S(2)}, u32[]{:S(2)}) collective-permute-start(f32[8,128]{1,0:T(8,128)S(1)} %get-tuple-element.9), channel_id=1, source_target_pairs={{0,2},{2,0},{4,6},{6,4},{8,10},{10,8},{12,14},{14,12},{16,18},{18,... | collective-permute-start | bytes 12296 | tf_op jit(solution)/shard_map/ppermute | solution.py:389

commit v17 on v16

--- a/solution.py
+++ b/solution.py
@@ -251,7 +251,7 @@
                 )
             return carry
 
-        lax.fori_loop(0, steps_side, back, 0, unroll=1 if final else 2)
+        lax.fori_loop(0, steps_side, back, 0, unroll=2 if final else 2)
         weight = scale / jnp.sum(total[...], 1, keepdims=True)
         qx[here, :LANES] = (acc[...] * weight).astype(jnp.bfloat16)
         return carry

time: 102 us -> 102 us (level)
  no operation moved by 1% of the time
where the time goes in v17:
time: 102 us; the launch traced here: 101 us
  blocking collectives  47.4 us (46%)
  Pallas kernels  24 us (24%)
  waiting for transfers between devices  20 us (20%)
  starting transfers between devices  8.58 us (8%)
    all_to_all x1, blocking collectives, local(): first_in = exchange(first_out)  47.4 us
    pallas_call x2, Pallas kernels, attend_some(): pl.pallas_call(functools.partial(attend, begin, count, q_at, ext_at, qblo...  18.9 us
    all_to_all x1, waiting for transfers between devices, local(): home = exchange(grad)  12.9 us
    all_to_all x1, waiting for transfers between devices, local(): second_in = exchange(second_out)  5.96 us
    all_to_all x1, starting transfers between devices, local(): home = exchange(grad)  4.85 us
    pallas_call x1, Pallas kernels, local(): pl.pallas_call(functools.partial(pack, heads, chunks, early), out_shape=(...  4.06 us
    all_to_all x1, starting transfers between devices, local(): second_in = exchange(second_out)  3.59 us
  transfers between devices with their start and end apart: 4, of which 3 were waited for; matrix products, arithmetic and copies ran while one was open for 1% of the time, Pallas kernels for 9%

profile of v17, /device:TPU:0, one launch (start us, length us, event | category | flops | bytes accessed | tf_op | source)
XLA Modules:
  0.0 101.3 jit_solution(6565560252255924062)
XLA Ops:
  0.6 4.1 %pack.1 = (bf16[16,392,128]{2,1,0:T(8,128)(2,1)S(1)}, bf16[16,128,128]{2,1,0:T(8,128)(2,1)}) custom-call(bf16[256,2048]{1,0:T(8,128)(2,1)} %k_hbm.1, bf16[256,2048]{1,0:T(8,128)(2,1)} %v_hbm.1, bf16[128,2048]{1,0:T(8,128)(2,1)} %bitcast.10, bf16[128,2048]{1,0:T(8,128)(2,1)} %bitcast.11, bf16[128,2048]{1,0:T(8,128)(2,1)} %bitcast.12, ...), custom_call_target="tpu_custom_call" | custom-call | tf_op jit(solution)/shard_map/pack/pallas_call | solution.py:314
  4.7 47.4 %all_to_all.15.in_ref.q_ref.ext_ref = bf16[16,392,128]{2,1,0:T(8,128)(2,1)S(1)} all-to-all(bf16[16,392,128]{2,1,0:T(8,128)(2,1)S(1)} %get-tuple-element.6), channel_id=1, replica_groups={{0,1,4,5,8,9,12,13,16,17,20,21,24,25,28,29},{2,3,6,7,10,11,14,15,18,19,..., dimensions={0} | all-to-all | bytes 3211264 | tf_op jit(solution)/shard_map/all_to_all | solution.py:332
  52.1 0.1 assemble.1.own_ref
  52.2 0.1 collective-permute-start
  52.3 3.6 %all-to-all-start.1 = ((bf16[16,128,128]{2,1,0:T(8,128)(2,1)}), bf16[16,128,128]{2,1,0:T(8,128)(2,1)S(1)}, u32[]{:S(2)}, u32[]{:S(2)}) async-start(bf16[16,128,128]{2,1,0:T(8,128)(2,1)} %get-tuple-element.7), calls=%async_computation.1 | async-start | bytes 1048576 | tf_op jit(solution)/shard_map/all_to_all | solution.py:333
  55.9 0.0 collective-permute-done.mate_ref
  55.9 9.1 %attend.2 = (bf16[16,64,128]{2,1,0:T(8,128)(2,1)S(1)}, f32[8,128]{1,0:T(8,128)S(1)}) custom-call(bf16[2,2048,128]{2,1,0:T(8,128)(2,1)S(1)} %assemble.1.own_ref, bf16[2,2048,128]{2,1,0:T(8,128)(2,1)} %collective-permute-done.mate_ref, bf16[16,392,128]{2,1,0:T(8,128)(2,1)S(1)} %all_to_all.15.in_ref.q_ref.ext_ref, ...), custom_call_target="tpu_custom_call" | custom-call | flops 5368709120 | bytes 2097152 | tf_op jit(solution)/shard_map/attend/pallas_call | solution.py:352
  65.0 6.0 %all-to-all-done.1.q_ref = bf16[16,128,128]{2,1,0:T(8,128)(2,1)S(1)} async-done(((bf16[16,128,128]{2,1,0:T(8,128)(2,1)}), bf16[16,128,128]{2,1,0:T(8,128)(2,1)S(1)}, u32[]{:S(2)}, u32[]{:S(2)}) %all-to-all-start.1) | async-done | bytes 524320 | tf_op jit(solution)/shard_map/all_to_all | solution.py:333
  70.9 0.0 copy-start
  70.9 9.9 %attend.3 = bf16[16,128,128]{2,1,0:T(8,128)(2,1)} custom-call(bf16[2,2048,128]{2,1,0:T(8,128)(2,1)S(1)} %assemble.1.own_ref, bf16[2,2048,128]{2,1,0:T(8,128)(2,1)} %collective-permute-done.mate_ref, bf16[16,128,128]{2,1,0:T(8,128)(2,1)S(1)} %all-to-all-done.1.q_ref, bf16[16,392,128]{2,1,0:T(8,128)(2,1)S(1)} %all_to_all.15.in_ref.q_ref.ext_ref, ...), custom_call_target="tpu_custom_call" | custom-call | flops 5368709120 | bytes 2097152 | tf_op jit(solution)/shard_map/attend/pallas_call | solution.py:352
  80.8 4.8 %all-to-all-start.2 = ((bf16[16,128,128]{2,1,0:T(8,128)(2,1)}), bf16[16,128,128]{2,1,0:T(8,128)(2,1)S(1)}, u32[]{:S(2)}, u32[]{:S(2)}) async-start(bf16[16,128,128]{2,1,0:T(8,128)(2,1)} %attend.3), calls=%async_computation.2 | async-start | bytes 1048576 | tf_op jit(solution)/shard_map/all_to_all | solution.py:403
  85.6 0.1 collective-permute-start.1
  85.7 1.2 %collective-permute-done.1 = f32[8,128]{1,0:T(8,128)S(1)} collective-permute-done((f32[8,128]{1,0:T(8,128)S(1)}, f32[8,128]{1,0:T(8,128)S(1)}, u32[]{:S(2)}, u32[]{:S(2)}) %collective-permute-start.1) | collective-permute-done | bytes 4128 | tf_op jit(solution)/shard_map/ppermute | solution.py:389
  86.9 0.0 copy-done
  86.9 0.6 fusion.1
  87.5 12.9 %all-to-all-done.2.in_ref = bf16[16,128,128]{2,1,0:T(8,128)(2,1)S(1)} async-done(((bf16[16,128,128]{2,1,0:T(8,128)(2,1)}), bf16[16,128,128]{2,1,0:T(8,128)(2,1)S(1)}, u32[]{:S(2)}, u32[]{:S(2)}) %all-to-all-start.2) | async-done | bytes 524320 | tf_op jit(solution)/shard_map/all_to_all | solution.py:403
  100.4 0.9 unpack.1
  (1 shorter events, 0.0 us)
Async XLA Ops:
  52.2 3.7 %collective-permute-start = (bf16[2,2048,128]{2,1,0:T(8,128)(2,1)S(1)}, bf16[2,2048,128]{2,1,0:T(8,128)(2,1)}, u32[]{:S(2)}, u32[]{:S(2)}) collective-permute-start(bf16[2,2048,128]{2,1,0:T(8,128)(2,1)S(1)} %assemble.1.own_ref), channel_id=1, source_target_pairs={{0,2},{2,0},{4,6},{6,4},{8,10},{10,8},{12,14},{14,12},{16,18},{18,... | collective-permute-start | bytes 3145736 | tf_op jit(solution)/shard_map/ppermute | solution.py:345
  52.3 18.7 %all-to-all-start.1 = ((bf16[16,128,128]{2,1,0:T(8,128)(2,1)}), bf16[16,128,128]{2,1,0:T(8,128)(2,1)S(1)}, u32[]{:S(2)}, u32[]{:S(2)}) async-start(bf16[16,128,128]{2,1,0:T(8,128)(2,1)} %get-tuple-element.7), calls=%async_computation.1 | async-start | bytes 1048576 | tf_op jit(solution)/shard_map/all_to_all | solution.py:333
  70.9 16.0 %copy-start = (f32[16]{0:T(128)S(1)}, f32[16]{0:T(128)}, u32[]{:S(2)}) copy-start(f32[16]{0:T(128)} %gate_ref.1) | copy-start | bytes 196
  80.8 19.6 %all-to-all-start.2 = ((bf16[16,128,128]{2,1,0:T(8,128)(2,1)}), bf16[16,128,128]{2,1,0:T(8,128)(2,1)S(1)}, u32[]{:S(2)}, u32[]{:S(2)}) async-start(bf16[16,128,128]{2,1,0:T(8,128)(2,1)} %attend.3), calls=%async_computation.2 | async-start | bytes 1048576 | tf_op jit(solution)/shard_map/all_to_all | solution.py:403
  85.6 1.2 %collective-permute-start.1 = (f32[8,128]{1,0:T(8,128)S(1)}, f32[8,128]{1,0:T(8,128)S(1)}, u32[]{:S(2)}, u32[]{:S(2)}) collective-permute-start(f32[8,128]{1,0:T(8,128)S(1)} %get-tuple-element.9), channel_id=1, source_target_pairs={{0,2},{2,0},{4,6},{6,4},{8,10},{10,8},{12,14},{14,12},{16,18},{18,... | collective-permute-start | bytes 12296 | tf_op jit(solution)/shard_map/ppermute | solution.py:389
